TPU v7x, 32 devices: a whole 2x2x4 slice. The times are simulated.
32 devices in a mesh: col: 8 (over z, x), row: 4 (over y, core).
Axes of the slice: x: 2, y: 2, z: 4, core: 2. Of those that a mesh axis runs over, the one named last changes fastest.
Arguments:
- trailing: float32 [12288, 4096], P('row', 'col'), may hold values from -6 to 6
- panel_rows: float32 [12288, 512], P(('row', 'col')), may hold values from -6 to 6
- pivot_block: float32 [512, 512], P('col'), as said below
- panel_fill: int32 [48, 2], replicated, may hold values 0 or 1
Outputs:
- updated: float32 [12288, 4096], P('row', 'col')
- panel_factor: float32 [12288, 512], P(('row', 'col'))
Inputs may be any that keep to these rules, and one draw needn't show every extreme that they name: `pivot_block`: Symmetric; each diagonal entry exceeds the sum of the magnitudes of the other entries of its row by at least 1. `panel_fill`: each entry is 1 with probability 0.15, independently of the others.
All inputs are finite; a program needn't handle non-finite values.
Results may differ from a plain program's by a relative error of at most 0.00008.
Values sent between devices are 32-bit elements; how exact they have to be, the bound alone decides.
No kernel may reach another device: no remote copies, remote signals or barrier semaphores. Data moves between devices by JAX's collectives and lax.ppermute only.
A program may use at most 128 MiB of HBM per device.

v0:
```python
import functools
import math

import jax
import jax.numpy as jnp
from jax import lax
from jax.experimental import pallas as pl
from jax.experimental.pallas import tpu as pltpu
from jax.sharding import PartitionSpec as P

F32, BF16 = jnp.float32, jnp.bfloat16
VMEM = pl.BlockSpec(memory_space=pltpu.VMEM)
SMEM = pl.BlockSpec(memory_space=pltpu.SMEM)
ANY = pl.BlockSpec(memory_space=pl.ANY)
COARSE_STEPS = 2
FINE_STEPS = 16
RESIDUAL = 5e-4


def halves(value):
    high = value.astype(BF16)
    return high, (value - high.astype(F32)).astype(BF16)


def dot(a, b, dims):
    return lax.dot_general(a, b, (dims, ((), ())), preferred_element_type=F32)


NN, NT, TN = ((1,), (0,)), ((1,), (1,)), ((0,), (0,))


def dot3(a, b, dims):
    (ah, al), (bh, bl) = a, b
    return dot(ah, bh, dims) + (dot(ah, bl, dims) + dot(al, bh, dims))


def inverse_factor_kernel(a_ref, w_ref, s_ref, flag):
    n = a_ref.shape[0]
    rows = lax.broadcasted_iota(jnp.int32, (n, n), 0)
    cols = lax.broadcasted_iota(jnp.int32, (n, n), 1)
    eye = (rows == cols).astype(F32)
    take = jnp.where(rows > cols, 1.0, 0.5 * eye)
    a = a_ref[...]
    diag_row = jnp.sum(a * eye, axis=0, keepdims=True)
    diag_col = jnp.sum(a * eye, axis=1, keepdims=True)
    scale_row, scale_col = lax.rsqrt(diag_row), lax.rsqrt(diag_col)
    scaled = jnp.where(rows == cols, 1.0, a * scale_row * scale_col)
    s_ref[...] = scaled
    scaled_parts = halves(scaled)
    w = eye - take * (scaled - eye)
    for _ in range(COARSE_STEPS):
        wh = w.astype(BF16)
        t = dot(wh, scaled_parts[0], NN).astype(BF16)
        change = take * (dot(t, wh, NT) - eye)
        w = w - dot(change.astype(BF16), wh, NN)
    w_ref[...] = w
    flag[0] = 0

    def fine(state):
        step, _ = state
        w = w_ref[...]
        parts = halves(w)
        t = halves(dot3(parts, halves(s_ref[...]), NN))
        residual = dot3(t, parts, NT) - eye
        w_ref[...] = w - dot((take * residual).astype(BF16), parts[0], NN)
        return step + 1, jnp.sum(residual * residual)

    _, left = lax.while_loop(
        lambda state: jnp.logical_and(state[0] < FINE_STEPS, jnp.logical_not(state[1] < RESIDUAL**2)),
        fine,
        (jnp.int32(0), jnp.float32(1.0)),
    )
    done = left < RESIDUAL**2

    @pl.when(jnp.logical_not(done))
    def _():
        w_ref[...] = eye

        def eliminate(j, carry):
            row = s_ref[pl.ds(j, 1), :]
            pick = lax.broadcasted_iota(jnp.int32, (1, n), 1) == j
            pivot = jnp.sum(jnp.where(pick, row, 0.0), axis=1, keepdims=True)
            column = jnp.sum(jnp.where(pick, s_ref[...], 0.0), axis=1, keepdims=True)
            below = lax.broadcasted_iota(jnp.int32, (n, 1), 0) > j
            ratio = jnp.where(below, column / pivot, 0.0)
            s_ref[...] = s_ref[...] - ratio * row
            w_ref[...] = w_ref[...] - ratio * w_ref[pl.ds(j, 1), :]
            return carry

        lax.fori_loop(0, n, eliminate, 0)
        pivots = jnp.sum(s_ref[...] * eye, axis=1, keepdims=True)
        w_ref[...] = w_ref[...] * lax.rsqrt(pivots)

    w_ref[...] = w_ref[...] * scale_row


def inverse_factor(pivot):
    n = pivot.shape[0]
    return pl.pallas_call(
        inverse_factor_kernel,
        out_shape=jax.ShapeDtypeStruct((n, n), F32),
        in_specs=[VMEM],
        out_specs=VMEM,
        scratch_shapes=[pltpu.VMEM((n, n), F32), pltpu.SMEM((1,), jnp.int32)],
        compiler_params=pltpu.CompilerParams(vmem_limit_bytes=32 * 2**20),
        cost_estimate=pl.CostEstimate(flops=40 * n**3, bytes_accessed=8 * n * n, transcendentals=0),
    )(pivot)


class Sizes:
    def __init__(self, trailing, panel_rows, panel_fill):
        self.cols, self.rows = lax.axis_size("col"), lax.axis_size("row")
        self.block = panel_rows.shape[1] // 2
        self.piece = panel_rows.shape[0]
        self.unit = math.gcd(self.piece, self.block)
        self.per_piece = self.piece // self.unit
        self.per_block = self.block // self.unit
        self.slab = self.piece * self.cols
        self.width = trailing.shape[1]
        self.tiles = self.cols * self.per_piece

    def source(self, c):
        slab = c * self.width // self.slab
        return slab, (c * self.width - slab * self.slab) // self.piece

    def sources(self):
        found = []
        for c in range(self.cols):
            slab, first = self.source(c)
            last = ((c + 1) * self.width - 1 - slab * self.slab) // self.piece
            found.append(last - first + 1)
        return found


def unit_flag(sizes, fill_ref, piece_index, unit, panel):
    block = (piece_index * sizes.per_piece + unit) // sizes.per_block
    return fill_ref[block * 2 + panel]


def pack_kernel(sizes, cap, where_ref, fill_ref, panel_ref, out_ref, sems):
    piece = where_ref[1] * sizes.cols + where_ref[0]
    slot = jnp.int32(0)
    started = []
    for u in range(sizes.per_piece):
        for p in range(2):
            flag = unit_flag(sizes, fill_ref, piece, u, p) != 0
            copy = pltpu.make_async_copy(
                panel_ref.at[pl.ds(u * sizes.unit, sizes.unit), pl.ds(p * sizes.block, sizes.block)],
                out_ref.at[jnp.minimum(slot, cap - 1)],
                sems.at[u * 2 + p],
            )
            keep = jnp.logical_and(flag, slot < cap)
            pl.when(keep)(copy.start)
            started.append((keep, copy))
            slot = slot + flag.astype(jnp.int32)
    for keep, copy in started:
        pl.when(keep)(copy.wait)


def pack(sizes, cap, where, fill, panel):
    return pl.pallas_call(
        functools.partial(pack_kernel, sizes, cap),
        out_shape=jax.ShapeDtypeStruct((cap, sizes.unit, sizes.block), F32),
        in_specs=[SMEM, SMEM, ANY],
        out_specs=ANY,
        scratch_shapes=[pltpu.SemaphoreType.DMA((2 * sizes.per_piece,))],
        cost_estimate=pl.CostEstimate(flops=0, bytes_accessed=2 * panel.size * 4, transcendentals=0),
    )(where, fill, panel)


def apply_factor_kernel(sizes, cap, lists, where_ref, fill_ref, w_ref, panel_ref, *refs):
    list_refs, (x_ref, high_ref, low_ref, masked, column) = refs[:lists], refs[lists:]
    c, r = where_ref[0], where_ref[1]
    own = r * sizes.cols + c
    for u in range(sizes.per_piece):
        for p in range(2):
            at = (pl.ds(u * sizes.unit, sizes.unit), pl.ds(p * sizes.block, sizes.block))
            flag = unit_flag(sizes, fill_ref, own, u, p) != 0
            masked[at] = jnp.where(flag, panel_ref[at], 0.0)
    w = halves(w_ref[...])
    x_ref[...] = dot3(halves(masked[...]), w, NT)
    column[...] = jnp.zeros_like(column)
    slab = c * sizes.width // sizes.slab
    first = (c * sizes.width - slab * sizes.slab) // sizes.piece
    for j, list_ref in enumerate(list_refs):
        piece = slab * sizes.cols + first + j
        inside = first + j < sizes.cols
        piece = jnp.where(inside, piece, 0)
        slot = jnp.int32(0)
        for u in range(sizes.per_piece):
            at_row = (piece * sizes.per_piece + u) * sizes.unit - c * sizes.width
            needed = jnp.logical_and(inside, jnp.logical_and(at_row >= 0, at_row < sizes.width))
            start = pl.multiple_of(jnp.where(needed, at_row, 0), sizes.unit)
            for p in range(2):
                flag = unit_flag(sizes, fill_ref, piece, u, p) != 0

                @pl.when(jnp.logical_and(flag, needed))
                def _(slot=slot, p=p, start=start, list_ref=list_ref):
                    column[pl.ds(start, sizes.unit), pl.ds(p * sizes.block, sizes.block)] = list_ref[
                        jnp.minimum(slot, cap - 1)
                    ]

                slot = slot + flag.astype(jnp.int32)
    solved = dot3(w, halves(column[...]), NT)
    high, low = halves(dot3(w, halves(solved), TN))
    high_ref[...] = high
    low_ref[...] = low


def apply_factor(sizes, cap, where, fill, w, panel, lists):
    n = w.shape[0]
    return pl.pallas_call(
        functools.partial(apply_factor_kernel, sizes, cap, len(lists)),
        out_shape=(
            jax.ShapeDtypeStruct(panel.shape, F32),
            jax.ShapeDtypeStruct((n, sizes.width), BF16),
            jax.ShapeDtypeStruct((n, sizes.width), BF16),
        ),
        in_specs=[SMEM, SMEM] + [VMEM] * (2 + len(lists)),
        out_specs=(VMEM, VMEM, VMEM),
        scratch_shapes=[pltpu.VMEM(panel.shape, F32), pltpu.VMEM((sizes.width, n), F32)],
        compiler_params=pltpu.CompilerParams(vmem_limit_bytes=40 * 2**20),
        cost_estimate=pl.CostEstimate(flops=16 * n**3, bytes_accessed=12 * n * n, transcendentals=0),
    )(where, fill, w, panel, *lists)


def update_kernel(sizes, cap, where_ref, fill_ref, high_ref, low_ref, window_ref, *refs):
    lists, (out_ref, tiles, units, in_sems, unit_sems, out_sems) = refs[: sizes.cols], refs[sizes.cols :]
    c, r = where_ref[0], where_ref[1]

    def place(k):
        return jnp.bitwise_xor(c, k)

    def flags_of(t):
        piece = r * sizes.cols + place(t // sizes.per_piece)
        return [unit_flag(sizes, fill_ref, piece, t % sizes.per_piece, p) != 0 for p in range(2)]

    def rows_of(t):
        start = (place(t // sizes.per_piece) * sizes.per_piece + t % sizes.per_piece) * sizes.unit
        return pl.ds(pl.multiple_of(start, sizes.unit), sizes.unit)

    def tile_in(t):
        return pltpu.make_async_copy(window_ref.at[rows_of(t)], tiles.at[t], in_sems.at[t])

    def tile_out(t):
        return pltpu.make_async_copy(tiles.at[t], out_ref.at[rows_of(t)], out_sems.at[t])

    for k in range(sizes.cols):
        slot = jnp.int32(0)
        for u in range(sizes.per_piece):
            t = k * sizes.per_piece + u
            flags = flags_of(t)
            pl.when(jnp.logical_or(*flags))(tile_in(t).start)
            for p in range(2):
                copy = pltpu.make_async_copy(
                    lists[k].at[jnp.minimum(slot, cap - 1)], units.at[t, p], unit_sems.at[t, p]
                )
                pl.when(flags[p])(copy.start)
                slot = slot + flags[p].astype(jnp.int32)

    @pl.loop(0, sizes.tiles)
    def _(t):
        flags = flags_of(t)

        @pl.when(jnp.logical_or(*flags))
        def _():
            tile_in(t).wait()
            for p in range(2):

                @pl.when(flags[p])
                def _(p=p):
                    pltpu.make_async_copy(lists[0].at[0], units.at[t, p], unit_sems.at[t, p]).wait()
                    at = pl.ds(p * sizes.block, sizes.block)
                    right = (high_ref[at, :], low_ref[at, :])
                    tiles[t] = tiles[t] - dot3(halves(units[t, p]), right, NN)

            tile_out(t).start()

    @pl.loop(0, sizes.tiles)
    def _(t):
        pl.when(jnp.logical_or(*flags_of(t)))(tile_out(t).wait)


def update(sizes, cap, where, fill, high, low, window, lists):
    tiles = sizes.tiles
    return pl.pallas_call(
        functools.partial(update_kernel, sizes, cap),
        out_shape=jax.ShapeDtypeStruct(window.shape, F32),
        in_specs=[SMEM, SMEM, VMEM, VMEM] + [ANY] * (1 + len(lists)),
        out_specs=ANY,
        input_output_aliases={4: 0},
        scratch_shapes=[
            pltpu.VMEM((tiles, sizes.unit, sizes.width), F32),
            pltpu.VMEM((tiles, 2, sizes.unit, sizes.block), F32),
            pltpu.SemaphoreType.DMA((tiles,)),
            pltpu.SemaphoreType.DMA((tiles, 2)),
            pltpu.SemaphoreType.DMA((tiles,)),
        ],
        compiler_params=pltpu.CompilerParams(vmem_limit_bytes=32 * 2**20),
        cost_estimate=pl.CostEstimate(flops=10**9, bytes_accessed=6 * 10**6, transcendentals=0),
    )(where, fill, high, low, window, *lists)


def swap(value, axis, step):
    size = lax.axis_size(axis)
    return lax.ppermute(value, axis, [(i, i ^ step) for i in range(size)])


def doubled(value, axis):
    size, step = lax.axis_size(axis), 1
    index = lax.axis_index(axis)
    while step < size:
        other = swap(value, axis, step)
        second = (index & step) != 0
        value = jnp.where(
            second, jnp.concatenate([other, value], 0), jnp.concatenate([value, other], 0)
        )
        step *= 2
    return value


def gather_pivot(pivot_block):
    share = pivot_block.shape[0] // lax.axis_size("row")
    own = lax.dynamic_slice_in_dim(pivot_block, lax.axis_index("row") * share, share, 0)
    cols, rows = lax.axis_size("col"), lax.axis_size("row")
    by_col = doubled(own[None], "col")
    both = doubled(by_col[None], "row")
    return both.transpose(1, 0, 2, 3).reshape(cols * rows * share, -1)


def gather_lists(own, cols):
    found = [own] + [swap(own, "col", k) for k in range(2, cols, 2)]
    lists = []
    for value in found:
        lists += [value, swap(value, "col", 1)]
    return lists


def gather_column(sizes, own):
    counts = sizes.sources()
    r, c = lax.axis_index("row"), lax.axis_index("col")
    target = c * sizes.width // sizes.slab
    values = []
    for j in range(max(counts)):
        pairs = []
        for at in range(sizes.cols):
            slab, first = sizes.source(at)
            if j < counts[at]:
                pairs.append(((first + j) * sizes.rows + slab, at * sizes.rows + slab))
        values.append(lax.ppermute(own, ("col", "row"), pairs))
    value = jnp.stack(values)
    step = sizes.rows // 2
    while step:
        other = swap(value, "row", step)
        value = jnp.where(((r ^ target) & step) != 0, other, value)
        step //= 2
    return [value[j] for j in range(max(counts))]


def per_device(trailing, panel_rows, pivot_block, panel_fill):
    sizes = Sizes(trailing, panel_rows, panel_fill)
    cap = 2 * sizes.per_piece
    fill = panel_fill.reshape(-1)
    where = jnp.stack([lax.axis_index("col"), lax.axis_index("row")]).astype(jnp.int32)
    own = pack(sizes, cap, where, fill, panel_rows)
    pivot = gather_pivot(pivot_block)
    column = gather_column(sizes, own)
    lists = gather_lists(own, sizes.cols)
    w = inverse_factor(pivot)
    own_factor, high, low = apply_factor(sizes, cap, where, fill, w, panel_rows, column)
    updated = update(sizes, cap, where, fill, high, low, trailing, lists)
    return updated, own_factor


def solution(mesh):
    in_specs = (P("row", "col"), P(("row", "col"), None), P("col", None), P())
    out_specs = (P("row", "col"), P(("row", "col"), None))
    return jax.shard_map(
        per_device, mesh=mesh, in_specs=in_specs, out_specs=out_specs, check_vma=False
    )
```

profile of v0, /device:TPU:0, one launch (start us, length us, event | category | flops | bytes accessed | tf_op | source)
XLA Modules:
  0.0 197.9 jit_solution(17188729837711483021)
XLA Ops:
  0.6 0.0 copy-start
  0.6 0.0 copy-start.9
  0.7 6.2 %copy.11.window_ref = f32[3072,512]{1,0:T(8,128)} copy(f32[3072,512]{1,0:T(8,128)} %param.4) | data formatting | bytes 12582912
  6.9 0.0 copy-done.9
  6.9 0.1 copy.8
  7.0 0.7 reshape.113.fill_ref
  7.7 0.6 pad_add_fusion.where_ref
  8.3 0.8 shard_map.60.refs_0_
  9.2 1.3 collective-permute-start.6
  10.5 1.8 collective-permute-start.5
  12.2 11.9 %collective-permute-done.6 = f32[6,128,256]{2,1,0:T(8,128)S(1)} collective-permute-done((f32[6,128,256]{2,1,0:T(8,128)}, f32[6,128,256]{2,1,0:T(8,128)S(1)}, u32[]{:S(2)}, u32[]{:S(2)}) %collective-permute-start.6) | collective-permute-done | bytes 786464 | tf_op jit(solution)/shard_map/ppermute | solution.py:350
  24.2 0.0 collective-permute-done.5
  24.2 1.5 pad_maximum_fusion
  25.7 0.0 collective-permute-start.7
  25.7 0.0 copy-done
  25.7 6.7 %collective-permute-start = (f32[1,16,512]{2,1,0:T(8,128)S(1)}, f32[1,16,512]{2,1,0:T(8,128)S(1)}, u32[]{:S(2)}, u32[]{:S(2)}) collective-permute-start(f32[1,16,512]{2,1,0:T(8,128)S(1)} %dynamic-slice_bitcast_fusion), channel_id=1, source_target_pairs={{0,4},{4,0},{8,12},{12,8},{16,20},{20,16},{24,28},{28,24},{1,5},{5... | collective-permute-start | bytes 98312 | tf_op jit(solution)/shard_map/ppermute | solution.py:306
  32.4 1.9 collective-permute-done
  34.3 5.5 %collective-permute-start.1 = (f32[2,16,512]{2,1,0:T(8,128)S(1)}, f32[2,16,512]{2,1,0:T(8,128)S(1)}, u32[]{:S(2)}, u32[]{:S(2)}) collective-permute-start(f32[2,16,512]{2,1,0:T(8,128)S(1)} %maximum_select_fusion.4), channel_id=1, source_target_pairs={{0,8},{4,12},{8,0},{12,4},{16,24},{20,28},{24,16},{28,20},{1,9},{5... | collective-permute-start | bytes 196616 | tf_op jit(solution)/shard_map/ppermute | solution.py:306
  39.8 2.3 %collective-permute-done.1 = f32[2,16,512]{2,1,0:T(8,128)S(1)} collective-permute-done((f32[2,16,512]{2,1,0:T(8,128)S(1)}, f32[2,16,512]{2,1,0:T(8,128)S(1)}, u32[]{:S(2)}, u32[]{:S(2)}) %collective-permute-start.1) | collective-permute-done | bytes 65568 | tf_op jit(solution)/shard_map/ppermute | solution.py:306
  42.2 0.0 copy-start.1
  42.2 7.8 %collective-permute-start.2 = (f32[4,16,512]{2,1,0:T(8,128)S(1)}, f32[4,16,512]{2,1,0:T(8,128)S(1)}, u32[]{:S(2)}, u32[]{:S(2)}) collective-permute-start(f32[4,16,512]{2,1,0:T(8,128)S(1)} %maximum_select_fusion.3), channel_id=1, source_target_pairs={{0,16},{4,20},{8,24},{12,28},{16,0},{20,4},{24,8},{28,12},{1,17},{... | collective-permute-start | bytes 393224 | tf_op jit(solution)/shard_map/ppermute | solution.py:306
  50.0 12.4 %collective-permute-done.7 = f32[2,6,128,256]{3,2,1,0:T(8,128)} collective-permute-done((f32[2,6,128,256]{3,2,1,0:T(8,128)}, f32[2,6,128,256]{3,2,1,0:T(8,128)}, u32[]{:S(2)}, u32[]{:S(2)}) %collective-permute-start.7) | collective-permute-done | bytes 1572896 | tf_op jit(solution)/shard_map/ppermute | solution.py:306
  62.4 0.0 copy-done.5
  62.4 0.0 copy-done.7
  62.4 1.4 broadcast_select_fusion
  63.8 0.8 collective-permute-start.8
  64.5 0.0 collective-permute-done.2
  64.5 0.1 collective-permute-start.3
  64.6 0.0 copy-done.1
  64.6 5.5 %collective-permute-start.14 = (f32[6,128,256]{2,1,0:T(8,128)S(1)}, f32[6,128,256]{2,1,0:T(8,128)S(1)}, u32[]{:S(2)}, u32[]{:S(2)}) collective-permute-start(f32[6,128,256]{2,1,0:T(8,128)S(1)} %copy-done.1), channel_id=1, source_target_pairs={{0,24},{4,28},{8,16},{12,20},{16,8},{20,12},{24,0},{28,4},{1,25},{... | collective-permute-start | bytes 2359304 | tf_op jit(solution)/shard_map/ppermute | solution.py:306
  70.2 3.1 %collective-permute-start.12 = (f32[6,128,256]{2,1,0:T(8,128)S(1)}, f32[6,128,256]{2,1,0:T(8,128)S(1)}, u32[]{:S(2)}, u32[]{:S(2)}) collective-permute-start(f32[6,128,256]{2,1,0:T(8,128)S(1)} %copy-done.1), channel_id=1, source_target_pairs={{0,16},{4,20},{8,24},{12,28},{16,0},{20,4},{24,8},{28,12},{1,17},{... | collective-permute-start | bytes 2359304 | tf_op jit(solution)/shard_map/ppermute | solution.py:306
  73.3 0.0 collective-permute-start.10
  73.3 0.0 collective-permute-done.3
  73.3 1.9 maximum_select_fusion.1
  75.2 1.4 collective-permute-start.4
  76.6 12.0 %collective-permute-done.14.refs_6_ = f32[6,128,256]{2,1,0:T(8,128)S(1)} collective-permute-done((f32[6,128,256]{2,1,0:T(8,128)S(1)}, f32[6,128,256]{2,1,0:T(8,128)S(1)}, u32[]{:S(2)}, u32[]{:S(2)}) %collective-permute-start.14) | collective-permute-done | bytes 786464 | tf_op jit(solution)/shard_map/ppermute | solution.py:306
  88.7 5.0 %collective-permute-start.9 = (f32[6,128,256]{2,1,0:T(8,128)S(1)}, f32[6,128,256]{2,1,0:T(8,128)S(1)}, u32[]{:S(2)}, u32[]{:S(2)}) collective-permute-start(f32[6,128,256]{2,1,0:T(8,128)S(1)} %copy-done.1), channel_id=1, source_target_pairs={{0,4},{4,0},{8,12},{12,8},{16,20},{20,16},{24,28},{28,24},{1,5},{5... | collective-permute-start | bytes 2359304 | tf_op jit(solution)/shard_map/ppermute | solution.py:306
  93.6 44.9 %collective-permute-done.12.refs_4_ = f32[6,128,256]{2,1,0:T(8,128)S(1)} collective-permute-done((f32[6,128,256]{2,1,0:T(8,128)S(1)}, f32[6,128,256]{2,1,0:T(8,128)S(1)}, u32[]{:S(2)}, u32[]{:S(2)}) %collective-permute-start.12) | collective-permute-done | bytes 786464 | tf_op jit(solution)/shard_map/ppermute | solution.py:306
  138.5 0.0 collective-permute-start.15
  138.5 0.0 collective-permute-done.10.refs_2_
  138.5 2.0 %collective-permute-start.13 = (f32[6,128,256]{2,1,0:T(8,128)S(1)}, f32[6,128,256]{2,1,0:T(8,128)S(1)}, u32[]{:S(2)}, u32[]{:S(2)}) collective-permute-start(f32[6,128,256]{2,1,0:T(8,128)S(1)} %collective-permute-done.12.refs_4_), channel_id=1, source_target_pairs={{0,4},{4,0},{8,12},{12,8},{16,20},{20,16},{24,28},{28,24},{1,5},{5... | collective-permute-start | bytes 2359304 | tf_op jit(solution)/shard_map/ppermute | solution.py:306
  140.6 0.0 collective-permute-done.4
  140.6 0.1 collective-permute-start.11
  140.6 1.9 maximum_select_fusion
  142.5 0.0 copy-start.6
  142.5 0.0 copy-start.8
  142.5 6.4 %shard_map.59.w_ref = f32[512,512]{1,0:T(8,128)S(1)} custom-call(f32[512,512]{1,0:T(8,128)S(1)} %bitcast.15), custom_call_target="tpu_custom_call" | custom-call | flops 5368709120 | bytes 2097152 | tf_op jit(solution)/shard_map/pallas_call | solution.py:99
  148.9 0.0 collective-permute-done.8
  148.9 0.0 copy-done.6
  148.9 0.0 copy-done.8
  148.9 0.3 broadcast_select_fusion.1
  149.3 0.0 copy-start.2
  149.3 0.0 copy-start.3
  149.3 0.0 copy-start.4
  149.3 0.2 slice_bitcast_fusion
  149.5 0.9 copy-done.2
  150.4 0.0 copy-done.3
  150.4 0.0 copy-done.4
  150.4 3.5 %shard_map.61 = (f32[384,512]{1,0:T(8,128)}, bf16[512,512]{1,0:T(8,128)(2,1)S(1)}, bf16[512,512]{1,0:T(8,128)(2,1)S(1)}) custom-call(s32[2]{0:T(128)S(1)} %copy-done.4, s32[96]{0:T(128)S(1)} %copy-done.3, f32[512,512]{1,0:T(8,128)S(1)} %shard_map.59.w_ref, f32[384,512]{1,0:T(8,128)S(1)} %copy-done.2, f32[6,128,256]{2,1,0:T(8,128)S(1)} %get-tuple-element.9.refs_0_, ...), custom_call_target="tpu_custom_call" | custom-call | flops 2147483648 | bytes 3145728 | tf_op jit(solution)/shard_map/pallas_call | solution.py:212
  153.9 0.0 collective-permute-done.9.refs_1_
  153.9 5.0 %collective-permute-done.15.refs_7_ = f32[6,128,256]{2,1,0:T(8,128)S(1)} collective-permute-done((f32[6,128,256]{2,1,0:T(8,128)S(1)}, f32[6,128,256]{2,1,0:T(8,128)S(1)}, u32[]{:S(2)}, u32[]{:S(2)}) %collective-permute-start.15) | collective-permute-done | bytes 786464 | tf_op jit(solution)/shard_map/ppermute | solution.py:306
  158.9 16.9 %collective-permute-done.13.refs_5_ = f32[6,128,256]{2,1,0:T(8,128)S(1)} collective-permute-done((f32[6,128,256]{2,1,0:T(8,128)S(1)}, f32[6,128,256]{2,1,0:T(8,128)S(1)}, u32[]{:S(2)}, u32[]{:S(2)}) %collective-permute-start.13) | collective-permute-done | bytes 786464 | tf_op jit(solution)/shard_map/ppermute | solution.py:306
  175.8 16.0 %collective-permute-done.11.refs_3_ = f32[6,128,256]{2,1,0:T(8,128)S(1)} collective-permute-done((f32[6,128,256]{2,1,0:T(8,128)S(1)}, f32[6,128,256]{2,1,0:T(8,128)S(1)}, u32[]{:S(2)}, u32[]{:S(2)}) %collective-permute-start.11) | collective-permute-done | bytes 786464 | tf_op jit(solution)/shard_map/ppermute | solution.py:306
  191.8 6.1 %shard_map.62 = f32[3072,512]{1,0:T(8,128)} custom-call(s32[2]{0:T(128)S(1)} %copy-done.4, s32[96]{0:T(128)S(1)} %copy-done.3, bf16[512,512]{1,0:T(8,128)(2,1)S(1)} %get-tuple-element.5.high_ref, bf16[512,512]{1,0:T(8,128)(2,1)S(1)} %get-tuple-element.6.low_ref, f32[3072,512]{1,0:T(8,128)} %copy.11.window_ref, ...), custom_call_target="tpu_custom_call", output_to_operand_aliasing={{}: (4, {})} | custom-call | flops 1000000000 | bytes 6000000 | tf_op jit(solution)/shard_map/pallas_call | solution.py:286
  (6 shorter events, 0.0 us)
Async XLA Ops:
  0.6 25.1 %copy-start = (f32[64,512]{1,0:T(8,128)S(1)}, f32[64,512]{1,0:T(8,128)}, u32[]{:S(2)}) copy-start(f32[64,512]{1,0:T(8,128)} %param.6) | copy-start | bytes 393220
  0.6 6.2 %copy-start.9 = (s32[48,2]{0,1:T(2,128)S(1)}, s32[48,2]{0,1:T(2,128)}, u32[]{:S(2)}) copy-start(s32[48,2]{0,1:T(2,128)} %param.7) | copy-start | bytes 1156
  9.2 15.0 %collective-permute-start.6 = (f32[6,128,256]{2,1,0:T(8,128)}, f32[6,128,256]{2,1,0:T(8,128)S(1)}, u32[]{:S(2)}, u32[]{:S(2)}) collective-permute-start(f32[6,128,256]{2,1,0:T(8,128)} %shard_map.60.refs_0_), channel_id=1, source_target_pairs={{4,0},{8,4},{12,8},{20,12},{24,16},{28,20},{5,25},{9,29}} | collective-permute-start | bytes 2359304 | tf_op jit(solution)/shard_map/ppermute | solution.py:350
  10.5 13.7 %collective-permute-start.5 = (f32[6,128,256]{2,1,0:T(8,128)}, f32[6,128,256]{2,1,0:T(8,128)S(1)}, u32[]{:S(2)}, u32[]{:S(2)}) collective-permute-start(f32[6,128,256]{2,1,0:T(8,128)} %shard_map.60.refs_0_), channel_id=1, source_target_pairs={{0,0},{4,4},{8,8},{16,12},{20,16},{24,20},{1,25},{5,29}} | collective-permute-start | bytes 2359304 | tf_op jit(solution)/shard_map/ppermute | solution.py:350
  24.2 38.2 %copy-start.5 = (f32[6,128,256]{2,1,0:T(8,128)}, f32[6,128,256]{2,1,0:T(8,128)S(1)}, u32[]{:S(2)}) copy-start(f32[6,128,256]{2,1,0:T(8,128)S(1)} %collective-permute-done.6) | copy-start | bytes 2359300
  24.2 38.2 %copy-start.7 = (f32[6,128,256]{2,1,0:T(8,128)}, f32[6,128,256]{2,1,0:T(8,128)S(1)}, u32[]{:S(2)}) copy-start(f32[6,128,256]{2,1,0:T(8,128)S(1)} %collective-permute-done.5) | copy-start | bytes 2359300
  25.7 36.7 %collective-permute-start.7 = (f32[2,6,128,256]{3,2,1,0:T(8,128)}, f32[2,6,128,256]{3,2,1,0:T(8,128)}, u32[]{:S(2)}, u32[]{:S(2)}) collective-permute-start(f32[2,6,128,256]{3,2,1,0:T(8,128)} %pad_maximum_fusion), channel_id=1, source_target_pairs={{0,2},{1,3},{2,0},{3,1},{4,6},{5,7},{6,4},{7,5},{8,10},{9,11},{10,... | collective-permute-start | bytes 4718600 | tf_op jit(solution)/shard_map/ppermute | solution.py:306
  25.7 8.6 %collective-permute-start = (f32[1,16,512]{2,1,0:T(8,128)S(1)}, f32[1,16,512]{2,1,0:T(8,128)S(1)}, u32[]{:S(2)}, u32[]{:S(2)}) collective-permute-start(f32[1,16,512]{2,1,0:T(8,128)S(1)} %dynamic-slice_bitcast_fusion), channel_id=1, source_target_pairs={{0,4},{4,0},{8,12},{12,8},{16,20},{20,16},{24,28},{28,24},{1,5},{5... | collective-permute-start | bytes 98312 | tf_op jit(solution)/shard_map/ppermute | solution.py:306
  34.3 7.8 %collective-permute-start.1 = (f32[2,16,512]{2,1,0:T(8,128)S(1)}, f32[2,16,512]{2,1,0:T(8,128)S(1)}, u32[]{:S(2)}, u32[]{:S(2)}) collective-permute-start(f32[2,16,512]{2,1,0:T(8,128)S(1)} %maximum_select_fusion.4), channel_id=1, source_target_pairs={{0,8},{4,12},{8,0},{12,4},{16,24},{20,28},{24,16},{28,20},{1,9},{5... | collective-permute-start | bytes 196616 | tf_op jit(solution)/shard_map/ppermute | solution.py:306
  42.2 22.5 %copy-start.1 = (f32[6,128,256]{2,1,0:T(8,128)S(1)}, f32[6,128,256]{2,1,0:T(8,128)}, u32[]{:S(2)}) copy-start(f32[6,128,256]{2,1,0:T(8,128)} %shard_map.60.refs_0_) | copy-start | bytes 2359300
  42.2 22.3 %collective-permute-start.2 = (f32[4,16,512]{2,1,0:T(8,128)S(1)}, f32[4,16,512]{2,1,0:T(8,128)S(1)}, u32[]{:S(2)}, u32[]{:S(2)}) collective-permute-start(f32[4,16,512]{2,1,0:T(8,128)S(1)} %maximum_select_fusion.3), channel_id=1, source_target_pairs={{0,16},{4,20},{8,24},{12,28},{16,0},{20,4},{24,8},{28,12},{1,17},{... | collective-permute-start | bytes 393224 | tf_op jit(solution)/shard_map/ppermute | solution.py:306
  63.8 85.1 %collective-permute-start.8 = (f32[2,6,128,256]{3,2,1,0:T(8,128)}, f32[2,6,128,256]{3,2,1,0:T(8,128)}, u32[]{:S(2)}, u32[]{:S(2)}) collective-permute-start(f32[2,6,128,256]{3,2,1,0:T(8,128)} %broadcast_select_fusion), channel_id=1, source_target_pairs={{0,1},{1,0},{2,3},{3,2},{4,5},{5,4},{6,7},{7,6},{8,9},{9,8},{10,11... | collective-permute-start | bytes 4718600 | tf_op jit(solution)/shard_map/ppermute | solution.py:306
  64.5 8.8 %collective-permute-start.3 = (f32[1,8,16,512]{3,2,0,1:T(8,128)S(1)}, f32[1,8,16,512]{3,2,0,1:T(8,128)}, u32[]{:S(2)}, u32[]{:S(2)}) collective-permute-start(f32[1,8,16,512]{3,2,0,1:T(8,128)S(1)} %maximum_select_fusion.2), channel_id=1, source_target_pairs={{0,1},{1,0},{2,3},{3,2},{4,5},{5,4},{6,7},{7,6},{8,9},{9,8},{10,11... | collective-permute-start | bytes 786440 | tf_op jit(solution)/shard_map/ppermute | solution.py:306
  64.6 24.0 %collective-permute-start.14 = (f32[6,128,256]{2,1,0:T(8,128)S(1)}, f32[6,128,256]{2,1,0:T(8,128)S(1)}, u32[]{:S(2)}, u32[]{:S(2)}) collective-permute-start(f32[6,128,256]{2,1,0:T(8,128)S(1)} %copy-done.1), channel_id=1, source_target_pairs={{0,24},{4,28},{8,16},{12,20},{16,8},{20,12},{24,0},{28,4},{1,25},{... | collective-permute-start | bytes 2359304 | tf_op jit(solution)/shard_map/ppermute | solution.py:306
  70.2 68.4 %collective-permute-start.12 = (f32[6,128,256]{2,1,0:T(8,128)S(1)}, f32[6,128,256]{2,1,0:T(8,128)S(1)}, u32[]{:S(2)}, u32[]{:S(2)}) collective-permute-start(f32[6,128,256]{2,1,0:T(8,128)S(1)} %copy-done.1), channel_id=1, source_target_pairs={{0,16},{4,20},{8,24},{12,28},{16,0},{20,4},{24,8},{28,12},{1,17},{... | collective-permute-start | bytes 2359304 | tf_op jit(solution)/shard_map/ppermute | solution.py:306
  73.3 65.2 %collective-permute-start.10 = (f32[6,128,256]{2,1,0:T(8,128)S(1)}, f32[6,128,256]{2,1,0:T(8,128)S(1)}, u32[]{:S(2)}, u32[]{:S(2)}) collective-permute-start(f32[6,128,256]{2,1,0:T(8,128)S(1)} %copy-done.1), channel_id=1, source_target_pairs={{0,8},{4,12},{8,0},{12,4},{16,24},{20,28},{24,16},{28,20},{1,9},{5... | collective-permute-start | bytes 2359304 | tf_op jit(solution)/shard_map/ppermute | solution.py:306
  75.2 65.4 %collective-permute-start.4 = (f32[2,8,16,512]{3,2,0,1:T(8,128)}, f32[2,8,16,512]{3,2,0,1:T(8,128)}, u32[]{:S(2)}, u32[]{:S(2)}) collective-permute-start(f32[2,8,16,512]{3,2,0,1:T(8,128)} %maximum_select_fusion.1), channel_id=1, source_target_pairs={{0,2},{1,3},{2,0},{3,1},{4,6},{5,7},{6,4},{7,5},{8,10},{9,11},{10,... | collective-permute-start | bytes 1572872 | tf_op jit(solution)/shard_map/ppermute | solution.py:306
  88.7 65.2 %collective-permute-start.9 = (f32[6,128,256]{2,1,0:T(8,128)S(1)}, f32[6,128,256]{2,1,0:T(8,128)S(1)}, u32[]{:S(2)}, u32[]{:S(2)}) collective-permute-start(f32[6,128,256]{2,1,0:T(8,128)S(1)} %copy-done.1), channel_id=1, source_target_pairs={{0,4},{4,0},{8,12},{12,8},{16,20},{20,16},{24,28},{28,24},{1,5},{5... | collective-permute-start | bytes 2359304 | tf_op jit(solution)/shard_map/ppermute | solution.py:306
  138.5 20.4 %collective-permute-start.15 = (f32[6,128,256]{2,1,0:T(8,128)S(1)}, f32[6,128,256]{2,1,0:T(8,128)S(1)}, u32[]{:S(2)}, u32[]{:S(2)}) collective-permute-start(f32[6,128,256]{2,1,0:T(8,128)S(1)} %collective-permute-done.14.refs_6_), channel_id=1, source_target_pairs={{0,4},{4,0},{8,12},{12,8},{16,20},{20,16},{24,28},{28,24},{1,5},{5... | collective-permute-start | bytes 2359304 | tf_op jit(solution)/shard_map/ppermute | solution.py:306
  138.5 37.2 %collective-permute-start.13 = (f32[6,128,256]{2,1,0:T(8,128)S(1)}, f32[6,128,256]{2,1,0:T(8,128)S(1)}, u32[]{:S(2)}, u32[]{:S(2)}) collective-permute-start(f32[6,128,256]{2,1,0:T(8,128)S(1)} %collective-permute-done.12.refs_4_), channel_id=1, source_target_pairs={{0,4},{4,0},{8,12},{12,8},{16,20},{20,16},{24,28},{28,24},{1,5},{5... | collective-permute-start | bytes 2359304 | tf_op jit(solution)/shard_map/ppermute | solution.py:306
  140.6 51.2 %collective-permute-start.11 = (f32[6,128,256]{2,1,0:T(8,128)S(1)}, f32[6,128,256]{2,1,0:T(8,128)S(1)}, u32[]{:S(2)}, u32[]{:S(2)}) collective-permute-start(f32[6,128,256]{2,1,0:T(8,128)S(1)} %collective-permute-done.10.refs_2_), channel_id=1, source_target_pairs={{0,4},{4,0},{8,12},{12,8},{16,20},{20,16},{24,28},{28,24},{1,5},{5... | collective-permute-start | bytes 2359304 | tf_op jit(solution)/shard_map/ppermute | solution.py:306
  142.5 6.4 %copy-start.6 = (f32[6,128,256]{2,1,0:T(8,128)S(1)}, f32[6,128,256]{2,1,0:T(8,128)}, u32[]{:S(2)}) copy-start(f32[6,128,256]{2,1,0:T(8,128)} %copy-done.5) | copy-start | bytes 2359300
  142.5 6.4 %copy-start.8 = (f32[6,128,256]{2,1,0:T(8,128)S(1)}, f32[6,128,256]{2,1,0:T(8,128)}, u32[]{:S(2)}) copy-start(f32[6,128,256]{2,1,0:T(8,128)} %copy-done.7) | copy-start | bytes 2359300
  149.3 1.1 copy-start.2
  149.3 1.1 copy-start.3
  149.3 1.1 copy-start.4
where the time goes:
time: 199 us; the launch traced here: 198 us
  waiting for transfers between devices  123 us (62%)
  starting transfers between devices  41.1 us (21%)
  Pallas kernels  16.8 us (8%)
  local copies, waits for them, and re-layouts  8.18 us (4%)
  other arithmetic  7.7 us (4%)
    ppermute x14, waiting for transfers between devices, swap(): return lax.ppermute(value, axis, [(i, i ^ step) for i in range(size)])  111 us
    ppermute x14, starting transfers between devices, swap(): return lax.ppermute(value, axis, [(i, i ^ step) for i in range(size)])  38 us
    ppermute x2, waiting for transfers between devices, gather_column(): values.append(lax.ppermute(own, ('col', 'row'), pairs))  11.9 us
    unnamed x22, local copies, waits for them, and re-layouts  7.3 us
    pallas_call x1, Pallas kernels, inverse_factor(): pl.pallas_call(inverse_factor_kernel, out_shape=jax.ShapeDtypeStruct((n,...  6.36 us
    pallas_call x1, Pallas kernels, update(): pl.pallas_call(functools.partial(update_kernel, sizes, cap), out_shape=ja...  6.15 us
  transfers between devices with their start and end apart: 16, of which 9 were waited for; matrix products, arithmetic and copies ran while one was open for 3% of the time, Pallas kernels for 5%

commit v1 on v0

v1 whole, which is shorter than its diff:
```python
import functools
import math

import jax
import jax.numpy as jnp
from jax import lax
from jax.experimental import pallas as pl
from jax.experimental.pallas import tpu as pltpu
from jax.sharding import PartitionSpec as P

F32, BF16 = jnp.float32, jnp.bfloat16
VMEM = pl.BlockSpec(memory_space=pltpu.VMEM)
SMEM = pl.BlockSpec(memory_space=pltpu.SMEM)
ANY = pl.BlockSpec(memory_space=pl.ANY)
COARSE_STEPS = 2
FINE_STEPS = 16
RESIDUAL = 5e-4


def halves(value):
    high = value.astype(BF16)
    return high, (value - high.astype(F32)).astype(BF16)


def dot(a, b, dims):
    return lax.dot_general(a, b, (dims, ((), ())), preferred_element_type=F32)


NN, NT, TN = ((1,), (0,)), ((1,), (1,)), ((0,), (0,))


def dot3(a, b, dims):
    (ah, al), (bh, bl) = a, b
    return dot(ah, bh, dims) + (dot(ah, bl, dims) + dot(al, bh, dims))


def inverse_factor_kernel(a_ref, w_ref, s_ref, flag):
    n = a_ref.shape[0]
    rows = lax.broadcasted_iota(jnp.int32, (n, n), 0)
    cols = lax.broadcasted_iota(jnp.int32, (n, n), 1)
    eye = (rows == cols).astype(F32)
    take = jnp.where(rows > cols, 1.0, 0.5 * eye)
    a = a_ref[...]
    diag_row = jnp.sum(a * eye, axis=0, keepdims=True)
    diag_col = jnp.sum(a * eye, axis=1, keepdims=True)
    scale_row, scale_col = lax.rsqrt(diag_row), lax.rsqrt(diag_col)
    scaled = jnp.where(rows == cols, 1.0, a * scale_row * scale_col)
    s_ref[...] = scaled
    scaled_parts = halves(scaled)
    w = eye - take * (scaled - eye)
    for _ in range(COARSE_STEPS):
        wh = w.astype(BF16)
        t = dot(wh, scaled_parts[0], NN).astype(BF16)
        change = take * (dot(t, wh, NT) - eye)
        w = w - dot(change.astype(BF16), wh, NN)
    w_ref[...] = w
    flag[0] = 0

    def fine(state):
        step, _ = state
        w = w_ref[...]
        parts = halves(w)
        t = halves(dot3(parts, halves(s_ref[...]), NN))
        residual = dot3(t, parts, NT) - eye
        w_ref[...] = w - dot((take * residual).astype(BF16), parts[0], NN)
        return step + 1, jnp.sum(residual * residual)

    _, left = lax.while_loop(
        lambda state: jnp.logical_and(state[0] < FINE_STEPS, jnp.logical_not(state[1] < RESIDUAL**2)),
        fine,
        (jnp.int32(0), jnp.float32(1.0)),
    )
    done = left < RESIDUAL**2

    @pl.when(jnp.logical_not(done))
    def _():
        w_ref[...] = eye

        def eliminate(j, carry):
            row = s_ref[pl.ds(j, 1), :]
            pick = lax.broadcasted_iota(jnp.int32, (1, n), 1) == j
            pivot = jnp.sum(jnp.where(pick, row, 0.0), axis=1, keepdims=True)
            column = jnp.sum(jnp.where(pick, s_ref[...], 0.0), axis=1, keepdims=True)
            below = lax.broadcasted_iota(jnp.int32, (n, 1), 0) > j
            ratio = jnp.where(below, column / pivot, 0.0)
            s_ref[...] = s_ref[...] - ratio * row
            w_ref[...] = w_ref[...] - ratio * w_ref[pl.ds(j, 1), :]
            return carry

        lax.fori_loop(0, n, eliminate, 0)
        pivots = jnp.sum(s_ref[...] * eye, axis=1, keepdims=True)
        w_ref[...] = w_ref[...] * lax.rsqrt(pivots)

    w_ref[...] = w_ref[...] * scale_row


def inverse_factor(pivot):
    n = pivot.shape[0]
    return pl.pallas_call(
        inverse_factor_kernel,
        out_shape=jax.ShapeDtypeStruct((n, n), F32),
        in_specs=[VMEM],
        out_specs=VMEM,
        scratch_shapes=[pltpu.VMEM((n, n), F32), pltpu.SMEM((1,), jnp.int32)],
        compiler_params=pltpu.CompilerParams(vmem_limit_bytes=32 * 2**20),
    )(pivot)


class Sizes:
    def __init__(self, trailing, panel_rows, panel_fill):
        self.cols, self.rows = lax.axis_size("col"), lax.axis_size("row")
        self.block = panel_rows.shape[1] // 2
        self.piece = panel_rows.shape[0]
        self.unit = math.gcd(self.piece, self.block)
        self.per_piece = self.piece // self.unit
        self.per_block = self.block // self.unit
        self.slab = self.piece * self.cols
        self.width = trailing.shape[1]
        self.tiles = self.cols * self.per_piece

    def source(self, c):
        slab = c * self.width // self.slab
        return slab, (c * self.width - slab * self.slab) // self.piece

    def sources(self):
        found = []
        for c in range(self.cols):
            slab, first = self.source(c)
            last = ((c + 1) * self.width - 1 - slab * self.slab) // self.piece
            found.append(last - first + 1)
        return found


def unit_flag(sizes, fill_ref, piece_index, unit, panel):
    block = (piece_index * sizes.per_piece + unit) // sizes.per_block
    return fill_ref[block * 2 + panel] != 0


def pool_pieces(sizes, pool_row, pool_col):
    for core in range(2):
        for side in range(2):
            yield core, side, (pool_row * 2 + core) * sizes.cols + pool_col * 2 + side


def fits_kernel(sizes, cap, fill_ref, out_ref):
    most = jnp.int32(0)
    for pool_row in range(sizes.rows // 2):
        for pool_col in range(sizes.cols // 2):
            count = jnp.int32(0)
            for _, _, piece in pool_pieces(sizes, pool_row, pool_col):
                for u in range(sizes.per_piece):
                    for p in range(2):
                        count = count + unit_flag(sizes, fill_ref, piece, u, p).astype(jnp.int32)
            most = jnp.maximum(most, count)
    out_ref[0] = (most <= cap).astype(jnp.int32)


def fits(sizes, cap, fill):
    return pl.pallas_call(
        functools.partial(fits_kernel, sizes, cap),
        out_shape=jax.ShapeDtypeStruct((1,), jnp.int32),
        in_specs=[SMEM],
        out_specs=SMEM,
    )(fill)


def pack_kernel(sizes, cap, where_ref, fill_ref, panel_ref, side_ref, core_ref, out_ref, pool):
    c, r = where_ref[0], where_ref[1]
    side, core = c % 2, r % 2
    half, quarter = sizes.unit // 2, sizes.unit // 4
    own_at = pl.multiple_of(side * half + core * quarter, quarter)
    side_at = pl.multiple_of(core * quarter, quarter)
    for u in range(sizes.per_piece):
        pool[core, side, u] = panel_ref[u, pl.ds(own_at, quarter), :]
        pool[core, 1 - side, u] = side_ref[u, pl.ds(side_at, quarter), :]
        pool[1 - core, side, u] = core_ref[0, u]
        pool[1 - core, 1 - side, u] = core_ref[1, u]
    slot = jnp.int32(0)
    for core_at, side_at, piece in pool_pieces(sizes, r // 2, c // 2):
        for u in range(sizes.per_piece):
            for p in range(2):
                flag = unit_flag(sizes, fill_ref, piece, u, p)

                @pl.when(flag)
                def _(slot=slot, core_at=core_at, side_at=side_at, u=u, p=p):
                    out_ref[jnp.minimum(slot, cap - 1)] = pool[
                        core_at, side_at, u, :, p * sizes.block : (p + 1) * sizes.block
                    ]

                slot = slot + flag.astype(jnp.int32)


def pack(sizes, cap, where, fill, panel, from_side, from_core):
    quarter = sizes.unit // 4
    return pl.pallas_call(
        functools.partial(pack_kernel, sizes, cap),
        out_shape=jax.ShapeDtypeStruct((cap, quarter, sizes.block), F32),
        in_specs=[SMEM, SMEM, VMEM, VMEM, VMEM],
        out_specs=VMEM,
        scratch_shapes=[pltpu.VMEM((2, 2, sizes.per_piece, quarter, 2 * sizes.block), F32)],
        compiler_params=pltpu.CompilerParams(vmem_limit_bytes=16 * 2**20),
    )(where, fill, panel, from_side, from_core)


def apply_factor_kernel(
    sizes, where_ref, fill_ref, w_ref, panel_ref, column_ref, x_ref, high_ref, low_ref, slot_ref, masked, column
):
    c, r = where_ref[0], where_ref[1]

    def mask(source, target, first_unit, count):
        for u in range(count):
            for p in range(2):
                at = (pl.ds(u * sizes.unit, sizes.unit), pl.ds(p * sizes.block, sizes.block))
                flag = fill_ref[(first_unit + u) // sizes.per_block * 2 + p] != 0
                target[at] = jnp.where(flag, source[at], 0.0)

    mask(panel_ref, masked, (r * sizes.cols + c) * sizes.per_piece, sizes.per_piece)
    mask(column_ref, column, c * (sizes.width // sizes.unit), sizes.width // sizes.unit)
    w = halves(w_ref[...])
    x_ref[...] = dot3(halves(masked[...]), w, NT)
    solved = dot3(w, halves(column[...]), NT)
    high_ref[...], low_ref[...] = halves(dot3(w, halves(solved), TN))

    @pl.loop(0, sizes.cols // 2)
    def _(group):
        pool_col = jnp.bitwise_xor(c // 2, group)
        slot = jnp.int32(0)
        for core, side, piece in pool_pieces(sizes, r // 2, pool_col):
            for u in range(sizes.per_piece):
                for p in range(2):
                    flag = unit_flag(sizes, fill_ref, piece, u, p)

                    @pl.when(core == r % 2)
                    def _(slot=slot, flag=flag, side=side, u=u, p=p):
                        at = ((group * 2 + side) * sizes.per_piece + u) * 2 + p
                        slot_ref[at] = jnp.where(flag, slot, -1)

                    slot = slot + flag.astype(jnp.int32)


def apply_factor(sizes, where, fill, w, panel, column):
    n = w.shape[0]
    return pl.pallas_call(
        functools.partial(apply_factor_kernel, sizes),
        out_shape=(
            jax.ShapeDtypeStruct(panel.shape, F32),
            jax.ShapeDtypeStruct((n, sizes.width), BF16),
            jax.ShapeDtypeStruct((n, sizes.width), BF16),
            jax.ShapeDtypeStruct((2 * sizes.tiles,), jnp.int32),
        ),
        in_specs=[SMEM, SMEM, VMEM, VMEM, VMEM],
        out_specs=(VMEM, VMEM, VMEM, SMEM),
        scratch_shapes=[pltpu.VMEM(panel.shape, F32), pltpu.VMEM((sizes.width, n), F32)],
        compiler_params=pltpu.CompilerParams(vmem_limit_bytes=32 * 2**20),
    )(where, fill, w, panel, column)


def update_kernel(sizes, where_ref, slot_ref, high_ref, low_ref, window_ref, *refs):
    groups = sizes.cols // 2
    lists, (out_ref, tiles, unit_data, in_sems, out_sems) = refs[: 4 * groups], refs[4 * groups :]
    c, r = where_ref[0], where_ref[1]
    side, core = c % 2, r % 2
    per_group = 2 * sizes.per_piece
    quarter = sizes.unit // 4

    def rows_of(t):
        group = jnp.bitwise_xor(c // 2, t // per_group)
        return pl.ds(pl.multiple_of((group * per_group + t % per_group) * sizes.unit, sizes.unit), sizes.unit)

    def tile_in(t):
        return pltpu.make_async_copy(window_ref.at[rows_of(t)], tiles.at[t], in_sems.at[t])

    def tile_out(t):
        return pltpu.make_async_copy(tiles.at[t], out_ref.at[rows_of(t)], out_sems.at[t])

    def active(t):
        return jnp.logical_or(slot_ref[2 * t] >= 0, slot_ref[2 * t + 1] >= 0)

    @pl.loop(0, sizes.tiles)
    def _(t):
        pl.when(active(t))(tile_in(t).start)

    for group in range(groups):

        @pl.loop(group * per_group, (group + 1) * per_group)
        def _(t, group=group):
            @pl.when(active(t))
            def _():
                tile_in(t).wait()
                for p in range(2):
                    slot = slot_ref[2 * t + p]

                    @pl.when(slot >= 0)
                    def _(p=p, slot=slot):
                        for flip in range(4):
                            from_side = jnp.bitwise_xor(side, flip // 2)
                            from_core = jnp.bitwise_xor(core, flip % 2)
                            at = pl.multiple_of((from_side * 2 + from_core) * quarter, quarter)
                            unit_data[pl.ds(at, quarter), :] = lists[4 * group + flip][slot]
                        at = pl.ds(p * sizes.block, sizes.block)
                        right = (high_ref[at, :], low_ref[at, :])
                        tiles[t] = tiles[t] - dot3(halves(unit_data[...]), right, NN)

                tile_out(t).start()

    @pl.loop(0, sizes.tiles)
    def _(t):
        pl.when(active(t))(tile_out(t).wait)


def update(sizes, where, slots, high, low, window, lists):
    tiles = sizes.tiles
    return pl.pallas_call(
        functools.partial(update_kernel, sizes),
        out_shape=jax.ShapeDtypeStruct(window.shape, F32),
        in_specs=[SMEM, SMEM, VMEM, VMEM, ANY] + [VMEM] * len(lists),
        out_specs=ANY,
        input_output_aliases={4: 0},
        scratch_shapes=[
            pltpu.VMEM((tiles, sizes.unit, sizes.width), F32),
            pltpu.VMEM((sizes.unit, sizes.block), F32),
            pltpu.SemaphoreType.DMA((tiles,)),
            pltpu.SemaphoreType.DMA((tiles,)),
        ],
        compiler_params=pltpu.CompilerParams(vmem_limit_bytes=40 * 2**20),
    )(where, slots, high, low, window, *lists)


def swap(value, axis, step):
    size = lax.axis_size(axis)
    return lax.ppermute(value, axis, [(i, i ^ step) for i in range(size)])


def join(index, step, own, other):
    second = (index & step) != 0
    return jnp.where(second, jnp.concatenate([other, own], 0), jnp.concatenate([own, other], 0))


def gather_pivot(sizes, pivot_block):
    r, c = lax.axis_index("row"), lax.axis_index("col")
    share = pivot_block.shape[0] // 2
    value = lax.dynamic_slice_in_dim(pivot_block, r % 2 * share, share, 0)[None]
    step = 1
    while step < sizes.cols:
        value = join(c, step, value, swap(value, "col", step))
        step *= 2
    value = join(r, 1, value[None], swap(value[None], "row", 1))
    return value.transpose(1, 0, 2, 3).reshape(2 * sizes.cols * share, -1)


def gather_column(sizes, panel):
    counts = sizes.sources()
    r, c = lax.axis_index("row"), lax.axis_index("col")
    target = c * sizes.width // sizes.slab
    values = []
    for j in range(max(counts)):
        pairs = []
        for at in range(sizes.cols):
            slab, first = sizes.source(at)
            if j < counts[at]:
                pairs.append(((first + j) * sizes.rows + slab, at * sizes.rows + slab))
        values.append(lax.ppermute(panel, ("col", "row"), pairs))
    start = (c * sizes.width - target * sizes.slab) % sizes.piece
    value = lax.dynamic_slice_in_dim(jnp.concatenate(values, 0), start, sizes.width, 0)
    step = sizes.rows // 2
    while step:
        value = jnp.where(((r ^ target) & step) != 0, swap(value, "row", step), value)
        step //= 2
    return value


def gather_pool(sizes, panel):
    side, core = lax.axis_index("col") % 2, lax.axis_index("row") % 2
    half, quarter = sizes.unit // 2, sizes.unit // 4
    own = lax.dynamic_slice_in_dim(panel, side * half, half, 1)
    from_side = swap(lax.dynamic_slice_in_dim(panel, (1 - side) * half, half, 1), "col", 1)
    both = jnp.stack([own, from_side])
    from_core = swap(lax.dynamic_slice_in_dim(both, (1 - core) * quarter, quarter, 2), "row", 1)
    return from_side, from_core


def per_device(trailing, panel_rows, pivot_block, panel_fill):
    sizes = Sizes(trailing, panel_rows, panel_fill)
    fill = panel_fill.reshape(-1)
    where = jnp.stack([lax.axis_index("col"), lax.axis_index("row")]).astype(jnp.int32)
    units = panel_rows.reshape(sizes.per_piece, sizes.unit, -1)
    most = 8 * sizes.per_piece

    def run(cap, trailing, panel_rows, pivot_block, fill, units):
        from_side, from_core = gather_pool(sizes, units)
        own = pack(sizes, cap, where, fill, units, from_side, from_core)
        pivot = gather_pivot(sizes, pivot_block)
        column = gather_column(sizes, panel_rows)
        arrived = [own] + [swap(own, "col", k) for k in range(2, sizes.cols, 2)]
        pivot, trailing, *arrived = lax.optimization_barrier((pivot, trailing, *arrived))
        w = inverse_factor(pivot)
        own_factor, high, low, slots = apply_factor(sizes, where, fill, w, panel_rows, column)
        lists = []
        for value in arrived:
            other = swap(value, "col", 1)
            lists += [value, swap(value, "row", 1), other, swap(other, "row", 1)]
        return update(sizes, where, slots, high, low, trailing, lists), own_factor

    cap = most * 5 // 12
    operands = (trailing, panel_rows, pivot_block, fill, units)
    return lax.cond(
        fits(sizes, cap, fill)[0] != 0,
        functools.partial(run, cap),
        functools.partial(run, most),
        *operands,
    )


def solution(mesh):
    in_specs = (P("row", "col"), P(("row", "col"), None), P("col", None), P())
    out_specs = (P("row", "col"), P(("row", "col"), None))
    return jax.shard_map(
        per_device, mesh=mesh, in_specs=in_specs, out_specs=out_specs, check_vma=False
    )
```

time: 199 us -> 146 us (0.73)
  waiting for transfers between devices: 123 us -> 75.9 us
  starting transfers between devices: 41.1 us -> 30.9 us
  Pallas kernels: 16.8 us -> 19.6 us
    ppermute x14 -> x23, waiting for transfers between devices: 111 us -> 63.9 us  [swap(): return lax.ppermute(value, axis, [(i, i ^ step) for i in range(size)])]
    ppermute x14 -> x23, starting transfers between devices: 38 us -> 28.1 us  [swap(): return lax.ppermute(value, axis, [(i, i ^ step) for i in range(size)])]
    pallas_call x2 -> x3, Pallas kernels: 9.62 us -> 12.4 us  [the longest x1 6.41 us: update(): pl.pallas_call(functools.partial(update_kernel, sizes), out_shape=jax.Sha...]
    select_n x7 -> x6, other arithmetic: 5.51 us -> 5.18 us  [the longest x2 2.7 us: gather_column(): value = jnp.where((r ^ target) & step != 0, swap(value, 'row', step), value)]
    unnamed x22 -> x8, local copies, waits for them, and re-layouts: 7.3 us -> 7.24 us
  transfers between devices with their start and end apart: 16 -> 25, of which waited for: 9 -> 10; matrix products, arithmetic and copies ran while one was open for 3% -> 4% of each run, Pallas kernels for 5% -> 8%
where the time goes in v1:
time: 146 us; the launch traced here: 145 us
  waiting for transfers between devices  75.9 us (52%)
  starting transfers between devices  30.9 us (21%)
  Pallas kernels  19.6 us (13%)
  local copies, waits for them, and re-layouts  9.78 us (7%)
  other arithmetic  6.72 us (5%)
    ppermute x23, waiting for transfers between devices, swap(): return lax.ppermute(value, axis, [(i, i ^ step) for i in range(size)])  63.9 us
    ppermute x23, starting transfers between devices, swap(): return lax.ppermute(value, axis, [(i, i ^ step) for i in range(size)])  28.1 us
    ppermute x2, waiting for transfers between devices, gather_column(): values.append(lax.ppermute(panel, ('col', 'row'), pairs))  11.9 us
    unnamed x8, local copies, waits for them, and re-layouts  7.24 us
    pallas_call x1, Pallas kernels, update(): pl.pallas_call(functools.partial(update_kernel, sizes), out_shape=jax.Sha...  6.41 us
    pallas_call x1, Pallas kernels, inverse_factor(): pl.pallas_call(inverse_factor_kernel, out_shape=jax.ShapeDtypeStruct((n,...  6.33 us
    pallas_call x1, Pallas kernels, apply_factor(): pl.pallas_call(functools.partial(apply_factor_kernel, sizes), out_shape=(...  4.77 us
  transfers between devices with their start and end apart: 25, of which 10 were waited for; matrix products, arithmetic and copies ran while one was open for 4% of the time, Pallas kernels for 8%

profile of v1, /device:TPU:0, one launch (start us, length us, event | category | flops | bytes accessed | tf_op | source)
XLA Modules:
  0.0 144.7 jit_solution(6444976366143344682)
XLA Ops:
  0.6 6.3 %copy.23 = f32[3072,512]{1,0:T(8,128)} copy(f32[3072,512]{1,0:T(8,128)} %param.6) | data formatting | bytes 12582912
  6.9 0.1 pad_add_fusion
  7.0 0.1 copy.15
  7.1 0.1 reshape.226.fill_ref
  7.2 1.2 shard_map.65
  9.1 134.7 %conditional.1 = (f32[384,512]{1,0:T(8,128)S(1)}, f32[3072,512]{1,0:T(8,128)}) conditional(s32[]{:T(128)} %bitcast.18, (f32[64,512]{1,0:T(8,128)}, f32[384,512]{1,0:T(8,128)S(1)}, s32[2]{0:T(128)S(1)}, s32[96]{0:T(128)S(1)}, f32[3072,512]{1,0:T(8,128)}, /*index=5*/f32[384,512]{1,0:T(8,128)S(1)}) %tuple.26, (f32[64,512]{1,0:T(8,128)}, ...), branch_computations={%region_0.1_spmd, %region_1.2_spmd} | conditional | flops 2359374 | bytes 102500328 | solution.py:406
  9.3 0.0 copy-start.10
  9.4 1.3 collective-permute-start.35
  10.7 1.6 %collective-permute-start.34 = (f32[384,512]{1,0:T(8,128)S(1)}, f32[384,512]{1,0:T(8,128)}, u32[]{:S(2)}, u32[]{:S(2)}) collective-permute-start(f32[384,512]{1,0:T(8,128)S(1)} %get-tuple-element.46.panel_ref), channel_id=1, source_target_pairs={{0,0},{4,4},{8,8},{16,12},{20,16},{24,20},{1,25},{5,29}} | collective-permute-start | bytes 2359304 | tf_op jit(solution)/shard_map/cond/branch_1_fun/ppermute | solution.py:362
  12.2 11.9 %collective-permute-done.35 = f32[384,512]{1,0:T(8,128)S(1)} collective-permute-done((f32[384,512]{1,0:T(8,128)S(1)}, f32[384,512]{1,0:T(8,128)S(1)}, u32[]{:S(2)}, u32[]{:S(2)}) %collective-permute-start.35) | collective-permute-done | bytes 786464 | tf_op jit(solution)/shard_map/cond/branch_1_fun/ppermute | solution.py:362
  24.2 0.0 collective-permute-done.34
  24.2 1.4 fusion.2
  25.6 0.1 collective-permute-start.36
  25.7 0.8 dynamic-slice_bitcast_fusion.3
  26.6 2.8 %collective-permute-start.25 = (f32[1,32,512]{2,1,0:T(8,128)S(1)}, f32[1,32,512]{2,1,0:T(8,128)S(1)}, u32[]{:S(2)}, u32[]{:S(2)}) collective-permute-start(f32[1,32,512]{2,1,0:T(8,128)S(1)} %dynamic-slice_bitcast_fusion.3), channel_id=1, source_target_pairs={{0,4},{4,0},{8,12},{12,8},{16,20},{20,16},{24,28},{28,24},{1,5},{5... | collective-permute-start | bytes 196616 | tf_op jit(solution)/shard_map/cond/branch_1_fun/ppermute | solution.py:331
  29.4 0.1 dynamic-slice_bitcast_fusion.2
  29.5 0.1 collective-permute-start.29
  29.5 2.1 %collective-permute-done.25 = f32[1,32,512]{2,1,0:T(8,128)S(1)} collective-permute-done((f32[1,32,512]{2,1,0:T(8,128)S(1)}, f32[1,32,512]{2,1,0:T(8,128)S(1)}, u32[]{:S(2)}, u32[]{:S(2)}) %collective-permute-start.25) | collective-permute-done | bytes 65568 | tf_op jit(solution)/shard_map/cond/branch_1_fun/ppermute | solution.py:331
  31.6 4.3 %collective-permute-start.26 = (f32[2,32,512]{2,1,0:T(8,128)S(1)}, f32[2,32,512]{2,1,0:T(8,128)S(1)}, u32[]{:S(2)}, u32[]{:S(2)}) collective-permute-start(f32[2,32,512]{2,1,0:T(8,128)S(1)} %maximum_select_fusion.7), channel_id=1, source_target_pairs={{0,8},{4,12},{8,0},{12,4},{16,24},{20,28},{24,16},{28,20},{1,9},{5... | collective-permute-start | bytes 393224 | tf_op jit(solution)/shard_map/cond/branch_1_fun/ppermute | solution.py:331
  35.9 2.9 %collective-permute-done.26 = f32[2,32,512]{2,1,0:T(8,128)S(1)} collective-permute-done((f32[2,32,512]{2,1,0:T(8,128)S(1)}, f32[2,32,512]{2,1,0:T(8,128)S(1)}, u32[]{:S(2)}, u32[]{:S(2)}) %collective-permute-start.26) | collective-permute-done | bytes 131104 | tf_op jit(solution)/shard_map/cond/branch_1_fun/ppermute | solution.py:331
  38.9 9.1 %collective-permute-start.27 = (f32[4,32,512]{2,1,0:T(8,128)S(1)}, f32[4,32,512]{2,1,0:T(8,128)}, u32[]{:S(2)}, u32[]{:S(2)}) collective-permute-start(f32[4,32,512]{2,1,0:T(8,128)S(1)} %maximum_select_fusion.6), channel_id=1, source_target_pairs={{0,16},{4,20},{8,24},{12,28},{16,0},{20,4},{24,8},{28,12},{1,17},{... | collective-permute-start | bytes 786440 | tf_op jit(solution)/shard_map/cond/branch_1_fun/ppermute | solution.py:331
  48.0 0.1 collective-permute-start.30
  48.1 11.7 %collective-permute-done.27 = f32[4,32,512]{2,1,0:T(8,128)} collective-permute-done((f32[4,32,512]{2,1,0:T(8,128)S(1)}, f32[4,32,512]{2,1,0:T(8,128)}, u32[]{:S(2)}, u32[]{:S(2)}) %collective-permute-start.27) | collective-permute-done | bytes 262176 | tf_op jit(solution)/shard_map/cond/branch_1_fun/ppermute | solution.py:331
  59.8 1.1 maximum_select_fusion.5
  60.9 0.1 collective-permute-start.28
  61.0 0.0 collective-permute-done.36
  61.1 1.2 broadcast_select_fusion.2
  62.3 0.5 collective-permute-start.37
  62.8 0.0 collective-permute-done.30.core_ref
  62.8 0.9 branch_1_fun.4.refs_0_
  63.7 2.8 %collective-permute-start.33 = (f32[10,32,256]{2,1,0:T(8,128)S(1)}, f32[10,32,256]{2,1,0:T(8,128)S(1)}, u32[]{:S(2)}, u32[]{:S(2)}) collective-permute-start(f32[10,32,256]{2,1,0:T(8,128)S(1)} %branch_1_fun.4.refs_0_), channel_id=1, source_target_pairs={{0,24},{4,28},{8,16},{12,20},{16,8},{20,12},{24,0},{28,4},{1,25},{... | collective-permute-start | bytes 983048 | tf_op jit(solution)/shard_map/cond/branch_1_fun/ppermute | solution.py:331
  66.5 1.6 %collective-permute-start.31 = (f32[10,32,256]{2,1,0:T(8,128)S(1)}, f32[10,32,256]{2,1,0:T(8,128)S(1)}, u32[]{:S(2)}, u32[]{:S(2)}) collective-permute-start(f32[10,32,256]{2,1,0:T(8,128)S(1)} %branch_1_fun.4.refs_0_), channel_id=1, source_target_pairs={{0,8},{4,12},{8,0},{12,4},{16,24},{20,28},{24,16},{28,20},{1,9},{5... | collective-permute-start | bytes 983048 | tf_op jit(solution)/shard_map/cond/branch_1_fun/ppermute | solution.py:331
  68.2 0.0 collective-permute-done.28
  68.2 1.4 maximum_select_fusion.4
  69.5 6.8 %collective-permute-done.33.refs_12_ = f32[10,32,256]{2,1,0:T(8,128)S(1)} collective-permute-done((f32[10,32,256]{2,1,0:T(8,128)S(1)}, f32[10,32,256]{2,1,0:T(8,128)S(1)}, u32[]{:S(2)}, u32[]{:S(2)}) %collective-permute-start.33) | collective-permute-done | bytes 327712 | tf_op jit(solution)/shard_map/cond/branch_1_fun/ppermute | solution.py:331
  76.3 17.7 %collective-permute-done.32.refs_8_ = f32[10,32,256]{2,1,0:T(8,128)S(1)} collective-permute-done((f32[10,32,256]{2,1,0:T(8,128)S(1)}, f32[10,32,256]{2,1,0:T(8,128)S(1)}, u32[]{:S(2)}, u32[]{:S(2)}) %collective-permute-start.32) | collective-permute-done | bytes 327712 | tf_op jit(solution)/shard_map/cond/branch_1_fun/ppermute | solution.py:331
  94.0 0.0 collective-permute-done.31.refs_4_
  94.0 1.7 %collective-permute-start.39 = (f32[10,32,256]{2,1,0:T(8,128)S(1)}, f32[10,32,256]{2,1,0:T(8,128)S(1)}, u32[]{:S(2)}, u32[]{:S(2)}) collective-permute-start(f32[10,32,256]{2,1,0:T(8,128)S(1)} %branch_1_fun.4.refs_0_), channel_id=1, source_target_pairs={{0,4},{4,0},{8,12},{12,8},{16,20},{20,16},{24,28},{28,24},{1,5},{5... | collective-permute-start | bytes 983048 | tf_op jit(solution)/shard_map/cond/branch_1_fun/ppermute | solution.py:331
  95.7 0.0 collective-permute-start.38
  95.7 0.3 collective-permute-start.42
  96.0 0.2 collective-permute-start.41
  96.3 8.4 %collective-permute-done.39.refs_2_ = f32[10,32,256]{2,1,0:T(8,128)S(1)} collective-permute-done((f32[10,32,256]{2,1,0:T(8,128)S(1)}, f32[10,32,256]{2,1,0:T(8,128)S(1)}, u32[]{:S(2)}, u32[]{:S(2)}) %collective-permute-start.39) | collective-permute-done | bytes 327712 | tf_op jit(solution)/shard_map/cond/branch_1_fun/ppermute | solution.py:331
  104.6 1.7 %collective-permute-start.45 = (f32[10,32,256]{2,1,0:T(8,128)S(1)}, f32[10,32,256]{2,1,0:T(8,128)}, u32[]{:S(2)}, u32[]{:S(2)}) collective-permute-start(f32[10,32,256]{2,1,0:T(8,128)S(1)} %collective-permute-done.32.refs_8_), channel_id=1, source_target_pairs={{0,4},{4,0},{8,12},{12,8},{16,20},{20,16},{24,28},{28,24},{1,5},{5... | collective-permute-start | bytes 983048 | tf_op jit(solution)/shard_map/cond/branch_1_fun/ppermute | solution.py:331
  106.3 0.0 collective-permute-done.38.refs_1_
  106.3 0.0 collective-permute-start.44
  106.3 5.3 %collective-permute-done.42.refs_6_ = f32[10,32,256]{2,1,0:T(8,128)S(1)} collective-permute-done((f32[10,32,256]{2,1,0:T(8,128)S(1)}, f32[10,32,256]{2,1,0:T(8,128)S(1)}, u32[]{:S(2)}, u32[]{:S(2)}) %collective-permute-start.42) | collective-permute-done | bytes 327712 | tf_op jit(solution)/shard_map/cond/branch_1_fun/ppermute | solution.py:331
  111.7 1.7 %collective-permute-start.48 = (f32[10,32,256]{2,1,0:T(8,128)S(1)}, f32[10,32,256]{2,1,0:T(8,128)}, u32[]{:S(2)}, u32[]{:S(2)}) collective-permute-start(f32[10,32,256]{2,1,0:T(8,128)S(1)} %collective-permute-done.33.refs_12_), channel_id=1, source_target_pairs={{0,4},{4,0},{8,12},{12,8},{16,20},{20,16},{24,28},{28,24},{1,5},{5... | collective-permute-start | bytes 983048 | tf_op jit(solution)/shard_map/cond/branch_1_fun/ppermute | solution.py:331
  113.3 0.0 collective-permute-done.41.refs_5_
  113.3 0.7 copy-done.4
  114.1 0.0 collective-permute-start.47
  114.1 4.7 %collective-permute-done.45.refs_10_ = f32[10,32,256]{2,1,0:T(8,128)} collective-permute-done((f32[10,32,256]{2,1,0:T(8,128)S(1)}, f32[10,32,256]{2,1,0:T(8,128)}, u32[]{:S(2)}, u32[]{:S(2)}) %collective-permute-start.45) | collective-permute-done | bytes 327712 | tf_op jit(solution)/shard_map/cond/branch_1_fun/ppermute | solution.py:331
  118.8 0.0 collective-permute-start.40
  118.8 0.7 copy-done.6
  119.5 0.5 collective-permute-start.43
  120.0 4.2 %collective-permute-done.48.refs_14_ = f32[10,32,256]{2,1,0:T(8,128)} collective-permute-done((f32[10,32,256]{2,1,0:T(8,128)S(1)}, f32[10,32,256]{2,1,0:T(8,128)}, u32[]{:S(2)}, u32[]{:S(2)}) %collective-permute-start.48) | collective-permute-done | bytes 327712 | tf_op jit(solution)/shard_map/cond/branch_1_fun/ppermute | solution.py:331
  124.3 0.0 collective-permute-start.46
  124.3 0.0 collective-permute-done.37
  124.3 0.5 collective-permute-start.49
  124.8 6.3 %branch_1_fun.5.w_ref = f32[512,512]{1,0:T(8,128)S(1)} custom-call(f32[512,512]{1,0:T(8,128)S(1)} %bitcast.26), custom_call_target="tpu_custom_call" | custom-call | tf_op jit(solution)/shard_map/cond/branch_1_fun/pallas_call | solution.py:99
  131.1 1.4 %broadcast_select_fusion.3.column_ref = f32[512,512]{1,0:T(8,128)S(1)} fusion(f32[512,512]{1,0:T(8,128)} %collective-permute-done.37, f32[512,512]{1,0:T(8,128)} %broadcast_select_fusion.2, pred[]{:T(512)S(6)} %ne.80), kind=kLoop, calls=%fused_computation.23 | loop fusion | flops 262144 | bytes 3145729 | tf_op jit(solution)/shard_map/cond/branch_1_fun/jit(_where)/select_n | solution.py:367
  132.6 4.8 %branch_1_fun.6 = (f32[384,512]{1,0:T(8,128)S(1)}, bf16[512,512]{1,0:T(8,128)(2,1)S(1)}, bf16[512,512]{1,0:T(8,128)(2,1)S(1)}, s32[48]{0:T(128)S(1)}) custom-call(s32[2]{0:T(128)S(1)} %get-tuple-element.40.where_ref, s32[96]{0:T(128)S(1)} %get-tuple-element.41.fill_ref, f32[512,512]{1,0:T(8,128)S(1)} %branch_1_fun.5.w_ref, f32[384,512]{1,0:T(8,128)} %copy-done.10, ...), custom_call_target="tpu_custom_call" | custom-call | tf_op jit(solution)/shard_map/cond/branch_1_fun/pallas_call | solution.py:243
  137.4 6.4 %branch_1_fun.7 = f32[3072,512]{1,0:T(8,128)} custom-call(s32[2]{0:T(128)S(1)} %get-tuple-element.40.where_ref, s32[48]{0:T(128)S(1)} %get-tuple-element.47.slot_ref, bf16[512,512]{1,0:T(8,128)(2,1)S(1)} %get-tuple-element.48.high_ref, bf16[512,512]{1,0:T(8,128)(2,1)S(1)} %get-tuple-element.49.low_ref, ...), custom_call_target="tpu_custom_call", output_to_operand_aliasing={{}: (4, {})} | custom-call | tf_op jit(solution)/shard_map/cond/branch_1_fun/pallas_call | solution.py:313
  143.9 0.0 copy-start.13
  143.9 0.9 copy-done.13
  (22 shorter events, 0.1 us)
Async XLA Ops:
  0.6 6.4 %copy-start.12 = (s32[48,2]{0,1:T(2,128)S(1)}, s32[48,2]{0,1:T(2,128)}, u32[]{:S(2)}) copy-start(s32[48,2]{0,1:T(2,128)} %param.9) | copy-start | bytes 1156
  0.6 8.5 %copy-start.8 = (f32[384,512]{1,0:T(8,128)S(1)}, f32[384,512]{1,0:T(8,128)}, u32[]{:S(2)}) copy-start(f32[384,512]{1,0:T(8,128)} %param.7) | copy-start | bytes 2359300
  9.3 54.4 %copy-start.10 = (f32[384,512]{1,0:T(8,128)}, f32[384,512]{1,0:T(8,128)S(1)}, u32[]{:S(2)}) copy-start(f32[384,512]{1,0:T(8,128)S(1)} %get-tuple-element.46.panel_ref) | copy-start | bytes 2359300 | tf_op jit(solution)/shard_map/cond
  9.4 14.8 %collective-permute-start.35 = (f32[384,512]{1,0:T(8,128)S(1)}, f32[384,512]{1,0:T(8,128)S(1)}, u32[]{:S(2)}, u32[]{:S(2)}) collective-permute-start(f32[384,512]{1,0:T(8,128)S(1)} %get-tuple-element.46.panel_ref), channel_id=1, source_target_pairs={{4,0},{8,4},{12,8},{20,12},{24,16},{28,20},{5,25},{9,29}} | collective-permute-start | bytes 2359304 | tf_op jit(solution)/shard_map/cond/branch_1_fun/ppermute | solution.py:362
  10.7 13.5 %collective-permute-start.34 = (f32[384,512]{1,0:T(8,128)S(1)}, f32[384,512]{1,0:T(8,128)}, u32[]{:S(2)}, u32[]{:S(2)}) collective-permute-start(f32[384,512]{1,0:T(8,128)S(1)} %get-tuple-element.46.panel_ref), channel_id=1, source_target_pairs={{0,0},{4,4},{8,8},{16,12},{20,16},{24,20},{1,25},{5,29}} | collective-permute-start | bytes 2359304 | tf_op jit(solution)/shard_map/cond/branch_1_fun/ppermute | solution.py:362
  25.6 35.4 %collective-permute-start.36 = (f32[512,512]{1,0:T(8,128)S(1)}, f32[512,512]{1,0:T(8,128)}, u32[]{:S(2)}, u32[]{:S(2)}) collective-permute-start(f32[512,512]{1,0:T(8,128)S(1)} %fusion.2), channel_id=1, source_target_pairs={{0,2},{1,3},{2,0},{3,1},{4,6},{5,7},{6,4},{7,5},{8,10},{9,11},{10,... | collective-permute-start | bytes 3145736 | tf_op jit(solution)/shard_map/cond/branch_1_fun/ppermute | solution.py:331
  26.6 5.1 %collective-permute-start.25 = (f32[1,32,512]{2,1,0:T(8,128)S(1)}, f32[1,32,512]{2,1,0:T(8,128)S(1)}, u32[]{:S(2)}, u32[]{:S(2)}) collective-permute-start(f32[1,32,512]{2,1,0:T(8,128)S(1)} %dynamic-slice_bitcast_fusion.3), channel_id=1, source_target_pairs={{0,4},{4,0},{8,12},{12,8},{16,20},{20,16},{24,28},{28,24},{1,5},{5... | collective-permute-start | bytes 196616 | tf_op jit(solution)/shard_map/cond/branch_1_fun/ppermute | solution.py:331
  29.5 18.5 %collective-permute-start.29 = (f32[3,64,512]{2,1,0:T(8,128)S(1)}, f32[3,64,512]{2,1,0:T(8,128)S(1)}, u32[]{:S(2)}, u32[]{:S(2)}) collective-permute-start(f32[3,64,512]{2,1,0:T(8,128)S(1)} %get-tuple-element.72), channel_id=1, source_target_pairs={{0,4},{4,0},{8,12},{12,8},{16,20},{20,16},{24,28},{28,24},{1,5},{5... | collective-permute-start | bytes 1179656 | tf_op jit(solution)/shard_map/cond/branch_1_fun/ppermute | solution.py:331
  31.6 7.2 %collective-permute-start.26 = (f32[2,32,512]{2,1,0:T(8,128)S(1)}, f32[2,32,512]{2,1,0:T(8,128)S(1)}, u32[]{:S(2)}, u32[]{:S(2)}) collective-permute-start(f32[2,32,512]{2,1,0:T(8,128)S(1)} %maximum_select_fusion.7), channel_id=1, source_target_pairs={{0,8},{4,12},{8,0},{12,4},{16,24},{20,28},{24,16},{28,20},{1,9},{5... | collective-permute-start | bytes 393224 | tf_op jit(solution)/shard_map/cond/branch_1_fun/ppermute | solution.py:331
  38.9 20.9 %collective-permute-start.27 = (f32[4,32,512]{2,1,0:T(8,128)S(1)}, f32[4,32,512]{2,1,0:T(8,128)}, u32[]{:S(2)}, u32[]{:S(2)}) collective-permute-start(f32[4,32,512]{2,1,0:T(8,128)S(1)} %maximum_select_fusion.6), channel_id=1, source_target_pairs={{0,16},{4,20},{8,24},{12,28},{16,0},{20,4},{24,8},{28,12},{1,17},{... | collective-permute-start | bytes 786440 | tf_op jit(solution)/shard_map/cond/branch_1_fun/ppermute | solution.py:331
  48.0 14.8 %collective-permute-start.30 = (f32[2,3,32,512]{3,2,1,0:T(8,128)S(1)}, f32[2,3,32,512]{3,2,1,0:T(8,128)S(1)}, u32[]{:S(2)}, u32[]{:S(2)}) collective-permute-start(f32[2,3,32,512]{3,2,1,0:T(8,128)S(1)} %fusion.3), channel_id=1, source_target_pairs={{0,1},{1,0},{2,3},{3,2},{4,5},{5,4},{6,7},{7,6},{8,9},{9,8},{10,11... | collective-permute-start | bytes 1179656 | tf_op jit(solution)/shard_map/cond/branch_1_fun/ppermute | solution.py:331
  60.9 7.2 %collective-permute-start.28 = (f32[1,8,32,512]{3,2,0,1:T(8,128)S(1)}, f32[1,8,32,512]{3,2,0,1:T(8,128)}, u32[]{:S(2)}, u32[]{:S(2)}) collective-permute-start(f32[1,8,32,512]{3,2,0,1:T(8,128)S(1)} %maximum_select_fusion.5), channel_id=1, source_target_pairs={{0,1},{1,0},{2,3},{3,2},{4,5},{5,4},{6,7},{7,6},{8,9},{9,8},{10,11... | collective-permute-start | bytes 1572872 | tf_op jit(solution)/shard_map/cond/branch_1_fun/ppermute | solution.py:331
  62.3 62.0 %collective-permute-start.37 = (f32[512,512]{1,0:T(8,128)}, f32[512,512]{1,0:T(8,128)}, u32[]{:S(2)}, u32[]{:S(2)}) collective-permute-start(f32[512,512]{1,0:T(8,128)} %broadcast_select_fusion.2), channel_id=1, source_target_pairs={{0,1},{1,0},{2,3},{3,2},{4,5},{5,4},{6,7},{7,6},{8,9},{9,8},{10,11... | collective-permute-start | bytes 3145736 | tf_op jit(solution)/shard_map/cond/branch_1_fun/ppermute | solution.py:331
  63.7 12.6 %collective-permute-start.33 = (f32[10,32,256]{2,1,0:T(8,128)S(1)}, f32[10,32,256]{2,1,0:T(8,128)S(1)}, u32[]{:S(2)}, u32[]{:S(2)}) collective-permute-start(f32[10,32,256]{2,1,0:T(8,128)S(1)} %branch_1_fun.4.refs_0_), channel_id=1, source_target_pairs={{0,24},{4,28},{8,16},{12,20},{16,8},{20,12},{24,0},{28,4},{1,25},{... | collective-permute-start | bytes 983048 | tf_op jit(solution)/shard_map/cond/branch_1_fun/ppermute | solution.py:331
  66.5 27.5 %collective-permute-start.32 = (f32[10,32,256]{2,1,0:T(8,128)S(1)}, f32[10,32,256]{2,1,0:T(8,128)S(1)}, u32[]{:S(2)}, u32[]{:S(2)}) collective-permute-start(f32[10,32,256]{2,1,0:T(8,128)S(1)} %branch_1_fun.4.refs_0_), channel_id=1, source_target_pairs={{0,16},{4,20},{8,24},{12,28},{16,0},{20,4},{24,8},{28,12},{1,17},{... | collective-permute-start | bytes 983048 | tf_op jit(solution)/shard_map/cond/branch_1_fun/ppermute | solution.py:331
  66.5 27.5 %collective-permute-start.31 = (f32[10,32,256]{2,1,0:T(8,128)S(1)}, f32[10,32,256]{2,1,0:T(8,128)S(1)}, u32[]{:S(2)}, u32[]{:S(2)}) collective-permute-start(f32[10,32,256]{2,1,0:T(8,128)S(1)} %branch_1_fun.4.refs_0_), channel_id=1, source_target_pairs={{0,8},{4,12},{8,0},{12,4},{16,24},{20,28},{24,16},{28,20},{1,9},{5... | collective-permute-start | bytes 983048 | tf_op jit(solution)/shard_map/cond/branch_1_fun/ppermute | solution.py:331
  94.0 10.6 %collective-permute-start.39 = (f32[10,32,256]{2,1,0:T(8,128)S(1)}, f32[10,32,256]{2,1,0:T(8,128)S(1)}, u32[]{:S(2)}, u32[]{:S(2)}) collective-permute-start(f32[10,32,256]{2,1,0:T(8,128)S(1)} %branch_1_fun.4.refs_0_), channel_id=1, source_target_pairs={{0,4},{4,0},{8,12},{12,8},{16,20},{20,16},{24,28},{28,24},{1,5},{5... | collective-permute-start | bytes 983048 | tf_op jit(solution)/shard_map/cond/branch_1_fun/ppermute | solution.py:331
  95.7 10.6 %collective-permute-start.38 = (f32[10,32,256]{2,1,0:T(8,128)S(1)}, f32[10,32,256]{2,1,0:T(8,128)S(1)}, u32[]{:S(2)}, u32[]{:S(2)}) collective-permute-start(f32[10,32,256]{2,1,0:T(8,128)S(1)} %branch_1_fun.4.refs_0_), channel_id=1, source_target_pairs={{0,1},{1,0},{2,3},{3,2},{4,5},{5,4},{6,7},{7,6},{8,9},{9,8},{10,11... | collective-permute-start | bytes 983048 | tf_op jit(solution)/shard_map/cond/branch_1_fun/ppermute | solution.py:331
  95.7 16.0 %collective-permute-start.42 = (f32[10,32,256]{2,1,0:T(8,128)S(1)}, f32[10,32,256]{2,1,0:T(8,128)S(1)}, u32[]{:S(2)}, u32[]{:S(2)}) collective-permute-start(f32[10,32,256]{2,1,0:T(8,128)S(1)} %collective-permute-done.31.refs_4_), channel_id=1, source_target_pairs={{0,4},{4,0},{8,12},{12,8},{16,20},{20,16},{24,28},{28,24},{1,5},{5... | collective-permute-start | bytes 983048 | tf_op jit(solution)/shard_map/cond/branch_1_fun/ppermute | solution.py:331
  96.0 17.3 %collective-permute-start.41 = (f32[10,32,256]{2,1,0:T(8,128)S(1)}, f32[10,32,256]{2,1,0:T(8,128)S(1)}, u32[]{:S(2)}, u32[]{:S(2)}) collective-permute-start(f32[10,32,256]{2,1,0:T(8,128)S(1)} %collective-permute-done.31.refs_4_), channel_id=1, source_target_pairs={{0,1},{1,0},{2,3},{3,2},{4,5},{5,4},{6,7},{7,6},{8,9},{9,8},{10,11... | collective-permute-start | bytes 983048 | tf_op jit(solution)/shard_map/cond/branch_1_fun/ppermute | solution.py:331
  104.6 14.1 %collective-permute-start.45 = (f32[10,32,256]{2,1,0:T(8,128)S(1)}, f32[10,32,256]{2,1,0:T(8,128)}, u32[]{:S(2)}, u32[]{:S(2)}) collective-permute-start(f32[10,32,256]{2,1,0:T(8,128)S(1)} %collective-permute-done.32.refs_8_), channel_id=1, source_target_pairs={{0,4},{4,0},{8,12},{12,8},{16,20},{20,16},{24,28},{28,24},{1,5},{5... | collective-permute-start | bytes 983048 | tf_op jit(solution)/shard_map/cond/branch_1_fun/ppermute | solution.py:331
  106.3 12.5 %collective-permute-start.44 = (f32[10,32,256]{2,1,0:T(8,128)S(1)}, f32[10,32,256]{2,1,0:T(8,128)S(1)}, u32[]{:S(2)}, u32[]{:S(2)}) collective-permute-start(f32[10,32,256]{2,1,0:T(8,128)S(1)} %collective-permute-done.32.refs_8_), channel_id=1, source_target_pairs={{0,1},{1,0},{2,3},{3,2},{4,5},{5,4},{6,7},{7,6},{8,9},{9,8},{10,11... | collective-permute-start | bytes 983048 | tf_op jit(solution)/shard_map/cond/branch_1_fun/ppermute | solution.py:331
  111.7 12.6 %collective-permute-start.48 = (f32[10,32,256]{2,1,0:T(8,128)S(1)}, f32[10,32,256]{2,1,0:T(8,128)}, u32[]{:S(2)}, u32[]{:S(2)}) collective-permute-start(f32[10,32,256]{2,1,0:T(8,128)S(1)} %collective-permute-done.33.refs_12_), channel_id=1, source_target_pairs={{0,4},{4,0},{8,12},{12,8},{16,20},{20,16},{24,28},{28,24},{1,5},{5... | collective-permute-start | bytes 983048 | tf_op jit(solution)/shard_map/cond/branch_1_fun/ppermute | solution.py:331
  113.3 0.7 copy-start.4
  114.1 23.3 %collective-permute-start.47 = (f32[10,32,256]{2,1,0:T(8,128)S(1)}, f32[10,32,256]{2,1,0:T(8,128)}, u32[]{:S(2)}, u32[]{:S(2)}) collective-permute-start(f32[10,32,256]{2,1,0:T(8,128)S(1)} %collective-permute-done.33.refs_12_), channel_id=1, source_target_pairs={{0,1},{1,0},{2,3},{3,2},{4,5},{5,4},{6,7},{7,6},{8,9},{9,8},{10,11... | collective-permute-start | bytes 983048 | tf_op jit(solution)/shard_map/cond/branch_1_fun/ppermute | solution.py:331
  118.8 18.6 %collective-permute-start.40 = (f32[10,32,256]{2,1,0:T(8,128)S(1)}, f32[10,32,256]{2,1,0:T(8,128)}, u32[]{:S(2)}, u32[]{:S(2)}) collective-permute-start(f32[10,32,256]{2,1,0:T(8,128)S(1)} %collective-permute-done.39.refs_2_), channel_id=1, source_target_pairs={{0,1},{1,0},{2,3},{3,2},{4,5},{5,4},{6,7},{7,6},{8,9},{9,8},{10,11... | collective-permute-start | bytes 983048 | tf_op jit(solution)/shard_map/cond/branch_1_fun/ppermute | solution.py:331
  118.8 0.7 copy-start.6
  119.5 17.9 %collective-permute-start.43 = (f32[10,32,256]{2,1,0:T(8,128)S(1)}, f32[10,32,256]{2,1,0:T(8,128)}, u32[]{:S(2)}, u32[]{:S(2)}) collective-permute-start(f32[10,32,256]{2,1,0:T(8,128)S(1)} %collective-permute-done.42.refs_6_), channel_id=1, source_target_pairs={{0,1},{1,0},{2,3},{3,2},{4,5},{5,4},{6,7},{7,6},{8,9},{9,8},{10,11... | collective-permute-start | bytes 983048 | tf_op jit(solution)/shard_map/cond/branch_1_fun/ppermute | solution.py:331
  124.3 13.1 %collective-permute-start.46 = (f32[10,32,256]{2,1,0:T(8,128)}, f32[10,32,256]{2,1,0:T(8,128)}, u32[]{:S(2)}, u32[]{:S(2)}) collective-permute-start(f32[10,32,256]{2,1,0:T(8,128)} %collective-permute-done.45.refs_10_), channel_id=1, source_target_pairs={{0,1},{1,0},{2,3},{3,2},{4,5},{5,4},{6,7},{7,6},{8,9},{9,8},{10,11... | collective-permute-start | bytes 983048 | tf_op jit(solution)/shard_map/cond/branch_1_fun/ppermute | solution.py:331
  124.3 13.1 %collective-permute-start.49 = (f32[10,32,256]{2,1,0:T(8,128)}, f32[10,32,256]{2,1,0:T(8,128)}, u32[]{:S(2)}, u32[]{:S(2)}) collective-permute-start(f32[10,32,256]{2,1,0:T(8,128)} %collective-permute-done.48.refs_14_), channel_id=1, source_target_pairs={{0,1},{1,0},{2,3},{3,2},{4,5},{5,4},{6,7},{7,6},{8,9},{9,8},{10,11... | collective-permute-start | bytes 983048 | tf_op jit(solution)/shard_map/cond/branch_1_fun/ppermute | solution.py:331
  124.8 12.6 %copy-start.5 = (f32[10,32,256]{2,1,0:T(8,128)S(1)}, f32[10,32,256]{2,1,0:T(8,128)}, u32[]{:S(2)}) copy-start(f32[10,32,256]{2,1,0:T(8,128)} %copy-done.4) | copy-start | bytes 983044 | tf_op jit(solution)/shard_map/cond
  124.8 12.6 %copy-start.7 = (f32[10,32,256]{2,1,0:T(8,128)S(1)}, f32[10,32,256]{2,1,0:T(8,128)}, u32[]{:S(2)}) copy-start(f32[10,32,256]{2,1,0:T(8,128)} %copy-done.6) | copy-start | bytes 983044 | tf_op jit(solution)/shard_map/cond
  143.9 0.9 copy-start.13

commit v2 on v1

--- a/solution.py
+++ b/solution.py
@@ -336,22 +336,12 @@
     return jnp.where(second, jnp.concatenate([other, own], 0), jnp.concatenate([own, other], 0))
 
 
-def gather_pivot(sizes, pivot_block):
-    r, c = lax.axis_index("row"), lax.axis_index("col")
-    share = pivot_block.shape[0] // 2
-    value = lax.dynamic_slice_in_dim(pivot_block, r % 2 * share, share, 0)[None]
-    step = 1
-    while step < sizes.cols:
-        value = join(c, step, value, swap(value, "col", step))
-        step *= 2
-    value = join(r, 1, value[None], swap(value[None], "row", 1))
-    return value.transpose(1, 0, 2, 3).reshape(2 * sizes.cols * share, -1)
+def after(value, *earlier):
+    return lax.optimization_barrier((value, *earlier))[0]
 
 
 def gather_column(sizes, panel):
     counts = sizes.sources()
-    r, c = lax.axis_index("row"), lax.axis_index("col")
-    target = c * sizes.width // sizes.slab
     values = []
     for j in range(max(counts)):
         pairs = []
@@ -360,23 +350,33 @@
             if j < counts[at]:
                 pairs.append(((first + j) * sizes.rows + slab, at * sizes.rows + slab))
         values.append(lax.ppermute(panel, ("col", "row"), pairs))
-    start = (c * sizes.width - target * sizes.slab) % sizes.piece
-    value = lax.dynamic_slice_in_dim(jnp.concatenate(values, 0), start, sizes.width, 0)
-    step = sizes.rows // 2
-    while step:
-        value = jnp.where(((r ^ target) & step) != 0, swap(value, "row", step), value)
-        step //= 2
-    return value
-
-
-def gather_pool(sizes, panel):
-    side, core = lax.axis_index("col") % 2, lax.axis_index("row") % 2
-    half, quarter = sizes.unit // 2, sizes.unit // 4
-    own = lax.dynamic_slice_in_dim(panel, side * half, half, 1)
-    from_side = swap(lax.dynamic_slice_in_dim(panel, (1 - side) * half, half, 1), "col", 1)
-    both = jnp.stack([own, from_side])
-    from_core = swap(lax.dynamic_slice_in_dim(both, (1 - core) * quarter, quarter, 2), "row", 1)
-    return from_side, from_core
+    return values
+
+
+def select_column(sizes, values):
+    start = lax.axis_index("col") * sizes.width % sizes.slab % sizes.piece
+    return lax.dynamic_slice_in_dim(jnp.concatenate(values, 0), start, sizes.width, 0)
+
+
+def spread_column(sizes, value, step):
+    r, c = lax.axis_index("row"), lax.axis_index("col")
+    target = c * sizes.width // sizes.slab
+    return jnp.where(((r ^ target) & step) != 0, swap(value, "row", step), value)
+
+
+def copy_kernel(source_ref, target_ref):
+    target_ref[...] = source_ref[...]
+
+
+def copy(window, rows):
+    spec = pl.BlockSpec((rows, window.shape[1]), lambda i: (i, 0))
+    return pl.pallas_call(
+        copy_kernel,
+        out_shape=jax.ShapeDtypeStruct(window.shape, F32),
+        grid=(window.shape[0] // rows,),
+        in_specs=[spec],
+        out_specs=spec,
+    )(window)
 
 
 def per_device(trailing, panel_rows, pivot_block, panel_fill):
@@ -387,19 +387,59 @@
     most = 8 * sizes.per_piece
 
     def run(cap, trailing, panel_rows, pivot_block, fill, units):
-        from_side, from_core = gather_pool(sizes, units)
+        r, c = lax.axis_index("row"), lax.axis_index("col")
+        side, core = c % 2, r % 2
+        half, quarter = sizes.unit // 2, sizes.unit // 4
+        share = pivot_block.shape[0] // 2
+
+        kept = lax.dynamic_slice_in_dim(units, side * half, half, 1)
+        from_side = swap(lax.dynamic_slice_in_dim(units, (1 - side) * half, half, 1), "col", 1)
+        pivot = lax.dynamic_slice_in_dim(pivot_block, core * share, share, 0)[None]
+        pivot = join(c, 1, pivot, swap(pivot, "col", 1))
+        column = gather_column(sizes, panel_rows)
+        from_side, pivot, *column = lax.optimization_barrier((from_side, pivot, *column))
+
+        both = jnp.stack([kept, from_side])
+        from_core = swap(lax.dynamic_slice_in_dim(both, (1 - core) * quarter, quarter, 2), "row", 1)
+        pivot = join(c, 2, pivot, swap(pivot, "col", 2))
+        from_core, pivot = lax.optimization_barrier((from_core, pivot))
         own = pack(sizes, cap, where, fill, units, from_side, from_core)
-        pivot = gather_pivot(sizes, pivot_block)
-        column = gather_column(sizes, panel_rows)
-        arrived = [own] + [swap(own, "col", k) for k in range(2, sizes.cols, 2)]
-        pivot, trailing, *arrived = lax.optimization_barrier((pivot, trailing, *arrived))
-        w = inverse_factor(pivot)
+
+        far = list(range(2, sizes.cols, 2))
+        first, later = [far[-1]] + far[:-2], far[-2:-1]
+        lists = {k: swap(own, "col", k) for k in first}
+        sides = {0: swap(own, "col", 1)}
+        step = 4
+        while step < sizes.cols:
+            pivot = join(c, step, pivot, swap(pivot, "col", step))
+            step *= 2
+        column = lax.optimization_barrier((own, *column))[1:]
+        column = select_column(sizes, column)
+        step = sizes.rows // 2
+        while step > 1:
+            column = spread_column(sizes, column, step)
+            step //= 2
+        held = lax.optimization_barrier((own, pivot, column, sides[0], *lists.values()))
+        own, pivot, column, sides[0] = held[:4]
+        lists = dict(zip(first, held[4:]))
+
+        lists |= {k: swap(own, "col", k) for k in later}
+        sides |= {k: swap(lists[k], "col", 1) for k in first}
+        pivot = join(r, 1, pivot[None], swap(pivot[None], "row", 1))
+        pivot = pivot.transpose(1, 0, 2, 3).reshape(2 * sizes.cols * share, -1)
+        window = copy(after(trailing, own), sizes.block)
+        w = inverse_factor(after(pivot, window))
+        column = spread_column(sizes, column, 1)
         own_factor, high, low, slots = apply_factor(sizes, where, fill, w, panel_rows, column)
-        lists = []
-        for value in arrived:
-            other = swap(value, "col", 1)
-            lists += [value, swap(value, "row", 1), other, swap(other, "row", 1)]
-        return update(sizes, where, slots, high, low, trailing, lists), own_factor
+        for k in later:
+            lists[k] = after(lists[k], high, *(sides[j] for j in first))
+            sides[k] = swap(lists[k], "col", 1)
+        lists[0] = own
+        ordered = []
+        for k in range(0, sizes.cols, 2):
+            value, other = lists[k], sides[k]
+            ordered += [value, swap(value, "row", 1), other, swap(other, "row", 1)]
+        return update(sizes, where, slots, high, low, window, ordered), own_factor
 
     cap = most * 5 // 12
     operands = (trailing, panel_rows, pivot_block, fill, units)

time: 146 us -> 114 us (0.78)
  waiting for transfers between devices: 75.9 us -> 46.8 us
  Pallas kernels: 19.6 us -> 26.5 us
  local copies, waits for them, and re-layouts: 9.78 us -> 3.78 us
  starting transfers between devices: 30.9 us -> 27.8 us
    ppermute x23, waiting for transfers between devices: 63.9 us -> 46.8 us  [swap(): return lax.ppermute(value, axis, [(i, i ^ step) for i in range(size)])]
    ppermute x2, waiting for transfers between devices: 11.9 us -> 0.01 us  [gather_column(): values.append(lax.ppermute(panel, ('col', 'row'), pairs))]
    pallas_call x0 -> x1, Pallas kernels: none -> 9.21 us  [copy(): pl.pallas_call(copy_kernel, out_shape=jax.ShapeDtypeStruct(window.shape,...]
    unnamed x8 -> x3, local copies, waits for them, and re-layouts: 7.24 us -> 1.64 us
    ppermute x23, starting transfers between devices: 28.1 us -> 24.8 us  [swap(): return lax.ppermute(value, axis, [(i, i ^ step) for i in range(size)])]
    pallas_call x1, Pallas kernels: 6.41 us -> 4.02 us  [update(): pl.pallas_call(functools.partial(update_kernel, sizes), out_shape=jax.Sha...]
    cond x10 -> x6, local copies, waits for them, and re-layouts: 1.49 us -> 0.02 us
  transfers between devices with their start and end apart: 25 -> 25, of which waited for: 10 -> 6; matrix products, arithmetic and copies ran while one was open for 4% -> 6% of each run, Pallas kernels for 8% -> 18%
where the time goes in v2:
time: 114 us; the launch traced here: 113 us
  waiting for transfers between devices  46.8 us (41%)
  starting transfers between devices  27.8 us (24%)
  Pallas kernels  26.5 us (23%)
  other arithmetic  5.88 us (5%)
  local copies, waits for them, and re-layouts  3.78 us (3%)
  between operations  1.31 us (1%)
    ppermute x23, waiting for transfers between devices, swap(): return lax.ppermute(value, axis, [(i, i ^ step) for i in range(size)])  46.8 us
    ppermute x23, starting transfers between devices, swap(): return lax.ppermute(value, axis, [(i, i ^ step) for i in range(size)])  24.8 us
    pallas_call x1, Pallas kernels, copy(): pl.pallas_call(copy_kernel, out_shape=jax.ShapeDtypeStruct(window.shape,...  9.21 us
    pallas_call x1, Pallas kernels, inverse_factor(): pl.pallas_call(inverse_factor_kernel, out_shape=jax.ShapeDtypeStruct((n,...  6.33 us
    pallas_call x1, Pallas kernels, apply_factor(): pl.pallas_call(functools.partial(apply_factor_kernel, sizes), out_shape=(...  4.18 us
    pallas_call x1, Pallas kernels, update(): pl.pallas_call(functools.partial(update_kernel, sizes), out_shape=jax.Sha...  4.02 us
    ppermute x2, starting transfers between devices, gather_column(): values.append(lax.ppermute(panel, ('col', 'row'), pairs))  3.09 us
    select_n x4, other arithmetic, join(): jnp.where(second, jnp.concatenate([other, own], 0), jnp.concatenate([own,...  2.66 us
  transfers between devices with their start and end apart: 25, of which 6 were waited for; matrix products, arithmetic and copies ran while one was open for 6% of the time, Pallas kernels for 18%

profile of v2, /device:TPU:0, one launch (start us, length us, event | category | flops | bytes accessed | tf_op | source)
XLA Modules:
  0.0 112.6 jit_solution(318254310011504003)
XLA Ops:
  0.6 0.1 pad_add_fusion
  0.7 0.8 copy.15
  1.5 0.1 reshape.20.fill_ref
  1.6 1.2 %shard_map.65 = s32[1]{0:T(128)} custom-call(s32[96]{0:T(128)S(1)} %reshape.20.fill_ref), custom_call_target="tpu_custom_call" | custom-call | tf_op jit(solution)/shard_map/pallas_call | solution.py:159
  3.5 108.2 %conditional.1 = (f32[384,512]{1,0:T(8,128)S(1)}, f32[3072,512]{1,0:T(8,128)}) conditional(s32[]{:T(128)} %bitcast.16, (f32[384,512]{1,0:T(8,128)}, f32[64,512]{1,0:T(8,128)}, f32[384,512]{1,0:T(8,128)}, s32[2]{0:T(128)S(1)}, s32[96]{0:T(128)S(1)}, /*index=5*/f32[3072,512]{1,0:T(8,128)}) %tuple.29, (f32[384,512]{1,0:T(8,128)}, f32[64,512]{1,0:T(8,128)}, ...), branch_computations={%region_0.1_spmd, %region_1.2_spmd} | conditional | flops 2359376 | bytes 87820128 | solution.py:446
  3.5 1.3 %collective-permute-start.28 = (f32[384,512]{1,0:T(8,128)}, f32[384,512]{1,0:T(8,128)S(1)}, u32[]{:S(2)}, u32[]{:S(2)}) collective-permute-start(f32[384,512]{1,0:T(8,128)} %get-tuple-element.55.panel_ref), channel_id=1, source_target_pairs={{4,0},{8,4},{12,8},{20,12},{24,16},{28,20},{5,25},{9,29}} | collective-permute-start | bytes 2359304 | tf_op jit(solution)/shard_map/cond/branch_1_fun/ppermute | solution.py:352
  4.8 1.8 %collective-permute-start.27 = (f32[384,512]{1,0:T(8,128)}, f32[384,512]{1,0:T(8,128)S(1)}, u32[]{:S(2)}, u32[]{:S(2)}) collective-permute-start(f32[384,512]{1,0:T(8,128)} %get-tuple-element.55.panel_ref), channel_id=1, source_target_pairs={{0,0},{4,4},{8,8},{16,12},{20,16},{24,20},{1,25},{5,29}} | collective-permute-start | bytes 2359304 | tf_op jit(solution)/shard_map/cond/branch_1_fun/ppermute | solution.py:352
  6.6 1.2 %dynamic-slice_bitcast_fusion.2 = (f32[1,3,64,512]{3,2,1,0:T(8,128)S(1)}, f32[3,64,512]{2,1,0:T(8,128)S(1)}) fusion(f32[3,128,512]{2,1,0:T(8,128)} %bitcast.29, s32[]{:T(128)S(6)} %select_n.141, s32[]{:T(128)S(6)} %select_n.136), kind=kLoop, calls=%fused_computation.25 | loop fusion | bytes 1572872 | tf_op jit(solution)/shard_map/cond/branch_1_fun/stack | solution.py:402
  7.8 3.6 %collective-permute-start.25 = (f32[3,64,512]{2,1,0:T(8,128)S(1)}, f32[3,64,512]{2,1,0:T(8,128)S(1)}, u32[]{:S(2)}, u32[]{:S(2)}) collective-permute-start(f32[3,64,512]{2,1,0:T(8,128)S(1)} %get-tuple-element.94), channel_id=1, source_target_pairs={{0,4},{4,0},{8,12},{12,8},{16,20},{20,16},{24,28},{28,24},{1,5},{5... | collective-permute-start | bytes 1179656 | tf_op jit(solution)/shard_map/cond/branch_1_fun/ppermute | solution.py:331
  11.4 0.8 dynamic-slice_bitcast_fusion.3
  12.2 0.0 collective-permute-start.26
  12.3 16.4 %collective-permute-done.26 = f32[1,32,512]{2,1,0:T(8,128)S(1)} collective-permute-done((f32[1,32,512]{2,1,0:T(8,128)S(1)}, f32[1,32,512]{2,1,0:T(8,128)S(1)}, u32[]{:S(2)}, u32[]{:S(2)}) %collective-permute-start.26) | collective-permute-done | bytes 65568 | tf_op jit(solution)/shard_map/cond/branch_1_fun/ppermute | solution.py:331
  28.7 0.0 collective-permute-done.25.side_ref
  28.7 0.0 collective-permute-done.28
  28.7 0.0 collective-permute-done.27
  28.7 0.0 copy-start.3
  28.8 0.4 collective-permute-start.29
  29.2 3.5 %collective-permute-start.30 = (f32[2,32,512]{2,1,0:T(8,128)S(1)}, f32[2,32,512]{2,1,0:T(8,128)S(1)}, u32[]{:S(2)}, u32[]{:S(2)}) collective-permute-start(f32[2,32,512]{2,1,0:T(8,128)S(1)} %maximum_select_fusion.7), channel_id=1, source_target_pairs={{0,8},{4,12},{8,0},{12,4},{16,24},{20,28},{24,16},{28,20},{1,9},{5... | collective-permute-start | bytes 393224 | tf_op jit(solution)/shard_map/cond/branch_1_fun/ppermute | solution.py:331
  32.6 4.1 %collective-permute-done.30 = f32[2,32,512]{2,1,0:T(8,128)S(1)} collective-permute-done((f32[2,32,512]{2,1,0:T(8,128)S(1)}, f32[2,32,512]{2,1,0:T(8,128)S(1)}, u32[]{:S(2)}, u32[]{:S(2)}) %collective-permute-start.30) | collective-permute-done | bytes 131104 | tf_op jit(solution)/shard_map/cond/branch_1_fun/ppermute | solution.py:331
  36.7 0.0 collective-permute-done.29.core_ref
  36.7 1.5 %branch_1_fun.5.refs_0_ = f32[10,32,256]{2,1,0:T(8,128)S(1)} custom-call(s32[2]{0:T(128)S(1)} %get-tuple-element.51.where_ref, s32[96]{0:T(128)S(1)} %get-tuple-element.52.fill_ref, f32[3,128,512]{2,1,0:T(8,128)} %bitcast.30, f32[3,64,512]{2,1,0:T(8,128)S(1)} %collective-permute-done.25.side_ref, f32[2,3,32,512]{3,2,1,0:T(8,128)S(1)} %collective-permute-done.29.core_ref), custom_call_target="tpu_custom_call" | custom-call | tf_op jit(solution)/shard_map/cond/branch_1_fun/pallas_call | solution.py:195
  38.3 1.4 %fusion.2 = f32[512,512]{1,0:T(8,128)S(1)} fusion(s32[]{:T(128)S(6)} %select_n.151, f32[384,512]{1,0:T(8,128)} %copy-done.3, f32[384,512]{1,0:T(8,128)S(1)} %collective-permute-done.28), kind=kLoop, calls=%fused_computation.17 | loop fusion | flops 262144 | bytes 2621444 | tf_op jit(solution)/shard_map/cond/branch_1_fun/concatenate | solution.py:358
  39.7 0.0 copy-start.2
  39.7 0.1 collective-permute-start.32
  39.8 1.4 %collective-permute-start.31 = (f32[4,32,512]{2,1,0:T(8,128)S(1)}, f32[4,32,512]{2,1,0:T(8,128)S(1)}, u32[]{:S(2)}, u32[]{:S(2)}) collective-permute-start(f32[4,32,512]{2,1,0:T(8,128)S(1)} %maximum_select_fusion.6), channel_id=1, source_target_pairs={{0,16},{4,20},{8,24},{12,28},{16,0},{20,4},{24,8},{28,12},{1,17},{... | collective-permute-start | bytes 786440 | tf_op jit(solution)/shard_map/cond/branch_1_fun/ppermute | solution.py:331
  41.3 1.9 %collective-permute-start.35 = (f32[10,32,256]{2,1,0:T(8,128)S(1)}, f32[10,32,256]{2,1,0:T(8,128)S(1)}, u32[]{:S(2)}, u32[]{:S(2)}) collective-permute-start(f32[10,32,256]{2,1,0:T(8,128)S(1)} %branch_1_fun.5.refs_0_), channel_id=1, source_target_pairs={{0,8},{4,12},{8,0},{12,4},{16,24},{20,28},{24,16},{28,20},{1,9},{5... | collective-permute-start | bytes 983048 | tf_op jit(solution)/shard_map/cond/branch_1_fun/ppermute | solution.py:331
  43.1 1.2 %collective-permute-start.34 = (f32[10,32,256]{2,1,0:T(8,128)S(1)}, f32[10,32,256]{2,1,0:T(8,128)S(1)}, u32[]{:S(2)}, u32[]{:S(2)}) collective-permute-start(f32[10,32,256]{2,1,0:T(8,128)S(1)} %branch_1_fun.5.refs_0_), channel_id=1, source_target_pairs={{0,24},{4,28},{8,16},{12,20},{16,8},{20,12},{24,0},{28,4},{1,25},{... | collective-permute-start | bytes 983048 | tf_op jit(solution)/shard_map/cond/branch_1_fun/ppermute | solution.py:331
  44.3 2.4 %collective-permute-start.33 = (f32[10,32,256]{2,1,0:T(8,128)S(1)}, f32[10,32,256]{2,1,0:T(8,128)S(1)}, u32[]{:S(2)}, u32[]{:S(2)}) collective-permute-start(f32[10,32,256]{2,1,0:T(8,128)S(1)} %branch_1_fun.5.refs_0_), channel_id=1, source_target_pairs={{0,4},{4,0},{8,12},{12,8},{16,20},{20,16},{24,28},{28,24},{1,5},{5... | collective-permute-start | bytes 983048 | tf_op jit(solution)/shard_map/cond/branch_1_fun/ppermute | solution.py:331
  46.7 8.8 %collective-permute-done.31 = f32[4,32,512]{2,1,0:T(8,128)S(1)} collective-permute-done((f32[4,32,512]{2,1,0:T(8,128)S(1)}, f32[4,32,512]{2,1,0:T(8,128)S(1)}, u32[]{:S(2)}, u32[]{:S(2)}) %collective-permute-start.31) | collective-permute-done | bytes 262176 | tf_op jit(solution)/shard_map/cond/branch_1_fun/ppermute | solution.py:331
  55.4 0.8 maximum_select_fusion.5
  56.3 8.5 %collective-permute-done.32 = f32[512,512]{1,0:T(8,128)} collective-permute-done((f32[512,512]{1,0:T(8,128)S(1)}, f32[512,512]{1,0:T(8,128)}, u32[]{:S(2)}, u32[]{:S(2)}) %collective-permute-start.32) | collective-permute-done | bytes 1048608 | tf_op jit(solution)/shard_map/cond/branch_1_fun/ppermute | solution.py:331
  64.8 1.4 %broadcast_select_fusion.3 = f32[512,512]{1,0:T(8,128)S(1)} fusion(f32[512,512]{1,0:T(8,128)} %collective-permute-done.32, f32[512,512]{1,0:T(8,128)} %copy-done.2, pred[]{:T(512)S(6)} %ne.84), kind=kLoop, calls=%fused_computation.23 | loop fusion | flops 262144 | bytes 3145729 | tf_op jit(solution)/shard_map/cond/branch_1_fun/jit(_where)/select_n | solution.py:364
  66.3 0.0 collective-permute-done.35.refs_4_
  66.3 0.0 collective-permute-done.33.refs_2_
  66.3 0.1 collective-permute-start.37
  66.4 0.5 collective-permute-start.36
  66.9 2.4 %collective-permute-start.41 = (f32[10,32,256]{2,1,0:T(8,128)S(1)}, f32[10,32,256]{2,1,0:T(8,128)S(1)}, u32[]{:S(2)}, u32[]{:S(2)}) collective-permute-start(f32[10,32,256]{2,1,0:T(8,128)S(1)} %collective-permute-done.35.refs_4_), channel_id=1, source_target_pairs={{0,4},{4,0},{8,12},{12,8},{16,20},{20,16},{24,28},{28,24},{1,5},{5... | collective-permute-start | bytes 983048 | tf_op jit(solution)/shard_map/cond/branch_1_fun/ppermute | solution.py:331
  69.3 0.0 collective-permute-start.40
  69.3 2.5 %collective-permute-start.43 = (f32[10,32,256]{2,1,0:T(8,128)S(1)}, f32[10,32,256]{2,1,0:T(8,128)S(1)}, u32[]{:S(2)}, u32[]{:S(2)}) collective-permute-start(f32[10,32,256]{2,1,0:T(8,128)S(1)} %branch_1_fun.5.refs_0_), channel_id=1, source_target_pairs={{0,16},{4,20},{8,24},{12,28},{16,0},{20,4},{24,8},{28,12},{1,17},{... | collective-permute-start | bytes 983048 | tf_op jit(solution)/shard_map/cond/branch_1_fun/ppermute | solution.py:331
  71.8 9.2 %branch_1_fun.6.window_ref = f32[3072,512]{1,0:T(8,128)} custom-call(f32[3072,512]{1,0:T(8,128)} %get-tuple-element.67.source_ref), custom_call_target="tpu_custom_call" | custom-call | tf_op jit(solution)/shard_map/cond/branch_1_fun/pallas_call | solution.py:373
  81.0 0.0 collective-permute-done.36
  81.0 0.7 collective-permute-start.44
  81.7 1.8 %maximum_select_fusion.4 = f32[2,8,32,512]{3,2,0,1:T(8,128)S(1)} fusion(f32[1,8,32,512]{3,2,0,1:T(8,128)} %bitcast.12, f32[1,8,32,512]{3,2,0,1:T(8,128)} %collective-permute-done.36, pred[]{:T(512)S(6)} %ne.76), kind=kLoop, calls=%fused_computation.18 | loop fusion | flops 786432 | bytes 2097153 | tf_op jit(solution)/shard_map/cond/branch_1_fun/jit(_where)/select_n | solution.py:336
  83.5 6.3 %branch_1_fun.7.w_ref = f32[512,512]{1,0:T(8,128)S(1)} custom-call(f32[512,512]{1,0:T(8,128)S(1)} %bitcast.24), custom_call_target="tpu_custom_call" | custom-call | tf_op jit(solution)/shard_map/cond/branch_1_fun/pallas_call | solution.py:99
  89.8 0.1 collective-permute-start.48
  89.9 0.2 broadcast_select_fusion.2.column_ref
  90.1 4.2 %branch_1_fun.8 = (f32[384,512]{1,0:T(8,128)S(1)}, bf16[512,512]{1,0:T(8,128)(2,1)S(1)}, bf16[512,512]{1,0:T(8,128)(2,1)S(1)}, s32[48]{0:T(128)S(1)}) custom-call(s32[2]{0:T(128)S(1)} %get-tuple-element.51.where_ref, s32[96]{0:T(128)S(1)} %get-tuple-element.52.fill_ref, f32[512,512]{1,0:T(8,128)S(1)} %branch_1_fun.7.w_ref, f32[384,512]{1,0:T(8,128)S(1)} %copy-done.1, ...), custom_call_target="tpu_custom_call" | custom-call | tf_op jit(solution)/shard_map/cond/branch_1_fun/pallas_call | solution.py:243
  94.3 0.0 collective-permute-done.41.refs_6_
  94.3 1.8 %collective-permute-start.39 = (f32[10,32,256]{2,1,0:T(8,128)S(1)}, f32[10,32,256]{2,1,0:T(8,128)S(1)}, u32[]{:S(2)}, u32[]{:S(2)}) collective-permute-start(f32[10,32,256]{2,1,0:T(8,128)S(1)} %collective-permute-done.33.refs_2_), channel_id=1, source_target_pairs={{0,1},{1,0},{2,3},{3,2},{4,5},{5,4},{6,7},{7,6},{8,9},{9,8},{10,11... | collective-permute-start | bytes 983048 | tf_op jit(solution)/shard_map/cond/branch_1_fun/ppermute | solution.py:331
  96.1 1.3 %collective-permute-start.46 = (f32[10,32,256]{2,1,0:T(8,128)S(1)}, f32[10,32,256]{2,1,0:T(8,128)S(1)}, u32[]{:S(2)}, u32[]{:S(2)}) collective-permute-start(f32[10,32,256]{2,1,0:T(8,128)S(1)} %collective-permute-done.43.refs_8_), channel_id=1, source_target_pairs={{0,4},{4,0},{8,12},{12,8},{16,20},{20,16},{24,28},{28,24},{1,5},{5... | collective-permute-start | bytes 983048 | tf_op jit(solution)/shard_map/cond/branch_1_fun/ppermute | solution.py:331
  97.4 0.0 collective-permute-start.38
  97.4 0.5 collective-permute-start.42
  97.9 0.1 collective-permute-start.49
  98.0 0.0 collective-permute-done.48.refs_13_
  98.0 0.4 collective-permute-start.45
  98.5 7.4 %collective-permute-done.46.refs_10_ = f32[10,32,256]{2,1,0:T(8,128)S(1)} collective-permute-done((f32[10,32,256]{2,1,0:T(8,128)S(1)}, f32[10,32,256]{2,1,0:T(8,128)S(1)}, u32[]{:S(2)}, u32[]{:S(2)}) %collective-permute-start.46) | collective-permute-done | bytes 327712 | tf_op jit(solution)/shard_map/cond/branch_1_fun/ppermute | solution.py:331
  105.8 0.0 collective-permute-start.47
  105.8 0.0 collective-permute-done.38.refs_1_
  105.8 0.0 collective-permute-done.42.refs_7_
  105.8 0.0 collective-permute-done.45.refs_9_
  105.9 1.6 %collective-permute-done.47.refs_11_ = f32[10,32,256]{2,1,0:T(8,128)S(1)} collective-permute-done((f32[10,32,256]{2,1,0:T(8,128)S(1)}, f32[10,32,256]{2,1,0:T(8,128)S(1)}, u32[]{:S(2)}, u32[]{:S(2)}) %collective-permute-start.47) | collective-permute-done | bytes 327712 | tf_op jit(solution)/shard_map/cond/branch_1_fun/ppermute | solution.py:331
  107.4 4.0 %branch_1_fun.9 = f32[3072,512]{1,0:T(8,128)} custom-call(s32[2]{0:T(128)S(1)} %get-tuple-element.51.where_ref, s32[48]{0:T(128)S(1)} %get-tuple-element.70.slot_ref, bf16[512,512]{1,0:T(8,128)(2,1)S(1)} %get-tuple-element.71.high_ref, bf16[512,512]{1,0:T(8,128)(2,1)S(1)} %get-tuple-element.72.low_ref, ...), custom_call_target="tpu_custom_call", output_to_operand_aliasing={{}: (4, {})} | custom-call | tf_op jit(solution)/shard_map/cond/branch_1_fun/pallas_call | solution.py:313
  111.7 0.0 copy-start.4
  111.7 0.9 copy-done.4
  (14 shorter events, 0.1 us)
Async XLA Ops:
  3.5 25.2 %collective-permute-start.28 = (f32[384,512]{1,0:T(8,128)}, f32[384,512]{1,0:T(8,128)S(1)}, u32[]{:S(2)}, u32[]{:S(2)}) collective-permute-start(f32[384,512]{1,0:T(8,128)} %get-tuple-element.55.panel_ref), channel_id=1, source_target_pairs={{4,0},{8,4},{12,8},{20,12},{24,16},{28,20},{5,25},{9,29}} | collective-permute-start | bytes 2359304 | tf_op jit(solution)/shard_map/cond/branch_1_fun/ppermute | solution.py:352
  4.8 23.9 %collective-permute-start.27 = (f32[384,512]{1,0:T(8,128)}, f32[384,512]{1,0:T(8,128)S(1)}, u32[]{:S(2)}, u32[]{:S(2)}) collective-permute-start(f32[384,512]{1,0:T(8,128)} %get-tuple-element.55.panel_ref), channel_id=1, source_target_pairs={{0,0},{4,4},{8,8},{16,12},{20,16},{24,20},{1,25},{5,29}} | collective-permute-start | bytes 2359304 | tf_op jit(solution)/shard_map/cond/branch_1_fun/ppermute | solution.py:352
  7.8 20.9 %collective-permute-start.25 = (f32[3,64,512]{2,1,0:T(8,128)S(1)}, f32[3,64,512]{2,1,0:T(8,128)S(1)}, u32[]{:S(2)}, u32[]{:S(2)}) collective-permute-start(f32[3,64,512]{2,1,0:T(8,128)S(1)} %get-tuple-element.94), channel_id=1, source_target_pairs={{0,4},{4,0},{8,12},{12,8},{16,20},{20,16},{24,28},{28,24},{1,5},{5... | collective-permute-start | bytes 1179656 | tf_op jit(solution)/shard_map/cond/branch_1_fun/ppermute | solution.py:331
  12.2 16.4 %collective-permute-start.26 = (f32[1,32,512]{2,1,0:T(8,128)S(1)}, f32[1,32,512]{2,1,0:T(8,128)S(1)}, u32[]{:S(2)}, u32[]{:S(2)}) collective-permute-start(f32[1,32,512]{2,1,0:T(8,128)S(1)} %dynamic-slice_bitcast_fusion.3), channel_id=1, source_target_pairs={{0,4},{4,0},{8,12},{12,8},{16,20},{20,16},{24,28},{28,24},{1,5},{5... | collective-permute-start | bytes 196616 | tf_op jit(solution)/shard_map/cond/branch_1_fun/ppermute | solution.py:331
  28.7 3.9 %copy-start.3 = (f32[384,512]{1,0:T(8,128)}, f32[384,512]{1,0:T(8,128)S(1)}, u32[]{:S(2)}) copy-start(f32[384,512]{1,0:T(8,128)S(1)} %collective-permute-done.27) | copy-start | bytes 2359300 | tf_op jit(solution)/shard_map/cond
  28.8 8.0 %collective-permute-start.29 = (f32[2,3,32,512]{3,2,1,0:T(8,128)S(1)}, f32[2,3,32,512]{3,2,1,0:T(8,128)S(1)}, u32[]{:S(2)}, u32[]{:S(2)}) collective-permute-start(f32[2,3,32,512]{3,2,1,0:T(8,128)S(1)} %fusion.3), channel_id=1, source_target_pairs={{0,1},{1,0},{2,3},{3,2},{4,5},{5,4},{6,7},{7,6},{8,9},{9,8},{10,11... | collective-permute-start | bytes 1179656 | tf_op jit(solution)/shard_map/cond/branch_1_fun/ppermute | solution.py:331
  29.2 7.6 %collective-permute-start.30 = (f32[2,32,512]{2,1,0:T(8,128)S(1)}, f32[2,32,512]{2,1,0:T(8,128)S(1)}, u32[]{:S(2)}, u32[]{:S(2)}) collective-permute-start(f32[2,32,512]{2,1,0:T(8,128)S(1)} %maximum_select_fusion.7), channel_id=1, source_target_pairs={{0,8},{4,12},{8,0},{12,4},{16,24},{20,28},{24,16},{28,20},{1,9},{5... | collective-permute-start | bytes 393224 | tf_op jit(solution)/shard_map/cond/branch_1_fun/ppermute | solution.py:331
  39.7 16.6 %copy-start.2 = (f32[512,512]{1,0:T(8,128)}, f32[512,512]{1,0:T(8,128)S(1)}, u32[]{:S(2)}) copy-start(f32[512,512]{1,0:T(8,128)S(1)} %fusion.2) | copy-start | bytes 3145732 | tf_op jit(solution)/shard_map/cond
  39.7 25.1 %collective-permute-start.32 = (f32[512,512]{1,0:T(8,128)S(1)}, f32[512,512]{1,0:T(8,128)}, u32[]{:S(2)}, u32[]{:S(2)}) collective-permute-start(f32[512,512]{1,0:T(8,128)S(1)} %fusion.2), channel_id=1, source_target_pairs={{0,2},{1,3},{2,0},{3,1},{4,6},{5,7},{6,4},{7,5},{8,10},{9,11},{10,... | collective-permute-start | bytes 3145736 | tf_op jit(solution)/shard_map/cond/branch_1_fun/ppermute | solution.py:331
  39.8 15.6 %collective-permute-start.31 = (f32[4,32,512]{2,1,0:T(8,128)S(1)}, f32[4,32,512]{2,1,0:T(8,128)S(1)}, u32[]{:S(2)}, u32[]{:S(2)}) collective-permute-start(f32[4,32,512]{2,1,0:T(8,128)S(1)} %maximum_select_fusion.6), channel_id=1, source_target_pairs={{0,16},{4,20},{8,24},{12,28},{16,0},{20,4},{24,8},{28,12},{1,17},{... | collective-permute-start | bytes 786440 | tf_op jit(solution)/shard_map/cond/branch_1_fun/ppermute | solution.py:331
  41.3 25.0 %collective-permute-start.35 = (f32[10,32,256]{2,1,0:T(8,128)S(1)}, f32[10,32,256]{2,1,0:T(8,128)S(1)}, u32[]{:S(2)}, u32[]{:S(2)}) collective-permute-start(f32[10,32,256]{2,1,0:T(8,128)S(1)} %branch_1_fun.5.refs_0_), channel_id=1, source_target_pairs={{0,8},{4,12},{8,0},{12,4},{16,24},{20,28},{24,16},{28,20},{1,9},{5... | collective-permute-start | bytes 983048 | tf_op jit(solution)/shard_map/cond/branch_1_fun/ppermute | solution.py:331
  43.1 23.2 %collective-permute-start.34 = (f32[10,32,256]{2,1,0:T(8,128)S(1)}, f32[10,32,256]{2,1,0:T(8,128)S(1)}, u32[]{:S(2)}, u32[]{:S(2)}) collective-permute-start(f32[10,32,256]{2,1,0:T(8,128)S(1)} %branch_1_fun.5.refs_0_), channel_id=1, source_target_pairs={{0,24},{4,28},{8,16},{12,20},{16,8},{20,12},{24,0},{28,4},{1,25},{... | collective-permute-start | bytes 983048 | tf_op jit(solution)/shard_map/cond/branch_1_fun/ppermute | solution.py:331
  44.3 22.0 %collective-permute-start.33 = (f32[10,32,256]{2,1,0:T(8,128)S(1)}, f32[10,32,256]{2,1,0:T(8,128)S(1)}, u32[]{:S(2)}, u32[]{:S(2)}) collective-permute-start(f32[10,32,256]{2,1,0:T(8,128)S(1)} %branch_1_fun.5.refs_0_), channel_id=1, source_target_pairs={{0,4},{4,0},{8,12},{12,8},{16,20},{20,16},{24,28},{28,24},{1,5},{5... | collective-permute-start | bytes 983048 | tf_op jit(solution)/shard_map/cond/branch_1_fun/ppermute | solution.py:331
  66.3 23.5 %collective-permute-start.37 = (f32[512,512]{1,0:T(8,128)S(1)}, f32[512,512]{1,0:T(8,128)}, u32[]{:S(2)}, u32[]{:S(2)}) collective-permute-start(f32[512,512]{1,0:T(8,128)S(1)} %broadcast_select_fusion.3), channel_id=1, source_target_pairs={{0,1},{1,0},{2,3},{3,2},{4,5},{5,4},{6,7},{7,6},{8,9},{9,8},{10,11... | collective-permute-start | bytes 3145736 | tf_op jit(solution)/shard_map/cond/branch_1_fun/ppermute | solution.py:331
  66.4 14.6 %collective-permute-start.36 = (f32[1,8,32,512]{3,2,0,1:T(8,128)}, f32[1,8,32,512]{3,2,0,1:T(8,128)}, u32[]{:S(2)}, u32[]{:S(2)}) collective-permute-start(f32[1,8,32,512]{3,2,0,1:T(8,128)} %bitcast.12), channel_id=1, source_target_pairs={{0,1},{1,0},{2,3},{3,2},{4,5},{5,4},{6,7},{7,6},{8,9},{9,8},{10,11... | collective-permute-start | bytes 1572872 | tf_op jit(solution)/shard_map/cond/branch_1_fun/ppermute | solution.py:331
  66.9 27.4 %collective-permute-start.41 = (f32[10,32,256]{2,1,0:T(8,128)S(1)}, f32[10,32,256]{2,1,0:T(8,128)S(1)}, u32[]{:S(2)}, u32[]{:S(2)}) collective-permute-start(f32[10,32,256]{2,1,0:T(8,128)S(1)} %collective-permute-done.35.refs_4_), channel_id=1, source_target_pairs={{0,4},{4,0},{8,12},{12,8},{16,20},{20,16},{24,28},{28,24},{1,5},{5... | collective-permute-start | bytes 983048 | tf_op jit(solution)/shard_map/cond/branch_1_fun/ppermute | solution.py:331
  69.3 28.7 %collective-permute-start.40 = (f32[10,32,256]{2,1,0:T(8,128)S(1)}, f32[10,32,256]{2,1,0:T(8,128)S(1)}, u32[]{:S(2)}, u32[]{:S(2)}) collective-permute-start(f32[10,32,256]{2,1,0:T(8,128)S(1)} %collective-permute-done.35.refs_4_), channel_id=1, source_target_pairs={{0,1},{1,0},{2,3},{3,2},{4,5},{5,4},{6,7},{7,6},{8,9},{9,8},{10,11... | collective-permute-start | bytes 983048 | tf_op jit(solution)/shard_map/cond/branch_1_fun/ppermute | solution.py:331
  69.3 26.8 %collective-permute-start.43 = (f32[10,32,256]{2,1,0:T(8,128)S(1)}, f32[10,32,256]{2,1,0:T(8,128)S(1)}, u32[]{:S(2)}, u32[]{:S(2)}) collective-permute-start(f32[10,32,256]{2,1,0:T(8,128)S(1)} %branch_1_fun.5.refs_0_), channel_id=1, source_target_pairs={{0,16},{4,20},{8,24},{12,28},{16,0},{20,4},{24,8},{28,12},{1,17},{... | collective-permute-start | bytes 983048 | tf_op jit(solution)/shard_map/cond/branch_1_fun/ppermute | solution.py:331
  81.0 9.2 %copy-start.1 = (f32[384,512]{1,0:T(8,128)S(1)}, f32[384,512]{1,0:T(8,128)}, u32[]{:S(2)}) copy-start(f32[384,512]{1,0:T(8,128)} %get-tuple-element.55.panel_ref) | copy-start | bytes 2359300 | tf_op jit(solution)/shard_map/cond
  81.0 15.1 %collective-permute-start.44 = (f32[10,32,256]{2,1,0:T(8,128)S(1)}, f32[10,32,256]{2,1,0:T(8,128)S(1)}, u32[]{:S(2)}, u32[]{:S(2)}) collective-permute-start(f32[10,32,256]{2,1,0:T(8,128)S(1)} %collective-permute-done.34.refs_12_), channel_id=1, source_target_pairs={{0,4},{4,0},{8,12},{12,8},{16,20},{20,16},{24,28},{28,24},{1,5},{5... | collective-permute-start | bytes 983048 | tf_op jit(solution)/shard_map/cond/branch_1_fun/ppermute | solution.py:331
  89.8 8.2 %collective-permute-start.48 = (f32[10,32,256]{2,1,0:T(8,128)S(1)}, f32[10,32,256]{2,1,0:T(8,128)S(1)}, u32[]{:S(2)}, u32[]{:S(2)}) collective-permute-start(f32[10,32,256]{2,1,0:T(8,128)S(1)} %collective-permute-done.34.refs_12_), channel_id=1, source_target_pairs={{0,1},{1,0},{2,3},{3,2},{4,5},{5,4},{6,7},{7,6},{8,9},{9,8},{10,11... | collective-permute-start | bytes 983048 | tf_op jit(solution)/shard_map/cond/branch_1_fun/ppermute | solution.py:331
  94.3 3.1 %collective-permute-start.39 = (f32[10,32,256]{2,1,0:T(8,128)S(1)}, f32[10,32,256]{2,1,0:T(8,128)S(1)}, u32[]{:S(2)}, u32[]{:S(2)}) collective-permute-start(f32[10,32,256]{2,1,0:T(8,128)S(1)} %collective-permute-done.33.refs_2_), channel_id=1, source_target_pairs={{0,1},{1,0},{2,3},{3,2},{4,5},{5,4},{6,7},{7,6},{8,9},{9,8},{10,11... | collective-permute-start | bytes 983048 | tf_op jit(solution)/shard_map/cond/branch_1_fun/ppermute | solution.py:331
  96.1 9.7 %collective-permute-start.46 = (f32[10,32,256]{2,1,0:T(8,128)S(1)}, f32[10,32,256]{2,1,0:T(8,128)S(1)}, u32[]{:S(2)}, u32[]{:S(2)}) collective-permute-start(f32[10,32,256]{2,1,0:T(8,128)S(1)} %collective-permute-done.43.refs_8_), channel_id=1, source_target_pairs={{0,4},{4,0},{8,12},{12,8},{16,20},{20,16},{24,28},{28,24},{1,5},{5... | collective-permute-start | bytes 983048 | tf_op jit(solution)/shard_map/cond/branch_1_fun/ppermute | solution.py:331
  97.4 8.4 %collective-permute-start.38 = (f32[10,32,256]{2,1,0:T(8,128)S(1)}, f32[10,32,256]{2,1,0:T(8,128)S(1)}, u32[]{:S(2)}, u32[]{:S(2)}) collective-permute-start(f32[10,32,256]{2,1,0:T(8,128)S(1)} %branch_1_fun.5.refs_0_), channel_id=1, source_target_pairs={{0,1},{1,0},{2,3},{3,2},{4,5},{5,4},{6,7},{7,6},{8,9},{9,8},{10,11... | collective-permute-start | bytes 983048 | tf_op jit(solution)/shard_map/cond/branch_1_fun/ppermute | solution.py:331
  97.4 8.4 %collective-permute-start.42 = (f32[10,32,256]{2,1,0:T(8,128)S(1)}, f32[10,32,256]{2,1,0:T(8,128)S(1)}, u32[]{:S(2)}, u32[]{:S(2)}) collective-permute-start(f32[10,32,256]{2,1,0:T(8,128)S(1)} %collective-permute-done.41.refs_6_), channel_id=1, source_target_pairs={{0,1},{1,0},{2,3},{3,2},{4,5},{5,4},{6,7},{7,6},{8,9},{9,8},{10,11... | collective-permute-start | bytes 983048 | tf_op jit(solution)/shard_map/cond/branch_1_fun/ppermute | solution.py:331
  97.9 7.9 %collective-permute-start.49 = (f32[10,32,256]{2,1,0:T(8,128)S(1)}, f32[10,32,256]{2,1,0:T(8,128)S(1)}, u32[]{:S(2)}, u32[]{:S(2)}) collective-permute-start(f32[10,32,256]{2,1,0:T(8,128)S(1)} %collective-permute-done.44.refs_14_), channel_id=1, source_target_pairs={{0,1},{1,0},{2,3},{3,2},{4,5},{5,4},{6,7},{7,6},{8,9},{9,8},{10,11... | collective-permute-start | bytes 983048 | tf_op jit(solution)/shard_map/cond/branch_1_fun/ppermute | solution.py:331
  98.0 7.8 %collective-permute-start.45 = (f32[10,32,256]{2,1,0:T(8,128)S(1)}, f32[10,32,256]{2,1,0:T(8,128)S(1)}, u32[]{:S(2)}, u32[]{:S(2)}) collective-permute-start(f32[10,32,256]{2,1,0:T(8,128)S(1)} %collective-permute-done.43.refs_8_), channel_id=1, source_target_pairs={{0,1},{1,0},{2,3},{3,2},{4,5},{5,4},{6,7},{7,6},{8,9},{9,8},{10,11... | collective-permute-start | bytes 983048 | tf_op jit(solution)/shard_map/cond/branch_1_fun/ppermute | solution.py:331
  105.8 1.6 %collective-permute-start.47 = (f32[10,32,256]{2,1,0:T(8,128)S(1)}, f32[10,32,256]{2,1,0:T(8,128)S(1)}, u32[]{:S(2)}, u32[]{:S(2)}) collective-permute-start(f32[10,32,256]{2,1,0:T(8,128)S(1)} %collective-permute-done.46.refs_10_), channel_id=1, source_target_pairs={{0,1},{1,0},{2,3},{3,2},{4,5},{5,4},{6,7},{7,6},{8,9},{9,8},{10,11... | collective-permute-start | bytes 983048 | tf_op jit(solution)/shard_map/cond/branch_1_fun/ppermute | solution.py:331
  111.7 0.9 copy-start.4

commit v3 on v2

--- a/solution.py
+++ b/solution.py
@@ -11,7 +11,7 @@
 F32, BF16 = jnp.float32, jnp.bfloat16
 VMEM = pl.BlockSpec(memory_space=pltpu.VMEM)
 SMEM = pl.BlockSpec(memory_space=pltpu.SMEM)
-ANY = pl.BlockSpec(memory_space=pl.ANY)
+HBM = pl.BlockSpec(memory_space=pltpu.HBM)
 COARSE_STEPS = 2
 FINE_STEPS = 16
 RESIDUAL = 5e-4
@@ -34,13 +34,18 @@
     return dot(ah, bh, dims) + (dot(ah, bl, dims) + dot(al, bh, dims))
 
 
-def inverse_factor_kernel(a_ref, w_ref, s_ref, flag):
-    n = a_ref.shape[0]
+def inverse_factor_kernel(where_ref, own_ref, other_ref, w_ref, s_ref):
+    n = w_ref.shape[0]
+    pieces, share = own_ref.shape[0], own_ref.shape[1]
+    core = where_ref[1] % 2
+    for i in range(pieces):
+        for ref, half in ((own_ref, core), (other_ref, 1 - core)):
+            s_ref[pl.ds(pl.multiple_of((2 * i + half) * share, share), share), :] = ref[i]
     rows = lax.broadcasted_iota(jnp.int32, (n, n), 0)
     cols = lax.broadcasted_iota(jnp.int32, (n, n), 1)
     eye = (rows == cols).astype(F32)
     take = jnp.where(rows > cols, 1.0, 0.5 * eye)
-    a = a_ref[...]
+    a = s_ref[...]
     diag_row = jnp.sum(a * eye, axis=0, keepdims=True)
     diag_col = jnp.sum(a * eye, axis=1, keepdims=True)
     scale_row, scale_col = lax.rsqrt(diag_row), lax.rsqrt(diag_col)
@@ -54,7 +59,6 @@
         change = take * (dot(t, wh, NT) - eye)
         w = w - dot(change.astype(BF16), wh, NN)
     w_ref[...] = w
-    flag[0] = 0
 
     def fine(state):
         step, _ = state
@@ -94,16 +98,16 @@
     w_ref[...] = w_ref[...] * scale_row
 
 
-def inverse_factor(pivot):
-    n = pivot.shape[0]
+def inverse_factor(where, own, other):
+    n = own.shape[-1]
     return pl.pallas_call(
         inverse_factor_kernel,
         out_shape=jax.ShapeDtypeStruct((n, n), F32),
-        in_specs=[VMEM],
+        in_specs=[SMEM, VMEM, VMEM],
         out_specs=VMEM,
-        scratch_shapes=[pltpu.VMEM((n, n), F32), pltpu.SMEM((1,), jnp.int32)],
+        scratch_shapes=[pltpu.VMEM((n, n), F32)],
         compiler_params=pltpu.CompilerParams(vmem_limit_bytes=32 * 2**20),
-    )(pivot)
+    )(where, own, other)
 
 
 class Sizes:
@@ -164,17 +168,16 @@
     )(fill)
 
 
-def pack_kernel(sizes, cap, where_ref, fill_ref, panel_ref, side_ref, core_ref, out_ref, pool):
+def pack_kernel(sizes, cap, where_ref, fill_ref, panel_ref, core_ref, side_ref, out_ref, pool):
     c, r = where_ref[0], where_ref[1]
     side, core = c % 2, r % 2
-    half, quarter = sizes.unit // 2, sizes.unit // 4
-    own_at = pl.multiple_of(side * half + core * quarter, quarter)
-    side_at = pl.multiple_of(core * quarter, quarter)
+    quarter = sizes.unit // 4
+    own_at = pl.multiple_of((side * 2 + core) * quarter, quarter)
     for u in range(sizes.per_piece):
         pool[core, side, u] = panel_ref[u, pl.ds(own_at, quarter), :]
-        pool[core, 1 - side, u] = side_ref[u, pl.ds(side_at, quarter), :]
-        pool[1 - core, side, u] = core_ref[0, u]
-        pool[1 - core, 1 - side, u] = core_ref[1, u]
+        pool[1 - core, side, u] = core_ref[u, side]
+        pool[core, 1 - side, u] = side_ref[0, u]
+        pool[1 - core, 1 - side, u] = side_ref[1, u]
     slot = jnp.int32(0)
     for core_at, side_at, piece in pool_pieces(sizes, r // 2, c // 2):
         for u in range(sizes.per_piece):
@@ -190,7 +193,7 @@
                 slot = slot + flag.astype(jnp.int32)
 
 
-def pack(sizes, cap, where, fill, panel, from_side, from_core):
+def pack(sizes, cap, where, fill, panel, from_core, from_side):
     quarter = sizes.unit // 4
     return pl.pallas_call(
         functools.partial(pack_kernel, sizes, cap),
@@ -199,11 +202,11 @@
         out_specs=VMEM,
         scratch_shapes=[pltpu.VMEM((2, 2, sizes.per_piece, quarter, 2 * sizes.block), F32)],
         compiler_params=pltpu.CompilerParams(vmem_limit_bytes=16 * 2**20),
-    )(where, fill, panel, from_side, from_core)
+    )(where, fill, panel, from_core, from_side)
 
 
 def apply_factor_kernel(
-    sizes, where_ref, fill_ref, w_ref, panel_ref, column_ref, x_ref, high_ref, low_ref, slot_ref, masked, column
+    sizes, where_ref, fill_ref, w_ref, panel_ref, column_ref, x_ref, high_ref, low_ref, slot_ref, masked, column, sem
 ):
     c, r = where_ref[0], where_ref[1]
 
@@ -217,7 +220,9 @@
     mask(panel_ref, masked, (r * sizes.cols + c) * sizes.per_piece, sizes.per_piece)
     mask(column_ref, column, c * (sizes.width // sizes.unit), sizes.width // sizes.unit)
     w = halves(w_ref[...])
-    x_ref[...] = dot3(halves(masked[...]), w, NT)
+    masked[...] = dot3(halves(masked[...]), w, NT)
+    copy_out = pltpu.make_async_copy(masked, x_ref, sem)
+    copy_out.start()
     solved = dot3(w, halves(column[...]), NT)
     high_ref[...], low_ref[...] = halves(dot3(w, halves(solved), TN))
 
@@ -236,6 +241,8 @@
                         slot_ref[at] = jnp.where(flag, slot, -1)
 
                     slot = slot + flag.astype(jnp.int32)
+
+    copy_out.wait()
 
 
 def apply_factor(sizes, where, fill, w, panel, column):
@@ -249,15 +256,19 @@
             jax.ShapeDtypeStruct((2 * sizes.tiles,), jnp.int32),
         ),
         in_specs=[SMEM, SMEM, VMEM, VMEM, VMEM],
-        out_specs=(VMEM, VMEM, VMEM, SMEM),
-        scratch_shapes=[pltpu.VMEM(panel.shape, F32), pltpu.VMEM((sizes.width, n), F32)],
+        out_specs=(HBM, VMEM, VMEM, SMEM),
+        scratch_shapes=[
+            pltpu.VMEM(panel.shape, F32),
+            pltpu.VMEM((sizes.width, n), F32),
+            pltpu.SemaphoreType.DMA,
+        ],
         compiler_params=pltpu.CompilerParams(vmem_limit_bytes=32 * 2**20),
     )(where, fill, w, panel, column)
 
 
 def update_kernel(sizes, where_ref, slot_ref, high_ref, low_ref, window_ref, *refs):
     groups = sizes.cols // 2
-    lists, (out_ref, tiles, unit_data, in_sems, out_sems) = refs[: 4 * groups], refs[4 * groups :]
+    lists, (out_ref, tiles, unit_data, out_sems) = refs[: 4 * groups], refs[4 * groups :]
     c, r = where_ref[0], where_ref[1]
     side, core = c % 2, r % 2
     per_group = 2 * sizes.per_piece
@@ -267,18 +278,15 @@
         group = jnp.bitwise_xor(c // 2, t // per_group)
         return pl.ds(pl.multiple_of((group * per_group + t % per_group) * sizes.unit, sizes.unit), sizes.unit)
 
-    def tile_in(t):
-        return pltpu.make_async_copy(window_ref.at[rows_of(t)], tiles.at[t], in_sems.at[t])
-
-    def tile_out(t):
-        return pltpu.make_async_copy(tiles.at[t], out_ref.at[rows_of(t)], out_sems.at[t])
+    def tile_out(t, source):
+        return pltpu.make_async_copy(source, out_ref.at[rows_of(t)], out_sems.at[t])
 
     def active(t):
         return jnp.logical_or(slot_ref[2 * t] >= 0, slot_ref[2 * t + 1] >= 0)
 
     @pl.loop(0, sizes.tiles)
     def _(t):
-        pl.when(active(t))(tile_in(t).start)
+        pl.when(jnp.logical_not(active(t)))(tile_out(t, window_ref.at[rows_of(t)]).start)
 
     for group in range(groups):
 
@@ -286,7 +294,7 @@
         def _(t, group=group):
             @pl.when(active(t))
             def _():
-                tile_in(t).wait()
+                tiles[t] = window_ref[rows_of(t), :]
                 for p in range(2):
                     slot = slot_ref[2 * t + p]
 
@@ -301,11 +309,11 @@
                         right = (high_ref[at, :], low_ref[at, :])
                         tiles[t] = tiles[t] - dot3(halves(unit_data[...]), right, NN)
 
-                tile_out(t).start()
+                tile_out(t, tiles.at[t]).start()
 
     @pl.loop(0, sizes.tiles)
     def _(t):
-        pl.when(active(t))(tile_out(t).wait)
+        tile_out(t, tiles.at[t]).wait()
 
 
 def update(sizes, where, slots, high, low, window, lists):
@@ -313,16 +321,14 @@
     return pl.pallas_call(
         functools.partial(update_kernel, sizes),
         out_shape=jax.ShapeDtypeStruct(window.shape, F32),
-        in_specs=[SMEM, SMEM, VMEM, VMEM, ANY] + [VMEM] * len(lists),
-        out_specs=ANY,
-        input_output_aliases={4: 0},
+        in_specs=[SMEM, SMEM, VMEM, VMEM, VMEM] + [VMEM] * len(lists),
+        out_specs=HBM,
         scratch_shapes=[
             pltpu.VMEM((tiles, sizes.unit, sizes.width), F32),
             pltpu.VMEM((sizes.unit, sizes.block), F32),
             pltpu.SemaphoreType.DMA((tiles,)),
-            pltpu.SemaphoreType.DMA((tiles,)),
         ],
-        compiler_params=pltpu.CompilerParams(vmem_limit_bytes=40 * 2**20),
+        compiler_params=pltpu.CompilerParams(vmem_limit_bytes=48 * 2**20),
     )(where, slots, high, low, window, *lists)
 
 
@@ -360,50 +366,43 @@
 
 def spread_column(sizes, value, step):
     r, c = lax.axis_index("row"), lax.axis_index("col")
-    target = c * sizes.width // sizes.slab
-    return jnp.where(((r ^ target) & step) != 0, swap(value, "row", step), value)
-
-
-def copy_kernel(source_ref, target_ref):
-    target_ref[...] = source_ref[...]
-
-
-def copy(window, rows):
-    spec = pl.BlockSpec((rows, window.shape[1]), lambda i: (i, 0))
-    return pl.pallas_call(
-        copy_kernel,
-        out_shape=jax.ShapeDtypeStruct(window.shape, F32),
-        grid=(window.shape[0] // rows,),
-        in_specs=[spec],
-        out_specs=spec,
-    )(window)
+    pairs = []
+    for at in range(sizes.cols):
+        slab, _ = sizes.source(at)
+        for row in range(sizes.rows):
+            if (row ^ slab) % (2 * step) == 0:
+                pairs.append((at * sizes.rows + row, at * sizes.rows + (row ^ step)))
+    other = lax.ppermute(value, ("col", "row"), pairs)
+    return jnp.where(((r ^ (c * sizes.width // sizes.slab)) & step) != 0, other, value)
 
 
 def per_device(trailing, panel_rows, pivot_block, panel_fill):
     sizes = Sizes(trailing, panel_rows, panel_fill)
     fill = panel_fill.reshape(-1)
-    where = jnp.stack([lax.axis_index("col"), lax.axis_index("row")]).astype(jnp.int32)
+    r, c = lax.axis_index("row"), lax.axis_index("col")
+    where = jnp.stack([c, r]).astype(jnp.int32)
+    side, core = c % 2, r % 2
+    quarter = sizes.unit // 4
+    share = pivot_block.shape[0] // 2
+    most = 8 * sizes.per_piece
+    cap = most * 5 // 12
+
     units = panel_rows.reshape(sizes.per_piece, sizes.unit, -1)
-    most = 8 * sizes.per_piece
-
-    def run(cap, trailing, panel_rows, pivot_block, fill, units):
-        r, c = lax.axis_index("row"), lax.axis_index("col")
-        side, core = c % 2, r % 2
-        half, quarter = sizes.unit // 2, sizes.unit // 4
-        share = pivot_block.shape[0] // 2
-
-        kept = lax.dynamic_slice_in_dim(units, side * half, half, 1)
-        from_side = swap(lax.dynamic_slice_in_dim(units, (1 - side) * half, half, 1), "col", 1)
-        pivot = lax.dynamic_slice_in_dim(pivot_block, core * share, share, 0)[None]
-        pivot = join(c, 1, pivot, swap(pivot, "col", 1))
-        column = gather_column(sizes, panel_rows)
-        from_side, pivot, *column = lax.optimization_barrier((from_side, pivot, *column))
-
-        both = jnp.stack([kept, from_side])
-        from_core = swap(lax.dynamic_slice_in_dim(both, (1 - core) * quarter, quarter, 2), "row", 1)
-        pivot = join(c, 2, pivot, swap(pivot, "col", 2))
-        from_core, pivot = lax.optimization_barrier((from_core, pivot))
-        own = pack(sizes, cap, where, fill, units, from_side, from_core)
+    quarters = panel_rows.reshape(sizes.per_piece, 2, 2, quarter, -1)
+
+    def at_core(which):
+        return lax.dynamic_index_in_dim(quarters, which, 2, keepdims=False)
+
+    from_core = swap(at_core(1 - core), "row", 1)
+    both = jnp.stack([at_core(core), from_core])
+    from_side = swap(lax.dynamic_index_in_dim(both, 1 - side, 2, keepdims=False), "col", 1)
+    pivot = lax.dynamic_slice_in_dim(pivot_block, core * share, share, 0)[None]
+    pivot = join(c, 1, pivot, swap(pivot, "col", 1))
+    pivot = join(c, 2, pivot, swap(pivot, "col", 2))
+    column = gather_column(sizes, panel_rows)
+
+    def run(cap, trailing, panel_rows, fill, units, from_core, from_side, pivot, *column):
+        own = pack(sizes, cap, where, fill, units, from_core, from_side)
 
         far = list(range(2, sizes.cols, 2))
         first, later = [far[-1]] + far[:-2], far[-2:-1]
@@ -425,24 +424,20 @@
 
         lists |= {k: swap(own, "col", k) for k in later}
         sides |= {k: swap(lists[k], "col", 1) for k in first}
-        pivot = join(r, 1, pivot[None], swap(pivot[None], "row", 1))
-        pivot = pivot.transpose(1, 0, 2, 3).reshape(2 * sizes.cols * share, -1)
-        window = copy(after(trailing, own), sizes.block)
-        w = inverse_factor(after(pivot, window))
+        w = inverse_factor(where, pivot, swap(pivot, "row", 1))
         column = spread_column(sizes, column, 1)
         own_factor, high, low, slots = apply_factor(sizes, where, fill, w, panel_rows, column)
         for k in later:
-            lists[k] = after(lists[k], high, *(sides[j] for j in first))
+            lists[k] = lax.optimization_barrier((lists[k], high, *(sides[j] for j in first)))[0]
             sides[k] = swap(lists[k], "col", 1)
         lists[0] = own
         ordered = []
         for k in range(0, sizes.cols, 2):
             value, other = lists[k], sides[k]
             ordered += [value, swap(value, "row", 1), other, swap(other, "row", 1)]
-        return update(sizes, where, slots, high, low, window, ordered), own_factor
-
-    cap = most * 5 // 12
-    operands = (trailing, panel_rows, pivot_block, fill, units)
+        return update(sizes, where, slots, high, low, trailing, ordered), own_factor
+
+    operands = (trailing, panel_rows, fill, units, from_core, from_side, pivot, *column)
     return lax.cond(
         fits(sizes, cap, fill)[0] != 0,
         functools.partial(run, cap),

time: 114 us -> 107 us (0.939)
  the two profiles are of different devices: /device:TPU:0 before, /device:TPU:1 now
where the time goes in v3:
time: 107 us
  waiting for transfers between devices  37.5 us (35%)
  starting transfers between devices  34.6 us (32%)
  Pallas kernels  24.3 us (23%)
  other arithmetic  5.47 us (5%)
  local copies, waits for them, and re-layouts  2.95 us (3%)
  between operations  1.58 us (1%)
    ppermute x21, waiting for transfers between devices, swap(): return lax.ppermute(value, axis, [(i, i ^ step) for i in range(size)])  37.5 us
    ppermute x21, starting transfers between devices, swap(): return lax.ppermute(value, axis, [(i, i ^ step) for i in range(size)])  23.6 us
    pallas_call x1, Pallas kernels, update(): pl.pallas_call(functools.partial(update_kernel, sizes), out_shape=jax.Sha...  9.5 us
    ppermute x2, starting transfers between devices, gather_column(): values.append(lax.ppermute(panel, ('col', 'row'), pairs))  8 us
    pallas_call x1, Pallas kernels, inverse_factor(): pl.pallas_call(inverse_factor_kernel, out_shape=jax.ShapeDtypeStruct((n,...  6.99 us
    pallas_call x1, Pallas kernels, apply_factor(): pl.pallas_call(functools.partial(apply_factor_kernel, sizes), out_shape=(...  4.8 us
    select_n x2, other arithmetic, spread_column(): jnp.where((r ^ c * sizes.width // sizes.slab) & step != 0, other, value)  3.86 us
    ppermute x2, starting transfers between devices, spread_column(): other = lax.ppermute(value, ('col', 'row'), pairs)  2.92 us
  transfers between devices with their start and end apart: 25, of which 7 were waited for; matrix products, arithmetic and copies ran while one was open for 5% of the time, Pallas kernels for 12%

profile of v3, /device:TPU:1, one launch (start us, length us, event | category | flops | bytes accessed | tf_op | source)
XLA Modules:
  0.0 106.7 jit_solution(11286738193659120273)
XLA Ops:
  0.6 0.0 copy-start
  0.7 1.2 %dynamic-slice_bitcast_fusion = (f32[1,3,2,32,512]{4,3,2,1,0:T(8,128)S(1)}, f32[3,2,32,512]{3,2,1,0:T(8,128)S(1)}) fusion(f32[3,2,2,32,512]{4,3,2,1,0:T(8,128)} %bitcast.19, s32[]{:T(128)S(6)} %select_n.114, s32[]{:T(128)S(6)} %select_n.113), kind=kLoop, calls=%fused_computation.18 | loop fusion | bytes 1572872 | tf_op jit(solution)/shard_map/stack | solution.py:397
  1.9 0.1 collective-permute-start.38
  2.0 0.7 collective-permute-start.43
  2.7 7.3 %collective-permute-start.42 = (f32[384,512]{1,0:T(8,128)}, f32[384,512]{1,0:T(8,128)S(1)}, u32[]{:S(2)}, u32[]{:S(2)}) collective-permute-start(f32[384,512]{1,0:T(8,128)} %param.7), channel_id=1, source_target_pairs={{0,0},{4,4},{8,8},{16,12},{20,16},{24,20},{1,25},{5,29}} | collective-permute-start | bytes 2359304 | tf_op jit(solution)/shard_map/ppermute | solution.py:358
  10.1 1.3 %collective-permute-start.40 = (f32[1,32,512]{2,1,0:T(8,128)S(1)}, f32[1,32,512]{2,1,0:T(8,128)S(1)}, u32[]{:S(2)}, u32[]{:S(2)}) collective-permute-start(f32[1,32,512]{2,1,0:T(8,128)S(1)} %dynamic-slice_bitcast_fusion.2), channel_id=1, source_target_pairs={{0,4},{4,0},{8,12},{12,8},{16,20},{20,16},{24,28},{28,24},{1,5},{5... | collective-permute-start | bytes 196616 | tf_op jit(solution)/shard_map/ppermute | solution.py:337
  11.4 0.0 collective-permute-done.38
  11.4 0.3 collective-permute-start.39
  11.7 6.9 %collective-permute-done.40 = f32[1,32,512]{2,1,0:T(8,128)S(1)} collective-permute-done((f32[1,32,512]{2,1,0:T(8,128)S(1)}, f32[1,32,512]{2,1,0:T(8,128)S(1)}, u32[]{:S(2)}, u32[]{:S(2)}) %collective-permute-start.40) | collective-permute-done | bytes 65568 | tf_op jit(solution)/shard_map/ppermute | solution.py:337
  18.6 0.1 collective-permute-start.41
  18.7 0.8 copy.13
  19.5 0.1 reshape.18.fill_ref
  19.6 1.2 %shard_map.63 = s32[1]{0:T(128)} custom-call(s32[96]{0:T(128)S(1)} %reshape.18.fill_ref), custom_call_target="tpu_custom_call" | custom-call | tf_op jit(solution)/shard_map/pallas_call | solution.py:163
  21.5 0.1 pad_add_fusion
  21.5 1.4 %collective-permute-done.41 = f32[2,32,512]{2,1,0:T(8,128)S(1)} collective-permute-done((f32[2,32,512]{2,1,0:T(8,128)S(1)}, f32[2,32,512]{2,1,0:T(8,128)S(1)}, u32[]{:S(2)}, u32[]{:S(2)}) %collective-permute-start.41) | collective-permute-done | bytes 131104 | tf_op jit(solution)/shard_map/ppermute | solution.py:337
  22.9 0.1 pad_maximum_fusion.1
  23.0 4.1 %collective-permute-done.39 = f32[2,3,32,512]{3,2,1,0:T(8,128)} collective-permute-done((f32[2,3,32,512]{3,2,1,0:T(8,128)S(1)}, f32[2,3,32,512]{3,2,1,0:T(8,128)}, u32[]{:S(2)}, u32[]{:S(2)}) %collective-permute-start.39) | collective-permute-done | bytes 393248 | tf_op jit(solution)/shard_map/ppermute | solution.py:337
  27.0 0.0 collective-permute-done.43
  27.0 0.0 collective-permute-done.42
  27.0 79.5 %conditional.1 = (f32[384,512]{1,0:T(8,128)}, f32[3072,512]{1,0:T(8,128)}) conditional(s32[]{:T(128)} %bitcast.2, (s32[2]{0:T(128)S(1)}, s32[96]{0:T(128)S(1)}, f32[384,512]{1,0:T(8,128)}, f32[3,2,32,512]{3,2,1,0:T(8,128)S(1)}, f32[2,3,32,512]{3,2,1,0:T(8,128)}, /*index=5*/s32[]{:T(128)}, s32[]{:T(128)}, f32[384,512]{1,0:T(8,128)S(1)}, ...), branch_computations={%region_0.1_spmd, %region_1.2_spmd} | conditional | flops 1245220 | bytes 88343848 | solution.py:441
  27.0 1.8 %branch_1_fun.4.refs_0_ = f32[10,32,256]{2,1,0:T(8,128)S(1)} custom-call(s32[2]{0:T(128)S(1)} %get-tuple-element.68.where_ref, s32[96]{0:T(128)S(1)} %get-tuple-element.69.fill_ref, f32[3,128,512]{2,1,0:T(8,128)} %bitcast.21, f32[3,2,32,512]{3,2,1,0:T(8,128)S(1)} %get-tuple-element.71.core_ref, f32[2,3,32,512]{3,2,1,0:T(8,128)} %get-tuple-element.72.side_ref), custom_call_target="tpu_custom_call" | custom-call | tf_op jit(solution)/shard_map/cond/branch_1_fun/pallas_call | solution.py:198
  28.8 1.4 %fusion.1 = f32[512,512]{1,0:T(8,128)} fusion(s32[]{:T(128)S(6)} %select_n.98, f32[384,512]{1,0:T(8,128)S(1)} %get-tuple-element.77, f32[384,512]{1,0:T(8,128)S(1)} %get-tuple-element.78), kind=kLoop, calls=%fused_computation.9 | loop fusion | flops 262144 | bytes 2621444 | tf_op jit(solution)/shard_map/cond/branch_1_fun/concatenate | solution.py:364
  30.2 1.6 %collective-permute-start.20 = (f32[512,512]{1,0:T(8,128)}, f32[512,512]{1,0:T(8,128)}, u32[]{:S(2)}, u32[]{:S(2)}) collective-permute-start(f32[512,512]{1,0:T(8,128)} %fusion.1), channel_id=1, source_target_pairs={{0,2},{4,6},{8,10},{12,14},{16,18},{20,22},{25,27},{29,31}} | collective-permute-start | bytes 3145736 | tf_op jit(solution)/shard_map/cond/branch_1_fun/ppermute | solution.py:375
  31.9 4.3 %collective-permute-start.19 = (f32[4,32,512]{2,1,0:T(8,128)S(1)}, f32[4,32,512]{2,1,0:T(8,128)S(1)}, u32[]{:S(2)}, u32[]{:S(2)}) collective-permute-start(f32[4,32,512]{2,1,0:T(8,128)S(1)} %broadcast_select_fusion.5), channel_id=1, source_target_pairs={{0,16},{4,20},{8,24},{12,28},{16,0},{20,4},{24,8},{28,12},{1,17},{... | collective-permute-start | bytes 786440 | tf_op jit(solution)/shard_map/cond/branch_1_fun/ppermute | solution.py:337
  36.2 2.8 %collective-permute-start.23 = (f32[10,32,256]{2,1,0:T(8,128)S(1)}, f32[10,32,256]{2,1,0:T(8,128)S(1)}, u32[]{:S(2)}, u32[]{:S(2)}) collective-permute-start(f32[10,32,256]{2,1,0:T(8,128)S(1)} %branch_1_fun.4.refs_0_), channel_id=1, source_target_pairs={{0,8},{4,12},{8,0},{12,4},{16,24},{20,28},{24,16},{28,20},{1,9},{5... | collective-permute-start | bytes 983048 | tf_op jit(solution)/shard_map/cond/branch_1_fun/ppermute | solution.py:337
  39.0 0.0 collective-permute-start.22
  39.0 1.2 %collective-permute-start.21 = (f32[10,32,256]{2,1,0:T(8,128)S(1)}, f32[10,32,256]{2,1,0:T(8,128)S(1)}, u32[]{:S(2)}, u32[]{:S(2)}) collective-permute-start(f32[10,32,256]{2,1,0:T(8,128)S(1)} %branch_1_fun.4.refs_0_), channel_id=1, source_target_pairs={{0,4},{4,0},{8,12},{12,8},{16,20},{20,16},{24,28},{28,24},{1,5},{5... | collective-permute-start | bytes 983048 | tf_op jit(solution)/shard_map/cond/branch_1_fun/ppermute | solution.py:337
  40.2 7.2 %collective-permute-done.19 = f32[4,32,512]{2,1,0:T(8,128)S(1)} collective-permute-done((f32[4,32,512]{2,1,0:T(8,128)S(1)}, f32[4,32,512]{2,1,0:T(8,128)S(1)}, u32[]{:S(2)}, u32[]{:S(2)}) %collective-permute-start.19) | collective-permute-done | bytes 262176 | tf_op jit(solution)/shard_map/cond/branch_1_fun/ppermute | solution.py:337
  47.4 0.0 collective-permute-done.20
  47.4 2.4 %broadcast_select_fusion.4 = f32[512,512]{1,0:T(8,128)} fusion(f32[512,512]{1,0:T(8,128)} %collective-permute-done.20, f32[512,512]{1,0:T(8,128)} %fusion.1, pred[]{:T(512)S(6)} %ne.60), kind=kLoop, calls=%fused_computation.12 | loop fusion | flops 262144 | bytes 3145729 | tf_op jit(solution)/shard_map/cond/branch_1_fun/jit(_where)/select_n | solution.py:376
  49.8 0.0 collective-permute-done.23.refs_4_
  49.8 9.8 %collective-permute-done.22.refs_12_ = f32[10,32,256]{2,1,0:T(8,128)S(1)} collective-permute-done((f32[10,32,256]{2,1,0:T(8,128)S(1)}, f32[10,32,256]{2,1,0:T(8,128)S(1)}, u32[]{:S(2)}, u32[]{:S(2)}) %collective-permute-start.22) | collective-permute-done | bytes 327712 | tf_op jit(solution)/shard_map/cond/branch_1_fun/ppermute | solution.py:337
  59.7 0.0 collective-permute-done.21.refs_2_
  59.7 1.3 %collective-permute-start.25 = (f32[512,512]{1,0:T(8,128)}, f32[512,512]{1,0:T(8,128)}, u32[]{:S(2)}, u32[]{:S(2)}) collective-permute-start(f32[512,512]{1,0:T(8,128)} %broadcast_select_fusion.4), channel_id=1, source_target_pairs={{0,1},{2,3},{4,5},{6,7},{8,9},{10,11},{12,13},{14,15},{16,17},{18,... | collective-permute-start | bytes 3145736 | tf_op jit(solution)/shard_map/cond/branch_1_fun/ppermute | solution.py:375
  61.0 2.1 %collective-permute-start.24 = (f32[8,32,512]{2,1,0:T(8,128)S(1)}, f32[8,32,512]{2,1,0:T(8,128)S(1)}, u32[]{:S(2)}, u32[]{:S(2)}) collective-permute-start(f32[8,32,512]{2,1,0:T(8,128)S(1)} %maximum_select_fusion.1.own_ref), channel_id=1, source_target_pairs={{0,1},{1,0},{2,3},{3,2},{4,5},{5,4},{6,7},{7,6},{8,9},{9,8},{10,11... | collective-permute-start | bytes 1572872 | tf_op jit(solution)/shard_map/cond/branch_1_fun/ppermute | solution.py:337
  63.1 5.4 %collective-permute-start.31 = (f32[10,32,256]{2,1,0:T(8,128)S(1)}, f32[10,32,256]{2,1,0:T(8,128)S(1)}, u32[]{:S(2)}, u32[]{:S(2)}) collective-permute-start(f32[10,32,256]{2,1,0:T(8,128)S(1)} %branch_1_fun.4.refs_0_), channel_id=1, source_target_pairs={{0,16},{4,20},{8,24},{12,28},{16,0},{20,4},{24,8},{28,12},{1,17},{... | collective-permute-start | bytes 983048 | tf_op jit(solution)/shard_map/cond/branch_1_fun/ppermute | solution.py:337
  68.5 1.2 %collective-permute-start.29 = (f32[10,32,256]{2,1,0:T(8,128)S(1)}, f32[10,32,256]{2,1,0:T(8,128)S(1)}, u32[]{:S(2)}, u32[]{:S(2)}) collective-permute-start(f32[10,32,256]{2,1,0:T(8,128)S(1)} %collective-permute-done.23.refs_4_), channel_id=1, source_target_pairs={{0,4},{4,0},{8,12},{12,8},{16,20},{20,16},{24,28},{28,24},{1,5},{5... | collective-permute-start | bytes 983048 | tf_op jit(solution)/shard_map/cond/branch_1_fun/ppermute | solution.py:337
  69.6 0.3 collective-permute-start.32
  69.9 0.0 collective-permute-done.24.other_ref
  70.0 0.8 collective-permute-start.26
  70.8 7.0 %branch_1_fun.5.w_ref = f32[512,512]{1,0:T(8,128)S(1)} custom-call(s32[2]{0:T(128)S(1)} %get-tuple-element.68.where_ref, f32[8,32,512]{2,1,0:T(8,128)S(1)} %maximum_select_fusion.1.own_ref, f32[8,32,512]{2,1,0:T(8,128)S(1)} %collective-permute-done.24.other_ref), custom_call_target="tpu_custom_call" | custom-call | tf_op jit(solution)/shard_map/cond/branch_1_fun/pallas_call | solution.py:103
  77.8 0.0 collective-permute-done.25
  77.8 0.1 collective-permute-start.28
  77.9 1.4 %broadcast_select_fusion.3.column_ref = f32[512,512]{1,0:T(8,128)S(1)} fusion(f32[512,512]{1,0:T(8,128)} %collective-permute-done.25, f32[512,512]{1,0:T(8,128)} %broadcast_select_fusion.4, pred[]{:T(512)S(6)} %ne.62), kind=kLoop, calls=%fused_computation.11 | loop fusion | flops 262144 | bytes 3145729 | tf_op jit(solution)/shard_map/cond/branch_1_fun/jit(_where)/select_n | solution.py:376
  79.3 4.8 %branch_1_fun.6 = (f32[384,512]{1,0:T(8,128)}, bf16[512,512]{1,0:T(8,128)(2,1)S(1)}, bf16[512,512]{1,0:T(8,128)(2,1)S(1)}, s32[48]{0:T(128)S(1)}) custom-call(s32[2]{0:T(128)S(1)} %get-tuple-element.68.where_ref, s32[96]{0:T(128)S(1)} %get-tuple-element.69.fill_ref, f32[512,512]{1,0:T(8,128)S(1)} %branch_1_fun.5.w_ref, ...), custom_call_target="tpu_custom_call" | custom-call | tf_op jit(solution)/shard_map/cond/branch_1_fun/pallas_call | solution.py:250
  84.2 0.8 copy-done.1
  85.0 0.0 collective-permute-done.31.refs_8_
  85.0 0.5 collective-permute-start.27
  85.5 0.0 collective-permute-done.29.refs_6_
  85.5 0.0 collective-permute-done.32.refs_14_
  85.5 1.2 %collective-permute-start.34 = (f32[10,32,256]{2,1,0:T(8,128)S(1)}, f32[10,32,256]{2,1,0:T(8,128)S(1)}, u32[]{:S(2)}, u32[]{:S(2)}) collective-permute-start(f32[10,32,256]{2,1,0:T(8,128)S(1)} %collective-permute-done.31.refs_8_), channel_id=1, source_target_pairs={{0,4},{4,0},{8,12},{12,8},{16,20},{20,16},{24,28},{28,24},{1,5},{5... | collective-permute-start | bytes 983048 | tf_op jit(solution)/shard_map/cond/branch_1_fun/ppermute | solution.py:337
  86.6 0.5 collective-permute-start.36
  87.1 0.0 collective-permute-done.27.refs_3_
  87.1 0.1 collective-permute-start.30
  87.1 0.0 collective-permute-done.26.refs_1_
  87.1 0.5 collective-permute-start.37
  87.6 0.0 collective-permute-done.28.refs_5_
  87.6 0.1 collective-permute-start.33
  87.7 7.0 %collective-permute-done.34.refs_10_ = f32[10,32,256]{2,1,0:T(8,128)S(1)} collective-permute-done((f32[10,32,256]{2,1,0:T(8,128)S(1)}, f32[10,32,256]{2,1,0:T(8,128)S(1)}, u32[]{:S(2)}, u32[]{:S(2)}) %collective-permute-start.34) | collective-permute-done | bytes 327712 | tf_op jit(solution)/shard_map/cond/branch_1_fun/ppermute | solution.py:337
  94.6 1.0 collective-permute-start.35
  95.6 0.0 collective-permute-done.37.refs_15_
  95.6 0.0 collective-permute-done.33.refs_9_
  95.6 1.2 %collective-permute-done.35.refs_11_ = f32[10,32,256]{2,1,0:T(8,128)S(1)} collective-permute-done((f32[10,32,256]{2,1,0:T(8,128)S(1)}, f32[10,32,256]{2,1,0:T(8,128)S(1)}, u32[]{:S(2)}, u32[]{:S(2)}) %collective-permute-start.35) | collective-permute-done | bytes 327712 | tf_op jit(solution)/shard_map/cond/branch_1_fun/ppermute | solution.py:337
  96.8 9.5 %branch_1_fun.7 = f32[3072,512]{1,0:T(8,128)} custom-call(s32[2]{0:T(128)S(1)} %get-tuple-element.68.where_ref, s32[48]{0:T(128)S(1)} %get-tuple-element.82.slot_ref, bf16[512,512]{1,0:T(8,128)(2,1)S(1)} %get-tuple-element.83.high_ref, bf16[512,512]{1,0:T(8,128)(2,1)} %copy-done.1, f32[3072,512]{1,0:T(8,128)} %get-tuple-element.108.window_ref, ...), custom_call_target="tpu_custom_call" | custom-call | tf_op jit(solution)/shard_map/cond/branch_1_fun/pallas_call | solution.py:321
  (9 shorter events, 0.1 us)
Async XLA Ops:
  0.6 9.4 %copy-start = (f32[64,512]{1,0:T(8,128)S(1)}, f32[64,512]{1,0:T(8,128)}, u32[]{:S(2)}) copy-start(f32[64,512]{1,0:T(8,128)} %param.8) | copy-start | bytes 393220
  1.9 9.5 %collective-permute-start.38 = (f32[3,2,32,512]{3,2,1,0:T(8,128)S(1)}, f32[3,2,32,512]{3,2,1,0:T(8,128)S(1)}, u32[]{:S(2)}, u32[]{:S(2)}) collective-permute-start(f32[3,2,32,512]{3,2,1,0:T(8,128)S(1)} %get-tuple-element.118), channel_id=1, source_target_pairs={{0,1},{1,0},{2,3},{3,2},{4,5},{5,4},{6,7},{7,6},{8,9},{9,8},{10,11... | collective-permute-start | bytes 1179656 | tf_op jit(solution)/shard_map/ppermute | solution.py:337
  2.0 25.0 %collective-permute-start.43 = (f32[384,512]{1,0:T(8,128)}, f32[384,512]{1,0:T(8,128)S(1)}, u32[]{:S(2)}, u32[]{:S(2)}) collective-permute-start(f32[384,512]{1,0:T(8,128)} %param.7), channel_id=1, source_target_pairs={{4,0},{8,4},{12,8},{20,12},{24,16},{28,20},{5,25},{9,29}} | collective-permute-start | bytes 2359304 | tf_op jit(solution)/shard_map/ppermute | solution.py:358
  2.7 24.3 %collective-permute-start.42 = (f32[384,512]{1,0:T(8,128)}, f32[384,512]{1,0:T(8,128)S(1)}, u32[]{:S(2)}, u32[]{:S(2)}) collective-permute-start(f32[384,512]{1,0:T(8,128)} %param.7), channel_id=1, source_target_pairs={{0,0},{4,4},{8,8},{16,12},{20,16},{24,20},{1,25},{5,29}} | collective-permute-start | bytes 2359304 | tf_op jit(solution)/shard_map/ppermute | solution.py:358
  10.1 8.5 %collective-permute-start.40 = (f32[1,32,512]{2,1,0:T(8,128)S(1)}, f32[1,32,512]{2,1,0:T(8,128)S(1)}, u32[]{:S(2)}, u32[]{:S(2)}) collective-permute-start(f32[1,32,512]{2,1,0:T(8,128)S(1)} %dynamic-slice_bitcast_fusion.2), channel_id=1, source_target_pairs={{0,4},{4,0},{8,12},{12,8},{16,20},{20,16},{24,28},{28,24},{1,5},{5... | collective-permute-start | bytes 196616 | tf_op jit(solution)/shard_map/ppermute | solution.py:337
  11.4 15.6 %collective-permute-start.39 = (f32[2,3,32,512]{3,2,1,0:T(8,128)S(1)}, f32[2,3,32,512]{3,2,1,0:T(8,128)}, u32[]{:S(2)}, u32[]{:S(2)}) collective-permute-start(f32[2,3,32,512]{3,2,1,0:T(8,128)S(1)} %fusion.3), channel_id=1, source_target_pairs={{0,4},{4,0},{8,12},{12,8},{16,20},{20,16},{24,28},{28,24},{1,5},{5... | collective-permute-start | bytes 1179656 | tf_op jit(solution)/shard_map/ppermute | solution.py:337
  18.6 4.3 %collective-permute-start.41 = (f32[2,32,512]{2,1,0:T(8,128)S(1)}, f32[2,32,512]{2,1,0:T(8,128)S(1)}, u32[]{:S(2)}, u32[]{:S(2)}) collective-permute-start(f32[2,32,512]{2,1,0:T(8,128)S(1)} %maximum_select_fusion.2), channel_id=1, source_target_pairs={{0,8},{4,12},{8,0},{12,4},{16,24},{20,28},{24,16},{28,20},{1,9},{5... | collective-permute-start | bytes 393224 | tf_op jit(solution)/shard_map/ppermute | solution.py:337
  30.2 17.2 %collective-permute-start.20 = (f32[512,512]{1,0:T(8,128)}, f32[512,512]{1,0:T(8,128)}, u32[]{:S(2)}, u32[]{:S(2)}) collective-permute-start(f32[512,512]{1,0:T(8,128)} %fusion.1), channel_id=1, source_target_pairs={{0,2},{4,6},{8,10},{12,14},{16,18},{20,22},{25,27},{29,31}} | collective-permute-start | bytes 3145736 | tf_op jit(solution)/shard_map/cond/branch_1_fun/ppermute | solution.py:375
  31.9 15.5 %collective-permute-start.19 = (f32[4,32,512]{2,1,0:T(8,128)S(1)}, f32[4,32,512]{2,1,0:T(8,128)S(1)}, u32[]{:S(2)}, u32[]{:S(2)}) collective-permute-start(f32[4,32,512]{2,1,0:T(8,128)S(1)} %broadcast_select_fusion.5), channel_id=1, source_target_pairs={{0,16},{4,20},{8,24},{12,28},{16,0},{20,4},{24,8},{28,12},{1,17},{... | collective-permute-start | bytes 786440 | tf_op jit(solution)/shard_map/cond/branch_1_fun/ppermute | solution.py:337
  36.2 13.7 %collective-permute-start.23 = (f32[10,32,256]{2,1,0:T(8,128)S(1)}, f32[10,32,256]{2,1,0:T(8,128)S(1)}, u32[]{:S(2)}, u32[]{:S(2)}) collective-permute-start(f32[10,32,256]{2,1,0:T(8,128)S(1)} %branch_1_fun.4.refs_0_), channel_id=1, source_target_pairs={{0,8},{4,12},{8,0},{12,4},{16,24},{20,28},{24,16},{28,20},{1,9},{5... | collective-permute-start | bytes 983048 | tf_op jit(solution)/shard_map/cond/branch_1_fun/ppermute | solution.py:337
  39.0 20.7 %collective-permute-start.22 = (f32[10,32,256]{2,1,0:T(8,128)S(1)}, f32[10,32,256]{2,1,0:T(8,128)S(1)}, u32[]{:S(2)}, u32[]{:S(2)}) collective-permute-start(f32[10,32,256]{2,1,0:T(8,128)S(1)} %branch_1_fun.4.refs_0_), channel_id=1, source_target_pairs={{0,24},{4,28},{8,16},{12,20},{16,8},{20,12},{24,0},{28,4},{1,25},{... | collective-permute-start | bytes 983048 | tf_op jit(solution)/shard_map/cond/branch_1_fun/ppermute | solution.py:337
  39.0 20.7 %collective-permute-start.21 = (f32[10,32,256]{2,1,0:T(8,128)S(1)}, f32[10,32,256]{2,1,0:T(8,128)S(1)}, u32[]{:S(2)}, u32[]{:S(2)}) collective-permute-start(f32[10,32,256]{2,1,0:T(8,128)S(1)} %branch_1_fun.4.refs_0_), channel_id=1, source_target_pairs={{0,4},{4,0},{8,12},{12,8},{16,20},{20,16},{24,28},{28,24},{1,5},{5... | collective-permute-start | bytes 983048 | tf_op jit(solution)/shard_map/cond/branch_1_fun/ppermute | solution.py:337
  59.7 18.1 %collective-permute-start.25 = (f32[512,512]{1,0:T(8,128)}, f32[512,512]{1,0:T(8,128)}, u32[]{:S(2)}, u32[]{:S(2)}) collective-permute-start(f32[512,512]{1,0:T(8,128)} %broadcast_select_fusion.4), channel_id=1, source_target_pairs={{0,1},{2,3},{4,5},{6,7},{8,9},{10,11},{12,13},{14,15},{16,17},{18,... | collective-permute-start | bytes 3145736 | tf_op jit(solution)/shard_map/cond/branch_1_fun/ppermute | solution.py:375
  61.0 9.0 %collective-permute-start.24 = (f32[8,32,512]{2,1,0:T(8,128)S(1)}, f32[8,32,512]{2,1,0:T(8,128)S(1)}, u32[]{:S(2)}, u32[]{:S(2)}) collective-permute-start(f32[8,32,512]{2,1,0:T(8,128)S(1)} %maximum_select_fusion.1.own_ref), channel_id=1, source_target_pairs={{0,1},{1,0},{2,3},{3,2},{4,5},{5,4},{6,7},{7,6},{8,9},{9,8},{10,11... | collective-permute-start | bytes 1572872 | tf_op jit(solution)/shard_map/cond/branch_1_fun/ppermute | solution.py:337
  63.1 21.9 %collective-permute-start.31 = (f32[10,32,256]{2,1,0:T(8,128)S(1)}, f32[10,32,256]{2,1,0:T(8,128)S(1)}, u32[]{:S(2)}, u32[]{:S(2)}) collective-permute-start(f32[10,32,256]{2,1,0:T(8,128)S(1)} %branch_1_fun.4.refs_0_), channel_id=1, source_target_pairs={{0,16},{4,20},{8,24},{12,28},{16,0},{20,4},{24,8},{28,12},{1,17},{... | collective-permute-start | bytes 983048 | tf_op jit(solution)/shard_map/cond/branch_1_fun/ppermute | solution.py:337
  68.5 17.0 %collective-permute-start.29 = (f32[10,32,256]{2,1,0:T(8,128)S(1)}, f32[10,32,256]{2,1,0:T(8,128)S(1)}, u32[]{:S(2)}, u32[]{:S(2)}) collective-permute-start(f32[10,32,256]{2,1,0:T(8,128)S(1)} %collective-permute-done.23.refs_4_), channel_id=1, source_target_pairs={{0,4},{4,0},{8,12},{12,8},{16,20},{20,16},{24,28},{28,24},{1,5},{5... | collective-permute-start | bytes 983048 | tf_op jit(solution)/shard_map/cond/branch_1_fun/ppermute | solution.py:337
  69.6 15.8 %collective-permute-start.32 = (f32[10,32,256]{2,1,0:T(8,128)S(1)}, f32[10,32,256]{2,1,0:T(8,128)S(1)}, u32[]{:S(2)}, u32[]{:S(2)}) collective-permute-start(f32[10,32,256]{2,1,0:T(8,128)S(1)} %collective-permute-done.22.refs_12_), channel_id=1, source_target_pairs={{0,4},{4,0},{8,12},{12,8},{16,20},{20,16},{24,28},{28,24},{1,5},{5... | collective-permute-start | bytes 983048 | tf_op jit(solution)/shard_map/cond/branch_1_fun/ppermute | solution.py:337
  70.0 17.2 %collective-permute-start.26 = (f32[10,32,256]{2,1,0:T(8,128)S(1)}, f32[10,32,256]{2,1,0:T(8,128)S(1)}, u32[]{:S(2)}, u32[]{:S(2)}) collective-permute-start(f32[10,32,256]{2,1,0:T(8,128)S(1)} %branch_1_fun.4.refs_0_), channel_id=1, source_target_pairs={{0,1},{1,0},{2,3},{3,2},{4,5},{5,4},{6,7},{7,6},{8,9},{9,8},{10,11... | collective-permute-start | bytes 983048 | tf_op jit(solution)/shard_map/cond/branch_1_fun/ppermute | solution.py:337
  77.8 9.8 %collective-permute-start.28 = (f32[10,32,256]{2,1,0:T(8,128)S(1)}, f32[10,32,256]{2,1,0:T(8,128)S(1)}, u32[]{:S(2)}, u32[]{:S(2)}) collective-permute-start(f32[10,32,256]{2,1,0:T(8,128)S(1)} %collective-permute-done.23.refs_4_), channel_id=1, source_target_pairs={{0,1},{1,0},{2,3},{3,2},{4,5},{5,4},{6,7},{7,6},{8,9},{9,8},{10,11... | collective-permute-start | bytes 983048 | tf_op jit(solution)/shard_map/cond/branch_1_fun/ppermute | solution.py:337
  84.1 0.8 copy-start.1
  85.0 2.1 %collective-permute-start.27 = (f32[10,32,256]{2,1,0:T(8,128)S(1)}, f32[10,32,256]{2,1,0:T(8,128)S(1)}, u32[]{:S(2)}, u32[]{:S(2)}) collective-permute-start(f32[10,32,256]{2,1,0:T(8,128)S(1)} %collective-permute-done.21.refs_2_), channel_id=1, source_target_pairs={{0,1},{1,0},{2,3},{3,2},{4,5},{5,4},{6,7},{7,6},{8,9},{9,8},{10,11... | collective-permute-start | bytes 983048 | tf_op jit(solution)/shard_map/cond/branch_1_fun/ppermute | solution.py:337
  85.5 9.2 %collective-permute-start.34 = (f32[10,32,256]{2,1,0:T(8,128)S(1)}, f32[10,32,256]{2,1,0:T(8,128)S(1)}, u32[]{:S(2)}, u32[]{:S(2)}) collective-permute-start(f32[10,32,256]{2,1,0:T(8,128)S(1)} %collective-permute-done.31.refs_8_), channel_id=1, source_target_pairs={{0,4},{4,0},{8,12},{12,8},{16,20},{20,16},{24,28},{28,24},{1,5},{5... | collective-permute-start | bytes 983048 | tf_op jit(solution)/shard_map/cond/branch_1_fun/ppermute | solution.py:337
  86.6 9.0 %collective-permute-start.36 = (f32[10,32,256]{2,1,0:T(8,128)S(1)}, f32[10,32,256]{2,1,0:T(8,128)S(1)}, u32[]{:S(2)}, u32[]{:S(2)}) collective-permute-start(f32[10,32,256]{2,1,0:T(8,128)S(1)} %collective-permute-done.22.refs_12_), channel_id=1, source_target_pairs={{0,1},{1,0},{2,3},{3,2},{4,5},{5,4},{6,7},{7,6},{8,9},{9,8},{10,11... | collective-permute-start | bytes 983048 | tf_op jit(solution)/shard_map/cond/branch_1_fun/ppermute | solution.py:337
  87.1 8.5 %collective-permute-start.30 = (f32[10,32,256]{2,1,0:T(8,128)S(1)}, f32[10,32,256]{2,1,0:T(8,128)S(1)}, u32[]{:S(2)}, u32[]{:S(2)}) collective-permute-start(f32[10,32,256]{2,1,0:T(8,128)S(1)} %collective-permute-done.29.refs_6_), channel_id=1, source_target_pairs={{0,1},{1,0},{2,3},{3,2},{4,5},{5,4},{6,7},{7,6},{8,9},{9,8},{10,11... | collective-permute-start | bytes 983048 | tf_op jit(solution)/shard_map/cond/branch_1_fun/ppermute | solution.py:337
  87.1 8.5 %collective-permute-start.37 = (f32[10,32,256]{2,1,0:T(8,128)S(1)}, f32[10,32,256]{2,1,0:T(8,128)S(1)}, u32[]{:S(2)}, u32[]{:S(2)}) collective-permute-start(f32[10,32,256]{2,1,0:T(8,128)S(1)} %collective-permute-done.32.refs_14_), channel_id=1, source_target_pairs={{0,1},{1,0},{2,3},{3,2},{4,5},{5,4},{6,7},{7,6},{8,9},{9,8},{10,11... | collective-permute-start | bytes 983048 | tf_op jit(solution)/shard_map/cond/branch_1_fun/ppermute | solution.py:337
  87.6 8.0 %collective-permute-start.33 = (f32[10,32,256]{2,1,0:T(8,128)S(1)}, f32[10,32,256]{2,1,0:T(8,128)S(1)}, u32[]{:S(2)}, u32[]{:S(2)}) collective-permute-start(f32[10,32,256]{2,1,0:T(8,128)S(1)} %collective-permute-done.31.refs_8_), channel_id=1, source_target_pairs={{0,1},{1,0},{2,3},{3,2},{4,5},{5,4},{6,7},{7,6},{8,9},{9,8},{10,11... | collective-permute-start | bytes 983048 | tf_op jit(solution)/shard_map/cond/branch_1_fun/ppermute | solution.py:337
  94.6 2.2 %collective-permute-start.35 = (f32[10,32,256]{2,1,0:T(8,128)S(1)}, f32[10,32,256]{2,1,0:T(8,128)S(1)}, u32[]{:S(2)}, u32[]{:S(2)}) collective-permute-start(f32[10,32,256]{2,1,0:T(8,128)S(1)} %collective-permute-done.34.refs_10_), channel_id=1, source_target_pairs={{0,1},{1,0},{2,3},{3,2},{4,5},{5,4},{6,7},{7,6},{8,9},{9,8},{10,11... | collective-permute-start | bytes 983048 | tf_op jit(solution)/shard_map/cond/branch_1_fun/ppermute | solution.py:337

commit v4 on v3

--- a/solution.py
+++ b/solution.py
@@ -34,13 +34,15 @@
     return dot(ah, bh, dims) + (dot(ah, bl, dims) + dot(al, bh, dims))
 
 
-def inverse_factor_kernel(where_ref, own_ref, other_ref, w_ref, s_ref):
+def inverse_factor_kernel(where_ref, *refs):
+    parts, (w_ref, s_ref) = refs[:-2], refs[-2:]
     n = w_ref.shape[0]
-    pieces, share = own_ref.shape[0], own_ref.shape[1]
-    core = where_ref[1] % 2
-    for i in range(pieces):
-        for ref, half in ((own_ref, core), (other_ref, 1 - core)):
-            s_ref[pl.ds(pl.multiple_of((2 * i + half) * share, share), share), :] = ref[i]
+    pieces, share = parts[0].shape[0], parts[0].shape[1]
+    own = where_ref[1] % len(parts)
+    for flip, ref in enumerate(parts):
+        at = jnp.bitwise_xor(own, flip) * share
+        for i in range(pieces):
+            s_ref[pl.ds(pl.multiple_of(i * len(parts) * share + at, share), share), :] = ref[i]
     rows = lax.broadcasted_iota(jnp.int32, (n, n), 0)
     cols = lax.broadcasted_iota(jnp.int32, (n, n), 1)
     eye = (rows == cols).astype(F32)
@@ -98,16 +100,16 @@
     w_ref[...] = w_ref[...] * scale_row
 
 
-def inverse_factor(where, own, other):
-    n = own.shape[-1]
+def inverse_factor(where, parts):
+    n = parts[0].shape[-1]
     return pl.pallas_call(
         inverse_factor_kernel,
         out_shape=jax.ShapeDtypeStruct((n, n), F32),
-        in_specs=[SMEM, VMEM, VMEM],
+        in_specs=[SMEM] + [VMEM] * len(parts),
         out_specs=VMEM,
         scratch_shapes=[pltpu.VMEM((n, n), F32)],
         compiler_params=pltpu.CompilerParams(vmem_limit_bytes=32 * 2**20),
-    )(where, own, other)
+    )(where, *parts)
 
 
 class Sizes:
@@ -122,17 +124,20 @@
         self.width = trailing.shape[1]
         self.tiles = self.cols * self.per_piece
 
-    def source(self, c):
-        slab = c * self.width // self.slab
-        return slab, (c * self.width - slab * self.slab) // self.piece
-
-    def sources(self):
-        found = []
-        for c in range(self.cols):
-            slab, first = self.source(c)
-            last = ((c + 1) * self.width - 1 - slab * self.slab) // self.piece
-            found.append(last - first + 1)
-        return found
+        self.groups = self.cols // 2
+        self.pair_units = 4 * self.width // self.unit
+        self.needed = sorted({s for g in range(self.groups) for s in self.shifts(g)})
+
+    def pair_slab(self, group):
+        return 2 * group * self.width // self.slab
+
+    def pair_start(self, group):
+        return (2 * group * self.width - self.pair_slab(group) * self.slab) // self.unit
+
+    def shifts(self, group):
+        start = self.pair_start(group) * self.unit
+        first, last = start // (2 * self.piece), (start + 2 * self.width - 1) // (2 * self.piece)
+        return [(g - group) % self.groups for g in range(first, last + 1)]
 
 
 def unit_flag(sizes, fill_ref, piece_index, unit, panel):
@@ -146,22 +151,32 @@
             yield core, side, (pool_row * 2 + core) * sizes.cols + pool_col * 2 + side
 
 
-def fits_kernel(sizes, cap, fill_ref, out_ref):
-    most = jnp.int32(0)
+def pair_flag(sizes, fill_ref, group, index):
+    unit = sizes.pair_slab(group) * sizes.tiles + sizes.pair_start(group) + index // 2
+    return fill_ref[unit // sizes.per_block * 2 + index % 2] != 0
+
+
+def fits_kernel(sizes, cap, pair_cap, fill_ref, out_ref):
+    over = jnp.int32(0)
     for pool_row in range(sizes.rows // 2):
-        for pool_col in range(sizes.cols // 2):
+        for pool_col in range(sizes.groups):
             count = jnp.int32(0)
             for _, _, piece in pool_pieces(sizes, pool_row, pool_col):
                 for u in range(sizes.per_piece):
                     for p in range(2):
                         count = count + unit_flag(sizes, fill_ref, piece, u, p).astype(jnp.int32)
-            most = jnp.maximum(most, count)
-    out_ref[0] = (most <= cap).astype(jnp.int32)
-
-
-def fits(sizes, cap, fill):
-    return pl.pallas_call(
-        functools.partial(fits_kernel, sizes, cap),
+            over = jnp.maximum(over, count - cap)
+    for group in range(sizes.groups):
+        count = jnp.int32(0)
+        for i in range(sizes.pair_units):
+            count = count + pair_flag(sizes, fill_ref, group, i).astype(jnp.int32)
+        over = jnp.maximum(over, count - pair_cap)
+    out_ref[0] = (over <= 0).astype(jnp.int32)
+
+
+def fits(sizes, cap, pair_cap, fill):
+    return pl.pallas_call(
+        functools.partial(fits_kernel, sizes, cap, pair_cap),
         out_shape=jax.ShapeDtypeStruct((1,), jnp.int32),
         in_specs=[SMEM],
         out_specs=SMEM,
@@ -205,39 +220,73 @@
     )(where, fill, panel, from_core, from_side)
 
 
-def apply_factor_kernel(
-    sizes, where_ref, fill_ref, w_ref, panel_ref, column_ref, x_ref, high_ref, low_ref, slot_ref, masked, column, sem
-):
-    c, r = where_ref[0], where_ref[1]
-
-    def mask(source, target, first_unit, count):
-        for u in range(count):
-            for p in range(2):
-                at = (pl.ds(u * sizes.unit, sizes.unit), pl.ds(p * sizes.block, sizes.block))
-                flag = fill_ref[(first_unit + u) // sizes.per_block * 2 + p] != 0
-                target[at] = jnp.where(flag, source[at], 0.0)
-
-    mask(panel_ref, masked, (r * sizes.cols + c) * sizes.per_piece, sizes.per_piece)
-    mask(column_ref, column, c * (sizes.width // sizes.unit), sizes.width // sizes.unit)
-    w = halves(w_ref[...])
-    masked[...] = dot3(halves(masked[...]), w, NT)
-    copy_out = pltpu.make_async_copy(masked, x_ref, sem)
-    copy_out.start()
-    solved = dot3(w, halves(column[...]), NT)
-    high_ref[...], low_ref[...] = halves(dot3(w, halves(solved), TN))
-
-    @pl.loop(0, sizes.cols // 2)
-    def _(group):
-        pool_col = jnp.bitwise_xor(c // 2, group)
+def pair_slots(sizes, fill_ref, group, slots):
+    def step(i, slot):
+        flag = pair_flag(sizes, fill_ref, group, i)
+        slots[i] = jnp.where(flag, slot, -1)
+        return slot + flag.astype(jnp.int32)
+
+    lax.fori_loop(0, sizes.pair_units, step, jnp.int32(0))
+
+
+def pack_column_kernel(sizes, cap, pair_cap, where_ref, fill_ref, *refs):
+    lists, (out_ref, slots) = refs[:-2], refs[-2:]
+    own = where_ref[0] // 2
+    slab, start = sizes.pair_slab(own), sizes.pair_start(own)
+    pair_slots(sizes, fill_ref, own, slots)
+    for shift, list_ref in zip(sizes.needed, lists):
+        group = lax.rem(own + shift, sizes.groups)
         slot = jnp.int32(0)
-        for core, side, piece in pool_pieces(sizes, r // 2, pool_col):
+        for core, side, piece in pool_pieces(sizes, slab // 2, group):
             for u in range(sizes.per_piece):
                 for p in range(2):
                     flag = unit_flag(sizes, fill_ref, piece, u, p)
+                    index = (((group * 2 + side) * sizes.per_piece + u) - start) * 2 + p
+                    inside = jnp.logical_and(index >= 0, index < sizes.pair_units)
+                    wanted = jnp.logical_and(jnp.logical_and(flag, inside), slab % 2 == core)
+
+                    @pl.when(wanted)
+                    def _(slot=slot, index=index, list_ref=list_ref):
+                        target = slots[jnp.clip(index, 0, sizes.pair_units - 1)]
+                        out_ref[jnp.clip(target, 0, pair_cap - 1)] = list_ref[jnp.minimum(slot, cap - 1)]
+
+                    slot = slot + flag.astype(jnp.int32)
+
+
+def pack_column(sizes, cap, pair_cap, where, fill, lists):
+    return pl.pallas_call(
+        functools.partial(pack_column_kernel, sizes, cap, pair_cap),
+        out_shape=jax.ShapeDtypeStruct((pair_cap, sizes.unit // 4, sizes.block), F32),
+        in_specs=[SMEM, SMEM] + [VMEM] * len(lists),
+        out_specs=VMEM,
+        scratch_shapes=[pltpu.SMEM((sizes.pair_units,), jnp.int32)],
+        compiler_params=pltpu.CompilerParams(vmem_limit_bytes=32 * 2**20),
+    )(where, fill, *lists)
+
+
+def own_factor_kernel(sizes, where_ref, fill_ref, w_ref, panel_ref, x_ref, slot_ref, masked, sem):
+    c, r = where_ref[0], where_ref[1]
+    own = r * sizes.cols + c
+    for u in range(sizes.per_piece):
+        for p in range(2):
+            at = (pl.ds(u * sizes.unit, sizes.unit), pl.ds(p * sizes.block, sizes.block))
+            masked[at] = jnp.where(unit_flag(sizes, fill_ref, own, u, p), panel_ref[at], 0.0)
+    masked[...] = dot3(halves(masked[...]), halves(w_ref[...]), NT)
+    copy_out = pltpu.make_async_copy(masked, x_ref, sem)
+    copy_out.start()
+
+    @pl.loop(0, sizes.groups)
+    def _(shift):
+        group = lax.rem(c // 2 + shift, sizes.groups)
+        slot = jnp.int32(0)
+        for core, side, piece in pool_pieces(sizes, r // 2, group):
+            for u in range(sizes.per_piece):
+                for p in range(2):
+                    flag = unit_flag(sizes, fill_ref, piece, u, p)
 
                     @pl.when(core == r % 2)
                     def _(slot=slot, flag=flag, side=side, u=u, p=p):
-                        at = ((group * 2 + side) * sizes.per_piece + u) * 2 + p
+                        at = ((shift * 2 + side) * sizes.per_piece + u) * 2 + p
                         slot_ref[at] = jnp.where(flag, slot, -1)
 
                     slot = slot + flag.astype(jnp.int32)
@@ -245,28 +294,59 @@
     copy_out.wait()
 
 
-def apply_factor(sizes, where, fill, w, panel, column):
-    n = w.shape[0]
-    return pl.pallas_call(
-        functools.partial(apply_factor_kernel, sizes),
+def own_factor(sizes, where, fill, w, panel):
+    return pl.pallas_call(
+        functools.partial(own_factor_kernel, sizes),
         out_shape=(
             jax.ShapeDtypeStruct(panel.shape, F32),
-            jax.ShapeDtypeStruct((n, sizes.width), BF16),
-            jax.ShapeDtypeStruct((n, sizes.width), BF16),
             jax.ShapeDtypeStruct((2 * sizes.tiles,), jnp.int32),
         ),
-        in_specs=[SMEM, SMEM, VMEM, VMEM, VMEM],
-        out_specs=(HBM, VMEM, VMEM, SMEM),
-        scratch_shapes=[
-            pltpu.VMEM(panel.shape, F32),
-            pltpu.VMEM((sizes.width, n), F32),
-            pltpu.SemaphoreType.DMA,
-        ],
+        in_specs=[SMEM, SMEM, VMEM, VMEM],
+        out_specs=(HBM, SMEM),
+        scratch_shapes=[pltpu.VMEM(panel.shape, F32), pltpu.SemaphoreType.DMA],
         compiler_params=pltpu.CompilerParams(vmem_limit_bytes=32 * 2**20),
-    )(where, fill, w, panel, column)
-
-
-def update_kernel(sizes, where_ref, slot_ref, high_ref, low_ref, window_ref, *refs):
+    )(where, fill, w, panel)
+
+
+def column_factor_kernel(sizes, where_ref, fill_ref, w_ref, *refs):
+    lists, (out_ref, column, slots) = refs[:4], refs[4:]
+    c, r = where_ref[0], where_ref[1]
+    side, core = c % 2, r % 2
+    quarter = sizes.unit // 4
+    pair_slots(sizes, fill_ref, c // 2, slots)
+    column[...] = jnp.zeros_like(column)
+
+    @pl.loop(0, sizes.pair_units // 4)
+    def _(unit):
+        for p in range(2):
+            slot = slots[(side * (sizes.pair_units // 4) + unit) * 2 + p]
+
+            @pl.when(slot >= 0)
+            def _(slot=slot, p=p):
+                for flip in range(4):
+                    from_side = jnp.bitwise_xor(side, flip // 2)
+                    from_core = jnp.bitwise_xor(core, flip % 2)
+                    at = pl.multiple_of(unit * sizes.unit + (from_side * 2 + from_core) * quarter, quarter)
+                    column[pl.ds(at, quarter), pl.ds(p * sizes.block, sizes.block)] = lists[flip][slot]
+
+    w = halves(w_ref[...])
+    solved = dot3(w, halves(column[...]), NT)
+    out_ref[0], out_ref[1] = halves(dot3(w, halves(solved), TN))
+
+
+def column_factor(sizes, where, fill, w, lists):
+    n = w.shape[0]
+    return pl.pallas_call(
+        functools.partial(column_factor_kernel, sizes),
+        out_shape=jax.ShapeDtypeStruct((2, n, sizes.width), BF16),
+        in_specs=[SMEM, SMEM, VMEM] + [VMEM] * 4,
+        out_specs=VMEM,
+        scratch_shapes=[pltpu.VMEM((sizes.width, n), F32), pltpu.SMEM((sizes.pair_units,), jnp.int32)],
+        compiler_params=pltpu.CompilerParams(vmem_limit_bytes=32 * 2**20),
+    )(where, fill, w, *lists)
+
+
+def update_kernel(sizes, where_ref, slot_ref, column_ref, window_ref, *refs):
     groups = sizes.cols // 2
     lists, (out_ref, tiles, unit_data, out_sems) = refs[: 4 * groups], refs[4 * groups :]
     c, r = where_ref[0], where_ref[1]
@@ -275,7 +355,7 @@
     quarter = sizes.unit // 4
 
     def rows_of(t):
-        group = jnp.bitwise_xor(c // 2, t // per_group)
+        group = lax.rem(c // 2 + t // per_group, groups)
         return pl.ds(pl.multiple_of((group * per_group + t % per_group) * sizes.unit, sizes.unit), sizes.unit)
 
     def tile_out(t, source):
@@ -306,7 +386,7 @@
                             at = pl.multiple_of((from_side * 2 + from_core) * quarter, quarter)
                             unit_data[pl.ds(at, quarter), :] = lists[4 * group + flip][slot]
                         at = pl.ds(p * sizes.block, sizes.block)
-                        right = (high_ref[at, :], low_ref[at, :])
+                        right = (column_ref[0, at, :], column_ref[1, at, :])
                         tiles[t] = tiles[t] - dot3(halves(unit_data[...]), right, NN)
 
                 tile_out(t, tiles.at[t]).start()
@@ -316,12 +396,12 @@
         tile_out(t, tiles.at[t]).wait()
 
 
-def update(sizes, where, slots, high, low, window, lists):
+def update(sizes, where, slots, column, window, lists):
     tiles = sizes.tiles
     return pl.pallas_call(
         functools.partial(update_kernel, sizes),
         out_shape=jax.ShapeDtypeStruct(window.shape, F32),
-        in_specs=[SMEM, SMEM, VMEM, VMEM, VMEM] + [VMEM] * len(lists),
+        in_specs=[SMEM, SMEM, VMEM, VMEM] + [VMEM] * len(lists),
         out_specs=HBM,
         scratch_shapes=[
             pltpu.VMEM((tiles, sizes.unit, sizes.width), F32),
@@ -329,7 +409,7 @@
             pltpu.SemaphoreType.DMA((tiles,)),
         ],
         compiler_params=pltpu.CompilerParams(vmem_limit_bytes=48 * 2**20),
-    )(where, slots, high, low, window, *lists)
+    )(where, slots, column, window, *lists)
 
 
 def swap(value, axis, step):
@@ -346,34 +426,21 @@
     return lax.optimization_barrier((value, *earlier))[0]
 
 
-def gather_column(sizes, panel):
-    counts = sizes.sources()
-    values = []
-    for j in range(max(counts)):
-        pairs = []
-        for at in range(sizes.cols):
-            slab, first = sizes.source(at)
-            if j < counts[at]:
-                pairs.append(((first + j) * sizes.rows + slab, at * sizes.rows + slab))
-        values.append(lax.ppermute(panel, ("col", "row"), pairs))
-    return values
-
-
-def select_column(sizes, values):
-    start = lax.axis_index("col") * sizes.width % sizes.slab % sizes.piece
-    return lax.dynamic_slice_in_dim(jnp.concatenate(values, 0), start, sizes.width, 0)
+def bring(sizes, value, shift):
+    pairs = [(i, (i - 2 * shift) % sizes.cols) for i in range(sizes.cols)]
+    return lax.ppermute(value, "col", pairs)
 
 
 def spread_column(sizes, value, step):
     r, c = lax.axis_index("row"), lax.axis_index("col")
     pairs = []
     for at in range(sizes.cols):
-        slab, _ = sizes.source(at)
+        slab = sizes.pair_slab(at // 2)
         for row in range(sizes.rows):
-            if (row ^ slab) % (2 * step) == 0:
+            if (row // 2 ^ slab // 2) % step == 0:
                 pairs.append((at * sizes.rows + row, at * sizes.rows + (row ^ step)))
     other = lax.ppermute(value, ("col", "row"), pairs)
-    return jnp.where(((r ^ (c * sizes.width // sizes.slab)) & step) != 0, other, value)
+    return jnp.where(((r ^ sizes.pair_slab(c // 2)) & step) != 0, other, value)
 
 
 def per_device(trailing, panel_rows, pivot_block, panel_fill):
@@ -383,9 +450,10 @@
     where = jnp.stack([c, r]).astype(jnp.int32)
     side, core = c % 2, r % 2
     quarter = sizes.unit // 4
-    share = pivot_block.shape[0] // 2
-    most = 8 * sizes.per_piece
-    cap = most * 5 // 12
+    split = min(4, pivot_block.shape[0] // 8)
+    share = pivot_block.shape[0] // split
+    most, pair_most = 8 * sizes.per_piece, sizes.pair_units
+    cap, pair_cap = most * 5 // 12, pair_most * 5 // 8
 
     units = panel_rows.reshape(sizes.per_piece, sizes.unit, -1)
     quarters = panel_rows.reshape(sizes.per_piece, 2, 2, quarter, -1)
@@ -396,52 +464,55 @@
     from_core = swap(at_core(1 - core), "row", 1)
     both = jnp.stack([at_core(core), from_core])
     from_side = swap(lax.dynamic_index_in_dim(both, 1 - side, 2, keepdims=False), "col", 1)
-    pivot = lax.dynamic_slice_in_dim(pivot_block, core * share, share, 0)[None]
+    pivot = lax.dynamic_slice_in_dim(pivot_block, r % split * share, share, 0)[None]
     pivot = join(c, 1, pivot, swap(pivot, "col", 1))
     pivot = join(c, 2, pivot, swap(pivot, "col", 2))
-    column = gather_column(sizes, panel_rows)
-
-    def run(cap, trailing, panel_rows, fill, units, from_core, from_side, pivot, *column):
+
+    def run(cap, pair_cap, trailing, panel_rows, fill, units, from_core, from_side, pivot):
         own = pack(sizes, cap, where, fill, units, from_core, from_side)
-
-        far = list(range(2, sizes.cols, 2))
-        first, later = [far[-1]] + far[:-2], far[-2:-1]
-        lists = {k: swap(own, "col", k) for k in first}
+        lists = {0: own}
+        first = [s for s in range(1, sizes.groups) if s in sizes.needed]
+        later = [s for s in range(1, sizes.groups) if s not in sizes.needed]
+        lists |= {s: bring(sizes, own, s) for s in first}
         sides = {0: swap(own, "col", 1)}
         step = 4
         while step < sizes.cols:
             pivot = join(c, step, pivot, swap(pivot, "col", step))
             step *= 2
-        column = lax.optimization_barrier((own, *column))[1:]
-        column = select_column(sizes, column)
+        near = first[0]
+        pivot, sides[0], lists[near] = lax.optimization_barrier((pivot, sides[0], lists[near]))
+        parts = [pivot] + ([swap(pivot, "row", 2)] if split == 4 else [])
+        parts = [part for value in parts for part in (value, swap(value, "row", 1))]
+        w = inverse_factor(where, parts)
+        held = lax.optimization_barrier((w, sides[0], *lists.values()))
+        w, sides[0] = held[:2]
+        lists = dict(zip(lists, held[2:]))
+
+        column = pack_column(sizes, cap, pair_cap, where, fill, [lists[s] for s in sizes.needed])
+        lists |= {s: bring(sizes, lists[0], s) for s in later}
+        sides |= {s: swap(lists[s], "col", 1) for s in first}
         step = sizes.rows // 2
         while step > 1:
             column = spread_column(sizes, column, step)
             step //= 2
-        held = lax.optimization_barrier((own, pivot, column, sides[0], *lists.values()))
-        own, pivot, column, sides[0] = held[:4]
-        lists = dict(zip(first, held[4:]))
-
-        lists |= {k: swap(own, "col", k) for k in later}
-        sides |= {k: swap(lists[k], "col", 1) for k in first}
-        w = inverse_factor(where, pivot, swap(pivot, "row", 1))
-        column = spread_column(sizes, column, 1)
-        own_factor, high, low, slots = apply_factor(sizes, where, fill, w, panel_rows, column)
-        for k in later:
-            lists[k] = lax.optimization_barrier((lists[k], high, *(sides[j] for j in first)))[0]
-            sides[k] = swap(lists[k], "col", 1)
-        lists[0] = own
+        across = swap(column, "col", 1)
+        columns = [column, swap(column, "row", 1), across, swap(across, "row", 1)]
+        panel_factor, slots = own_factor(sizes, where, fill, w, panel_rows)
+        for s in later:
+            lists[s] = lax.optimization_barrier((lists[s], slots, *(sides[j] for j in first)))[0]
+            sides[s] = swap(lists[s], "col", 1)
+        column = column_factor(sizes, where, fill, w, columns)
         ordered = []
-        for k in range(0, sizes.cols, 2):
-            value, other = lists[k], sides[k]
+        for s in range(sizes.groups):
+            value, other = lists[s], sides[s]
             ordered += [value, swap(value, "row", 1), other, swap(other, "row", 1)]
-        return update(sizes, where, slots, high, low, trailing, ordered), own_factor
-
-    operands = (trailing, panel_rows, fill, units, from_core, from_side, pivot, *column)
+        return update(sizes, where, slots, column, trailing, ordered), panel_factor
+
+    operands = (trailing, panel_rows, fill, units, from_core, from_side, pivot)
     return lax.cond(
-        fits(sizes, cap, fill)[0] != 0,
-        functools.partial(run, cap),
-        functools.partial(run, most),
+        fits(sizes, cap, pair_cap, fill)[0] != 0,
+        functools.partial(run, cap, pair_cap),
+        functools.partial(run, most, pair_most),
         *operands,
     )
 

time: 107 us -> 112 us (1.047)
  the two profiles are of different devices: /device:TPU:1 before, /device:TPU:0 now
where the time goes in v4:
time: 112 us
  waiting for transfers between devices  48.9 us (44%)
  starting transfers between devices  31.3 us (28%)
  Pallas kernels  26.3 us (23%)
  local copies, waits for them, and re-layouts  3.13 us (3%)
  between operations  1.54 us (1%)
    ppermute x23, waiting for transfers between devices, swap(): return lax.ppermute(value, axis, [(i, i ^ step) for i in range(size)])  43.9 us
    ppermute x3, starting transfers between devices, bring(): return lax.ppermute(value, 'col', pairs)  14.9 us
    ppermute x23, starting transfers between devices, swap(): return lax.ppermute(value, axis, [(i, i ^ step) for i in range(size)])  12.8 us
    pallas_call x1, Pallas kernels, update(): pl.pallas_call(functools.partial(update_kernel, sizes), out_shape=jax.Sha...  7.99 us
    pallas_call x1, Pallas kernels, inverse_factor(): pl.pallas_call(inverse_factor_kernel, out_shape=jax.ShapeDtypeStruct((n,...  6.89 us
    ppermute x3, waiting for transfers between devices, bring(): return lax.ppermute(value, 'col', pairs)  4.96 us
    ppermute x1, starting transfers between devices, spread_column(): other = lax.ppermute(value, ('col', 'row'), pairs)  3.57 us
    pallas_call x1, Pallas kernels, own_factor(): pl.pallas_call(functools.partial(own_factor_kernel, sizes), out_shape=(ja...  3.44 us
  transfers between devices with their start and end apart: 27, of which 11 were waited for; matrix products, arithmetic and copies ran while one was open for 1% of the time, Pallas kernels for 13%

profile of v4, /device:TPU:0, one launch (start us, length us, event | category | flops | bytes accessed | tf_op | source)
XLA Modules:
  0.0 111.8 jit_solution(6944813232933744369)
XLA Ops:
  0.6 0.0 copy-start
  0.7 1.2 %dynamic-slice_bitcast_fusion = (f32[1,3,2,32,512]{4,3,2,1,0:T(8,128)S(1)}, f32[3,2,32,512]{3,2,1,0:T(8,128)S(1)}) fusion(f32[3,2,2,32,512]{4,3,2,1,0:T(8,128)} %bitcast.19, s32[]{:T(128)S(6)} %select_n.96, s32[]{:T(128)S(6)} %select_n.95), kind=kLoop, calls=%fused_computation.10 | loop fusion | bytes 1572872 | tf_op jit(solution)/shard_map/stack | solution.py:465
  1.9 0.5 collective-permute-start.48
  2.4 1.3 %collective-permute-done.48 = f32[3,2,32,512]{3,2,1,0:T(8,128)S(1)} collective-permute-done((f32[3,2,32,512]{3,2,1,0:T(8,128)S(1)}, f32[3,2,32,512]{3,2,1,0:T(8,128)S(1)}, u32[]{:S(2)}, u32[]{:S(2)}) %collective-permute-start.48) | collective-permute-done | bytes 393248 | tf_op jit(solution)/shard_map/ppermute | solution.py:417
  3.8 2.9 %collective-permute-start.49 = (f32[2,3,32,512]{3,2,1,0:T(8,128)S(1)}, f32[2,3,32,512]{3,2,1,0:T(8,128)S(1)}, u32[]{:S(2)}, u32[]{:S(2)}) collective-permute-start(f32[2,3,32,512]{3,2,1,0:T(8,128)S(1)} %fusion.1), channel_id=1, source_target_pairs={{0,4},{4,0},{8,12},{12,8},{16,20},{20,16},{24,28},{28,24},{1,5},{5... | collective-permute-start | bytes 1179656 | tf_op jit(solution)/shard_map/ppermute | solution.py:417
  6.7 0.1 collective-permute-start.46
  6.8 0.8 copy.13
  7.6 0.1 reshape.18.fill_ref
  7.7 1.2 %shard_map.63 = s32[1]{0:T(128)} custom-call(s32[96]{0:T(128)S(1)} %reshape.18.fill_ref), custom_call_target="tpu_custom_call" | custom-call | tf_op jit(solution)/shard_map/pallas_call | solution.py:178
  9.6 7.2 %collective-permute-done.46 = f32[1,16,512]{2,1,0:T(8,128)S(1)} collective-permute-done((f32[1,16,512]{2,1,0:T(8,128)S(1)}, f32[1,16,512]{2,1,0:T(8,128)S(1)}, u32[]{:S(2)}, u32[]{:S(2)}) %collective-permute-start.46) | collective-permute-done | bytes 32800 | tf_op jit(solution)/shard_map/ppermute | solution.py:417
  16.9 1.9 %collective-permute-start.47 = (f32[2,16,512]{2,1,0:T(8,128)S(1)}, f32[2,16,512]{2,1,0:T(8,128)S(1)}, u32[]{:S(2)}, u32[]{:S(2)}) collective-permute-start(f32[2,16,512]{2,1,0:T(8,128)S(1)} %maximum_select_fusion.2), channel_id=1, source_target_pairs={{0,8},{4,12},{8,0},{12,4},{16,24},{20,28},{24,16},{28,20},{1,9},{5... | collective-permute-start | bytes 196616 | tf_op jit(solution)/shard_map/ppermute | solution.py:417
  18.8 0.1 pad_add_fusion
  18.8 2.4 %collective-permute-done.47 = f32[2,16,512]{2,1,0:T(8,128)S(1)} collective-permute-done((f32[2,16,512]{2,1,0:T(8,128)S(1)}, f32[2,16,512]{2,1,0:T(8,128)S(1)}, u32[]{:S(2)}, u32[]{:S(2)}) %collective-permute-start.47) | collective-permute-done | bytes 65568 | tf_op jit(solution)/shard_map/ppermute | solution.py:417
  21.2 0.0 collective-permute-done.49
  21.2 90.4 %conditional.1 = (f32[384,512]{1,0:T(8,128)}, f32[3072,512]{1,0:T(8,128)}) conditional(s32[]{:T(128)} %bitcast.2, (s32[]{:T(128)}, s32[]{:T(128)}, s32[2]{0:T(128)S(1)}, s32[96]{0:T(128)S(1)}, f32[384,512]{1,0:T(8,128)}, /*index=5*/f32[3,2,32,512]{3,2,1,0:T(8,128)S(1)}, f32[2,3,32,512]{3,2,1,0:T(8,128)S(1)}, f32[384,512]{1,0:T(8,128)}, ...), branch_computations={%region_0.1_spmd, %region_1.2_spmd} | conditional | flops 360484 | bytes 94242344 | solution.py:512
  21.5 1.5 %branch_1_fun.6.refs_0_ = f32[10,32,256]{2,1,0:T(8,128)S(1)} custom-call(s32[2]{0:T(128)S(1)} %get-tuple-element.56.where_ref, s32[96]{0:T(128)S(1)} %get-tuple-element.57.fill_ref, f32[3,128,512]{2,1,0:T(8,128)} %bitcast.21, f32[3,2,32,512]{3,2,1,0:T(8,128)S(1)} %get-tuple-element.61.core_ref, f32[2,3,32,512]{3,2,1,0:T(8,128)S(1)} %get-tuple-element.62.side_ref), custom_call_target="tpu_custom_call" | custom-call | tf_op jit(solution)/shard_map/cond/branch_1_fun/pallas_call | solution.py:213
  23.0 3.9 %collective-permute-start.25 = (f32[10,32,256]{2,1,0:T(8,128)S(1)}, f32[10,32,256]{2,1,0:T(8,128)S(1)}, u32[]{:S(2)}, u32[]{:S(2)}) collective-permute-start(f32[10,32,256]{2,1,0:T(8,128)S(1)} %branch_1_fun.6.refs_0_), channel_id=1, source_target_pairs={{0,24},{4,28},{8,0},{12,4},{16,8},{20,12},{24,16},{28,20},{1,25},{... | collective-permute-start | bytes 983048 | tf_op jit(solution)/shard_map/cond/branch_1_fun/ppermute | solution.py:431
  26.9 1.5 %collective-permute-start.24 = (f32[10,32,256]{2,1,0:T(8,128)S(1)}, f32[10,32,256]{2,1,0:T(8,128)S(1)}, u32[]{:S(2)}, u32[]{:S(2)}) collective-permute-start(f32[10,32,256]{2,1,0:T(8,128)S(1)} %branch_1_fun.6.refs_0_), channel_id=1, source_target_pairs={{0,4},{4,0},{8,12},{12,8},{16,20},{20,16},{24,28},{28,24},{1,5},{5... | collective-permute-start | bytes 983048 | tf_op jit(solution)/shard_map/cond/branch_1_fun/ppermute | solution.py:417
  28.4 0.1 collective-permute-start.23
  28.5 9.2 %collective-permute-done.23 = f32[4,16,512]{2,1,0:T(8,128)S(1)} collective-permute-done((f32[4,16,512]{2,1,0:T(8,128)S(1)}, f32[4,16,512]{2,1,0:T(8,128)S(1)}, u32[]{:S(2)}, u32[]{:S(2)}) %collective-permute-start.23) | collective-permute-done | bytes 131104 | tf_op jit(solution)/shard_map/cond/branch_1_fun/ppermute | solution.py:417
  37.7 0.0 collective-permute-done.25.refs_1_.refs_4_
  37.7 0.0 collective-permute-done.24.refs_2_
  37.8 1.7 %collective-permute-start.27 = (f32[8,16,512]{2,1,0:T(8,128)S(1)}, f32[8,16,512]{2,1,0:T(8,128)S(1)}, u32[]{:S(2)}, u32[]{:S(2)}) collective-permute-start(f32[8,16,512]{2,1,0:T(8,128)S(1)} %maximum_select_fusion.1.refs_0_), channel_id=1, source_target_pairs={{0,2},{1,3},{2,0},{3,1},{4,6},{5,7},{6,4},{7,5},{8,10},{9,11},{10,... | collective-permute-start | bytes 786440 | tf_op jit(solution)/shard_map/cond/branch_1_fun/ppermute | solution.py:417
  39.5 0.6 collective-permute-start.29
  40.1 0.0 collective-permute-start.26
  40.1 4.1 %collective-permute-done.27.refs_2_ = f32[8,16,512]{2,1,0:T(8,128)S(1)} collective-permute-done((f32[8,16,512]{2,1,0:T(8,128)S(1)}, f32[8,16,512]{2,1,0:T(8,128)S(1)}, u32[]{:S(2)}, u32[]{:S(2)}) %collective-permute-start.27) | collective-permute-done | bytes 262176 | tf_op jit(solution)/shard_map/cond/branch_1_fun/ppermute | solution.py:417
  44.2 0.0 collective-permute-start.28
  44.2 0.0 collective-permute-done.26.refs_1_
  44.2 1.5 %collective-permute-done.28.refs_3_ = f32[8,16,512]{2,1,0:T(8,128)S(1)} collective-permute-done((f32[8,16,512]{2,1,0:T(8,128)S(1)}, f32[8,16,512]{2,1,0:T(8,128)S(1)}, u32[]{:S(2)}, u32[]{:S(2)}) %collective-permute-start.28) | collective-permute-done | bytes 262176 | tf_op jit(solution)/shard_map/cond/branch_1_fun/ppermute | solution.py:417
  45.7 6.9 %branch_1_fun.7.w_ref = f32[512,512]{1,0:T(8,128)S(1)} custom-call(s32[2]{0:T(128)S(1)} %get-tuple-element.56.where_ref, f32[8,16,512]{2,1,0:T(8,128)S(1)} %maximum_select_fusion.1.refs_0_, f32[8,16,512]{2,1,0:T(8,128)S(1)} %collective-permute-done.26.refs_1_, f32[8,16,512]{2,1,0:T(8,128)S(1)} %collective-permute-done.27.refs_2_, ...), custom_call_target="tpu_custom_call" | custom-call | tf_op jit(solution)/shard_map/cond/branch_1_fun/pallas_call | solution.py:105
  52.6 0.0 collective-permute-done.29.refs_2_.refs_8_
  52.6 2.0 %branch_1_fun.9 = f32[10,32,256]{2,1,0:T(8,128)S(1)} custom-call(s32[2]{0:T(128)S(1)} %get-tuple-element.56.where_ref, s32[96]{0:T(128)S(1)} %get-tuple-element.57.fill_ref, f32[10,32,256]{2,1,0:T(8,128)S(1)} %branch_1_fun.6.refs_0_, f32[10,32,256]{2,1,0:T(8,128)S(1)} %collective-permute-done.25.refs_1_.refs_4_, ...), custom_call_target="tpu_custom_call" | custom-call | tf_op jit(solution)/shard_map/cond/branch_1_fun/pallas_call | solution.py:257
  54.7 3.6 %collective-permute-start.30 = (f32[10,32,256]{2,1,0:T(8,128)S(1)}, f32[10,32,256]{2,1,0:T(8,128)S(1)}, u32[]{:S(2)}, u32[]{:S(2)}) collective-permute-start(f32[10,32,256]{2,1,0:T(8,128)S(1)} %branch_1_fun.9), channel_id=1, source_target_pairs={{0,2},{1,3},{4,6},{5,7},{8,10},{9,11},{12,14},{13,15},{16,18},{17,... | collective-permute-start | bytes 983048 | tf_op jit(solution)/shard_map/cond/branch_1_fun/ppermute | solution.py:442
  58.3 10.3 %collective-permute-start.42 = (f32[10,32,256]{2,1,0:T(8,128)S(1)}, f32[10,32,256]{2,1,0:T(8,128)S(1)}, u32[]{:S(2)}, u32[]{:S(2)}) collective-permute-start(f32[10,32,256]{2,1,0:T(8,128)S(1)} %branch_1_fun.6.refs_0_), channel_id=1, source_target_pairs={{0,8},{4,12},{8,16},{12,20},{16,24},{20,28},{24,0},{28,4},{1,9},{5... | collective-permute-start | bytes 983048 | tf_op jit(solution)/shard_map/cond/branch_1_fun/ppermute | solution.py:431
  68.6 0.0 collective-permute-start.37
  68.6 2.0 %collective-permute-start.40 = (f32[10,32,256]{2,1,0:T(8,128)S(1)}, f32[10,32,256]{2,1,0:T(8,128)S(1)}, u32[]{:S(2)}, u32[]{:S(2)}) collective-permute-start(f32[10,32,256]{2,1,0:T(8,128)S(1)} %collective-permute-done.29.refs_2_.refs_8_), channel_id=1, source_target_pairs={{0,4},{4,0},{8,12},{12,8},{16,20},{20,16},{24,28},{28,24},{1,5},{5... | collective-permute-start | bytes 983048 | tf_op jit(solution)/shard_map/cond/branch_1_fun/ppermute | solution.py:417
  70.6 0.0 collective-permute-start.35
  70.6 0.0 collective-permute-done.30
  70.7 0.1 collective-permute-start.32
  70.8 3.4 %branch_1_fun.8 = (f32[384,512]{1,0:T(8,128)}, s32[48]{0:T(128)S(1)}) custom-call(s32[2]{0:T(128)S(1)} %get-tuple-element.56.where_ref, s32[96]{0:T(128)S(1)} %get-tuple-element.57.fill_ref, f32[512,512]{1,0:T(8,128)S(1)} %branch_1_fun.7.w_ref, f32[384,512]{1,0:T(8,128)} %get-tuple-element.67.panel_ref), custom_call_target="tpu_custom_call" | custom-call | tf_op jit(solution)/shard_map/cond/branch_1_fun/pallas_call | solution.py:298
  74.2 5.0 %collective-permute-done.42.refs_12_ = f32[10,32,256]{2,1,0:T(8,128)S(1)} collective-permute-done((f32[10,32,256]{2,1,0:T(8,128)S(1)}, f32[10,32,256]{2,1,0:T(8,128)S(1)}, u32[]{:S(2)}, u32[]{:S(2)}) %collective-permute-start.42) | collective-permute-done | bytes 327712 | tf_op jit(solution)/shard_map/cond/branch_1_fun/ppermute | solution.py:431
  79.2 0.0 collective-permute-start.34
  79.2 0.1 collective-permute-done.37.refs_6_
  79.3 0.5 collective-permute-start.36
  79.7 6.6 %collective-permute-done.40.refs_10_ = f32[10,32,256]{2,1,0:T(8,128)S(1)} collective-permute-done((f32[10,32,256]{2,1,0:T(8,128)S(1)}, f32[10,32,256]{2,1,0:T(8,128)S(1)}, u32[]{:S(2)}, u32[]{:S(2)}) %collective-permute-start.40) | collective-permute-done | bytes 327712 | tf_op jit(solution)/shard_map/cond/branch_1_fun/ppermute | solution.py:417
  86.3 0.0 collective-permute-start.31
  86.3 0.0 collective-permute-done.35.refs_3_
  86.3 0.0 collective-permute-start.44
  86.3 7.0 %collective-permute-done.32.refs_2_ = f32[10,32,256]{2,1,0:T(8,128)S(1)} collective-permute-done((f32[10,32,256]{2,1,0:T(8,128)S(1)}, f32[10,32,256]{2,1,0:T(8,128)S(1)}, u32[]{:S(2)}, u32[]{:S(2)}) %collective-permute-start.32) | collective-permute-done | bytes 327712 | tf_op jit(solution)/shard_map/cond/branch_1_fun/ppermute | solution.py:417
  93.3 0.0 collective-permute-start.33
  93.3 0.0 collective-permute-done.34.refs_1_
  93.3 0.5 collective-permute-start.39
  93.8 0.0 collective-permute-done.36.refs_5_
  93.8 0.1 collective-permute-start.43
  93.9 0.0 collective-permute-done.31.refs_1_
  93.9 0.4 collective-permute-start.38
  94.3 4.5 %collective-permute-done.44.refs_14_ = f32[10,32,256]{2,1,0:T(8,128)S(1)} collective-permute-done((f32[10,32,256]{2,1,0:T(8,128)S(1)}, f32[10,32,256]{2,1,0:T(8,128)S(1)}, u32[]{:S(2)}, u32[]{:S(2)}) %collective-permute-start.44) | collective-permute-done | bytes 327712 | tf_op jit(solution)/shard_map/cond/branch_1_fun/ppermute | solution.py:417
  98.9 0.5 collective-permute-start.45
  99.4 3.1 %branch_1_fun.10.column_ref = bf16[2,512,512]{2,1,0:T(8,128)(2,1)S(1)} custom-call(s32[2]{0:T(128)S(1)} %get-tuple-element.56.where_ref, s32[96]{0:T(128)S(1)} %get-tuple-element.57.fill_ref, f32[512,512]{1,0:T(8,128)S(1)} %branch_1_fun.7.w_ref, f32[10,32,256]{2,1,0:T(8,128)S(1)} %broadcast_select_fusion.2.refs_0_, ...), custom_call_target="tpu_custom_call" | custom-call | tf_op jit(solution)/shard_map/cond/branch_1_fun/pallas_call | solution.py:339
  102.6 1.0 copy-done.2
  103.6 0.0 collective-permute-done.38.refs_7_
  103.6 0.0 collective-permute-done.43.refs_13_
  103.6 0.0 collective-permute-done.45.refs_15_
  103.6 8.0 %branch_1_fun.11 = f32[3072,512]{1,0:T(8,128)} custom-call(s32[2]{0:T(128)S(1)} %get-tuple-element.56.where_ref, s32[48]{0:T(128)S(1)} %get-tuple-element.68.slot_ref, bf16[2,512,512]{2,1,0:T(8,128)(2,1)} %copy-done.2, f32[3072,512]{1,0:T(8,128)} %get-tuple-element.92.window_ref, f32[10,32,256]{2,1,0:T(8,128)S(1)} %branch_1_fun.6.refs_0_, ...), custom_call_target="tpu_custom_call" | custom-call | tf_op jit(solution)/shard_map/cond/branch_1_fun/pallas_call | solution.py:401
  (13 shorter events, 0.2 us)
Async XLA Ops:
  0.6 6.1 %copy-start = (f32[64,512]{1,0:T(8,128)S(1)}, f32[64,512]{1,0:T(8,128)}, u32[]{:S(2)}) copy-start(f32[64,512]{1,0:T(8,128)} %param.8) | copy-start | bytes 393220
  1.9 1.9 %collective-permute-start.48 = (f32[3,2,32,512]{3,2,1,0:T(8,128)S(1)}, f32[3,2,32,512]{3,2,1,0:T(8,128)S(1)}, u32[]{:S(2)}, u32[]{:S(2)}) collective-permute-start(f32[3,2,32,512]{3,2,1,0:T(8,128)S(1)} %get-tuple-element.102), channel_id=1, source_target_pairs={{0,1},{1,0},{2,3},{3,2},{4,5},{5,4},{6,7},{7,6},{8,9},{9,8},{10,11... | collective-permute-start | bytes 1179656 | tf_op jit(solution)/shard_map/ppermute | solution.py:417
  3.8 17.4 %collective-permute-start.49 = (f32[2,3,32,512]{3,2,1,0:T(8,128)S(1)}, f32[2,3,32,512]{3,2,1,0:T(8,128)S(1)}, u32[]{:S(2)}, u32[]{:S(2)}) collective-permute-start(f32[2,3,32,512]{3,2,1,0:T(8,128)S(1)} %fusion.1), channel_id=1, source_target_pairs={{0,4},{4,0},{8,12},{12,8},{16,20},{20,16},{24,28},{28,24},{1,5},{5... | collective-permute-start | bytes 1179656 | tf_op jit(solution)/shard_map/ppermute | solution.py:417
  6.7 10.1 %collective-permute-start.46 = (f32[1,16,512]{2,1,0:T(8,128)S(1)}, f32[1,16,512]{2,1,0:T(8,128)S(1)}, u32[]{:S(2)}, u32[]{:S(2)}) collective-permute-start(f32[1,16,512]{2,1,0:T(8,128)S(1)} %dynamic-slice_bitcast_fusion.2), channel_id=1, source_target_pairs={{0,4},{4,0},{8,12},{12,8},{16,20},{20,16},{24,28},{28,24},{1,5},{5... | collective-permute-start | bytes 98312 | tf_op jit(solution)/shard_map/ppermute | solution.py:417
  16.9 4.3 %collective-permute-start.47 = (f32[2,16,512]{2,1,0:T(8,128)S(1)}, f32[2,16,512]{2,1,0:T(8,128)S(1)}, u32[]{:S(2)}, u32[]{:S(2)}) collective-permute-start(f32[2,16,512]{2,1,0:T(8,128)S(1)} %maximum_select_fusion.2), channel_id=1, source_target_pairs={{0,8},{4,12},{8,0},{12,4},{16,24},{20,28},{24,16},{28,20},{1,9},{5... | collective-permute-start | bytes 196616 | tf_op jit(solution)/shard_map/ppermute | solution.py:417
  23.0 14.7 %collective-permute-start.25 = (f32[10,32,256]{2,1,0:T(8,128)S(1)}, f32[10,32,256]{2,1,0:T(8,128)S(1)}, u32[]{:S(2)}, u32[]{:S(2)}) collective-permute-start(f32[10,32,256]{2,1,0:T(8,128)S(1)} %branch_1_fun.6.refs_0_), channel_id=1, source_target_pairs={{0,24},{4,28},{8,0},{12,4},{16,8},{20,12},{24,16},{28,20},{1,25},{... | collective-permute-start | bytes 983048 | tf_op jit(solution)/shard_map/cond/branch_1_fun/ppermute | solution.py:431
  26.9 10.8 %collective-permute-start.24 = (f32[10,32,256]{2,1,0:T(8,128)S(1)}, f32[10,32,256]{2,1,0:T(8,128)S(1)}, u32[]{:S(2)}, u32[]{:S(2)}) collective-permute-start(f32[10,32,256]{2,1,0:T(8,128)S(1)} %branch_1_fun.6.refs_0_), channel_id=1, source_target_pairs={{0,4},{4,0},{8,12},{12,8},{16,20},{20,16},{24,28},{28,24},{1,5},{5... | collective-permute-start | bytes 983048 | tf_op jit(solution)/shard_map/cond/branch_1_fun/ppermute | solution.py:417
  28.4 9.3 %collective-permute-start.23 = (f32[4,16,512]{2,1,0:T(8,128)S(1)}, f32[4,16,512]{2,1,0:T(8,128)S(1)}, u32[]{:S(2)}, u32[]{:S(2)}) collective-permute-start(f32[4,16,512]{2,1,0:T(8,128)S(1)} %broadcast_select_fusion.3), channel_id=1, source_target_pairs={{0,16},{4,20},{8,24},{12,28},{16,0},{20,4},{24,8},{28,12},{1,17},{... | collective-permute-start | bytes 393224 | tf_op jit(solution)/shard_map/cond/branch_1_fun/ppermute | solution.py:417
  37.8 6.4 %collective-permute-start.27 = (f32[8,16,512]{2,1,0:T(8,128)S(1)}, f32[8,16,512]{2,1,0:T(8,128)S(1)}, u32[]{:S(2)}, u32[]{:S(2)}) collective-permute-start(f32[8,16,512]{2,1,0:T(8,128)S(1)} %maximum_select_fusion.1.refs_0_), channel_id=1, source_target_pairs={{0,2},{1,3},{2,0},{3,1},{4,6},{5,7},{6,4},{7,5},{8,10},{9,11},{10,... | collective-permute-start | bytes 786440 | tf_op jit(solution)/shard_map/cond/branch_1_fun/ppermute | solution.py:417
  39.5 13.2 %collective-permute-start.29 = (f32[10,32,256]{2,1,0:T(8,128)S(1)}, f32[10,32,256]{2,1,0:T(8,128)S(1)}, u32[]{:S(2)}, u32[]{:S(2)}) collective-permute-start(f32[10,32,256]{2,1,0:T(8,128)S(1)} %branch_1_fun.6.refs_0_), channel_id=1, source_target_pairs={{0,16},{4,20},{8,24},{12,28},{16,0},{20,4},{24,8},{28,12},{1,17},{... | collective-permute-start | bytes 983048 | tf_op jit(solution)/shard_map/cond/branch_1_fun/ppermute | solution.py:431
  40.1 4.1 %collective-permute-start.26 = (f32[8,16,512]{2,1,0:T(8,128)S(1)}, f32[8,16,512]{2,1,0:T(8,128)S(1)}, u32[]{:S(2)}, u32[]{:S(2)}) collective-permute-start(f32[8,16,512]{2,1,0:T(8,128)S(1)} %maximum_select_fusion.1.refs_0_), channel_id=1, source_target_pairs={{0,1},{1,0},{2,3},{3,2},{4,5},{5,4},{6,7},{7,6},{8,9},{9,8},{10,11... | collective-permute-start | bytes 786440 | tf_op jit(solution)/shard_map/cond/branch_1_fun/ppermute | solution.py:417
  44.2 1.5 %collective-permute-start.28 = (f32[8,16,512]{2,1,0:T(8,128)S(1)}, f32[8,16,512]{2,1,0:T(8,128)S(1)}, u32[]{:S(2)}, u32[]{:S(2)}) collective-permute-start(f32[8,16,512]{2,1,0:T(8,128)S(1)} %collective-permute-done.27.refs_2_), channel_id=1, source_target_pairs={{0,1},{1,0},{2,3},{3,2},{4,5},{5,4},{6,7},{7,6},{8,9},{9,8},{10,11... | collective-permute-start | bytes 786440 | tf_op jit(solution)/shard_map/cond/branch_1_fun/ppermute | solution.py:417
  54.7 16.0 %collective-permute-start.30 = (f32[10,32,256]{2,1,0:T(8,128)S(1)}, f32[10,32,256]{2,1,0:T(8,128)S(1)}, u32[]{:S(2)}, u32[]{:S(2)}) collective-permute-start(f32[10,32,256]{2,1,0:T(8,128)S(1)} %branch_1_fun.9), channel_id=1, source_target_pairs={{0,2},{1,3},{4,6},{5,7},{8,10},{9,11},{12,14},{13,15},{16,18},{17,... | collective-permute-start | bytes 983048 | tf_op jit(solution)/shard_map/cond/branch_1_fun/ppermute | solution.py:442
  58.3 20.9 %collective-permute-start.42 = (f32[10,32,256]{2,1,0:T(8,128)S(1)}, f32[10,32,256]{2,1,0:T(8,128)S(1)}, u32[]{:S(2)}, u32[]{:S(2)}) collective-permute-start(f32[10,32,256]{2,1,0:T(8,128)S(1)} %branch_1_fun.6.refs_0_), channel_id=1, source_target_pairs={{0,8},{4,12},{8,16},{12,20},{16,24},{20,28},{24,0},{28,4},{1,9},{5... | collective-permute-start | bytes 983048 | tf_op jit(solution)/shard_map/cond/branch_1_fun/ppermute | solution.py:431
  68.6 10.6 %collective-permute-start.37 = (f32[10,32,256]{2,1,0:T(8,128)S(1)}, f32[10,32,256]{2,1,0:T(8,128)S(1)}, u32[]{:S(2)}, u32[]{:S(2)}) collective-permute-start(f32[10,32,256]{2,1,0:T(8,128)S(1)} %collective-permute-done.25.refs_1_.refs_4_), channel_id=1, source_target_pairs={{0,4},{4,0},{8,12},{12,8},{16,20},{20,16},{24,28},{28,24},{1,5},{5... | collective-permute-start | bytes 983048 | tf_op jit(solution)/shard_map/cond/branch_1_fun/ppermute | solution.py:417
  68.6 17.7 %collective-permute-start.40 = (f32[10,32,256]{2,1,0:T(8,128)S(1)}, f32[10,32,256]{2,1,0:T(8,128)S(1)}, u32[]{:S(2)}, u32[]{:S(2)}) collective-permute-start(f32[10,32,256]{2,1,0:T(8,128)S(1)} %collective-permute-done.29.refs_2_.refs_8_), channel_id=1, source_target_pairs={{0,4},{4,0},{8,12},{12,8},{16,20},{20,16},{24,28},{28,24},{1,5},{5... | collective-permute-start | bytes 983048 | tf_op jit(solution)/shard_map/cond/branch_1_fun/ppermute | solution.py:417
  70.6 15.6 %collective-permute-start.35 = (f32[10,32,256]{2,1,0:T(8,128)S(1)}, f32[10,32,256]{2,1,0:T(8,128)S(1)}, u32[]{:S(2)}, u32[]{:S(2)}) collective-permute-start(f32[10,32,256]{2,1,0:T(8,128)S(1)} %collective-permute-done.24.refs_2_), channel_id=1, source_target_pairs={{0,1},{1,0},{2,3},{3,2},{4,5},{5,4},{6,7},{7,6},{8,9},{9,8},{10,11... | collective-permute-start | bytes 983048 | tf_op jit(solution)/shard_map/cond/branch_1_fun/ppermute | solution.py:417
  70.7 22.6 %collective-permute-start.32 = (f32[10,32,256]{2,1,0:T(8,128)S(1)}, f32[10,32,256]{2,1,0:T(8,128)S(1)}, u32[]{:S(2)}, u32[]{:S(2)}) collective-permute-start(f32[10,32,256]{2,1,0:T(8,128)S(1)} %broadcast_select_fusion.2.refs_0_), channel_id=1, source_target_pairs={{0,4},{4,0},{8,12},{12,8},{16,20},{20,16},{24,28},{28,24},{1,5},{5... | collective-permute-start | bytes 983048 | tf_op jit(solution)/shard_map/cond/branch_1_fun/ppermute | solution.py:417
  79.2 14.1 %collective-permute-start.34 = (f32[10,32,256]{2,1,0:T(8,128)S(1)}, f32[10,32,256]{2,1,0:T(8,128)S(1)}, u32[]{:S(2)}, u32[]{:S(2)}) collective-permute-start(f32[10,32,256]{2,1,0:T(8,128)S(1)} %branch_1_fun.6.refs_0_), channel_id=1, source_target_pairs={{0,1},{1,0},{2,3},{3,2},{4,5},{5,4},{6,7},{7,6},{8,9},{9,8},{10,11... | collective-permute-start | bytes 983048 | tf_op jit(solution)/shard_map/cond/branch_1_fun/ppermute | solution.py:417
  79.3 14.6 %collective-permute-start.36 = (f32[10,32,256]{2,1,0:T(8,128)S(1)}, f32[10,32,256]{2,1,0:T(8,128)S(1)}, u32[]{:S(2)}, u32[]{:S(2)}) collective-permute-start(f32[10,32,256]{2,1,0:T(8,128)S(1)} %collective-permute-done.25.refs_1_.refs_4_), channel_id=1, source_target_pairs={{0,1},{1,0},{2,3},{3,2},{4,5},{5,4},{6,7},{7,6},{8,9},{9,8},{10,11... | collective-permute-start | bytes 983048 | tf_op jit(solution)/shard_map/cond/branch_1_fun/ppermute | solution.py:417
  86.3 7.6 %collective-permute-start.31 = (f32[10,32,256]{2,1,0:T(8,128)S(1)}, f32[10,32,256]{2,1,0:T(8,128)S(1)}, u32[]{:S(2)}, u32[]{:S(2)}) collective-permute-start(f32[10,32,256]{2,1,0:T(8,128)S(1)} %broadcast_select_fusion.2.refs_0_), channel_id=1, source_target_pairs={{0,1},{1,0},{2,3},{3,2},{4,5},{5,4},{6,7},{7,6},{8,9},{9,8},{10,11... | collective-permute-start | bytes 983048 | tf_op jit(solution)/shard_map/cond/branch_1_fun/ppermute | solution.py:417
  86.3 12.6 %collective-permute-start.44 = (f32[10,32,256]{2,1,0:T(8,128)S(1)}, f32[10,32,256]{2,1,0:T(8,128)S(1)}, u32[]{:S(2)}, u32[]{:S(2)}) collective-permute-start(f32[10,32,256]{2,1,0:T(8,128)S(1)} %collective-permute-done.42.refs_12_), channel_id=1, source_target_pairs={{0,4},{4,0},{8,12},{12,8},{16,20},{20,16},{24,28},{28,24},{1,5},{5... | collective-permute-start | bytes 983048 | tf_op jit(solution)/shard_map/cond/branch_1_fun/ppermute | solution.py:417
  93.3 5.6 %collective-permute-start.33 = (f32[10,32,256]{2,1,0:T(8,128)S(1)}, f32[10,32,256]{2,1,0:T(8,128)S(1)}, u32[]{:S(2)}, u32[]{:S(2)}) collective-permute-start(f32[10,32,256]{2,1,0:T(8,128)S(1)} %collective-permute-done.32.refs_2_), channel_id=1, source_target_pairs={{0,1},{1,0},{2,3},{3,2},{4,5},{5,4},{6,7},{7,6},{8,9},{9,8},{10,11... | collective-permute-start | bytes 983048 | tf_op jit(solution)/shard_map/cond/branch_1_fun/ppermute | solution.py:417
  93.3 10.3 %collective-permute-start.39 = (f32[10,32,256]{2,1,0:T(8,128)S(1)}, f32[10,32,256]{2,1,0:T(8,128)S(1)}, u32[]{:S(2)}, u32[]{:S(2)}) collective-permute-start(f32[10,32,256]{2,1,0:T(8,128)S(1)} %collective-permute-done.29.refs_2_.refs_8_), channel_id=1, source_target_pairs={{0,1},{1,0},{2,3},{3,2},{4,5},{5,4},{6,7},{7,6},{8,9},{9,8},{10,11... | collective-permute-start | bytes 983048 | tf_op jit(solution)/shard_map/cond/branch_1_fun/ppermute | solution.py:417
  93.8 9.8 %collective-permute-start.43 = (f32[10,32,256]{2,1,0:T(8,128)S(1)}, f32[10,32,256]{2,1,0:T(8,128)S(1)}, u32[]{:S(2)}, u32[]{:S(2)}) collective-permute-start(f32[10,32,256]{2,1,0:T(8,128)S(1)} %collective-permute-done.42.refs_12_), channel_id=1, source_target_pairs={{0,1},{1,0},{2,3},{3,2},{4,5},{5,4},{6,7},{7,6},{8,9},{9,8},{10,11... | collective-permute-start | bytes 983048 | tf_op jit(solution)/shard_map/cond/branch_1_fun/ppermute | solution.py:417
  93.9 9.7 %collective-permute-start.38 = (f32[10,32,256]{2,1,0:T(8,128)S(1)}, f32[10,32,256]{2,1,0:T(8,128)S(1)}, u32[]{:S(2)}, u32[]{:S(2)}) collective-permute-start(f32[10,32,256]{2,1,0:T(8,128)S(1)} %collective-permute-done.37.refs_6_), channel_id=1, source_target_pairs={{0,1},{1,0},{2,3},{3,2},{4,5},{5,4},{6,7},{7,6},{8,9},{9,8},{10,11... | collective-permute-start | bytes 983048 | tf_op jit(solution)/shard_map/cond/branch_1_fun/ppermute | solution.py:417
  98.9 4.7 %collective-permute-start.41 = (f32[10,32,256]{2,1,0:T(8,128)S(1)}, f32[10,32,256]{2,1,0:T(8,128)S(1)}, u32[]{:S(2)}, u32[]{:S(2)}) collective-permute-start(f32[10,32,256]{2,1,0:T(8,128)S(1)} %collective-permute-done.40.refs_10_), channel_id=1, source_target_pairs={{0,1},{1,0},{2,3},{3,2},{4,5},{5,4},{6,7},{7,6},{8,9},{9,8},{10,11... | collective-permute-start | bytes 983048 | tf_op jit(solution)/shard_map/cond/branch_1_fun/ppermute | solution.py:417
  98.9 4.7 %collective-permute-start.45 = (f32[10,32,256]{2,1,0:T(8,128)S(1)}, f32[10,32,256]{2,1,0:T(8,128)S(1)}, u32[]{:S(2)}, u32[]{:S(2)}) collective-permute-start(f32[10,32,256]{2,1,0:T(8,128)S(1)} %collective-permute-done.44.refs_14_), channel_id=1, source_target_pairs={{0,1},{1,0},{2,3},{3,2},{4,5},{5,4},{6,7},{7,6},{8,9},{9,8},{10,11... | collective-permute-start | bytes 983048 | tf_op jit(solution)/shard_map/cond/branch_1_fun/ppermute | solution.py:417
  102.5 1.0 copy-start.2

commit v5 on v4

--- a/solution.py
+++ b/solution.py
@@ -108,7 +108,7 @@
         in_specs=[SMEM] + [VMEM] * len(parts),
         out_specs=VMEM,
         scratch_shapes=[pltpu.VMEM((n, n), F32)],
-        compiler_params=pltpu.CompilerParams(vmem_limit_bytes=32 * 2**20),
+        compiler_params=pltpu.CompilerParams(vmem_limit_bytes=20 * 2**20),
     )(where, *parts)
 
 
@@ -121,11 +121,12 @@
         self.per_piece = self.piece // self.unit
         self.per_block = self.block // self.unit
         self.slab = self.piece * self.cols
+        self.merge = self.per_block if 2 * self.piece % self.block == 0 else 1
         self.width = trailing.shape[1]
         self.tiles = self.cols * self.per_piece
 
         self.groups = self.cols // 2
-        self.pair_units = 4 * self.width // self.unit
+        self.column_units = 2 * self.width // self.unit
         self.needed = sorted({s for g in range(self.groups) for s in self.shifts(g)})
 
     def pair_slab(self, group):
@@ -156,7 +157,7 @@
     return fill_ref[unit // sizes.per_block * 2 + index % 2] != 0
 
 
-def fits_kernel(sizes, cap, pair_cap, fill_ref, out_ref):
+def fits_kernel(sizes, cap, column_cap, fill_ref, out_ref):
     over = jnp.int32(0)
     for pool_row in range(sizes.rows // 2):
         for pool_col in range(sizes.groups):
@@ -167,16 +168,18 @@
                         count = count + unit_flag(sizes, fill_ref, piece, u, p).astype(jnp.int32)
             over = jnp.maximum(over, count - cap)
     for group in range(sizes.groups):
-        count = jnp.int32(0)
-        for i in range(sizes.pair_units):
-            count = count + pair_flag(sizes, fill_ref, group, i).astype(jnp.int32)
-        over = jnp.maximum(over, count - pair_cap)
+        for side in range(2):
+            count = jnp.int32(0)
+            for i in range(sizes.column_units):
+                flag = pair_flag(sizes, fill_ref, group, side * sizes.column_units + i)
+                count = count + flag.astype(jnp.int32)
+            over = jnp.maximum(over, count - column_cap)
     out_ref[0] = (over <= 0).astype(jnp.int32)
 
 
-def fits(sizes, cap, pair_cap, fill):
-    return pl.pallas_call(
-        functools.partial(fits_kernel, sizes, cap, pair_cap),
+def fits(sizes, cap, column_cap, fill):
+    return pl.pallas_call(
+        functools.partial(fits_kernel, sizes, cap, column_cap),
         out_shape=jax.ShapeDtypeStruct((1,), jnp.int32),
         in_specs=[SMEM],
         out_specs=SMEM,
@@ -223,13 +226,14 @@
 def pair_slots(sizes, fill_ref, group, slots):
     def step(i, slot):
         flag = pair_flag(sizes, fill_ref, group, i)
+        slot = jnp.where(i == sizes.column_units, 0, slot)
         slots[i] = jnp.where(flag, slot, -1)
         return slot + flag.astype(jnp.int32)
 
-    lax.fori_loop(0, sizes.pair_units, step, jnp.int32(0))
-
-
-def pack_column_kernel(sizes, cap, pair_cap, where_ref, fill_ref, *refs):
+    lax.fori_loop(0, 2 * sizes.column_units, step, jnp.int32(0))
+
+
+def pack_column_kernel(sizes, cap, column_cap, where_ref, fill_ref, *refs):
     lists, (out_ref, slots) = refs[:-2], refs[-2:]
     own = where_ref[0] // 2
     slab, start = sizes.pair_slab(own), sizes.pair_start(own)
@@ -242,25 +246,26 @@
                 for p in range(2):
                     flag = unit_flag(sizes, fill_ref, piece, u, p)
                     index = (((group * 2 + side) * sizes.per_piece + u) - start) * 2 + p
-                    inside = jnp.logical_and(index >= 0, index < sizes.pair_units)
+                    inside = jnp.logical_and(index >= 0, index < 2 * sizes.column_units)
                     wanted = jnp.logical_and(jnp.logical_and(flag, inside), slab % 2 == core)
 
                     @pl.when(wanted)
                     def _(slot=slot, index=index, list_ref=list_ref):
-                        target = slots[jnp.clip(index, 0, sizes.pair_units - 1)]
-                        out_ref[jnp.clip(target, 0, pair_cap - 1)] = list_ref[jnp.minimum(slot, cap - 1)]
+                        index = jnp.clip(index, 0, 2 * sizes.column_units - 1)
+                        target = jnp.clip(slots[index], 0, column_cap - 1)
+                        out_ref[index // sizes.column_units, target] = list_ref[jnp.minimum(slot, cap - 1)]
 
                     slot = slot + flag.astype(jnp.int32)
 
 
-def pack_column(sizes, cap, pair_cap, where, fill, lists):
-    return pl.pallas_call(
-        functools.partial(pack_column_kernel, sizes, cap, pair_cap),
-        out_shape=jax.ShapeDtypeStruct((pair_cap, sizes.unit // 4, sizes.block), F32),
+def pack_column(sizes, cap, column_cap, where, fill, lists):
+    return pl.pallas_call(
+        functools.partial(pack_column_kernel, sizes, cap, column_cap),
+        out_shape=jax.ShapeDtypeStruct((2, column_cap, sizes.unit // 4, sizes.block), F32),
         in_specs=[SMEM, SMEM] + [VMEM] * len(lists),
         out_specs=VMEM,
-        scratch_shapes=[pltpu.SMEM((sizes.pair_units,), jnp.int32)],
-        compiler_params=pltpu.CompilerParams(vmem_limit_bytes=32 * 2**20),
+        scratch_shapes=[pltpu.SMEM((2 * sizes.column_units,), jnp.int32)],
+        compiler_params=pltpu.CompilerParams(vmem_limit_bytes=20 * 2**20),
     )(where, fill, *lists)
 
 
@@ -298,13 +303,13 @@
     return pl.pallas_call(
         functools.partial(own_factor_kernel, sizes),
         out_shape=(
-            jax.ShapeDtypeStruct(panel.shape, F32),
+            pltpu.HBM(panel.shape, F32),
             jax.ShapeDtypeStruct((2 * sizes.tiles,), jnp.int32),
         ),
         in_specs=[SMEM, SMEM, VMEM, VMEM],
         out_specs=(HBM, SMEM),
         scratch_shapes=[pltpu.VMEM(panel.shape, F32), pltpu.SemaphoreType.DMA],
-        compiler_params=pltpu.CompilerParams(vmem_limit_bytes=32 * 2**20),
+        compiler_params=pltpu.CompilerParams(vmem_limit_bytes=20 * 2**20),
     )(where, fill, w, panel)
 
 
@@ -316,10 +321,10 @@
     pair_slots(sizes, fill_ref, c // 2, slots)
     column[...] = jnp.zeros_like(column)
 
-    @pl.loop(0, sizes.pair_units // 4)
+    @pl.loop(0, sizes.column_units // 2)
     def _(unit):
         for p in range(2):
-            slot = slots[(side * (sizes.pair_units // 4) + unit) * 2 + p]
+            slot = slots[side * sizes.column_units + unit * 2 + p]
 
             @pl.when(slot >= 0)
             def _(slot=slot, p=p):
@@ -331,42 +336,51 @@
 
     w = halves(w_ref[...])
     solved = dot3(w, halves(column[...]), NT)
-    out_ref[0], out_ref[1] = halves(dot3(w, halves(solved), TN))
+    out_ref[...] = dot3(w, halves(solved), TN)
 
 
 def column_factor(sizes, where, fill, w, lists):
     n = w.shape[0]
     return pl.pallas_call(
         functools.partial(column_factor_kernel, sizes),
-        out_shape=jax.ShapeDtypeStruct((2, n, sizes.width), BF16),
+        out_shape=jax.ShapeDtypeStruct((n, sizes.width), F32),
         in_specs=[SMEM, SMEM, VMEM] + [VMEM] * 4,
         out_specs=VMEM,
-        scratch_shapes=[pltpu.VMEM((sizes.width, n), F32), pltpu.SMEM((sizes.pair_units,), jnp.int32)],
-        compiler_params=pltpu.CompilerParams(vmem_limit_bytes=32 * 2**20),
+        scratch_shapes=[pltpu.VMEM((sizes.width, n), F32), pltpu.SMEM((2 * sizes.column_units,), jnp.int32)],
+        compiler_params=pltpu.CompilerParams(vmem_limit_bytes=20 * 2**20),
     )(where, fill, w, *lists)
 
 
 def update_kernel(sizes, where_ref, slot_ref, column_ref, window_ref, *refs):
-    groups = sizes.cols // 2
-    lists, (out_ref, tiles, unit_data, out_sems) = refs[: 4 * groups], refs[4 * groups :]
+    groups, merge = sizes.groups, sizes.merge
+    lists, (out_ref, tiles, data, right, out_sems) = refs[: 4 * groups], refs[4 * groups :]
     c, r = where_ref[0], where_ref[1]
     side, core = c % 2, r % 2
-    per_group = 2 * sizes.per_piece
+    per_group = 2 * sizes.per_piece // merge
+    rows = merge * sizes.unit
     quarter = sizes.unit // 4
 
     def rows_of(t):
         group = lax.rem(c // 2 + t // per_group, groups)
-        return pl.ds(pl.multiple_of((group * per_group + t % per_group) * sizes.unit, sizes.unit), sizes.unit)
+        return pl.ds(pl.multiple_of((group * per_group + t % per_group) * rows, rows), rows)
 
     def tile_out(t, source):
         return pltpu.make_async_copy(source, out_ref.at[rows_of(t)], out_sems.at[t])
 
+    def slot_of(t, p, part):
+        return slot_ref[(t * merge + part) * 2 + p]
+
     def active(t):
-        return jnp.logical_or(slot_ref[2 * t] >= 0, slot_ref[2 * t + 1] >= 0)
-
-    @pl.loop(0, sizes.tiles)
+        return jnp.logical_or(slot_of(t, 0, 0) >= 0, slot_of(t, 1, 0) >= 0)
+
+    @pl.loop(0, per_group * groups)
     def _(t):
         pl.when(jnp.logical_not(active(t)))(tile_out(t, window_ref.at[rows_of(t)]).start)
+
+    for p in range(2):
+        high, low = halves(column_ref[p * sizes.block : (p + 1) * sizes.block, :])
+        for i, part in enumerate((high, low, high)):
+            right[p, i * sizes.block : (i + 1) * sizes.block, :] = part
 
     for group in range(groups):
 
@@ -376,39 +390,42 @@
             def _():
                 tiles[t] = window_ref[rows_of(t), :]
                 for p in range(2):
-                    slot = slot_ref[2 * t + p]
-
-                    @pl.when(slot >= 0)
-                    def _(p=p, slot=slot):
-                        for flip in range(4):
-                            from_side = jnp.bitwise_xor(side, flip // 2)
-                            from_core = jnp.bitwise_xor(core, flip % 2)
-                            at = pl.multiple_of((from_side * 2 + from_core) * quarter, quarter)
-                            unit_data[pl.ds(at, quarter), :] = lists[4 * group + flip][slot]
-                        at = pl.ds(p * sizes.block, sizes.block)
-                        right = (column_ref[0, at, :], column_ref[1, at, :])
-                        tiles[t] = tiles[t] - dot3(halves(unit_data[...]), right, NN)
+
+                    @pl.when(slot_of(t, p, 0) >= 0)
+                    def _(p=p):
+                        for part in range(merge):
+                            slot = slot_of(t, p, part)
+                            for flip in range(4):
+                                from_side = jnp.bitwise_xor(side, flip // 2)
+                                from_core = jnp.bitwise_xor(core, flip % 2)
+                                at = pl.multiple_of((part * 4 + from_side * 2 + from_core) * quarter, quarter)
+                                data[pl.ds(at, quarter), :] = lists[4 * group + flip][slot]
+                        high, low = halves(data[...])
+                        left = jnp.concatenate([high, high, low], axis=1)
+                        tiles[t] = tiles[t] - dot(left, right[p], NN)
 
                 tile_out(t, tiles.at[t]).start()
 
-    @pl.loop(0, sizes.tiles)
+    @pl.loop(0, per_group * groups)
     def _(t):
         tile_out(t, tiles.at[t]).wait()
 
 
 def update(sizes, where, slots, column, window, lists):
-    tiles = sizes.tiles
+    rows = sizes.merge * sizes.unit
+    tiles = sizes.slab // rows
     return pl.pallas_call(
         functools.partial(update_kernel, sizes),
-        out_shape=jax.ShapeDtypeStruct(window.shape, F32),
+        out_shape=pltpu.HBM(window.shape, F32),
         in_specs=[SMEM, SMEM, VMEM, VMEM] + [VMEM] * len(lists),
         out_specs=HBM,
         scratch_shapes=[
-            pltpu.VMEM((tiles, sizes.unit, sizes.width), F32),
-            pltpu.VMEM((sizes.unit, sizes.block), F32),
+            pltpu.VMEM((tiles, rows, sizes.width), F32),
+            pltpu.VMEM((rows, sizes.block), F32),
+            pltpu.VMEM((2, 3 * sizes.block, sizes.width), BF16),
             pltpu.SemaphoreType.DMA((tiles,)),
         ],
-        compiler_params=pltpu.CompilerParams(vmem_limit_bytes=48 * 2**20),
+        compiler_params=pltpu.CompilerParams(vmem_limit_bytes=36 * 2**20),
     )(where, slots, column, window, *lists)
 
 
@@ -452,8 +469,8 @@
     quarter = sizes.unit // 4
     split = min(4, pivot_block.shape[0] // 8)
     share = pivot_block.shape[0] // split
-    most, pair_most = 8 * sizes.per_piece, sizes.pair_units
-    cap, pair_cap = most * 5 // 12, pair_most * 5 // 8
+    most, column_most = 8 * sizes.per_piece, sizes.column_units
+    cap, column_cap = most * 5 // 12, column_most * 3 // 4
 
     units = panel_rows.reshape(sizes.per_piece, sizes.unit, -1)
     quarters = panel_rows.reshape(sizes.per_piece, 2, 2, quarter, -1)
@@ -461,41 +478,43 @@
     def at_core(which):
         return lax.dynamic_index_in_dim(quarters, which, 2, keepdims=False)
 
+    pivot = lax.dynamic_slice_in_dim(pivot_block, r % split * share, share, 0)[None]
+    pivot = join(c, 1, pivot, swap(pivot, "col", 1))
     from_core = swap(at_core(1 - core), "row", 1)
+    from_core, pivot = lax.optimization_barrier((from_core, pivot))
     both = jnp.stack([at_core(core), from_core])
     from_side = swap(lax.dynamic_index_in_dim(both, 1 - side, 2, keepdims=False), "col", 1)
-    pivot = lax.dynamic_slice_in_dim(pivot_block, r % split * share, share, 0)[None]
-    pivot = join(c, 1, pivot, swap(pivot, "col", 1))
-    pivot = join(c, 2, pivot, swap(pivot, "col", 2))
-
-    def run(cap, pair_cap, trailing, panel_rows, fill, units, from_core, from_side, pivot):
+    step = 2
+    while step < sizes.cols:
+        pivot = join(c, step, pivot, swap(pivot, "col", step))
+        step *= 2
+
+    def run(cap, column_cap, trailing, panel_rows, fill, units, from_core, from_side, pivot):
         own = pack(sizes, cap, where, fill, units, from_core, from_side)
         lists = {0: own}
         first = [s for s in range(1, sizes.groups) if s in sizes.needed]
         later = [s for s in range(1, sizes.groups) if s not in sizes.needed]
         lists |= {s: bring(sizes, own, s) for s in first}
         sides = {0: swap(own, "col", 1)}
-        step = 4
-        while step < sizes.cols:
-            pivot = join(c, step, pivot, swap(pivot, "col", step))
-            step *= 2
-        near = first[0]
-        pivot, sides[0], lists[near] = lax.optimization_barrier((pivot, sides[0], lists[near]))
         parts = [pivot] + ([swap(pivot, "row", 2)] if split == 4 else [])
         parts = [part for value in parts for part in (value, swap(value, "row", 1))]
+        near = first[0]
+        lists[near], sides[0], *parts = lax.optimization_barrier((lists[near], sides[0], *parts))
+        sides[near] = swap(lists[near], "col", 1)
         w = inverse_factor(where, parts)
-        held = lax.optimization_barrier((w, sides[0], *lists.values()))
-        w, sides[0] = held[:2]
-        lists = dict(zip(lists, held[2:]))
-
-        column = pack_column(sizes, cap, pair_cap, where, fill, [lists[s] for s in sizes.needed])
+        held = lax.optimization_barrier((w, sides[0], sides[near], *lists.values()))
+        w, sides[0], sides[near] = held[:3]
+        lists = dict(zip(lists, held[3:]))
+
+        column = pack_column(sizes, cap, column_cap, where, fill, [lists[s] for s in sizes.needed])
         lists |= {s: bring(sizes, lists[0], s) for s in later}
-        sides |= {s: swap(lists[s], "col", 1) for s in first}
+        sides |= {s: swap(lists[s], "col", 1) for s in first[1:]}
         step = sizes.rows // 2
         while step > 1:
             column = spread_column(sizes, column, step)
             step //= 2
-        across = swap(column, "col", 1)
+        across = swap(lax.dynamic_index_in_dim(column, 1 - side, 0, keepdims=False), "col", 1)
+        column = lax.dynamic_index_in_dim(column, side, 0, keepdims=False)
         columns = [column, swap(column, "row", 1), across, swap(across, "row", 1)]
         panel_factor, slots = own_factor(sizes, where, fill, w, panel_rows)
         for s in later:
@@ -510,9 +529,9 @@
 
     operands = (trailing, panel_rows, fill, units, from_core, from_side, pivot)
     return lax.cond(
-        fits(sizes, cap, pair_cap, fill)[0] != 0,
-        functools.partial(run, cap, pair_cap),
-        functools.partial(run, most, pair_most),
+        fits(sizes, cap, column_cap, fill)[0] != 0,
+        functools.partial(run, cap, column_cap),
+        functools.partial(run, most, column_most),
         *operands,
     )
 

time: 112 us -> 83.6 us (0.75)
  the two profiles are of different devices: /device:TPU:0 before, /device:TPU:31 now
where the time goes in v5:
time: 83.6 us; the launch traced here: 82.9 us
  waiting for transfers between devices  35.2 us (42%)
  Pallas kernels  21.6 us (26%)
  starting transfers between devices  20.3 us (24%)
  local copies, waits for them, and re-layouts  2.17 us (3%)
  between operations  1.58 us (2%)
  other arithmetic  1.26 us (2%)
    ppermute x23, starting transfers between devices, swap(): return lax.ppermute(value, axis, [(i, i ^ step) for i in range(size)])  17.6 us
    ppermute x23, waiting for transfers between devices, swap(): return lax.ppermute(value, axis, [(i, i ^ step) for i in range(size)])  16.3 us
    ppermute x3, waiting for transfers between devices, bring(): return lax.ppermute(value, 'col', pairs)  10.4 us
    ppermute x1, waiting for transfers between devices, spread_column(): other = lax.ppermute(value, ('col', 'row'), pairs)  8.57 us
    pallas_call x1, Pallas kernels, inverse_factor(): pl.pallas_call(inverse_factor_kernel, out_shape=jax.ShapeDtypeStruct((n,...  6.89 us
    pallas_call x1, Pallas kernels, own_factor(): pl.pallas_call(functools.partial(own_factor_kernel, sizes), out_shape=(pl...  3.43 us
    pallas_call x1, Pallas kernels, update(): pl.pallas_call(functools.partial(update_kernel, sizes), out_shape=pltpu.H...  3.35 us
    pallas_call x1, Pallas kernels, column_factor(): pl.pallas_call(functools.partial(column_factor_kernel, sizes), out_shape=...  3.17 us
  transfers between devices with their start and end apart: 27, of which 9 were waited for; matrix products, arithmetic and copies ran while one was open for 3% of the time, Pallas kernels for 20%

profile of v5, /device:TPU:31, one launch (start us, length us, event | category | flops | bytes accessed | tf_op | source)
XLA Modules:
  0.0 82.9 jit_solution(3293648878076737836)
XLA Ops:
  0.6 0.0 copy-start
  0.7 1.2 %dynamic-slice_bitcast_fusion.4 = (f32[1,3,2,32,512]{4,3,2,1,0:T(8,128)S(1)}, f32[3,2,32,512]{3,2,1,0:T(8,128)S(1)}) fusion(f32[3,2,2,32,512]{4,3,2,1,0:T(8,128)} %bitcast.27, s32[]{:T(128)S(6)} %select_n.102, s32[]{:T(128)S(6)} %select_n.97), kind=kLoop, calls=%fused_computation.12 | loop fusion | bytes 1572872 | tf_op jit(solution)/shard_map/stack | solution.py:485
  1.9 0.7 collective-permute-start.44
  2.7 0.3 collective-permute-start.45
  2.9 2.5 %collective-permute-done.45 = f32[1,16,512]{2,1,0:T(8,128)S(1)} collective-permute-done((f32[1,16,512]{2,1,0:T(8,128)S(1)}, f32[1,16,512]{2,1,0:T(8,128)S(1)}, u32[]{:S(2)}, u32[]{:S(2)}) %collective-permute-start.45) | collective-permute-done | bytes 32800 | tf_op jit(solution)/shard_map/ppermute | solution.py:434
  5.4 0.0 collective-permute-done.44
  5.4 0.2 collective-permute-start.47
  5.7 0.3 collective-permute-start.46
  6.0 2.6 %collective-permute-done.47 = f32[2,16,512]{2,1,0:T(8,128)S(1)} collective-permute-done((f32[2,16,512]{2,1,0:T(8,128)S(1)}, f32[2,16,512]{2,1,0:T(8,128)S(1)}, u32[]{:S(2)}, u32[]{:S(2)}) %collective-permute-start.47) | collective-permute-done | bytes 65568 | tf_op jit(solution)/shard_map/ppermute | solution.py:434
  8.6 0.1 collective-permute-start.48
  8.8 0.8 copy.13
  9.5 0.1 reshape.18.fill_ref
  9.6 1.2 %shard_map.63 = s32[1]{0:T(128)} custom-call(s32[96]{0:T(128)S(1)} %reshape.18.fill_ref), custom_call_target="tpu_custom_call" | custom-call | tf_op jit(solution)/shard_map/pallas_call | solution.py:181
  11.5 0.1 pad_add_fusion
  11.6 3.1 %collective-permute-done.48 = f32[4,16,512]{2,1,0:T(8,128)S(1)} collective-permute-done((f32[4,16,512]{2,1,0:T(8,128)S(1)}, f32[4,16,512]{2,1,0:T(8,128)S(1)}, u32[]{:S(2)}, u32[]{:S(2)}) %collective-permute-start.48) | collective-permute-done | bytes 131104 | tf_op jit(solution)/shard_map/ppermute | solution.py:434
  14.7 0.1 pad_maximum_fusion.1
  14.8 0.0 collective-permute-done.46
  14.8 67.9 %conditional.1 = (f32[384,512]{1,0:T(8,128)}, f32[3072,512]{1,0:T(8,128)}) conditional(s32[]{:T(128)} %bitcast.6, (s32[2]{0:T(128)S(1)}, s32[96]{0:T(128)S(1)}, f32[384,512]{1,0:T(8,128)}, f32[3,2,32,512]{3,2,1,0:T(8,128)S(1)}, f32[2,3,32,512]{3,2,1,0:T(8,128)S(1)}, /*index=5*/s32[]{:T(128)}, f32[384,512]{1,0:T(8,128)}, s32[]{:T(128)}, ...), branch_computations={%region_0.1_spmd, %region_1.2_spmd} | conditional | flops 196649 | bytes 71566760 | solution.py:531
  15.1 0.3 collective-permute-start.25
  15.4 1.5 %branch_1_fun.6.refs_0_ = f32[10,32,256]{2,1,0:T(8,128)S(1)} custom-call(s32[2]{0:T(128)S(1)} %get-tuple-element.60.where_ref, s32[96]{0:T(128)S(1)} %get-tuple-element.61.fill_ref, f32[3,128,512]{2,1,0:T(8,128)} %bitcast.29, f32[3,2,32,512]{3,2,1,0:T(8,128)S(1)} %get-tuple-element.63.core_ref, f32[2,3,32,512]{3,2,1,0:T(8,128)S(1)} %get-tuple-element.64.side_ref), custom_call_target="tpu_custom_call" | custom-call | tf_op jit(solution)/shard_map/cond/branch_1_fun/pallas_call | solution.py:216
  16.9 0.3 collective-permute-start.23
  17.2 1.1 %collective-permute-start.22 = (f32[10,32,256]{2,1,0:T(8,128)S(1)}, f32[10,32,256]{2,1,0:T(8,128)S(1)}, u32[]{:S(2)}, u32[]{:S(2)}) collective-permute-start(f32[10,32,256]{2,1,0:T(8,128)S(1)} %branch_1_fun.6.refs_0_), channel_id=1, source_target_pairs={{0,24},{4,28},{8,0},{12,4},{16,8},{20,12},{24,16},{28,20},{1,25},{... | collective-permute-start | bytes 983048 | tf_op jit(solution)/shard_map/cond/branch_1_fun/ppermute | solution.py:448
  18.3 3.3 %collective-permute-start.24 = (f32[8,16,512]{2,1,0:T(8,128)S(1)}, f32[8,16,512]{2,1,0:T(8,128)S(1)}, u32[]{:S(2)}, u32[]{:S(2)}) collective-permute-start(f32[8,16,512]{2,1,0:T(8,128)S(1)} %broadcast_select_fusion.3.refs_0_), channel_id=1, source_target_pairs={{0,1},{1,0},{2,3},{3,2},{4,5},{5,4},{6,7},{7,6},{8,9},{9,8},{10,11... | collective-permute-start | bytes 786440 | tf_op jit(solution)/shard_map/cond/branch_1_fun/ppermute | solution.py:434
  21.6 0.0 collective-permute-done.25.refs_2_
  21.6 3.5 %collective-permute-start.26 = (f32[8,16,512]{2,1,0:T(8,128)S(1)}, f32[8,16,512]{2,1,0:T(8,128)S(1)}, u32[]{:S(2)}, u32[]{:S(2)}) collective-permute-start(f32[8,16,512]{2,1,0:T(8,128)S(1)} %collective-permute-done.25.refs_2_), channel_id=1, source_target_pairs={{0,1},{1,0},{2,3},{3,2},{4,5},{5,4},{6,7},{7,6},{8,9},{9,8},{10,11... | collective-permute-start | bytes 786440 | tf_op jit(solution)/shard_map/cond/branch_1_fun/ppermute | solution.py:434
  25.1 0.0 collective-permute-start.28
  25.1 0.0 collective-permute-done.24.refs_1_
  25.1 0.0 collective-permute-done.23.refs_2_
  25.1 0.0 collective-permute-done.22.refs_1_.refs_4_
  25.1 1.1 %collective-permute-done.26.refs_3_ = f32[8,16,512]{2,1,0:T(8,128)S(1)} collective-permute-done((f32[8,16,512]{2,1,0:T(8,128)S(1)}, f32[8,16,512]{2,1,0:T(8,128)S(1)}, u32[]{:S(2)}, u32[]{:S(2)}) %collective-permute-start.26) | collective-permute-done | bytes 262176 | tf_op jit(solution)/shard_map/cond/branch_1_fun/ppermute | solution.py:434
  26.3 0.3 collective-permute-start.27
  26.5 6.9 %branch_1_fun.7.w_ref = f32[512,512]{1,0:T(8,128)S(1)} custom-call(s32[2]{0:T(128)S(1)} %get-tuple-element.60.where_ref, f32[8,16,512]{2,1,0:T(8,128)S(1)} %broadcast_select_fusion.3.refs_0_, f32[8,16,512]{2,1,0:T(8,128)S(1)} %collective-permute-done.24.refs_1_, f32[8,16,512]{2,1,0:T(8,128)S(1)} %collective-permute-done.25.refs_2_, ...), custom_call_target="tpu_custom_call" | custom-call | tf_op jit(solution)/shard_map/cond/branch_1_fun/pallas_call | solution.py:105
  33.4 10.4 %collective-permute-done.28.refs_2_.refs_8_ = f32[10,32,256]{2,1,0:T(8,128)S(1)} collective-permute-done((f32[10,32,256]{2,1,0:T(8,128)S(1)}, f32[10,32,256]{2,1,0:T(8,128)S(1)}, u32[]{:S(2)}, u32[]{:S(2)}) %collective-permute-start.28) | collective-permute-done | bytes 327712 | tf_op jit(solution)/shard_map/cond/branch_1_fun/ppermute | solution.py:448
  43.8 0.0 collective-permute-done.27.refs_6_
  43.8 2.0 %branch_1_fun.9 = f32[2,6,32,256]{3,2,1,0:T(8,128)S(1)} custom-call(s32[2]{0:T(128)S(1)} %get-tuple-element.60.where_ref, s32[96]{0:T(128)S(1)} %get-tuple-element.61.fill_ref, f32[10,32,256]{2,1,0:T(8,128)S(1)} %branch_1_fun.6.refs_0_, f32[10,32,256]{2,1,0:T(8,128)S(1)} %collective-permute-done.22.refs_1_.refs_4_, ...), custom_call_target="tpu_custom_call" | custom-call | tf_op jit(solution)/shard_map/cond/branch_1_fun/pallas_call | solution.py:262
  45.9 1.3 %collective-permute-start.29 = (f32[2,6,32,256]{3,2,1,0:T(8,128)S(1)}, f32[2,6,32,256]{3,2,1,0:T(8,128)}, u32[]{:S(2)}, u32[]{:S(2)}) collective-permute-start(f32[2,6,32,256]{3,2,1,0:T(8,128)S(1)} %branch_1_fun.9), channel_id=1, source_target_pairs={{0,2},{1,3},{4,6},{5,7},{8,10},{9,11},{12,14},{13,15},{16,18},{17,... | collective-permute-start | bytes 1179656 | tf_op jit(solution)/shard_map/cond/branch_1_fun/ppermute | solution.py:459
  47.2 0.0 copy-start.5
  47.2 0.3 collective-permute-start.40
  47.6 1.3 %collective-permute-start.38 = (f32[10,32,256]{2,1,0:T(8,128)S(1)}, f32[10,32,256]{2,1,0:T(8,128)S(1)}, u32[]{:S(2)}, u32[]{:S(2)}) collective-permute-start(f32[10,32,256]{2,1,0:T(8,128)S(1)} %collective-permute-done.28.refs_2_.refs_8_), channel_id=1, source_target_pairs={{0,4},{4,0},{8,12},{12,8},{16,20},{20,16},{24,28},{28,24},{1,5},{5... | collective-permute-start | bytes 983048 | tf_op jit(solution)/shard_map/cond/branch_1_fun/ppermute | solution.py:434
  48.9 0.7 collective-permute-start.34
  49.6 8.6 %collective-permute-done.29 = f32[2,6,32,256]{3,2,1,0:T(8,128)} collective-permute-done((f32[2,6,32,256]{3,2,1,0:T(8,128)S(1)}, f32[2,6,32,256]{3,2,1,0:T(8,128)}, u32[]{:S(2)}, u32[]{:S(2)}) %collective-permute-start.29) | collective-permute-done | bytes 393248 | tf_op jit(solution)/shard_map/cond/branch_1_fun/ppermute | solution.py:459
  58.1 1.0 %broadcast_select_fusion.2 = f32[2,6,32,256]{3,2,1,0:T(8,128)S(1)} fusion(f32[2,6,32,256]{3,2,1,0:T(8,128)} %collective-permute-done.29, f32[2,6,32,256]{3,2,1,0:T(8,128)S(1)} %branch_1_fun.9, pred[]{:T(512)S(6)} %ne.51), kind=kLoop, calls=%fused_computation.6 | loop fusion | flops 98304 | bytes 1179649 | tf_op jit(solution)/shard_map/cond/branch_1_fun/jit(_where)/select_n | solution.py:460
  59.2 1.3 %collective-permute-start.31 = (f32[6,32,256]{2,1,0:T(8,128)S(1)}, f32[6,32,256]{2,1,0:T(8,128)S(1)}, u32[]{:S(2)}, u32[]{:S(2)}) collective-permute-start(f32[6,32,256]{2,1,0:T(8,128)S(1)} %get-tuple-element.115), channel_id=1, source_target_pairs={{0,4},{4,0},{8,12},{12,8},{16,20},{20,16},{24,28},{28,24},{1,5},{5... | collective-permute-start | bytes 589832 | tf_op jit(solution)/shard_map/cond/branch_1_fun/ppermute | solution.py:434
  60.5 1.6 %collective-permute-start.35 = (f32[10,32,256]{2,1,0:T(8,128)S(1)}, f32[10,32,256]{2,1,0:T(8,128)S(1)}, u32[]{:S(2)}, u32[]{:S(2)}) collective-permute-start(f32[10,32,256]{2,1,0:T(8,128)S(1)} %collective-permute-done.22.refs_1_.refs_4_), channel_id=1, source_target_pairs={{0,1},{1,0},{2,3},{3,2},{4,5},{5,4},{6,7},{7,6},{8,9},{9,8},{10,11... | collective-permute-start | bytes 983048 | tf_op jit(solution)/shard_map/cond/branch_1_fun/ppermute | solution.py:434
  62.1 3.4 %branch_1_fun.8 = (f32[384,512]{1,0:T(8,128)}, s32[48]{0:T(128)S(1)}) custom-call(s32[2]{0:T(128)S(1)} %get-tuple-element.60.where_ref, s32[96]{0:T(128)S(1)} %get-tuple-element.61.fill_ref, f32[512,512]{1,0:T(8,128)S(1)} %branch_1_fun.7.w_ref, f32[384,512]{1,0:T(8,128)} %get-tuple-element.73.panel_ref), custom_call_target="tpu_custom_call" | custom-call | tf_op jit(solution)/shard_map/cond/branch_1_fun/pallas_call | solution.py:303
  65.5 0.1 collective-permute-start.36
  65.6 0.0 collective-permute-done.38.refs_10_
  65.6 0.3 collective-permute-start.42
  65.9 0.7 collective-permute-start.30
  66.6 0.0 collective-permute-done.31.refs_2_
  66.7 0.1 collective-permute-start.32
  66.7 0.0 collective-permute-done.35.refs_5_
  66.7 0.4 collective-permute-start.33
  67.2 0.1 collective-permute-done.36.refs_7_
  67.2 0.1 collective-permute-start.37
  67.4 0.4 collective-permute-done.30.refs_1_
  67.7 0.4 collective-permute-start.41
  68.1 6.4 %collective-permute-done.42.refs_14_ = f32[10,32,256]{2,1,0:T(8,128)S(1)} collective-permute-done((f32[10,32,256]{2,1,0:T(8,128)S(1)}, f32[10,32,256]{2,1,0:T(8,128)S(1)}, u32[]{:S(2)}, u32[]{:S(2)}) %collective-permute-start.42) | collective-permute-done | bytes 327712 | tf_op jit(solution)/shard_map/cond/branch_1_fun/ppermute | solution.py:434
  74.5 1.3 %collective-permute-start.39 = (f32[10,32,256]{2,1,0:T(8,128)S(1)}, f32[10,32,256]{2,1,0:T(8,128)S(1)}, u32[]{:S(2)}, u32[]{:S(2)}) collective-permute-start(f32[10,32,256]{2,1,0:T(8,128)S(1)} %collective-permute-done.38.refs_10_), channel_id=1, source_target_pairs={{0,1},{1,0},{2,3},{3,2},{4,5},{5,4},{6,7},{7,6},{8,9},{9,8},{10,11... | collective-permute-start | bytes 983048 | tf_op jit(solution)/shard_map/cond/branch_1_fun/ppermute | solution.py:434
  75.8 0.0 collective-permute-done.32.refs_3_
  75.8 0.0 collective-permute-start.43
  75.8 3.2 %branch_1_fun.10.column_ref = f32[512,512]{1,0:T(8,128)S(1)} custom-call(s32[2]{0:T(128)S(1)} %get-tuple-element.60.where_ref, s32[96]{0:T(128)S(1)} %get-tuple-element.61.fill_ref, f32[512,512]{1,0:T(8,128)S(1)} %branch_1_fun.7.w_ref, f32[6,32,256]{2,1,0:T(8,128)S(1)} %get-tuple-element.116.refs_0_, f32[6,32,256]{2,1,0:T(8,128)S(1)} %collective-permute-done.30.refs_1_, ...), custom_call_target="tpu_custom_call" | custom-call | tf_op jit(solution)/shard_map/cond/branch_1_fun/pallas_call | solution.py:344
  79.0 0.0 collective-permute-done.39.refs_11_
  79.0 3.4 %branch_1_fun.11 = f32[3072,512]{1,0:T(8,128)} custom-call(s32[2]{0:T(128)S(1)} %get-tuple-element.60.where_ref, s32[48]{0:T(128)S(1)} %get-tuple-element.74.slot_ref, f32[512,512]{1,0:T(8,128)S(1)} %branch_1_fun.10.column_ref, f32[3072,512]{1,0:T(8,128)S(1)} %copy-done.5, f32[10,32,256]{2,1,0:T(8,128)S(1)} %branch_1_fun.6.refs_0_, ...), custom_call_target="tpu_custom_call" | custom-call | tf_op jit(solution)/shard_map/cond/branch_1_fun/pallas_call | solution.py:417
  (14 shorter events, 0.1 us)
Async XLA Ops:
  0.6 2.0 %copy-start = (f32[64,512]{1,0:T(8,128)S(1)}, f32[64,512]{1,0:T(8,128)}, u32[]{:S(2)}) copy-start(f32[64,512]{1,0:T(8,128)} %param.8) | copy-start | bytes 393220
  1.9 3.5 %collective-permute-start.44 = (f32[3,2,32,512]{3,2,1,0:T(8,128)S(1)}, f32[3,2,32,512]{3,2,1,0:T(8,128)S(1)}, u32[]{:S(2)}, u32[]{:S(2)}) collective-permute-start(f32[3,2,32,512]{3,2,1,0:T(8,128)S(1)} %get-tuple-element.118), channel_id=1, source_target_pairs={{0,1},{1,0},{2,3},{3,2},{4,5},{5,4},{6,7},{7,6},{8,9},{9,8},{10,11... | collective-permute-start | bytes 1179656 | tf_op jit(solution)/shard_map/ppermute | solution.py:434
  2.7 2.8 %collective-permute-start.45 = (f32[1,16,512]{2,1,0:T(8,128)S(1)}, f32[1,16,512]{2,1,0:T(8,128)S(1)}, u32[]{:S(2)}, u32[]{:S(2)}) collective-permute-start(f32[1,16,512]{2,1,0:T(8,128)S(1)} %dynamic-slice_bitcast_fusion.6), channel_id=1, source_target_pairs={{0,4},{4,0},{8,12},{12,8},{16,20},{20,16},{24,28},{28,24},{1,5},{5... | collective-permute-start | bytes 98312 | tf_op jit(solution)/shard_map/ppermute | solution.py:434
  5.4 3.2 %collective-permute-start.47 = (f32[2,16,512]{2,1,0:T(8,128)S(1)}, f32[2,16,512]{2,1,0:T(8,128)S(1)}, u32[]{:S(2)}, u32[]{:S(2)}) collective-permute-start(f32[2,16,512]{2,1,0:T(8,128)S(1)} %maximum_select_fusion.1), channel_id=1, source_target_pairs={{0,8},{4,12},{8,0},{12,4},{16,24},{20,28},{24,16},{28,20},{1,9},{5... | collective-permute-start | bytes 196616 | tf_op jit(solution)/shard_map/ppermute | solution.py:434
  5.7 9.1 %collective-permute-start.46 = (f32[2,3,32,512]{3,2,1,0:T(8,128)S(1)}, f32[2,3,32,512]{3,2,1,0:T(8,128)S(1)}, u32[]{:S(2)}, u32[]{:S(2)}) collective-permute-start(f32[2,3,32,512]{3,2,1,0:T(8,128)S(1)} %fusion.1), channel_id=1, source_target_pairs={{0,4},{4,0},{8,12},{12,8},{16,20},{20,16},{24,28},{28,24},{1,5},{5... | collective-permute-start | bytes 1179656 | tf_op jit(solution)/shard_map/ppermute | solution.py:434
  8.6 6.1 %collective-permute-start.48 = (f32[4,16,512]{2,1,0:T(8,128)S(1)}, f32[4,16,512]{2,1,0:T(8,128)S(1)}, u32[]{:S(2)}, u32[]{:S(2)}) collective-permute-start(f32[4,16,512]{2,1,0:T(8,128)S(1)} %maximum_select_fusion), channel_id=1, source_target_pairs={{0,16},{4,20},{8,24},{12,28},{16,0},{20,4},{24,8},{28,12},{1,17},{... | collective-permute-start | bytes 393224 | tf_op jit(solution)/shard_map/ppermute | solution.py:434
  15.1 6.5 %collective-permute-start.25 = (f32[8,16,512]{2,1,0:T(8,128)S(1)}, f32[8,16,512]{2,1,0:T(8,128)S(1)}, u32[]{:S(2)}, u32[]{:S(2)}) collective-permute-start(f32[8,16,512]{2,1,0:T(8,128)S(1)} %broadcast_select_fusion.3.refs_0_), channel_id=1, source_target_pairs={{0,2},{1,3},{2,0},{3,1},{4,6},{5,7},{6,4},{7,5},{8,10},{9,11},{10,... | collective-permute-start | bytes 786440 | tf_op jit(solution)/shard_map/cond/branch_1_fun/ppermute | solution.py:434
  16.9 8.2 %collective-permute-start.23 = (f32[10,32,256]{2,1,0:T(8,128)S(1)}, f32[10,32,256]{2,1,0:T(8,128)S(1)}, u32[]{:S(2)}, u32[]{:S(2)}) collective-permute-start(f32[10,32,256]{2,1,0:T(8,128)S(1)} %branch_1_fun.6.refs_0_), channel_id=1, source_target_pairs={{0,4},{4,0},{8,12},{12,8},{16,20},{20,16},{24,28},{28,24},{1,5},{5... | collective-permute-start | bytes 983048 | tf_op jit(solution)/shard_map/cond/branch_1_fun/ppermute | solution.py:434
  17.2 7.9 %collective-permute-start.22 = (f32[10,32,256]{2,1,0:T(8,128)S(1)}, f32[10,32,256]{2,1,0:T(8,128)S(1)}, u32[]{:S(2)}, u32[]{:S(2)}) collective-permute-start(f32[10,32,256]{2,1,0:T(8,128)S(1)} %branch_1_fun.6.refs_0_), channel_id=1, source_target_pairs={{0,24},{4,28},{8,0},{12,4},{16,8},{20,12},{24,16},{28,20},{1,25},{... | collective-permute-start | bytes 983048 | tf_op jit(solution)/shard_map/cond/branch_1_fun/ppermute | solution.py:448
  18.3 6.8 %collective-permute-start.24 = (f32[8,16,512]{2,1,0:T(8,128)S(1)}, f32[8,16,512]{2,1,0:T(8,128)S(1)}, u32[]{:S(2)}, u32[]{:S(2)}) collective-permute-start(f32[8,16,512]{2,1,0:T(8,128)S(1)} %broadcast_select_fusion.3.refs_0_), channel_id=1, source_target_pairs={{0,1},{1,0},{2,3},{3,2},{4,5},{5,4},{6,7},{7,6},{8,9},{9,8},{10,11... | collective-permute-start | bytes 786440 | tf_op jit(solution)/shard_map/cond/branch_1_fun/ppermute | solution.py:434
  21.6 4.7 %collective-permute-start.26 = (f32[8,16,512]{2,1,0:T(8,128)S(1)}, f32[8,16,512]{2,1,0:T(8,128)S(1)}, u32[]{:S(2)}, u32[]{:S(2)}) collective-permute-start(f32[8,16,512]{2,1,0:T(8,128)S(1)} %collective-permute-done.25.refs_2_), channel_id=1, source_target_pairs={{0,1},{1,0},{2,3},{3,2},{4,5},{5,4},{6,7},{7,6},{8,9},{9,8},{10,11... | collective-permute-start | bytes 786440 | tf_op jit(solution)/shard_map/cond/branch_1_fun/ppermute | solution.py:434
  25.1 18.7 %collective-permute-start.28 = (f32[10,32,256]{2,1,0:T(8,128)S(1)}, f32[10,32,256]{2,1,0:T(8,128)S(1)}, u32[]{:S(2)}, u32[]{:S(2)}) collective-permute-start(f32[10,32,256]{2,1,0:T(8,128)S(1)} %branch_1_fun.6.refs_0_), channel_id=1, source_target_pairs={{0,16},{4,20},{8,24},{12,28},{16,0},{20,4},{24,8},{28,12},{1,17},{... | collective-permute-start | bytes 983048 | tf_op jit(solution)/shard_map/cond/branch_1_fun/ppermute | solution.py:448
  26.3 17.6 %collective-permute-start.27 = (f32[10,32,256]{2,1,0:T(8,128)S(1)}, f32[10,32,256]{2,1,0:T(8,128)S(1)}, u32[]{:S(2)}, u32[]{:S(2)}) collective-permute-start(f32[10,32,256]{2,1,0:T(8,128)S(1)} %collective-permute-done.22.refs_1_.refs_4_), channel_id=1, source_target_pairs={{0,4},{4,0},{8,12},{12,8},{16,20},{20,16},{24,28},{28,24},{1,5},{5... | collective-permute-start | bytes 983048 | tf_op jit(solution)/shard_map/cond/branch_1_fun/ppermute | solution.py:434
  45.9 12.3 %collective-permute-start.29 = (f32[2,6,32,256]{3,2,1,0:T(8,128)S(1)}, f32[2,6,32,256]{3,2,1,0:T(8,128)}, u32[]{:S(2)}, u32[]{:S(2)}) collective-permute-start(f32[2,6,32,256]{3,2,1,0:T(8,128)S(1)} %branch_1_fun.9), channel_id=1, source_target_pairs={{0,2},{1,3},{4,6},{5,7},{8,10},{9,11},{12,14},{13,15},{16,18},{17,... | collective-permute-start | bytes 1179656 | tf_op jit(solution)/shard_map/cond/branch_1_fun/ppermute | solution.py:459
  47.2 31.8 %copy-start.5 = (f32[3072,512]{1,0:T(8,128)S(1)}, f32[3072,512]{1,0:T(8,128)}, u32[]{:S(2)}) copy-start(f32[3072,512]{1,0:T(8,128)} %get-tuple-element.104.window_ref) | copy-start | bytes 18874372 | tf_op jit(solution)/shard_map/cond
  47.2 18.3 %collective-permute-start.40 = (f32[10,32,256]{2,1,0:T(8,128)S(1)}, f32[10,32,256]{2,1,0:T(8,128)S(1)}, u32[]{:S(2)}, u32[]{:S(2)}) collective-permute-start(f32[10,32,256]{2,1,0:T(8,128)S(1)} %branch_1_fun.6.refs_0_), channel_id=1, source_target_pairs={{0,8},{4,12},{8,16},{12,20},{16,24},{20,28},{24,0},{28,4},{1,9},{5... | collective-permute-start | bytes 983048 | tf_op jit(solution)/shard_map/cond/branch_1_fun/ppermute | solution.py:448
  47.6 18.0 %collective-permute-start.38 = (f32[10,32,256]{2,1,0:T(8,128)S(1)}, f32[10,32,256]{2,1,0:T(8,128)S(1)}, u32[]{:S(2)}, u32[]{:S(2)}) collective-permute-start(f32[10,32,256]{2,1,0:T(8,128)S(1)} %collective-permute-done.28.refs_2_.refs_8_), channel_id=1, source_target_pairs={{0,4},{4,0},{8,12},{12,8},{16,20},{20,16},{24,28},{28,24},{1,5},{5... | collective-permute-start | bytes 983048 | tf_op jit(solution)/shard_map/cond/branch_1_fun/ppermute | solution.py:434
  48.9 17.1 %collective-permute-start.34 = (f32[10,32,256]{2,1,0:T(8,128)S(1)}, f32[10,32,256]{2,1,0:T(8,128)S(1)}, u32[]{:S(2)}, u32[]{:S(2)}) collective-permute-start(f32[10,32,256]{2,1,0:T(8,128)S(1)} %collective-permute-done.23.refs_2_), channel_id=1, source_target_pairs={{0,1},{1,0},{2,3},{3,2},{4,5},{5,4},{6,7},{7,6},{8,9},{9,8},{10,11... | collective-permute-start | bytes 983048 | tf_op jit(solution)/shard_map/cond/branch_1_fun/ppermute | solution.py:434
  59.2 7.4 %collective-permute-start.31 = (f32[6,32,256]{2,1,0:T(8,128)S(1)}, f32[6,32,256]{2,1,0:T(8,128)S(1)}, u32[]{:S(2)}, u32[]{:S(2)}) collective-permute-start(f32[6,32,256]{2,1,0:T(8,128)S(1)} %get-tuple-element.115), channel_id=1, source_target_pairs={{0,4},{4,0},{8,12},{12,8},{16,20},{20,16},{24,28},{28,24},{1,5},{5... | collective-permute-start | bytes 589832 | tf_op jit(solution)/shard_map/cond/branch_1_fun/ppermute | solution.py:434
  60.5 6.2 %collective-permute-start.35 = (f32[10,32,256]{2,1,0:T(8,128)S(1)}, f32[10,32,256]{2,1,0:T(8,128)S(1)}, u32[]{:S(2)}, u32[]{:S(2)}) collective-permute-start(f32[10,32,256]{2,1,0:T(8,128)S(1)} %collective-permute-done.22.refs_1_.refs_4_), channel_id=1, source_target_pairs={{0,1},{1,0},{2,3},{3,2},{4,5},{5,4},{6,7},{7,6},{8,9},{9,8},{10,11... | collective-permute-start | bytes 983048 | tf_op jit(solution)/shard_map/cond/branch_1_fun/ppermute | solution.py:434
  65.5 1.7 %collective-permute-start.36 = (f32[10,32,256]{2,1,0:T(8,128)S(1)}, f32[10,32,256]{2,1,0:T(8,128)S(1)}, u32[]{:S(2)}, u32[]{:S(2)}) collective-permute-start(f32[10,32,256]{2,1,0:T(8,128)S(1)} %collective-permute-done.27.refs_6_), channel_id=1, source_target_pairs={{0,1},{1,0},{2,3},{3,2},{4,5},{5,4},{6,7},{7,6},{8,9},{9,8},{10,11... | collective-permute-start | bytes 983048 | tf_op jit(solution)/shard_map/cond/branch_1_fun/ppermute | solution.py:434
  65.6 8.9 %collective-permute-start.42 = (f32[10,32,256]{2,1,0:T(8,128)S(1)}, f32[10,32,256]{2,1,0:T(8,128)S(1)}, u32[]{:S(2)}, u32[]{:S(2)}) collective-permute-start(f32[10,32,256]{2,1,0:T(8,128)S(1)} %collective-permute-done.40.refs_12_), channel_id=1, source_target_pairs={{0,4},{4,0},{8,12},{12,8},{16,20},{20,16},{24,28},{28,24},{1,5},{5... | collective-permute-start | bytes 983048 | tf_op jit(solution)/shard_map/cond/branch_1_fun/ppermute | solution.py:434
  65.9 1.8 %collective-permute-start.30 = (f32[6,32,256]{2,1,0:T(8,128)S(1)}, f32[6,32,256]{2,1,0:T(8,128)S(1)}, u32[]{:S(2)}, u32[]{:S(2)}) collective-permute-start(f32[6,32,256]{2,1,0:T(8,128)S(1)} %get-tuple-element.116.refs_0_), channel_id=1, source_target_pairs={{0,1},{1,0},{2,3},{3,2},{4,5},{5,4},{6,7},{7,6},{8,9},{9,8},{10,11... | collective-permute-start | bytes 589832 | tf_op jit(solution)/shard_map/cond/branch_1_fun/ppermute | solution.py:434
  66.7 9.2 %collective-permute-start.32 = (f32[6,32,256]{2,1,0:T(8,128)S(1)}, f32[6,32,256]{2,1,0:T(8,128)S(1)}, u32[]{:S(2)}, u32[]{:S(2)}) collective-permute-start(f32[6,32,256]{2,1,0:T(8,128)S(1)} %collective-permute-done.31.refs_2_), channel_id=1, source_target_pairs={{0,1},{1,0},{2,3},{3,2},{4,5},{5,4},{6,7},{7,6},{8,9},{9,8},{10,11... | collective-permute-start | bytes 589832 | tf_op jit(solution)/shard_map/cond/branch_1_fun/ppermute | solution.py:434
  66.7 12.3 %collective-permute-start.33 = (f32[10,32,256]{2,1,0:T(8,128)S(1)}, f32[10,32,256]{2,1,0:T(8,128)S(1)}, u32[]{:S(2)}, u32[]{:S(2)}) collective-permute-start(f32[10,32,256]{2,1,0:T(8,128)S(1)} %branch_1_fun.6.refs_0_), channel_id=1, source_target_pairs={{0,1},{1,0},{2,3},{3,2},{4,5},{5,4},{6,7},{7,6},{8,9},{9,8},{10,11... | collective-permute-start | bytes 983048 | tf_op jit(solution)/shard_map/cond/branch_1_fun/ppermute | solution.py:434
  67.2 11.8 %collective-permute-start.37 = (f32[10,32,256]{2,1,0:T(8,128)S(1)}, f32[10,32,256]{2,1,0:T(8,128)S(1)}, u32[]{:S(2)}, u32[]{:S(2)}) collective-permute-start(f32[10,32,256]{2,1,0:T(8,128)S(1)} %collective-permute-done.28.refs_2_.refs_8_), channel_id=1, source_target_pairs={{0,1},{1,0},{2,3},{3,2},{4,5},{5,4},{6,7},{7,6},{8,9},{9,8},{10,11... | collective-permute-start | bytes 983048 | tf_op jit(solution)/shard_map/cond/branch_1_fun/ppermute | solution.py:434
  67.7 11.3 %collective-permute-start.41 = (f32[10,32,256]{2,1,0:T(8,128)S(1)}, f32[10,32,256]{2,1,0:T(8,128)S(1)}, u32[]{:S(2)}, u32[]{:S(2)}) collective-permute-start(f32[10,32,256]{2,1,0:T(8,128)S(1)} %collective-permute-done.40.refs_12_), channel_id=1, source_target_pairs={{0,1},{1,0},{2,3},{3,2},{4,5},{5,4},{6,7},{7,6},{8,9},{9,8},{10,11... | collective-permute-start | bytes 983048 | tf_op jit(solution)/shard_map/cond/branch_1_fun/ppermute | solution.py:434
  74.5 4.5 %collective-permute-start.39 = (f32[10,32,256]{2,1,0:T(8,128)S(1)}, f32[10,32,256]{2,1,0:T(8,128)S(1)}, u32[]{:S(2)}, u32[]{:S(2)}) collective-permute-start(f32[10,32,256]{2,1,0:T(8,128)S(1)} %collective-permute-done.38.refs_10_), channel_id=1, source_target_pairs={{0,1},{1,0},{2,3},{3,2},{4,5},{5,4},{6,7},{7,6},{8,9},{9,8},{10,11... | collective-permute-start | bytes 983048 | tf_op jit(solution)/shard_map/cond/branch_1_fun/ppermute | solution.py:434
  75.8 3.2 %collective-permute-start.43 = (f32[10,32,256]{2,1,0:T(8,128)S(1)}, f32[10,32,256]{2,1,0:T(8,128)S(1)}, u32[]{:S(2)}, u32[]{:S(2)}) collective-permute-start(f32[10,32,256]{2,1,0:T(8,128)S(1)} %collective-permute-done.42.refs_14_), channel_id=1, source_target_pairs={{0,1},{1,0},{2,3},{3,2},{4,5},{5,4},{6,7},{7,6},{8,9},{9,8},{10,11... | collective-permute-start | bytes 983048 | tf_op jit(solution)/shard_map/cond/branch_1_fun/ppermute | solution.py:434

commit v6 on v5

--- a/solution.py
+++ b/solution.py
@@ -269,9 +269,8 @@
     )(where, fill, *lists)
 
 
-def own_factor_kernel(sizes, where_ref, fill_ref, w_ref, panel_ref, x_ref, slot_ref, masked, sem):
-    c, r = where_ref[0], where_ref[1]
-    own = r * sizes.cols + c
+def own_factor_kernel(sizes, where_ref, fill_ref, w_ref, panel_ref, x_ref, masked, sem):
+    own = where_ref[1] * sizes.cols + where_ref[0]
     for u in range(sizes.per_piece):
         for p in range(2):
             at = (pl.ds(u * sizes.unit, sizes.unit), pl.ds(p * sizes.block, sizes.block))
@@ -279,6 +278,22 @@
     masked[...] = dot3(halves(masked[...]), halves(w_ref[...]), NT)
     copy_out = pltpu.make_async_copy(masked, x_ref, sem)
     copy_out.start()
+    copy_out.wait()
+
+
+def own_factor(sizes, where, fill, w, panel):
+    return pl.pallas_call(
+        functools.partial(own_factor_kernel, sizes),
+        out_shape=pltpu.HBM(panel.shape, F32),
+        in_specs=[SMEM, SMEM, VMEM, VMEM],
+        out_specs=HBM,
+        scratch_shapes=[pltpu.VMEM(panel.shape, F32), pltpu.SemaphoreType.DMA],
+        compiler_params=pltpu.CompilerParams(vmem_limit_bytes=20 * 2**20),
+    )(where, fill, w, panel)
+
+
+def list_slots_kernel(sizes, where_ref, fill_ref, slot_ref):
+    c, r = where_ref[0], where_ref[1]
 
     @pl.loop(0, sizes.groups)
     def _(shift):
@@ -296,21 +311,15 @@
 
                     slot = slot + flag.astype(jnp.int32)
 
-    copy_out.wait()
-
-
-def own_factor(sizes, where, fill, w, panel):
-    return pl.pallas_call(
-        functools.partial(own_factor_kernel, sizes),
-        out_shape=(
-            pltpu.HBM(panel.shape, F32),
-            jax.ShapeDtypeStruct((2 * sizes.tiles,), jnp.int32),
-        ),
-        in_specs=[SMEM, SMEM, VMEM, VMEM],
-        out_specs=(HBM, SMEM),
-        scratch_shapes=[pltpu.VMEM(panel.shape, F32), pltpu.SemaphoreType.DMA],
-        compiler_params=pltpu.CompilerParams(vmem_limit_bytes=20 * 2**20),
-    )(where, fill, w, panel)
+
+def list_slots(sizes, where, fill):
+    return pl.pallas_call(
+        functools.partial(list_slots_kernel, sizes),
+        out_shape=jax.ShapeDtypeStruct((2 * sizes.tiles,), jnp.int32),
+        in_specs=[SMEM, SMEM],
+        out_specs=SMEM,
+        cost_estimate=pl.CostEstimate(flops=2 * 10**10, bytes_accessed=6 * 10**7, transcendentals=0),
+    )(where, fill)
 
 
 def column_factor_kernel(sizes, where_ref, fill_ref, w_ref, *refs):
@@ -484,10 +493,7 @@
     from_core, pivot = lax.optimization_barrier((from_core, pivot))
     both = jnp.stack([at_core(core), from_core])
     from_side = swap(lax.dynamic_index_in_dim(both, 1 - side, 2, keepdims=False), "col", 1)
-    step = 2
-    while step < sizes.cols:
-        pivot = join(c, step, pivot, swap(pivot, "col", step))
-        step *= 2
+    pivot = join(c, 2, pivot, swap(pivot, "col", 2))
 
     def run(cap, column_cap, trailing, panel_rows, fill, units, from_core, from_side, pivot):
         own = pack(sizes, cap, where, fill, units, from_core, from_side)
@@ -496,15 +502,20 @@
         later = [s for s in range(1, sizes.groups) if s not in sizes.needed]
         lists |= {s: bring(sizes, own, s) for s in first}
         sides = {0: swap(own, "col", 1)}
+        pivot = lax.optimization_barrier((pivot, own))[0]
+        step = 4
+        while step < sizes.cols:
+            pivot = join(c, step, pivot, swap(pivot, "col", step))
+            step *= 2
         parts = [pivot] + ([swap(pivot, "row", 2)] if split == 4 else [])
         parts = [part for value in parts for part in (value, swap(value, "row", 1))]
         near = first[0]
-        lists[near], sides[0], *parts = lax.optimization_barrier((lists[near], sides[0], *parts))
+        lists[near], sides[0] = lax.optimization_barrier((lists[near], sides[0]))
         sides[near] = swap(lists[near], "col", 1)
-        w = inverse_factor(where, parts)
-        held = lax.optimization_barrier((w, sides[0], sides[near], *lists.values()))
-        w, sides[0], sides[near] = held[:3]
-        lists = dict(zip(lists, held[3:]))
+        count = len(parts)
+        held = lax.optimization_barrier((*parts, sides[0], sides[near], *lists.values()))
+        parts, sides[0], sides[near] = held[:count], held[count], held[count + 1]
+        lists = dict(zip(lists, held[count + 2 :]))
 
         column = pack_column(sizes, cap, column_cap, where, fill, [lists[s] for s in sizes.needed])
         lists |= {s: bring(sizes, lists[0], s) for s in later}
@@ -513,14 +524,22 @@
         while step > 1:
             column = spread_column(sizes, column, step)
             step //= 2
+        w = inverse_factor(where, parts)
+        held = lax.optimization_barrier((fill, w, *(lists[s] for s in later), *(sides[s] for s in first[1:])))
+        lists |= dict(zip(later, held[2:]))
+        sides |= dict(zip(first[1:], held[2 + len(later) :]))
+        slots = list_slots(sizes, where, held[0])
+        w, column, slots, *late = lax.optimization_barrier((held[1], column, slots, *(lists[s] for s in later)))
+        lists |= dict(zip(later, late))
+
         across = swap(lax.dynamic_index_in_dim(column, 1 - side, 0, keepdims=False), "col", 1)
         column = lax.dynamic_index_in_dim(column, side, 0, keepdims=False)
         columns = [column, swap(column, "row", 1), across, swap(across, "row", 1)]
-        panel_factor, slots = own_factor(sizes, where, fill, w, panel_rows)
+        sides |= {s: swap(lists[s], "col", 1) for s in later}
+        panel_factor = own_factor(sizes, where, fill, w, panel_rows)
+        column = column_factor(sizes, where, fill, w, columns)
         for s in later:
-            lists[s] = lax.optimization_barrier((lists[s], slots, *(sides[j] for j in first)))[0]
-            sides[s] = swap(lists[s], "col", 1)
-        column = column_factor(sizes, where, fill, w, columns)
+            sides[s], column, panel_factor = lax.optimization_barrier((sides[s], column, panel_factor))
         ordered = []
         for s in range(sizes.groups):
             value, other = lists[s], sides[s]

time: 83.6 us -> 99.1 us (1.19)
  the two profiles are of different devices: /device:TPU:31 before, /device:TPU:0 now
where the time goes in v6:
time: 99.1 us; the launch traced here: 98.8 us
  starting transfers between devices  39.5 us (40%)
  waiting for transfers between devices  26.2 us (26%)
  Pallas kernels  25.7 us (26%)
  local copies, waits for them, and re-layouts  5.03 us (5%)
  between operations  1.58 us (2%)
    ppermute x23, starting transfers between devices, swap(): return lax.ppermute(value, axis, [(i, i ^ step) for i in range(size)])  19 us
    ppermute x23, waiting for transfers between devices, swap(): return lax.ppermute(value, axis, [(i, i ^ step) for i in range(size)])  17.3 us
    ppermute x3, starting transfers between devices, bring(): return lax.ppermute(value, 'col', pairs)  17.3 us
    ppermute x3, waiting for transfers between devices, bring(): return lax.ppermute(value, 'col', pairs)  8.88 us
    pallas_call x1, Pallas kernels, inverse_factor(): pl.pallas_call(inverse_factor_kernel, out_shape=jax.ShapeDtypeStruct((n,...  7.15 us
    pallas_call x1, Pallas kernels, update(): pl.pallas_call(functools.partial(update_kernel, sizes), out_shape=pltpu.H...  6.15 us
    ppermute x1, starting transfers between devices, spread_column(): other = lax.ppermute(value, ('col', 'row'), pairs)  3.19 us
    pallas_call x1, Pallas kernels, column_factor(): pl.pallas_call(functools.partial(column_factor_kernel, sizes), out_shape=...  3.18 us
  transfers between devices with their start and end apart: 27, of which 11 were waited for; matrix products, arithmetic and copies ran while one was open for 1% of the time, Pallas kernels for 18%

profile of v6, /device:TPU:0, one launch (start us, length us, event | category | flops | bytes accessed | tf_op | source)
XLA Modules:
  0.0 98.8 jit_solution(9555179433441043760)
XLA Ops:
  0.6 0.0 copy-start
  0.7 1.2 %dynamic-slice_bitcast_fusion.4 = (f32[1,3,2,32,512]{4,3,2,1,0:T(8,128)S(1)}, f32[3,2,32,512]{3,2,1,0:T(8,128)S(1)}) fusion(f32[3,2,2,32,512]{4,3,2,1,0:T(8,128)} %bitcast.27, s32[]{:T(128)S(6)} %select_n.108, s32[]{:T(128)S(6)} %select_n.103), kind=kLoop, calls=%fused_computation.14 | loop fusion | bytes 1572872 | tf_op jit(solution)/shard_map/stack | solution.py:494
  1.9 0.5 collective-permute-start.46
  2.4 2.6 %collective-permute-start.47 = (f32[1,16,512]{2,1,0:T(8,128)S(1)}, f32[1,16,512]{2,1,0:T(8,128)S(1)}, u32[]{:S(2)}, u32[]{:S(2)}) collective-permute-start(f32[1,16,512]{2,1,0:T(8,128)S(1)} %dynamic-slice_bitcast_fusion.6), channel_id=1, source_target_pairs={{0,4},{4,0},{8,12},{12,8},{16,20},{20,16},{24,28},{28,24},{1,5},{5... | collective-permute-start | bytes 98312 | tf_op jit(solution)/shard_map/ppermute | solution.py:443
  5.1 1.9 %collective-permute-done.47 = f32[1,16,512]{2,1,0:T(8,128)S(1)} collective-permute-done((f32[1,16,512]{2,1,0:T(8,128)S(1)}, f32[1,16,512]{2,1,0:T(8,128)S(1)}, u32[]{:S(2)}, u32[]{:S(2)}) %collective-permute-start.47) | collective-permute-done | bytes 32800 | tf_op jit(solution)/shard_map/ppermute | solution.py:443
  7.0 0.0 collective-permute-done.46
  7.0 2.1 %collective-permute-start.48 = (f32[2,3,32,512]{3,2,1,0:T(8,128)S(1)}, f32[2,3,32,512]{3,2,1,0:T(8,128)S(1)}, u32[]{:S(2)}, u32[]{:S(2)}) collective-permute-start(f32[2,3,32,512]{3,2,1,0:T(8,128)S(1)} %fusion.1), channel_id=1, source_target_pairs={{0,4},{4,0},{8,12},{12,8},{16,20},{20,16},{24,28},{28,24},{1,5},{5... | collective-permute-start | bytes 1179656 | tf_op jit(solution)/shard_map/ppermute | solution.py:443
  9.1 0.8 copy.13
  9.9 0.1 reshape.18.fill_ref
  10.0 1.2 %shard_map.63 = s32[1]{0:T(128)} custom-call(s32[96]{0:T(128)S(1)} %reshape.18.fill_ref), custom_call_target="tpu_custom_call" | custom-call | tf_op jit(solution)/shard_map/pallas_call | solution.py:181
  11.9 1.6 %collective-permute-start.49 = (f32[2,16,512]{2,1,0:T(8,128)S(1)}, f32[2,16,512]{2,1,0:T(8,128)S(1)}, u32[]{:S(2)}, u32[]{:S(2)}) collective-permute-start(f32[2,16,512]{2,1,0:T(8,128)S(1)} %maximum_select_fusion.2), channel_id=1, source_target_pairs={{0,8},{4,12},{8,0},{12,4},{16,24},{20,28},{24,16},{28,20},{1,9},{5... | collective-permute-start | bytes 196616 | tf_op jit(solution)/shard_map/ppermute | solution.py:443
  13.5 0.1 pad_add_fusion
  13.6 2.6 %collective-permute-done.49 = f32[2,16,512]{2,1,0:T(8,128)S(1)} collective-permute-done((f32[2,16,512]{2,1,0:T(8,128)S(1)}, f32[2,16,512]{2,1,0:T(8,128)S(1)}, u32[]{:S(2)}, u32[]{:S(2)}) %collective-permute-start.49) | collective-permute-done | bytes 65568 | tf_op jit(solution)/shard_map/ppermute | solution.py:443
  16.3 1.7 %collective-permute-done.48 = f32[2,3,32,512]{3,2,1,0:T(8,128)S(1)} collective-permute-done((f32[2,3,32,512]{3,2,1,0:T(8,128)S(1)}, f32[2,3,32,512]{3,2,1,0:T(8,128)S(1)}, u32[]{:S(2)}, u32[]{:S(2)}) %collective-permute-start.48) | collective-permute-done | bytes 393248 | tf_op jit(solution)/shard_map/ppermute | solution.py:443
  17.9 80.6 %conditional.1 = (f32[384,512]{1,0:T(8,128)}, f32[3072,512]{1,0:T(8,128)}) conditional(s32[]{:T(128)} %bitcast.6, (s32[]{:T(128)}, s32[2]{0:T(128)S(1)}, s32[96]{0:T(128)S(1)}, f32[384,512]{1,0:T(8,128)}, f32[3,2,32,512]{3,2,1,0:T(8,128)S(1)}, /*index=5*/f32[2,3,32,512]{3,2,1,0:T(8,128)S(1)}, s32[]{:T(128)}, s32[]{:T(128)}, f32[384,512]{1,0:T(8,128)}, ...), branch_computations={%region_0.1_spmd, %region_1.2_spmd} | conditional | flops 20000360448 | bytes 134320304 | solution.py:550
  18.0 1.5 %branch_1_fun.7.refs_0_ = f32[10,32,256]{2,1,0:T(8,128)S(1)} custom-call(s32[2]{0:T(128)S(1)} %get-tuple-element.73.where_ref, s32[96]{0:T(128)S(1)} %get-tuple-element.91.fill_ref, f32[3,128,512]{2,1,0:T(8,128)} %bitcast.29, f32[3,2,32,512]{3,2,1,0:T(8,128)S(1)} %get-tuple-element.78.core_ref, f32[2,3,32,512]{3,2,1,0:T(8,128)S(1)} %get-tuple-element.79.side_ref), custom_call_target="tpu_custom_call" | custom-call | tf_op jit(solution)/shard_map/cond/branch_1_fun/pallas_call | solution.py:216
  19.5 2.6 %collective-permute-start.23 = (f32[4,16,512]{2,1,0:T(8,128)S(1)}, f32[4,16,512]{2,1,0:T(8,128)S(1)}, u32[]{:S(2)}, u32[]{:S(2)}) collective-permute-start(f32[4,16,512]{2,1,0:T(8,128)S(1)} %broadcast_select_fusion.3), channel_id=1, source_target_pairs={{0,16},{4,20},{8,24},{12,28},{16,0},{20,4},{24,8},{28,12},{1,17},{... | collective-permute-start | bytes 393224 | tf_op jit(solution)/shard_map/cond/branch_1_fun/ppermute | solution.py:443
  22.0 1.5 %collective-permute-start.28 = (f32[10,32,256]{2,1,0:T(8,128)S(1)}, f32[10,32,256]{2,1,0:T(8,128)S(1)}, u32[]{:S(2)}, u32[]{:S(2)}) collective-permute-start(f32[10,32,256]{2,1,0:T(8,128)S(1)} %branch_1_fun.7.refs_0_), channel_id=1, source_target_pairs={{0,4},{4,0},{8,12},{12,8},{16,20},{20,16},{24,28},{28,24},{1,5},{5... | collective-permute-start | bytes 983048 | tf_op jit(solution)/shard_map/cond/branch_1_fun/ppermute | solution.py:443
  23.5 1.4 %collective-permute-start.27 = (f32[10,32,256]{2,1,0:T(8,128)S(1)}, f32[10,32,256]{2,1,0:T(8,128)S(1)}, u32[]{:S(2)}, u32[]{:S(2)}) collective-permute-start(f32[10,32,256]{2,1,0:T(8,128)S(1)} %branch_1_fun.7.refs_0_), channel_id=1, source_target_pairs={{0,24},{4,28},{8,0},{12,4},{16,8},{20,12},{24,16},{28,20},{1,25},{... | collective-permute-start | bytes 983048 | tf_op jit(solution)/shard_map/cond/branch_1_fun/ppermute | solution.py:457
  24.9 3.4 %collective-permute-done.23 = f32[4,16,512]{2,1,0:T(8,128)S(1)} collective-permute-done((f32[4,16,512]{2,1,0:T(8,128)S(1)}, f32[4,16,512]{2,1,0:T(8,128)S(1)}, u32[]{:S(2)}, u32[]{:S(2)}) %collective-permute-start.23) | collective-permute-done | bytes 131104 | tf_op jit(solution)/shard_map/cond/branch_1_fun/ppermute | solution.py:443
  28.3 0.4 collective-permute-start.25
  28.7 2.3 %collective-permute-start.30 = (f32[10,32,256]{2,1,0:T(8,128)S(1)}, f32[10,32,256]{2,1,0:T(8,128)S(1)}, u32[]{:S(2)}, u32[]{:S(2)}) collective-permute-start(f32[10,32,256]{2,1,0:T(8,128)S(1)} %branch_1_fun.7.refs_0_), channel_id=1, source_target_pairs={{0,16},{4,20},{8,24},{12,28},{16,0},{20,4},{24,8},{28,12},{1,17},{... | collective-permute-start | bytes 983048 | tf_op jit(solution)/shard_map/cond/branch_1_fun/ppermute | solution.py:457
  30.9 0.0 collective-permute-done.28.refs_2_
  30.9 2.3 %collective-permute-done.27.refs_1_.refs_4_ = f32[10,32,256]{2,1,0:T(8,128)S(1)} collective-permute-done((f32[10,32,256]{2,1,0:T(8,128)S(1)}, f32[10,32,256]{2,1,0:T(8,128)S(1)}, u32[]{:S(2)}, u32[]{:S(2)}) %collective-permute-start.27) | collective-permute-done | bytes 327712 | tf_op jit(solution)/shard_map/cond/branch_1_fun/ppermute | solution.py:457
  33.2 1.3 %collective-permute-start.29 = (f32[10,32,256]{2,1,0:T(8,128)S(1)}, f32[10,32,256]{2,1,0:T(8,128)S(1)}, u32[]{:S(2)}, u32[]{:S(2)}) collective-permute-start(f32[10,32,256]{2,1,0:T(8,128)S(1)} %collective-permute-done.27.refs_1_.refs_4_), channel_id=1, source_target_pairs={{0,4},{4,0},{8,12},{12,8},{16,20},{20,16},{24,28},{28,24},{1,5},{5... | collective-permute-start | bytes 983048 | tf_op jit(solution)/shard_map/cond/branch_1_fun/ppermute | solution.py:443
  34.5 0.0 collective-permute-start.24
  34.5 0.2 collective-permute-done.25.refs_2_
  34.7 0.3 collective-permute-start.26
  35.0 6.6 %collective-permute-done.30.refs_2_.refs_8_ = f32[10,32,256]{2,1,0:T(8,128)S(1)} collective-permute-done((f32[10,32,256]{2,1,0:T(8,128)S(1)}, f32[10,32,256]{2,1,0:T(8,128)S(1)}, u32[]{:S(2)}, u32[]{:S(2)}) %collective-permute-start.30) | collective-permute-done | bytes 327712 | tf_op jit(solution)/shard_map/cond/branch_1_fun/ppermute | solution.py:457
  41.6 0.0 collective-permute-done.24.refs_1_
  41.6 0.0 collective-permute-done.26.refs_3_
  41.7 13.7 %collective-permute-start.31 = (f32[10,32,256]{2,1,0:T(8,128)S(1)}, f32[10,32,256]{2,1,0:T(8,128)}, u32[]{:S(2)}, u32[]{:S(2)}) collective-permute-start(f32[10,32,256]{2,1,0:T(8,128)S(1)} %branch_1_fun.7.refs_0_), channel_id=1, source_target_pairs={{0,8},{4,12},{8,16},{12,20},{16,24},{20,28},{24,0},{28,4},{1,9},{5... | collective-permute-start | bytes 983048 | tf_op jit(solution)/shard_map/cond/branch_1_fun/ppermute | solution.py:457
  55.4 1.7 %collective-permute-start.32 = (f32[10,32,256]{2,1,0:T(8,128)S(1)}, f32[10,32,256]{2,1,0:T(8,128)}, u32[]{:S(2)}, u32[]{:S(2)}) collective-permute-start(f32[10,32,256]{2,1,0:T(8,128)S(1)} %collective-permute-done.30.refs_2_.refs_8_), channel_id=1, source_target_pairs={{0,4},{4,0},{8,12},{12,8},{16,20},{20,16},{24,28},{28,24},{1,5},{5... | collective-permute-start | bytes 983048 | tf_op jit(solution)/shard_map/cond/branch_1_fun/ppermute | solution.py:443
  57.1 2.1 %branch_1_fun.9 = f32[2,6,32,256]{3,2,1,0:T(8,128)S(1)} custom-call(s32[2]{0:T(128)S(1)} %get-tuple-element.73.where_ref, s32[96]{0:T(128)S(1)} %get-tuple-element.91.fill_ref, f32[10,32,256]{2,1,0:T(8,128)S(1)} %branch_1_fun.7.refs_0_, f32[10,32,256]{2,1,0:T(8,128)S(1)} %collective-permute-done.27.refs_1_.refs_4_, ...), custom_call_target="tpu_custom_call" | custom-call | tf_op jit(solution)/shard_map/cond/branch_1_fun/pallas_call | solution.py:262
  59.2 3.2 %collective-permute-start.33 = (f32[2,6,32,256]{3,2,1,0:T(8,128)S(1)}, f32[2,6,32,256]{3,2,1,0:T(8,128)}, u32[]{:S(2)}, u32[]{:S(2)}) collective-permute-start(f32[2,6,32,256]{3,2,1,0:T(8,128)S(1)} %branch_1_fun.9), channel_id=1, source_target_pairs={{0,2},{1,3},{4,6},{5,7},{8,10},{9,11},{12,14},{13,15},{16,18},{17,... | collective-permute-start | bytes 1179656 | tf_op jit(solution)/shard_map/cond/branch_1_fun/ppermute | solution.py:468
  62.4 0.9 copy-done.6
  63.4 0.9 copy-done.12
  64.3 0.9 copy-done.16
  65.3 7.2 %branch_1_fun.8.w_ref = f32[512,512]{1,0:T(8,128)S(1)} custom-call(s32[2]{0:T(128)S(1)} %get-tuple-element.73.where_ref, f32[8,16,512]{2,1,0:T(8,128)S(1)} %maximum_select_fusion.1.refs_0_, f32[8,16,512]{2,1,0:T(8,128)S(1)} %copy-done.12, f32[8,16,512]{2,1,0:T(8,128)S(1)} %copy-done.6, f32[8,16,512]{2,1,0:T(8,128)S(1)} %copy-done.16), custom_call_target="tpu_custom_call" | custom-call | tf_op jit(solution)/shard_map/cond/branch_1_fun/pallas_call | solution.py:105
  72.4 0.0 collective-permute-done.31.refs_12_
  72.4 0.0 collective-permute-done.32.refs_10_
  72.4 1.6 %branch_1_fun.10.slot_ref = s32[48]{0:T(128)} custom-call(s32[2]{0:T(128)S(1)} %get-tuple-element.73.where_ref, s32[96]{0:T(128)S(1)} %get-tuple-element.91.fill_ref), custom_call_target="tpu_custom_call" | custom-call | flops 20000000000 | bytes 60000000 | tf_op jit(solution)/shard_map/cond/branch_1_fun/pallas_call | solution.py:316
  74.1 0.0 copy-start.17
  74.1 0.1 broadcast_select_fusion.2
  74.2 0.4 collective-permute-start.36
  74.5 0.0 collective-permute-start.35
  74.5 1.7 %collective-permute-start.34 = (f32[10,32,256]{2,1,0:T(8,128)}, f32[10,32,256]{2,1,0:T(8,128)S(1)}, u32[]{:S(2)}, u32[]{:S(2)}) collective-permute-start(f32[10,32,256]{2,1,0:T(8,128)} %collective-permute-done.31.refs_12_), channel_id=1, source_target_pairs={{0,4},{4,0},{8,12},{12,8},{16,20},{20,16},{24,28},{28,24},{1,5},{5... | collective-permute-start | bytes 983048 | tf_op jit(solution)/shard_map/cond/branch_1_fun/ppermute | solution.py:443
  76.3 0.2 collective-permute-start.39
  76.5 0.3 collective-permute-start.41
  76.8 5.2 %collective-permute-done.36.refs_2_ = f32[6,32,256]{2,1,0:T(8,128)S(1)} collective-permute-done((f32[6,32,256]{2,1,0:T(8,128)S(1)}, f32[6,32,256]{2,1,0:T(8,128)S(1)}, u32[]{:S(2)}, u32[]{:S(2)}) %collective-permute-start.36) | collective-permute-done | bytes 196640 | tf_op jit(solution)/shard_map/cond/branch_1_fun/ppermute | solution.py:443
  82.0 0.0 collective-permute-start.40
  82.0 0.0 collective-permute-done.35.refs_1_
  82.0 0.5 collective-permute-start.37
  82.5 2.8 %branch_1_fun.12 = f32[384,512]{1,0:T(8,128)} custom-call(s32[2]{0:T(128)S(1)} %get-tuple-element.73.where_ref, s32[96]{0:T(128)S(1)} %get-tuple-element.91.fill_ref, f32[512,512]{1,0:T(8,128)S(1)} %branch_1_fun.8.w_ref, f32[384,512]{1,0:T(8,128)} %get-tuple-element.98.panel_ref), custom_call_target="tpu_custom_call" | custom-call | tf_op jit(solution)/shard_map/cond/branch_1_fun/pallas_call | solution.py:285
  85.4 0.1 collective-permute-start.38
  85.5 3.2 %branch_1_fun.11.column_ref = f32[512,512]{1,0:T(8,128)S(1)} custom-call(s32[2]{0:T(128)S(1)} %get-tuple-element.73.where_ref, s32[96]{0:T(128)S(1)} %get-tuple-element.91.fill_ref, f32[512,512]{1,0:T(8,128)S(1)} %branch_1_fun.8.w_ref, f32[6,32,256]{2,1,0:T(8,128)S(1)} %get-tuple-element.138.refs_0_, f32[6,32,256]{2,1,0:T(8,128)S(1)} %collective-permute-done.35.refs_1_, ...), custom_call_target="tpu_custom_call" | custom-call | tf_op jit(solution)/shard_map/cond/branch_1_fun/pallas_call | solution.py:353
  88.6 0.6 collective-permute-start.42
  89.2 0.1 collective-permute-start.43
  89.3 0.4 collective-permute-start.44
  89.7 0.1 collective-permute-start.45
  89.8 0.6 collective-permute-done.42.refs_9_
  90.5 0.7 collective-permute-done.43.refs_11_
  91.1 0.9 collective-permute-done.44.refs_13_
  92.1 6.1 %branch_1_fun.13 = f32[3072,512]{1,0:T(8,128)} custom-call(s32[2]{0:T(128)S(1)} %get-tuple-element.73.where_ref, s32[48]{0:T(128)S(1)} %copy-done.17, f32[512,512]{1,0:T(8,128)S(1)} %branch_1_fun.11.column_ref, f32[3072,512]{1,0:T(8,128)} %get-tuple-element.126.window_ref, f32[10,32,256]{2,1,0:T(8,128)S(1)} %branch_1_fun.7.refs_0_, ...), custom_call_target="tpu_custom_call" | custom-call | tf_op jit(solution)/shard_map/cond/branch_1_fun/pallas_call | solution.py:426
  (27 shorter events, 0.2 us)
Async XLA Ops:
  0.6 1.8 %copy-start = (f32[64,512]{1,0:T(8,128)S(1)}, f32[64,512]{1,0:T(8,128)}, u32[]{:S(2)}) copy-start(f32[64,512]{1,0:T(8,128)} %param.8) | copy-start | bytes 393220
  1.9 5.1 %collective-permute-start.46 = (f32[3,2,32,512]{3,2,1,0:T(8,128)S(1)}, f32[3,2,32,512]{3,2,1,0:T(8,128)S(1)}, u32[]{:S(2)}, u32[]{:S(2)}) collective-permute-start(f32[3,2,32,512]{3,2,1,0:T(8,128)S(1)} %get-tuple-element.140), channel_id=1, source_target_pairs={{0,1},{1,0},{2,3},{3,2},{4,5},{5,4},{6,7},{7,6},{8,9},{9,8},{10,11... | collective-permute-start | bytes 1179656 | tf_op jit(solution)/shard_map/ppermute | solution.py:443
  2.4 4.5 %collective-permute-start.47 = (f32[1,16,512]{2,1,0:T(8,128)S(1)}, f32[1,16,512]{2,1,0:T(8,128)S(1)}, u32[]{:S(2)}, u32[]{:S(2)}) collective-permute-start(f32[1,16,512]{2,1,0:T(8,128)S(1)} %dynamic-slice_bitcast_fusion.6), channel_id=1, source_target_pairs={{0,4},{4,0},{8,12},{12,8},{16,20},{20,16},{24,28},{28,24},{1,5},{5... | collective-permute-start | bytes 98312 | tf_op jit(solution)/shard_map/ppermute | solution.py:443
  7.0 10.9 %collective-permute-start.48 = (f32[2,3,32,512]{3,2,1,0:T(8,128)S(1)}, f32[2,3,32,512]{3,2,1,0:T(8,128)S(1)}, u32[]{:S(2)}, u32[]{:S(2)}) collective-permute-start(f32[2,3,32,512]{3,2,1,0:T(8,128)S(1)} %fusion.1), channel_id=1, source_target_pairs={{0,4},{4,0},{8,12},{12,8},{16,20},{20,16},{24,28},{28,24},{1,5},{5... | collective-permute-start | bytes 1179656 | tf_op jit(solution)/shard_map/ppermute | solution.py:443
  11.9 4.3 %collective-permute-start.49 = (f32[2,16,512]{2,1,0:T(8,128)S(1)}, f32[2,16,512]{2,1,0:T(8,128)S(1)}, u32[]{:S(2)}, u32[]{:S(2)}) collective-permute-start(f32[2,16,512]{2,1,0:T(8,128)S(1)} %maximum_select_fusion.2), channel_id=1, source_target_pairs={{0,8},{4,12},{8,0},{12,4},{16,24},{20,28},{24,16},{28,20},{1,9},{5... | collective-permute-start | bytes 196616 | tf_op jit(solution)/shard_map/ppermute | solution.py:443
  19.5 8.8 %collective-permute-start.23 = (f32[4,16,512]{2,1,0:T(8,128)S(1)}, f32[4,16,512]{2,1,0:T(8,128)S(1)}, u32[]{:S(2)}, u32[]{:S(2)}) collective-permute-start(f32[4,16,512]{2,1,0:T(8,128)S(1)} %broadcast_select_fusion.3), channel_id=1, source_target_pairs={{0,16},{4,20},{8,24},{12,28},{16,0},{20,4},{24,8},{28,12},{1,17},{... | collective-permute-start | bytes 393224 | tf_op jit(solution)/shard_map/cond/branch_1_fun/ppermute | solution.py:443
  22.0 8.9 %collective-permute-start.28 = (f32[10,32,256]{2,1,0:T(8,128)S(1)}, f32[10,32,256]{2,1,0:T(8,128)S(1)}, u32[]{:S(2)}, u32[]{:S(2)}) collective-permute-start(f32[10,32,256]{2,1,0:T(8,128)S(1)} %branch_1_fun.7.refs_0_), channel_id=1, source_target_pairs={{0,4},{4,0},{8,12},{12,8},{16,20},{20,16},{24,28},{28,24},{1,5},{5... | collective-permute-start | bytes 983048 | tf_op jit(solution)/shard_map/cond/branch_1_fun/ppermute | solution.py:443
  23.5 9.7 %collective-permute-start.27 = (f32[10,32,256]{2,1,0:T(8,128)S(1)}, f32[10,32,256]{2,1,0:T(8,128)S(1)}, u32[]{:S(2)}, u32[]{:S(2)}) collective-permute-start(f32[10,32,256]{2,1,0:T(8,128)S(1)} %branch_1_fun.7.refs_0_), channel_id=1, source_target_pairs={{0,24},{4,28},{8,0},{12,4},{16,8},{20,12},{24,16},{28,20},{1,25},{... | collective-permute-start | bytes 983048 | tf_op jit(solution)/shard_map/cond/branch_1_fun/ppermute | solution.py:457
  28.3 6.4 %collective-permute-start.25 = (f32[8,16,512]{2,1,0:T(8,128)S(1)}, f32[8,16,512]{2,1,0:T(8,128)S(1)}, u32[]{:S(2)}, u32[]{:S(2)}) collective-permute-start(f32[8,16,512]{2,1,0:T(8,128)S(1)} %maximum_select_fusion.1.refs_0_), channel_id=1, source_target_pairs={{0,2},{1,3},{2,0},{3,1},{4,6},{5,7},{6,4},{7,5},{8,10},{9,11},{10,... | collective-permute-start | bytes 786440 | tf_op jit(solution)/shard_map/cond/branch_1_fun/ppermute | solution.py:443
  28.7 13.0 %collective-permute-start.30 = (f32[10,32,256]{2,1,0:T(8,128)S(1)}, f32[10,32,256]{2,1,0:T(8,128)S(1)}, u32[]{:S(2)}, u32[]{:S(2)}) collective-permute-start(f32[10,32,256]{2,1,0:T(8,128)S(1)} %branch_1_fun.7.refs_0_), channel_id=1, source_target_pairs={{0,16},{4,20},{8,24},{12,28},{16,0},{20,4},{24,8},{28,12},{1,17},{... | collective-permute-start | bytes 983048 | tf_op jit(solution)/shard_map/cond/branch_1_fun/ppermute | solution.py:457
  33.2 8.4 %collective-permute-start.29 = (f32[10,32,256]{2,1,0:T(8,128)S(1)}, f32[10,32,256]{2,1,0:T(8,128)S(1)}, u32[]{:S(2)}, u32[]{:S(2)}) collective-permute-start(f32[10,32,256]{2,1,0:T(8,128)S(1)} %collective-permute-done.27.refs_1_.refs_4_), channel_id=1, source_target_pairs={{0,4},{4,0},{8,12},{12,8},{16,20},{20,16},{24,28},{28,24},{1,5},{5... | collective-permute-start | bytes 983048 | tf_op jit(solution)/shard_map/cond/branch_1_fun/ppermute | solution.py:443
  34.5 7.1 %collective-permute-start.24 = (f32[8,16,512]{2,1,0:T(8,128)S(1)}, f32[8,16,512]{2,1,0:T(8,128)S(1)}, u32[]{:S(2)}, u32[]{:S(2)}) collective-permute-start(f32[8,16,512]{2,1,0:T(8,128)S(1)} %maximum_select_fusion.1.refs_0_), channel_id=1, source_target_pairs={{0,1},{1,0},{2,3},{3,2},{4,5},{5,4},{6,7},{7,6},{8,9},{9,8},{10,11... | collective-permute-start | bytes 786440 | tf_op jit(solution)/shard_map/cond/branch_1_fun/ppermute | solution.py:443
  34.7 24.5 %copy-start.5 = (f32[8,16,512]{2,1,0:T(8,128)}, f32[8,16,512]{2,1,0:T(8,128)S(1)}, u32[]{:S(2)}) copy-start(f32[8,16,512]{2,1,0:T(8,128)S(1)} %collective-permute-done.25.refs_2_) | copy-start | bytes 786436 | tf_op jit(solution)/shard_map/cond
  34.7 6.9 %collective-permute-start.26 = (f32[8,16,512]{2,1,0:T(8,128)S(1)}, f32[8,16,512]{2,1,0:T(8,128)S(1)}, u32[]{:S(2)}, u32[]{:S(2)}) collective-permute-start(f32[8,16,512]{2,1,0:T(8,128)S(1)} %collective-permute-done.25.refs_2_), channel_id=1, source_target_pairs={{0,1},{1,0},{2,3},{3,2},{4,5},{5,4},{6,7},{7,6},{8,9},{9,8},{10,11... | collective-permute-start | bytes 786440 | tf_op jit(solution)/shard_map/cond/branch_1_fun/ppermute | solution.py:443
  41.6 17.6 %copy-start.11 = (f32[8,16,512]{2,1,0:T(8,128)}, f32[8,16,512]{2,1,0:T(8,128)S(1)}, u32[]{:S(2)}) copy-start(f32[8,16,512]{2,1,0:T(8,128)S(1)} %collective-permute-done.24.refs_1_) | copy-start | bytes 786436 | tf_op jit(solution)/shard_map/cond
  41.6 17.6 %copy-start.15 = (f32[8,16,512]{2,1,0:T(8,128)}, f32[8,16,512]{2,1,0:T(8,128)S(1)}, u32[]{:S(2)}) copy-start(f32[8,16,512]{2,1,0:T(8,128)S(1)} %collective-permute-done.26.refs_3_) | copy-start | bytes 786436 | tf_op jit(solution)/shard_map/cond
  41.7 30.8 %collective-permute-start.31 = (f32[10,32,256]{2,1,0:T(8,128)S(1)}, f32[10,32,256]{2,1,0:T(8,128)}, u32[]{:S(2)}, u32[]{:S(2)}) collective-permute-start(f32[10,32,256]{2,1,0:T(8,128)S(1)} %branch_1_fun.7.refs_0_), channel_id=1, source_target_pairs={{0,8},{4,12},{8,16},{12,20},{16,24},{20,28},{24,0},{28,4},{1,9},{5... | collective-permute-start | bytes 983048 | tf_op jit(solution)/shard_map/cond/branch_1_fun/ppermute | solution.py:457
  55.4 17.1 %collective-permute-start.32 = (f32[10,32,256]{2,1,0:T(8,128)S(1)}, f32[10,32,256]{2,1,0:T(8,128)}, u32[]{:S(2)}, u32[]{:S(2)}) collective-permute-start(f32[10,32,256]{2,1,0:T(8,128)S(1)} %collective-permute-done.30.refs_2_.refs_8_), channel_id=1, source_target_pairs={{0,4},{4,0},{8,12},{12,8},{16,20},{20,16},{24,28},{28,24},{1,5},{5... | collective-permute-start | bytes 983048 | tf_op jit(solution)/shard_map/cond/branch_1_fun/ppermute | solution.py:443
  59.2 14.8 %collective-permute-start.33 = (f32[2,6,32,256]{3,2,1,0:T(8,128)S(1)}, f32[2,6,32,256]{3,2,1,0:T(8,128)}, u32[]{:S(2)}, u32[]{:S(2)}) collective-permute-start(f32[2,6,32,256]{3,2,1,0:T(8,128)S(1)} %branch_1_fun.9), channel_id=1, source_target_pairs={{0,2},{1,3},{4,6},{5,7},{8,10},{9,11},{12,14},{13,15},{16,18},{17,... | collective-permute-start | bytes 1179656 | tf_op jit(solution)/shard_map/cond/branch_1_fun/ppermute | solution.py:468
  62.4 0.9 copy-start.6
  63.4 0.9 copy-start.12
  64.3 0.9 copy-start.16
  74.1 18.0 %copy-start.17 = (s32[48]{0:T(128)S(1)}, s32[48]{0:T(128)}, u32[]{:S(2)}) copy-start(s32[48]{0:T(128)} %branch_1_fun.10.slot_ref) | copy-start | bytes 580 | tf_op jit(solution)/shard_map/cond
  74.2 7.8 %collective-permute-start.36 = (f32[6,32,256]{2,1,0:T(8,128)S(1)}, f32[6,32,256]{2,1,0:T(8,128)S(1)}, u32[]{:S(2)}, u32[]{:S(2)}) collective-permute-start(f32[6,32,256]{2,1,0:T(8,128)S(1)} %get-tuple-element.137), channel_id=1, source_target_pairs={{0,4},{4,0},{8,12},{12,8},{16,20},{20,16},{24,28},{28,24},{1,5},{5... | collective-permute-start | bytes 589832 | tf_op jit(solution)/shard_map/cond/branch_1_fun/ppermute | solution.py:443
  74.5 7.5 %collective-permute-start.35 = (f32[6,32,256]{2,1,0:T(8,128)S(1)}, f32[6,32,256]{2,1,0:T(8,128)S(1)}, u32[]{:S(2)}, u32[]{:S(2)}) collective-permute-start(f32[6,32,256]{2,1,0:T(8,128)S(1)} %get-tuple-element.138.refs_0_), channel_id=1, source_target_pairs={{0,1},{1,0},{2,3},{3,2},{4,5},{5,4},{6,7},{7,6},{8,9},{9,8},{10,11... | collective-permute-start | bytes 589832 | tf_op jit(solution)/shard_map/cond/branch_1_fun/ppermute | solution.py:443
  74.5 14.1 %collective-permute-start.34 = (f32[10,32,256]{2,1,0:T(8,128)}, f32[10,32,256]{2,1,0:T(8,128)S(1)}, u32[]{:S(2)}, u32[]{:S(2)}) collective-permute-start(f32[10,32,256]{2,1,0:T(8,128)} %collective-permute-done.31.refs_12_), channel_id=1, source_target_pairs={{0,4},{4,0},{8,12},{12,8},{16,20},{20,16},{24,28},{28,24},{1,5},{5... | collective-permute-start | bytes 983048 | tf_op jit(solution)/shard_map/cond/branch_1_fun/ppermute | solution.py:443
  76.3 12.9 %collective-permute-start.39 = (f32[10,32,256]{2,1,0:T(8,128)S(1)}, f32[10,32,256]{2,1,0:T(8,128)S(1)}, u32[]{:S(2)}, u32[]{:S(2)}) collective-permute-start(f32[10,32,256]{2,1,0:T(8,128)S(1)} %collective-permute-done.28.refs_2_), channel_id=1, source_target_pairs={{0,1},{1,0},{2,3},{3,2},{4,5},{5,4},{6,7},{7,6},{8,9},{9,8},{10,11... | collective-permute-start | bytes 983048 | tf_op jit(solution)/shard_map/cond/branch_1_fun/ppermute | solution.py:443
  76.5 12.8 %collective-permute-start.41 = (f32[10,32,256]{2,1,0:T(8,128)S(1)}, f32[10,32,256]{2,1,0:T(8,128)S(1)}, u32[]{:S(2)}, u32[]{:S(2)}) collective-permute-start(f32[10,32,256]{2,1,0:T(8,128)S(1)} %collective-permute-done.29.refs_6_), channel_id=1, source_target_pairs={{0,1},{1,0},{2,3},{3,2},{4,5},{5,4},{6,7},{7,6},{8,9},{9,8},{10,11... | collective-permute-start | bytes 983048 | tf_op jit(solution)/shard_map/cond/branch_1_fun/ppermute | solution.py:443
  82.0 7.7 %collective-permute-start.40 = (f32[10,32,256]{2,1,0:T(8,128)S(1)}, f32[10,32,256]{2,1,0:T(8,128)S(1)}, u32[]{:S(2)}, u32[]{:S(2)}) collective-permute-start(f32[10,32,256]{2,1,0:T(8,128)S(1)} %collective-permute-done.27.refs_1_.refs_4_), channel_id=1, source_target_pairs={{0,1},{1,0},{2,3},{3,2},{4,5},{5,4},{6,7},{7,6},{8,9},{9,8},{10,11... | collective-permute-start | bytes 983048 | tf_op jit(solution)/shard_map/cond/branch_1_fun/ppermute | solution.py:443
  82.0 3.4 %collective-permute-start.37 = (f32[6,32,256]{2,1,0:T(8,128)S(1)}, f32[6,32,256]{2,1,0:T(8,128)S(1)}, u32[]{:S(2)}, u32[]{:S(2)}) collective-permute-start(f32[6,32,256]{2,1,0:T(8,128)S(1)} %collective-permute-done.36.refs_2_), channel_id=1, source_target_pairs={{0,1},{1,0},{2,3},{3,2},{4,5},{5,4},{6,7},{7,6},{8,9},{9,8},{10,11... | collective-permute-start | bytes 589832 | tf_op jit(solution)/shard_map/cond/branch_1_fun/ppermute | solution.py:443
  85.4 4.4 %collective-permute-start.38 = (f32[10,32,256]{2,1,0:T(8,128)S(1)}, f32[10,32,256]{2,1,0:T(8,128)S(1)}, u32[]{:S(2)}, u32[]{:S(2)}) collective-permute-start(f32[10,32,256]{2,1,0:T(8,128)S(1)} %branch_1_fun.7.refs_0_), channel_id=1, source_target_pairs={{0,1},{1,0},{2,3},{3,2},{4,5},{5,4},{6,7},{7,6},{8,9},{9,8},{10,11... | collective-permute-start | bytes 983048 | tf_op jit(solution)/shard_map/cond/branch_1_fun/ppermute | solution.py:443
  88.6 1.8 %collective-permute-start.42 = (f32[10,32,256]{2,1,0:T(8,128)S(1)}, f32[10,32,256]{2,1,0:T(8,128)S(1)}, u32[]{:S(2)}, u32[]{:S(2)}) collective-permute-start(f32[10,32,256]{2,1,0:T(8,128)S(1)} %collective-permute-done.30.refs_2_.refs_8_), channel_id=1, source_target_pairs={{0,1},{1,0},{2,3},{3,2},{4,5},{5,4},{6,7},{7,6},{8,9},{9,8},{10,11... | collective-permute-start | bytes 983048 | tf_op jit(solution)/shard_map/cond/branch_1_fun/ppermute | solution.py:443
  89.2 1.9 %collective-permute-start.43 = (f32[10,32,256]{2,1,0:T(8,128)}, f32[10,32,256]{2,1,0:T(8,128)S(1)}, u32[]{:S(2)}, u32[]{:S(2)}) collective-permute-start(f32[10,32,256]{2,1,0:T(8,128)} %collective-permute-done.32.refs_10_), channel_id=1, source_target_pairs={{0,1},{1,0},{2,3},{3,2},{4,5},{5,4},{6,7},{7,6},{8,9},{9,8},{10,11... | collective-permute-start | bytes 983048 | tf_op jit(solution)/shard_map/cond/branch_1_fun/ppermute | solution.py:443
  89.3 2.8 %collective-permute-start.44 = (f32[10,32,256]{2,1,0:T(8,128)}, f32[10,32,256]{2,1,0:T(8,128)S(1)}, u32[]{:S(2)}, u32[]{:S(2)}) collective-permute-start(f32[10,32,256]{2,1,0:T(8,128)} %collective-permute-done.31.refs_12_), channel_id=1, source_target_pairs={{0,1},{1,0},{2,3},{3,2},{4,5},{5,4},{6,7},{7,6},{8,9},{9,8},{10,11... | collective-permute-start | bytes 983048 | tf_op jit(solution)/shard_map/cond/branch_1_fun/ppermute | solution.py:443
  89.7 2.4 %collective-permute-start.45 = (f32[10,32,256]{2,1,0:T(8,128)S(1)}, f32[10,32,256]{2,1,0:T(8,128)S(1)}, u32[]{:S(2)}, u32[]{:S(2)}) collective-permute-start(f32[10,32,256]{2,1,0:T(8,128)S(1)} %collective-permute-done.34.refs_14_), channel_id=1, source_target_pairs={{0,1},{1,0},{2,3},{3,2},{4,5},{5,4},{6,7},{7,6},{8,9},{9,8},{10,11... | collective-permute-start | bytes 983048 | tf_op jit(solution)/shard_map/cond/branch_1_fun/ppermute | solution.py:443

commit v7 on v6

--- a/solution.py
+++ b/solution.py
@@ -108,7 +108,7 @@
         in_specs=[SMEM] + [VMEM] * len(parts),
         out_specs=VMEM,
         scratch_shapes=[pltpu.VMEM((n, n), F32)],
-        compiler_params=pltpu.CompilerParams(vmem_limit_bytes=20 * 2**20),
+        compiler_params=pltpu.CompilerParams(vmem_limit_bytes=16 * 2**20),
     )(where, *parts)
 
 
@@ -265,7 +265,7 @@
         in_specs=[SMEM, SMEM] + [VMEM] * len(lists),
         out_specs=VMEM,
         scratch_shapes=[pltpu.SMEM((2 * sizes.column_units,), jnp.int32)],
-        compiler_params=pltpu.CompilerParams(vmem_limit_bytes=20 * 2**20),
+        compiler_params=pltpu.CompilerParams(vmem_limit_bytes=16 * 2**20),
     )(where, fill, *lists)
 
 
@@ -288,7 +288,7 @@
         in_specs=[SMEM, SMEM, VMEM, VMEM],
         out_specs=HBM,
         scratch_shapes=[pltpu.VMEM(panel.shape, F32), pltpu.SemaphoreType.DMA],
-        compiler_params=pltpu.CompilerParams(vmem_limit_bytes=20 * 2**20),
+        compiler_params=pltpu.CompilerParams(vmem_limit_bytes=16 * 2**20),
     )(where, fill, w, panel)
 
 
@@ -356,7 +356,7 @@
         in_specs=[SMEM, SMEM, VMEM] + [VMEM] * 4,
         out_specs=VMEM,
         scratch_shapes=[pltpu.VMEM((sizes.width, n), F32), pltpu.SMEM((2 * sizes.column_units,), jnp.int32)],
-        compiler_params=pltpu.CompilerParams(vmem_limit_bytes=20 * 2**20),
+        compiler_params=pltpu.CompilerParams(vmem_limit_bytes=16 * 2**20),
     )(where, fill, w, *lists)
 
 
@@ -434,7 +434,7 @@
             pltpu.VMEM((2, 3 * sizes.block, sizes.width), BF16),
             pltpu.SemaphoreType.DMA((tiles,)),
         ],
-        compiler_params=pltpu.CompilerParams(vmem_limit_bytes=36 * 2**20),
+        compiler_params=pltpu.CompilerParams(vmem_limit_bytes=30 * 2**20),
     )(where, slots, column, window, *lists)
 
 
@@ -493,7 +493,10 @@
     from_core, pivot = lax.optimization_barrier((from_core, pivot))
     both = jnp.stack([at_core(core), from_core])
     from_side = swap(lax.dynamic_index_in_dim(both, 1 - side, 2, keepdims=False), "col", 1)
-    pivot = join(c, 2, pivot, swap(pivot, "col", 2))
+    step = 2
+    while step < sizes.cols:
+        pivot = join(c, step, pivot, swap(pivot, "col", step))
+        step *= 2
 
     def run(cap, column_cap, trailing, panel_rows, fill, units, from_core, from_side, pivot):
         own = pack(sizes, cap, where, fill, units, from_core, from_side)
@@ -503,19 +506,15 @@
         lists |= {s: bring(sizes, own, s) for s in first}
         sides = {0: swap(own, "col", 1)}
         pivot = lax.optimization_barrier((pivot, own))[0]
-        step = 4
-        while step < sizes.cols:
-            pivot = join(c, step, pivot, swap(pivot, "col", step))
-            step *= 2
         parts = [pivot] + ([swap(pivot, "row", 2)] if split == 4 else [])
         parts = [part for value in parts for part in (value, swap(value, "row", 1))]
         near = first[0]
-        lists[near], sides[0] = lax.optimization_barrier((lists[near], sides[0]))
+        lists[near], sides[0], *parts = lax.optimization_barrier((lists[near], sides[0], *parts))
         sides[near] = swap(lists[near], "col", 1)
-        count = len(parts)
-        held = lax.optimization_barrier((*parts, sides[0], sides[near], *lists.values()))
-        parts, sides[0], sides[near] = held[:count], held[count], held[count + 1]
-        lists = dict(zip(lists, held[count + 2 :]))
+        w = inverse_factor(where, parts)
+        held = lax.optimization_barrier((w, sides[0], sides[near], *lists.values()))
+        w, sides[0], sides[near] = held[:3]
+        lists = dict(zip(lists, held[3:]))
 
         column = pack_column(sizes, cap, column_cap, where, fill, [lists[s] for s in sizes.needed])
         lists |= {s: bring(sizes, lists[0], s) for s in later}
@@ -524,7 +523,6 @@
         while step > 1:
             column = spread_column(sizes, column, step)
             step //= 2
-        w = inverse_factor(where, parts)
         held = lax.optimization_barrier((fill, w, *(lists[s] for s in later), *(sides[s] for s in first[1:])))
         lists |= dict(zip(later, held[2:]))
         sides |= dict(zip(first[1:], held[2 + len(later) :]))

time: 99.1 us -> 88.7 us (0.90); the launches traced: 98.8 us -> 87 us
  starting transfers between devices: 39.5 us -> 28.9 us
  local copies, waits for them, and re-layouts: 5.03 us -> 2.94 us
    ppermute x3, starting transfers between devices: 17.3 us -> 7.11 us  [bring(): return lax.ppermute(value, 'col', pairs)]
    ppermute x23, waiting for transfers between devices: 17.3 us -> 10.8 us  [swap(): return lax.ppermute(value, axis, [(i, i ^ step) for i in range(size)])]
    ppermute x3, waiting for transfers between devices: 8.88 us -> 13.9 us  [bring(): return lax.ppermute(value, 'col', pairs)]
    cond x14 -> x6, local copies, waits for them, and re-layouts: 2.87 us -> 0.78 us
  transfers between devices with their start and end apart: 27 -> 27, of which waited for: 11 -> 12; matrix products, arithmetic and copies ran while one was open for 1% -> 1% of each run, Pallas kernels for 18% -> 20%
where the time goes in v7:
time: 88.7 us; the launch traced here: 87 us
  starting transfers between devices  28.9 us (33%)
  Pallas kernels  26.1 us (29%)
  waiting for transfers between devices  25.6 us (29%)
  local copies, waits for them, and re-layouts  2.94 us (3%)
  between operations  1.59 us (2%)
  other arithmetic  1.22 us (1%)
    ppermute x23, starting transfers between devices, swap(): return lax.ppermute(value, axis, [(i, i ^ step) for i in range(size)])  18.4 us
    ppermute x3, waiting for transfers between devices, bring(): return lax.ppermute(value, 'col', pairs)  13.9 us
    ppermute x23, waiting for transfers between devices, swap(): return lax.ppermute(value, axis, [(i, i ^ step) for i in range(size)])  10.8 us
    ppermute x3, starting transfers between devices, bring(): return lax.ppermute(value, 'col', pairs)  7.11 us
    pallas_call x1, Pallas kernels, inverse_factor(): pl.pallas_call(inverse_factor_kernel, out_shape=jax.ShapeDtypeStruct((n,...  6.89 us
    pallas_call x1, Pallas kernels, update(): pl.pallas_call(functools.partial(update_kernel, sizes), out_shape=pltpu.H...  6.83 us
    ppermute x1, starting transfers between devices, spread_column(): other = lax.ppermute(value, ('col', 'row'), pairs)  3.32 us
    pallas_call x1, Pallas kernels, column_factor(): pl.pallas_call(functools.partial(column_factor_kernel, sizes), out_shape=...  3.17 us
  transfers between devices with their start and end apart: 27, of which 12 were waited for; matrix products, arithmetic and copies ran while one was open for 1% of the time, Pallas kernels for 20%

profile of v7, /device:TPU:0, one launch (start us, length us, event | category | flops | bytes accessed | tf_op | source)
XLA Modules:
  0.0 87.0 jit_solution(18146931543279770533)
XLA Ops:
  0.6 0.0 copy-start
  0.7 1.2 %dynamic-slice_bitcast_fusion.4 = (f32[1,3,2,32,512]{4,3,2,1,0:T(8,128)S(1)}, f32[3,2,32,512]{3,2,1,0:T(8,128)S(1)}) fusion(f32[3,2,2,32,512]{4,3,2,1,0:T(8,128)} %bitcast.27, s32[]{:T(128)S(6)} %select_n.102, s32[]{:T(128)S(6)} %select_n.97), kind=kLoop, calls=%fused_computation.12 | loop fusion | bytes 1572872 | tf_op jit(solution)/shard_map/stack | solution.py:494
  1.9 0.5 collective-permute-start.44
  2.4 2.6 %collective-permute-start.45 = (f32[1,16,512]{2,1,0:T(8,128)S(1)}, f32[1,16,512]{2,1,0:T(8,128)S(1)}, u32[]{:S(2)}, u32[]{:S(2)}) collective-permute-start(f32[1,16,512]{2,1,0:T(8,128)S(1)} %dynamic-slice_bitcast_fusion.6), channel_id=1, source_target_pairs={{0,4},{4,0},{8,12},{12,8},{16,20},{20,16},{24,28},{28,24},{1,5},{5... | collective-permute-start | bytes 98312 | tf_op jit(solution)/shard_map/ppermute | solution.py:443
  5.1 1.9 %collective-permute-done.45 = f32[1,16,512]{2,1,0:T(8,128)S(1)} collective-permute-done((f32[1,16,512]{2,1,0:T(8,128)S(1)}, f32[1,16,512]{2,1,0:T(8,128)S(1)}, u32[]{:S(2)}, u32[]{:S(2)}) %collective-permute-start.45) | collective-permute-done | bytes 32800 | tf_op jit(solution)/shard_map/ppermute | solution.py:443
  7.0 0.0 collective-permute-done.44
  7.0 2.2 %collective-permute-start.47 = (f32[2,16,512]{2,1,0:T(8,128)S(1)}, f32[2,16,512]{2,1,0:T(8,128)S(1)}, u32[]{:S(2)}, u32[]{:S(2)}) collective-permute-start(f32[2,16,512]{2,1,0:T(8,128)S(1)} %maximum_select_fusion.1), channel_id=1, source_target_pairs={{0,8},{4,12},{8,0},{12,4},{16,24},{20,28},{24,16},{28,20},{1,9},{5... | collective-permute-start | bytes 196616 | tf_op jit(solution)/shard_map/ppermute | solution.py:443
  9.2 1.6 %collective-permute-start.46 = (f32[2,3,32,512]{3,2,1,0:T(8,128)S(1)}, f32[2,3,32,512]{3,2,1,0:T(8,128)S(1)}, u32[]{:S(2)}, u32[]{:S(2)}) collective-permute-start(f32[2,3,32,512]{3,2,1,0:T(8,128)S(1)} %fusion.1), channel_id=1, source_target_pairs={{0,4},{4,0},{8,12},{12,8},{16,20},{20,16},{24,28},{28,24},{1,5},{5... | collective-permute-start | bytes 1179656 | tf_op jit(solution)/shard_map/ppermute | solution.py:443
  10.7 0.7 collective-permute-done.47
  11.4 3.1 %collective-permute-start.48 = (f32[4,16,512]{2,1,0:T(8,128)S(1)}, f32[4,16,512]{2,1,0:T(8,128)S(1)}, u32[]{:S(2)}, u32[]{:S(2)}) collective-permute-start(f32[4,16,512]{2,1,0:T(8,128)S(1)} %maximum_select_fusion), channel_id=1, source_target_pairs={{0,16},{4,20},{8,24},{12,28},{16,0},{20,4},{24,8},{28,12},{1,17},{... | collective-permute-start | bytes 393224 | tf_op jit(solution)/shard_map/ppermute | solution.py:443
  14.5 0.8 copy.13
  15.3 0.1 reshape.18.fill_ref
  15.4 1.2 %shard_map.63 = s32[1]{0:T(128)} custom-call(s32[96]{0:T(128)S(1)} %reshape.18.fill_ref), custom_call_target="tpu_custom_call" | custom-call | tf_op jit(solution)/shard_map/pallas_call | solution.py:181
  17.3 0.1 pad_add_fusion
  17.4 1.8 %collective-permute-done.48 = f32[4,16,512]{2,1,0:T(8,128)S(1)} collective-permute-done((f32[4,16,512]{2,1,0:T(8,128)S(1)}, f32[4,16,512]{2,1,0:T(8,128)S(1)}, u32[]{:S(2)}, u32[]{:S(2)}) %collective-permute-start.48) | collective-permute-done | bytes 131104 | tf_op jit(solution)/shard_map/ppermute | solution.py:443
  19.2 0.1 pad_maximum_fusion.1
  19.2 0.0 collective-permute-done.46
  19.3 67.5 %conditional.1 = (f32[384,512]{1,0:T(8,128)}, f32[3072,512]{1,0:T(8,128)}) conditional(s32[]{:T(128)} %bitcast.6, (s32[2]{0:T(128)S(1)}, s32[96]{0:T(128)S(1)}, f32[384,512]{1,0:T(8,128)}, f32[3,2,32,512]{3,2,1,0:T(8,128)S(1)}, f32[2,3,32,512]{3,2,1,0:T(8,128)S(1)}, /*index=5*/s32[]{:T(128)}, s32[]{:T(128)}, f32[384,512]{1,0:T(8,128)}, ...), branch_computations={%region_0.1_spmd, %region_1.2_spmd} | conditional | flops 20000196608 | bytes 131567560 | solution.py:548
  19.5 0.0 copy-start.7
  19.5 0.0 copy-start.8
  19.5 0.7 copy-done.7
  20.2 0.1 copy-done.8
  20.3 1.0 %broadcast_select_fusion.3.refs_0_ = f32[8,16,512]{2,1,0:T(8,128)S(1)} fusion(f32[8,16,512]{2,1,0:T(8,128)} %copy-done.8, f32[8,16,512]{2,1,0:T(8,128)} %copy-done.7, pred[]{:T(512)S(6)} %ne.67), kind=kLoop, calls=%fused_computation.7 | loop fusion | flops 65536 | bytes 786433 | tf_op jit(solution)/shard_map/jit(_where)/select_n | solution.py:448
  21.3 1.5 %branch_1_fun.7.refs_0_ = f32[10,32,256]{2,1,0:T(8,128)S(1)} custom-call(s32[2]{0:T(128)S(1)} %get-tuple-element.69.where_ref, s32[96]{0:T(128)S(1)} %get-tuple-element.87.fill_ref, f32[3,128,512]{2,1,0:T(8,128)} %bitcast.29, f32[3,2,32,512]{3,2,1,0:T(8,128)S(1)} %get-tuple-element.72.core_ref, f32[2,3,32,512]{3,2,1,0:T(8,128)S(1)} %get-tuple-element.73.side_ref), custom_call_target="tpu_custom_call" | custom-call | tf_op jit(solution)/shard_map/cond/branch_1_fun/pallas_call | solution.py:216
  22.8 1.6 %collective-permute-start.25 = (f32[8,16,512]{2,1,0:T(8,128)S(1)}, f32[8,16,512]{2,1,0:T(8,128)S(1)}, u32[]{:S(2)}, u32[]{:S(2)}) collective-permute-start(f32[8,16,512]{2,1,0:T(8,128)S(1)} %broadcast_select_fusion.3.refs_0_), channel_id=1, source_target_pairs={{0,2},{1,3},{2,0},{3,1},{4,6},{5,7},{6,4},{7,5},{8,10},{9,11},{10,... | collective-permute-start | bytes 786440 | tf_op jit(solution)/shard_map/cond/branch_1_fun/ppermute | solution.py:443
  24.4 1.5 %collective-permute-start.23 = (f32[10,32,256]{2,1,0:T(8,128)S(1)}, f32[10,32,256]{2,1,0:T(8,128)S(1)}, u32[]{:S(2)}, u32[]{:S(2)}) collective-permute-start(f32[10,32,256]{2,1,0:T(8,128)S(1)} %branch_1_fun.7.refs_0_), channel_id=1, source_target_pairs={{0,4},{4,0},{8,12},{12,8},{16,20},{20,16},{24,28},{28,24},{1,5},{5... | collective-permute-start | bytes 983048 | tf_op jit(solution)/shard_map/cond/branch_1_fun/ppermute | solution.py:443
  25.9 3.5 %collective-permute-start.22 = (f32[10,32,256]{2,1,0:T(8,128)S(1)}, f32[10,32,256]{2,1,0:T(8,128)S(1)}, u32[]{:S(2)}, u32[]{:S(2)}) collective-permute-start(f32[10,32,256]{2,1,0:T(8,128)S(1)} %branch_1_fun.7.refs_0_), channel_id=1, source_target_pairs={{0,24},{4,28},{8,0},{12,4},{16,8},{20,12},{24,16},{28,20},{1,25},{... | collective-permute-start | bytes 983048 | tf_op jit(solution)/shard_map/cond/branch_1_fun/ppermute | solution.py:457
  29.4 0.5 collective-permute-start.26
  29.9 1.6 %collective-permute-start.28 = (f32[10,32,256]{2,1,0:T(8,128)S(1)}, f32[10,32,256]{2,1,0:T(8,128)S(1)}, u32[]{:S(2)}, u32[]{:S(2)}) collective-permute-start(f32[10,32,256]{2,1,0:T(8,128)S(1)} %branch_1_fun.7.refs_0_), channel_id=1, source_target_pairs={{0,16},{4,20},{8,24},{12,28},{16,0},{20,4},{24,8},{28,12},{1,17},{... | collective-permute-start | bytes 983048 | tf_op jit(solution)/shard_map/cond/branch_1_fun/ppermute | solution.py:457
  31.5 0.0 collective-permute-done.24.refs_1_
  31.5 4.2 %collective-permute-done.22.refs_1_.refs_4_ = f32[10,32,256]{2,1,0:T(8,128)S(1)} collective-permute-done((f32[10,32,256]{2,1,0:T(8,128)S(1)}, f32[10,32,256]{2,1,0:T(8,128)S(1)}, u32[]{:S(2)}, u32[]{:S(2)}) %collective-permute-start.22) | collective-permute-done | bytes 327712 | tf_op jit(solution)/shard_map/cond/branch_1_fun/ppermute | solution.py:457
  35.8 0.0 collective-permute-done.26.refs_3_
  35.8 6.9 %branch_1_fun.8.w_ref = f32[512,512]{1,0:T(8,128)S(1)} custom-call(s32[2]{0:T(128)S(1)} %get-tuple-element.69.where_ref, f32[8,16,512]{2,1,0:T(8,128)S(1)} %broadcast_select_fusion.3.refs_0_, f32[8,16,512]{2,1,0:T(8,128)S(1)} %collective-permute-done.24.refs_1_, f32[8,16,512]{2,1,0:T(8,128)S(1)} %collective-permute-done.25.refs_2_, ...), custom_call_target="tpu_custom_call" | custom-call | tf_op jit(solution)/shard_map/cond/branch_1_fun/pallas_call | solution.py:105
  42.7 4.9 %collective-permute-done.28.refs_2_.refs_8_ = f32[10,32,256]{2,1,0:T(8,128)S(1)} collective-permute-done((f32[10,32,256]{2,1,0:T(8,128)S(1)}, f32[10,32,256]{2,1,0:T(8,128)S(1)}, u32[]{:S(2)}, u32[]{:S(2)}) %collective-permute-start.28) | collective-permute-done | bytes 327712 | tf_op jit(solution)/shard_map/cond/branch_1_fun/ppermute | solution.py:457
  47.5 2.0 %collective-permute-start.29 = (f32[10,32,256]{2,1,0:T(8,128)S(1)}, f32[10,32,256]{2,1,0:T(8,128)S(1)}, u32[]{:S(2)}, u32[]{:S(2)}) collective-permute-start(f32[10,32,256]{2,1,0:T(8,128)S(1)} %branch_1_fun.7.refs_0_), channel_id=1, source_target_pairs={{0,8},{4,12},{8,16},{12,20},{16,24},{20,28},{24,0},{28,4},{1,9},{5... | collective-permute-start | bytes 983048 | tf_op jit(solution)/shard_map/cond/branch_1_fun/ppermute | solution.py:457
  49.5 0.5 collective-permute-start.30
  50.0 2.1 %branch_1_fun.9 = f32[2,6,32,256]{3,2,1,0:T(8,128)S(1)} custom-call(s32[2]{0:T(128)S(1)} %get-tuple-element.69.where_ref, s32[96]{0:T(128)S(1)} %get-tuple-element.87.fill_ref, f32[10,32,256]{2,1,0:T(8,128)S(1)} %branch_1_fun.7.refs_0_, f32[10,32,256]{2,1,0:T(8,128)S(1)} %collective-permute-done.22.refs_1_.refs_4_, ...), custom_call_target="tpu_custom_call" | custom-call | tf_op jit(solution)/shard_map/cond/branch_1_fun/pallas_call | solution.py:262
  52.1 3.3 %collective-permute-start.31 = (f32[2,6,32,256]{3,2,1,0:T(8,128)S(1)}, f32[2,6,32,256]{3,2,1,0:T(8,128)}, u32[]{:S(2)}, u32[]{:S(2)}) collective-permute-start(f32[2,6,32,256]{3,2,1,0:T(8,128)S(1)} %branch_1_fun.9), channel_id=1, source_target_pairs={{0,2},{1,3},{4,6},{5,7},{8,10},{9,11},{12,14},{13,15},{16,18},{17,... | collective-permute-start | bytes 1179656 | tf_op jit(solution)/shard_map/cond/branch_1_fun/ppermute | solution.py:468
  55.4 4.8 %collective-permute-done.29.refs_12_ = f32[10,32,256]{2,1,0:T(8,128)S(1)} collective-permute-done((f32[10,32,256]{2,1,0:T(8,128)S(1)}, f32[10,32,256]{2,1,0:T(8,128)S(1)}, u32[]{:S(2)}, u32[]{:S(2)}) %collective-permute-start.29) | collective-permute-done | bytes 327712 | tf_op jit(solution)/shard_map/cond/branch_1_fun/ppermute | solution.py:457
  60.2 0.0 collective-permute-done.30.refs_10_
  60.2 1.6 %branch_1_fun.10.slot_ref = s32[48]{0:T(128)} custom-call(s32[2]{0:T(128)S(1)} %get-tuple-element.69.where_ref, s32[96]{0:T(128)S(1)} %get-tuple-element.87.fill_ref), custom_call_target="tpu_custom_call" | custom-call | flops 20000000000 | bytes 60000000 | tf_op jit(solution)/shard_map/cond/branch_1_fun/pallas_call | solution.py:316
  61.8 0.0 copy-start.5
  61.9 0.8 collective-permute-done.31
  62.7 0.1 broadcast_select_fusion.2
  62.8 1.4 %collective-permute-start.34 = (f32[6,32,256]{2,1,0:T(8,128)S(1)}, f32[6,32,256]{2,1,0:T(8,128)S(1)}, u32[]{:S(2)}, u32[]{:S(2)}) collective-permute-start(f32[6,32,256]{2,1,0:T(8,128)S(1)} %get-tuple-element.133), channel_id=1, source_target_pairs={{0,4},{4,0},{8,12},{12,8},{16,20},{20,16},{24,28},{28,24},{1,5},{5... | collective-permute-start | bytes 589832 | tf_op jit(solution)/shard_map/cond/branch_1_fun/ppermute | solution.py:443
  64.2 0.7 collective-permute-start.32
  64.9 0.2 collective-permute-start.37
  65.1 0.3 collective-permute-start.39
  65.4 4.4 %collective-permute-done.34.refs_2_ = f32[6,32,256]{2,1,0:T(8,128)S(1)} collective-permute-done((f32[6,32,256]{2,1,0:T(8,128)S(1)}, f32[6,32,256]{2,1,0:T(8,128)S(1)}, u32[]{:S(2)}, u32[]{:S(2)}) %collective-permute-start.34) | collective-permute-done | bytes 196640 | tf_op jit(solution)/shard_map/cond/branch_1_fun/ppermute | solution.py:443
  69.8 0.0 collective-permute-start.38
  69.8 0.5 collective-permute-start.35
  70.3 2.8 %branch_1_fun.12 = f32[384,512]{1,0:T(8,128)} custom-call(s32[2]{0:T(128)S(1)} %get-tuple-element.69.where_ref, s32[96]{0:T(128)S(1)} %get-tuple-element.87.fill_ref, f32[512,512]{1,0:T(8,128)S(1)} %branch_1_fun.8.w_ref, f32[384,512]{1,0:T(8,128)} %get-tuple-element.94.panel_ref), custom_call_target="tpu_custom_call" | custom-call | tf_op jit(solution)/shard_map/cond/branch_1_fun/pallas_call | solution.py:285
  73.2 0.1 collective-permute-start.36
  73.2 3.2 %branch_1_fun.11.column_ref = f32[512,512]{1,0:T(8,128)S(1)} custom-call(s32[2]{0:T(128)S(1)} %get-tuple-element.69.where_ref, s32[96]{0:T(128)S(1)} %get-tuple-element.87.fill_ref, f32[512,512]{1,0:T(8,128)S(1)} %branch_1_fun.8.w_ref, f32[6,32,256]{2,1,0:T(8,128)S(1)} %get-tuple-element.134.refs_0_, f32[6,32,256]{2,1,0:T(8,128)S(1)} %collective-permute-done.33.refs_1_, ...), custom_call_target="tpu_custom_call" | custom-call | tf_op jit(solution)/shard_map/cond/branch_1_fun/pallas_call | solution.py:353
  76.4 0.0 collective-permute-done.32.refs_14_
  76.4 0.6 collective-permute-start.40
  77.0 0.1 collective-permute-start.41
  77.1 0.4 collective-permute-start.42
  77.5 0.1 collective-permute-start.43
  77.6 0.6 collective-permute-done.40.refs_9_
  78.2 0.7 collective-permute-done.41.refs_11_
  78.9 0.3 collective-permute-done.42.refs_13_
  79.2 0.5 collective-permute-done.43.refs_15_
  79.7 6.8 %branch_1_fun.13 = f32[3072,512]{1,0:T(8,128)} custom-call(s32[2]{0:T(128)S(1)} %get-tuple-element.69.where_ref, s32[48]{0:T(128)S(1)} %copy-done.5, f32[512,512]{1,0:T(8,128)S(1)} %branch_1_fun.11.column_ref, f32[3072,512]{1,0:T(8,128)} %get-tuple-element.122.window_ref, f32[10,32,256]{2,1,0:T(8,128)S(1)} %branch_1_fun.7.refs_0_, ...), custom_call_target="tpu_custom_call" | custom-call | tf_op jit(solution)/shard_map/cond/branch_1_fun/pallas_call | solution.py:426
  (19 shorter events, 0.1 us)
Async XLA Ops:
  0.6 1.8 %copy-start = (f32[64,512]{1,0:T(8,128)S(1)}, f32[64,512]{1,0:T(8,128)}, u32[]{:S(2)}) copy-start(f32[64,512]{1,0:T(8,128)} %param.8) | copy-start | bytes 393220
  1.9 5.1 %collective-permute-start.44 = (f32[3,2,32,512]{3,2,1,0:T(8,128)S(1)}, f32[3,2,32,512]{3,2,1,0:T(8,128)S(1)}, u32[]{:S(2)}, u32[]{:S(2)}) collective-permute-start(f32[3,2,32,512]{3,2,1,0:T(8,128)S(1)} %get-tuple-element.136), channel_id=1, source_target_pairs={{0,1},{1,0},{2,3},{3,2},{4,5},{5,4},{6,7},{7,6},{8,9},{9,8},{10,11... | collective-permute-start | bytes 1179656 | tf_op jit(solution)/shard_map/ppermute | solution.py:443
  2.4 4.5 %collective-permute-start.45 = (f32[1,16,512]{2,1,0:T(8,128)S(1)}, f32[1,16,512]{2,1,0:T(8,128)S(1)}, u32[]{:S(2)}, u32[]{:S(2)}) collective-permute-start(f32[1,16,512]{2,1,0:T(8,128)S(1)} %dynamic-slice_bitcast_fusion.6), channel_id=1, source_target_pairs={{0,4},{4,0},{8,12},{12,8},{16,20},{20,16},{24,28},{28,24},{1,5},{5... | collective-permute-start | bytes 98312 | tf_op jit(solution)/shard_map/ppermute | solution.py:443
  7.0 4.4 %collective-permute-start.47 = (f32[2,16,512]{2,1,0:T(8,128)S(1)}, f32[2,16,512]{2,1,0:T(8,128)S(1)}, u32[]{:S(2)}, u32[]{:S(2)}) collective-permute-start(f32[2,16,512]{2,1,0:T(8,128)S(1)} %maximum_select_fusion.1), channel_id=1, source_target_pairs={{0,8},{4,12},{8,0},{12,4},{16,24},{20,28},{24,16},{28,20},{1,9},{5... | collective-permute-start | bytes 196616 | tf_op jit(solution)/shard_map/ppermute | solution.py:443
  9.2 10.1 %collective-permute-start.46 = (f32[2,3,32,512]{3,2,1,0:T(8,128)S(1)}, f32[2,3,32,512]{3,2,1,0:T(8,128)S(1)}, u32[]{:S(2)}, u32[]{:S(2)}) collective-permute-start(f32[2,3,32,512]{3,2,1,0:T(8,128)S(1)} %fusion.1), channel_id=1, source_target_pairs={{0,4},{4,0},{8,12},{12,8},{16,20},{20,16},{24,28},{28,24},{1,5},{5... | collective-permute-start | bytes 1179656 | tf_op jit(solution)/shard_map/ppermute | solution.py:443
  11.4 7.8 %collective-permute-start.48 = (f32[4,16,512]{2,1,0:T(8,128)S(1)}, f32[4,16,512]{2,1,0:T(8,128)S(1)}, u32[]{:S(2)}, u32[]{:S(2)}) collective-permute-start(f32[4,16,512]{2,1,0:T(8,128)S(1)} %maximum_select_fusion), channel_id=1, source_target_pairs={{0,16},{4,20},{8,24},{12,28},{16,0},{20,4},{24,8},{28,12},{1,17},{... | collective-permute-start | bytes 393224 | tf_op jit(solution)/shard_map/ppermute | solution.py:443
  19.5 0.7 copy-start.7
  19.5 0.8 copy-start.8
  22.8 6.6 %collective-permute-start.25 = (f32[8,16,512]{2,1,0:T(8,128)S(1)}, f32[8,16,512]{2,1,0:T(8,128)S(1)}, u32[]{:S(2)}, u32[]{:S(2)}) collective-permute-start(f32[8,16,512]{2,1,0:T(8,128)S(1)} %broadcast_select_fusion.3.refs_0_), channel_id=1, source_target_pairs={{0,2},{1,3},{2,0},{3,1},{4,6},{5,7},{6,4},{7,5},{8,10},{9,11},{10,... | collective-permute-start | bytes 786440 | tf_op jit(solution)/shard_map/cond/branch_1_fun/ppermute | solution.py:443
  24.4 7.2 %collective-permute-start.23 = (f32[10,32,256]{2,1,0:T(8,128)S(1)}, f32[10,32,256]{2,1,0:T(8,128)S(1)}, u32[]{:S(2)}, u32[]{:S(2)}) collective-permute-start(f32[10,32,256]{2,1,0:T(8,128)S(1)} %branch_1_fun.7.refs_0_), channel_id=1, source_target_pairs={{0,4},{4,0},{8,12},{12,8},{16,20},{20,16},{24,28},{28,24},{1,5},{5... | collective-permute-start | bytes 983048 | tf_op jit(solution)/shard_map/cond/branch_1_fun/ppermute | solution.py:443
  25.9 9.9 %collective-permute-start.22 = (f32[10,32,256]{2,1,0:T(8,128)S(1)}, f32[10,32,256]{2,1,0:T(8,128)S(1)}, u32[]{:S(2)}, u32[]{:S(2)}) collective-permute-start(f32[10,32,256]{2,1,0:T(8,128)S(1)} %branch_1_fun.7.refs_0_), channel_id=1, source_target_pairs={{0,24},{4,28},{8,0},{12,4},{16,8},{20,12},{24,16},{28,20},{1,25},{... | collective-permute-start | bytes 983048 | tf_op jit(solution)/shard_map/cond/branch_1_fun/ppermute | solution.py:457
  29.4 2.2 %collective-permute-start.24 = (f32[8,16,512]{2,1,0:T(8,128)S(1)}, f32[8,16,512]{2,1,0:T(8,128)S(1)}, u32[]{:S(2)}, u32[]{:S(2)}) collective-permute-start(f32[8,16,512]{2,1,0:T(8,128)S(1)} %broadcast_select_fusion.3.refs_0_), channel_id=1, source_target_pairs={{0,1},{1,0},{2,3},{3,2},{4,5},{5,4},{6,7},{7,6},{8,9},{9,8},{10,11... | collective-permute-start | bytes 786440 | tf_op jit(solution)/shard_map/cond/branch_1_fun/ppermute | solution.py:443
  29.4 6.4 %collective-permute-start.26 = (f32[8,16,512]{2,1,0:T(8,128)S(1)}, f32[8,16,512]{2,1,0:T(8,128)S(1)}, u32[]{:S(2)}, u32[]{:S(2)}) collective-permute-start(f32[8,16,512]{2,1,0:T(8,128)S(1)} %collective-permute-done.25.refs_2_), channel_id=1, source_target_pairs={{0,1},{1,0},{2,3},{3,2},{4,5},{5,4},{6,7},{7,6},{8,9},{9,8},{10,11... | collective-permute-start | bytes 786440 | tf_op jit(solution)/shard_map/cond/branch_1_fun/ppermute | solution.py:443
  29.9 17.6 %collective-permute-start.28 = (f32[10,32,256]{2,1,0:T(8,128)S(1)}, f32[10,32,256]{2,1,0:T(8,128)S(1)}, u32[]{:S(2)}, u32[]{:S(2)}) collective-permute-start(f32[10,32,256]{2,1,0:T(8,128)S(1)} %branch_1_fun.7.refs_0_), channel_id=1, source_target_pairs={{0,16},{4,20},{8,24},{12,28},{16,0},{20,4},{24,8},{28,12},{1,17},{... | collective-permute-start | bytes 983048 | tf_op jit(solution)/shard_map/cond/branch_1_fun/ppermute | solution.py:457
  35.8 11.8 %collective-permute-start.27 = (f32[10,32,256]{2,1,0:T(8,128)S(1)}, f32[10,32,256]{2,1,0:T(8,128)S(1)}, u32[]{:S(2)}, u32[]{:S(2)}) collective-permute-start(f32[10,32,256]{2,1,0:T(8,128)S(1)} %collective-permute-done.22.refs_1_.refs_4_), channel_id=1, source_target_pairs={{0,4},{4,0},{8,12},{12,8},{16,20},{20,16},{24,28},{28,24},{1,5},{5... | collective-permute-start | bytes 983048 | tf_op jit(solution)/shard_map/cond/branch_1_fun/ppermute | solution.py:443
  47.5 12.7 %collective-permute-start.29 = (f32[10,32,256]{2,1,0:T(8,128)S(1)}, f32[10,32,256]{2,1,0:T(8,128)S(1)}, u32[]{:S(2)}, u32[]{:S(2)}) collective-permute-start(f32[10,32,256]{2,1,0:T(8,128)S(1)} %branch_1_fun.7.refs_0_), channel_id=1, source_target_pairs={{0,8},{4,12},{8,16},{12,20},{16,24},{20,28},{24,0},{28,4},{1,9},{5... | collective-permute-start | bytes 983048 | tf_op jit(solution)/shard_map/cond/branch_1_fun/ppermute | solution.py:457
  49.5 10.7 %collective-permute-start.30 = (f32[10,32,256]{2,1,0:T(8,128)S(1)}, f32[10,32,256]{2,1,0:T(8,128)}, u32[]{:S(2)}, u32[]{:S(2)}) collective-permute-start(f32[10,32,256]{2,1,0:T(8,128)S(1)} %collective-permute-done.28.refs_2_.refs_8_), channel_id=1, source_target_pairs={{0,4},{4,0},{8,12},{12,8},{16,20},{20,16},{24,28},{28,24},{1,5},{5... | collective-permute-start | bytes 983048 | tf_op jit(solution)/shard_map/cond/branch_1_fun/ppermute | solution.py:443
  52.1 10.6 %collective-permute-start.31 = (f32[2,6,32,256]{3,2,1,0:T(8,128)S(1)}, f32[2,6,32,256]{3,2,1,0:T(8,128)}, u32[]{:S(2)}, u32[]{:S(2)}) collective-permute-start(f32[2,6,32,256]{3,2,1,0:T(8,128)S(1)} %branch_1_fun.9), channel_id=1, source_target_pairs={{0,2},{1,3},{4,6},{5,7},{8,10},{9,11},{12,14},{13,15},{16,18},{17,... | collective-permute-start | bytes 1179656 | tf_op jit(solution)/shard_map/cond/branch_1_fun/ppermute | solution.py:468
  61.8 17.8 %copy-start.5 = (s32[48]{0:T(128)S(1)}, s32[48]{0:T(128)}, u32[]{:S(2)}) copy-start(s32[48]{0:T(128)} %branch_1_fun.10.slot_ref) | copy-start | bytes 580 | tf_op jit(solution)/shard_map/cond
  62.8 7.0 %collective-permute-start.34 = (f32[6,32,256]{2,1,0:T(8,128)S(1)}, f32[6,32,256]{2,1,0:T(8,128)S(1)}, u32[]{:S(2)}, u32[]{:S(2)}) collective-permute-start(f32[6,32,256]{2,1,0:T(8,128)S(1)} %get-tuple-element.133), channel_id=1, source_target_pairs={{0,4},{4,0},{8,12},{12,8},{16,20},{20,16},{24,28},{28,24},{1,5},{5... | collective-permute-start | bytes 589832 | tf_op jit(solution)/shard_map/cond/branch_1_fun/ppermute | solution.py:443
  64.2 5.6 %collective-permute-start.33 = (f32[6,32,256]{2,1,0:T(8,128)S(1)}, f32[6,32,256]{2,1,0:T(8,128)S(1)}, u32[]{:S(2)}, u32[]{:S(2)}) collective-permute-start(f32[6,32,256]{2,1,0:T(8,128)S(1)} %get-tuple-element.134.refs_0_), channel_id=1, source_target_pairs={{0,1},{1,0},{2,3},{3,2},{4,5},{5,4},{6,7},{7,6},{8,9},{9,8},{10,11... | collective-permute-start | bytes 589832 | tf_op jit(solution)/shard_map/cond/branch_1_fun/ppermute | solution.py:443
  64.2 12.2 %collective-permute-start.32 = (f32[10,32,256]{2,1,0:T(8,128)S(1)}, f32[10,32,256]{2,1,0:T(8,128)S(1)}, u32[]{:S(2)}, u32[]{:S(2)}) collective-permute-start(f32[10,32,256]{2,1,0:T(8,128)S(1)} %collective-permute-done.29.refs_12_), channel_id=1, source_target_pairs={{0,4},{4,0},{8,12},{12,8},{16,20},{20,16},{24,28},{28,24},{1,5},{5... | collective-permute-start | bytes 983048 | tf_op jit(solution)/shard_map/cond/branch_1_fun/ppermute | solution.py:443
  64.9 12.1 %collective-permute-start.37 = (f32[10,32,256]{2,1,0:T(8,128)S(1)}, f32[10,32,256]{2,1,0:T(8,128)S(1)}, u32[]{:S(2)}, u32[]{:S(2)}) collective-permute-start(f32[10,32,256]{2,1,0:T(8,128)S(1)} %collective-permute-done.23.refs_2_), channel_id=1, source_target_pairs={{0,1},{1,0},{2,3},{3,2},{4,5},{5,4},{6,7},{7,6},{8,9},{9,8},{10,11... | collective-permute-start | bytes 983048 | tf_op jit(solution)/shard_map/cond/branch_1_fun/ppermute | solution.py:443
  65.1 12.0 %collective-permute-start.39 = (f32[10,32,256]{2,1,0:T(8,128)S(1)}, f32[10,32,256]{2,1,0:T(8,128)S(1)}, u32[]{:S(2)}, u32[]{:S(2)}) collective-permute-start(f32[10,32,256]{2,1,0:T(8,128)S(1)} %collective-permute-done.27.refs_6_), channel_id=1, source_target_pairs={{0,1},{1,0},{2,3},{3,2},{4,5},{5,4},{6,7},{7,6},{8,9},{9,8},{10,11... | collective-permute-start | bytes 983048 | tf_op jit(solution)/shard_map/cond/branch_1_fun/ppermute | solution.py:443
  69.8 7.7 %collective-permute-start.38 = (f32[10,32,256]{2,1,0:T(8,128)S(1)}, f32[10,32,256]{2,1,0:T(8,128)S(1)}, u32[]{:S(2)}, u32[]{:S(2)}) collective-permute-start(f32[10,32,256]{2,1,0:T(8,128)S(1)} %collective-permute-done.22.refs_1_.refs_4_), channel_id=1, source_target_pairs={{0,1},{1,0},{2,3},{3,2},{4,5},{5,4},{6,7},{7,6},{8,9},{9,8},{10,11... | collective-permute-start | bytes 983048 | tf_op jit(solution)/shard_map/cond/branch_1_fun/ppermute | solution.py:443
  69.8 3.4 %collective-permute-start.35 = (f32[6,32,256]{2,1,0:T(8,128)S(1)}, f32[6,32,256]{2,1,0:T(8,128)S(1)}, u32[]{:S(2)}, u32[]{:S(2)}) collective-permute-start(f32[6,32,256]{2,1,0:T(8,128)S(1)} %collective-permute-done.34.refs_2_), channel_id=1, source_target_pairs={{0,1},{1,0},{2,3},{3,2},{4,5},{5,4},{6,7},{7,6},{8,9},{9,8},{10,11... | collective-permute-start | bytes 589832 | tf_op jit(solution)/shard_map/cond/branch_1_fun/ppermute | solution.py:443
  73.2 4.4 %collective-permute-start.36 = (f32[10,32,256]{2,1,0:T(8,128)S(1)}, f32[10,32,256]{2,1,0:T(8,128)S(1)}, u32[]{:S(2)}, u32[]{:S(2)}) collective-permute-start(f32[10,32,256]{2,1,0:T(8,128)S(1)} %branch_1_fun.7.refs_0_), channel_id=1, source_target_pairs={{0,1},{1,0},{2,3},{3,2},{4,5},{5,4},{6,7},{7,6},{8,9},{9,8},{10,11... | collective-permute-start | bytes 983048 | tf_op jit(solution)/shard_map/cond/branch_1_fun/ppermute | solution.py:443
  76.4 1.8 %collective-permute-start.40 = (f32[10,32,256]{2,1,0:T(8,128)S(1)}, f32[10,32,256]{2,1,0:T(8,128)S(1)}, u32[]{:S(2)}, u32[]{:S(2)}) collective-permute-start(f32[10,32,256]{2,1,0:T(8,128)S(1)} %collective-permute-done.28.refs_2_.refs_8_), channel_id=1, source_target_pairs={{0,1},{1,0},{2,3},{3,2},{4,5},{5,4},{6,7},{7,6},{8,9},{9,8},{10,11... | collective-permute-start | bytes 983048 | tf_op jit(solution)/shard_map/cond/branch_1_fun/ppermute | solution.py:443
  77.0 1.9 %collective-permute-start.41 = (f32[10,32,256]{2,1,0:T(8,128)}, f32[10,32,256]{2,1,0:T(8,128)S(1)}, u32[]{:S(2)}, u32[]{:S(2)}) collective-permute-start(f32[10,32,256]{2,1,0:T(8,128)} %collective-permute-done.30.refs_10_), channel_id=1, source_target_pairs={{0,1},{1,0},{2,3},{3,2},{4,5},{5,4},{6,7},{7,6},{8,9},{9,8},{10,11... | collective-permute-start | bytes 983048 | tf_op jit(solution)/shard_map/cond/branch_1_fun/ppermute | solution.py:443
  77.1 2.1 %collective-permute-start.42 = (f32[10,32,256]{2,1,0:T(8,128)S(1)}, f32[10,32,256]{2,1,0:T(8,128)S(1)}, u32[]{:S(2)}, u32[]{:S(2)}) collective-permute-start(f32[10,32,256]{2,1,0:T(8,128)S(1)} %collective-permute-done.29.refs_12_), channel_id=1, source_target_pairs={{0,1},{1,0},{2,3},{3,2},{4,5},{5,4},{6,7},{7,6},{8,9},{9,8},{10,11... | collective-permute-start | bytes 983048 | tf_op jit(solution)/shard_map/cond/branch_1_fun/ppermute | solution.py:443
  77.5 2.1 %collective-permute-start.43 = (f32[10,32,256]{2,1,0:T(8,128)S(1)}, f32[10,32,256]{2,1,0:T(8,128)S(1)}, u32[]{:S(2)}, u32[]{:S(2)}) collective-permute-start(f32[10,32,256]{2,1,0:T(8,128)S(1)} %collective-permute-done.32.refs_14_), channel_id=1, source_target_pairs={{0,1},{1,0},{2,3},{3,2},{4,5},{5,4},{6,7},{7,6},{8,9},{9,8},{10,11... | collective-permute-start | bytes 983048 | tf_op jit(solution)/shard_map/cond/branch_1_fun/ppermute | solution.py:443

commit v8 on v5

--- a/solution.py
+++ b/solution.py
@@ -521,6 +521,8 @@
             lists[s] = lax.optimization_barrier((lists[s], slots, *(sides[j] for j in first)))[0]
             sides[s] = swap(lists[s], "col", 1)
         column = column_factor(sizes, where, fill, w, columns)
+        for s in later:
+            sides[s], column = lax.optimization_barrier((sides[s], column))
         ordered = []
         for s in range(sizes.groups):
             value, other = lists[s], sides[s]

time: 83.6 us -> 82.7 us (0.989)
  the two profiles are of different devices: /device:TPU:31 before, /device:TPU:29 now
where the time goes in v8:
time: 82.7 us; the launch traced here: 82.3 us
  waiting for transfers between devices  33.9 us (41%)
  Pallas kernels  21.6 us (26%)
  starting transfers between devices  21.1 us (26%)
  local copies, waits for them, and re-layouts  2.17 us (3%)
  between operations  1.58 us (2%)
  other arithmetic  1.26 us (2%)
    ppermute x23, starting transfers between devices, swap(): return lax.ppermute(value, axis, [(i, i ^ step) for i in range(size)])  18.4 us
    ppermute x23, waiting for transfers between devices, swap(): return lax.ppermute(value, axis, [(i, i ^ step) for i in range(size)])  12.4 us
    ppermute x3, waiting for transfers between devices, bring(): return lax.ppermute(value, 'col', pairs)  11.2 us
    ppermute x1, waiting for transfers between devices, spread_column(): other = lax.ppermute(value, ('col', 'row'), pairs)  10.2 us
    pallas_call x1, Pallas kernels, inverse_factor(): pl.pallas_call(inverse_factor_kernel, out_shape=jax.ShapeDtypeStruct((n,...  6.89 us
    pallas_call x1, Pallas kernels, own_factor(): pl.pallas_call(functools.partial(own_factor_kernel, sizes), out_shape=(pl...  3.44 us
    pallas_call x1, Pallas kernels, update(): pl.pallas_call(functools.partial(update_kernel, sizes), out_shape=pltpu.H...  3.33 us
    pallas_call x1, Pallas kernels, column_factor(): pl.pallas_call(functools.partial(column_factor_kernel, sizes), out_shape=...  3.16 us
  transfers between devices with their start and end apart: 27, of which 12 were waited for; matrix products, arithmetic and copies ran while one was open for 3% of the time, Pallas kernels for 20%

profile of v8, /device:TPU:29, one launch (start us, length us, event | category | flops | bytes accessed | tf_op | source)
XLA Modules:
  0.0 82.3 jit_solution(1273938485614600176)
XLA Ops:
  0.6 0.0 copy-start
  0.7 1.2 %dynamic-slice_bitcast_fusion.4 = (f32[1,3,2,32,512]{4,3,2,1,0:T(8,128)S(1)}, f32[3,2,32,512]{3,2,1,0:T(8,128)S(1)}) fusion(f32[3,2,2,32,512]{4,3,2,1,0:T(8,128)} %bitcast.27, s32[]{:T(128)S(6)} %select_n.102, s32[]{:T(128)S(6)} %select_n.97), kind=kLoop, calls=%fused_computation.12 | loop fusion | bytes 1572872 | tf_op jit(solution)/shard_map/stack | solution.py:485
  1.9 0.7 collective-permute-start.44
  2.7 1.2 %collective-permute-start.45 = (f32[1,16,512]{2,1,0:T(8,128)S(1)}, f32[1,16,512]{2,1,0:T(8,128)S(1)}, u32[]{:S(2)}, u32[]{:S(2)}) collective-permute-start(f32[1,16,512]{2,1,0:T(8,128)S(1)} %dynamic-slice_bitcast_fusion.6), channel_id=1, source_target_pairs={{0,4},{4,0},{8,12},{12,8},{16,20},{20,16},{24,28},{28,24},{1,5},{5... | collective-permute-start | bytes 98312 | tf_op jit(solution)/shard_map/ppermute | solution.py:434
  3.9 1.6 %collective-permute-done.45 = f32[1,16,512]{2,1,0:T(8,128)S(1)} collective-permute-done((f32[1,16,512]{2,1,0:T(8,128)S(1)}, f32[1,16,512]{2,1,0:T(8,128)S(1)}, u32[]{:S(2)}, u32[]{:S(2)}) %collective-permute-start.45) | collective-permute-done | bytes 32800 | tf_op jit(solution)/shard_map/ppermute | solution.py:434
  5.4 0.0 collective-permute-done.44
  5.4 0.2 collective-permute-start.47
  5.7 1.3 %collective-permute-start.46 = (f32[2,3,32,512]{3,2,1,0:T(8,128)S(1)}, f32[2,3,32,512]{3,2,1,0:T(8,128)S(1)}, u32[]{:S(2)}, u32[]{:S(2)}) collective-permute-start(f32[2,3,32,512]{3,2,1,0:T(8,128)S(1)} %fusion.1), channel_id=1, source_target_pairs={{0,4},{4,0},{8,12},{12,8},{16,20},{20,16},{24,28},{28,24},{1,5},{5... | collective-permute-start | bytes 1179656 | tf_op jit(solution)/shard_map/ppermute | solution.py:434
  7.0 1.6 %collective-permute-done.47 = f32[2,16,512]{2,1,0:T(8,128)S(1)} collective-permute-done((f32[2,16,512]{2,1,0:T(8,128)S(1)}, f32[2,16,512]{2,1,0:T(8,128)S(1)}, u32[]{:S(2)}, u32[]{:S(2)}) %collective-permute-start.47) | collective-permute-done | bytes 65568 | tf_op jit(solution)/shard_map/ppermute | solution.py:434
  8.6 0.1 collective-permute-start.48
  8.8 0.8 copy.13
  9.5 0.1 reshape.18.fill_ref
  9.6 1.2 %shard_map.63 = s32[1]{0:T(128)} custom-call(s32[96]{0:T(128)S(1)} %reshape.18.fill_ref), custom_call_target="tpu_custom_call" | custom-call | tf_op jit(solution)/shard_map/pallas_call | solution.py:181
  11.5 0.1 pad_add_fusion
  11.6 3.1 %collective-permute-done.48 = f32[4,16,512]{2,1,0:T(8,128)S(1)} collective-permute-done((f32[4,16,512]{2,1,0:T(8,128)S(1)}, f32[4,16,512]{2,1,0:T(8,128)S(1)}, u32[]{:S(2)}, u32[]{:S(2)}) %collective-permute-start.48) | collective-permute-done | bytes 131104 | tf_op jit(solution)/shard_map/ppermute | solution.py:434
  14.7 0.1 pad_maximum_fusion.1
  14.8 0.0 collective-permute-done.46
  14.8 67.2 %conditional.1 = (f32[384,512]{1,0:T(8,128)}, f32[3072,512]{1,0:T(8,128)}) conditional(s32[]{:T(128)} %bitcast.6, (s32[2]{0:T(128)S(1)}, s32[96]{0:T(128)S(1)}, f32[384,512]{1,0:T(8,128)}, f32[3,2,32,512]{3,2,1,0:T(8,128)S(1)}, f32[2,3,32,512]{3,2,1,0:T(8,128)S(1)}, /*index=5*/s32[]{:T(128)}, f32[384,512]{1,0:T(8,128)}, s32[]{:T(128)}, ...), branch_computations={%region_0.1_spmd, %region_1.2_spmd} | conditional | flops 196649 | bytes 71566760 | solution.py:533
  15.1 0.3 collective-permute-start.25
  15.4 1.5 %branch_1_fun.6.refs_0_ = f32[10,32,256]{2,1,0:T(8,128)S(1)} custom-call(s32[2]{0:T(128)S(1)} %get-tuple-element.62.where_ref, s32[96]{0:T(128)S(1)} %get-tuple-element.63.fill_ref, f32[3,128,512]{2,1,0:T(8,128)} %bitcast.29, f32[3,2,32,512]{3,2,1,0:T(8,128)S(1)} %get-tuple-element.65.core_ref, f32[2,3,32,512]{3,2,1,0:T(8,128)S(1)} %get-tuple-element.66.side_ref), custom_call_target="tpu_custom_call" | custom-call | tf_op jit(solution)/shard_map/cond/branch_1_fun/pallas_call | solution.py:216
  16.9 1.3 %collective-permute-start.23 = (f32[10,32,256]{2,1,0:T(8,128)S(1)}, f32[10,32,256]{2,1,0:T(8,128)S(1)}, u32[]{:S(2)}, u32[]{:S(2)}) collective-permute-start(f32[10,32,256]{2,1,0:T(8,128)S(1)} %branch_1_fun.6.refs_0_), channel_id=1, source_target_pairs={{0,4},{4,0},{8,12},{12,8},{16,20},{20,16},{24,28},{28,24},{1,5},{5... | collective-permute-start | bytes 983048 | tf_op jit(solution)/shard_map/cond/branch_1_fun/ppermute | solution.py:434
  18.2 1.1 %collective-permute-start.22 = (f32[10,32,256]{2,1,0:T(8,128)S(1)}, f32[10,32,256]{2,1,0:T(8,128)S(1)}, u32[]{:S(2)}, u32[]{:S(2)}) collective-permute-start(f32[10,32,256]{2,1,0:T(8,128)S(1)} %branch_1_fun.6.refs_0_), channel_id=1, source_target_pairs={{0,24},{4,28},{8,0},{12,4},{16,8},{20,12},{24,16},{28,20},{1,25},{... | collective-permute-start | bytes 983048 | tf_op jit(solution)/shard_map/cond/branch_1_fun/ppermute | solution.py:448
  19.2 3.3 %collective-permute-start.24 = (f32[8,16,512]{2,1,0:T(8,128)S(1)}, f32[8,16,512]{2,1,0:T(8,128)S(1)}, u32[]{:S(2)}, u32[]{:S(2)}) collective-permute-start(f32[8,16,512]{2,1,0:T(8,128)S(1)} %broadcast_select_fusion.3.refs_0_), channel_id=1, source_target_pairs={{0,1},{1,0},{2,3},{3,2},{4,5},{5,4},{6,7},{7,6},{8,9},{9,8},{10,11... | collective-permute-start | bytes 786440 | tf_op jit(solution)/shard_map/cond/branch_1_fun/ppermute | solution.py:434
  22.6 0.0 collective-permute-done.25.refs_2_
  22.6 2.5 %collective-permute-start.26 = (f32[8,16,512]{2,1,0:T(8,128)S(1)}, f32[8,16,512]{2,1,0:T(8,128)S(1)}, u32[]{:S(2)}, u32[]{:S(2)}) collective-permute-start(f32[8,16,512]{2,1,0:T(8,128)S(1)} %collective-permute-done.25.refs_2_), channel_id=1, source_target_pairs={{0,1},{1,0},{2,3},{3,2},{4,5},{5,4},{6,7},{7,6},{8,9},{9,8},{10,11... | collective-permute-start | bytes 786440 | tf_op jit(solution)/shard_map/cond/branch_1_fun/ppermute | solution.py:434
  25.1 0.0 collective-permute-start.28
  25.1 0.8 collective-permute-done.22.refs_1_.refs_4_
  25.9 0.4 collective-permute-done.26.refs_3_
  26.3 1.2 %collective-permute-start.27 = (f32[10,32,256]{2,1,0:T(8,128)S(1)}, f32[10,32,256]{2,1,0:T(8,128)S(1)}, u32[]{:S(2)}, u32[]{:S(2)}) collective-permute-start(f32[10,32,256]{2,1,0:T(8,128)S(1)} %collective-permute-done.22.refs_1_.refs_4_), channel_id=1, source_target_pairs={{0,4},{4,0},{8,12},{12,8},{16,20},{20,16},{24,28},{28,24},{1,5},{5... | collective-permute-start | bytes 983048 | tf_op jit(solution)/shard_map/cond/branch_1_fun/ppermute | solution.py:434
  27.5 6.9 %branch_1_fun.7.w_ref = f32[512,512]{1,0:T(8,128)S(1)} custom-call(s32[2]{0:T(128)S(1)} %get-tuple-element.62.where_ref, f32[8,16,512]{2,1,0:T(8,128)S(1)} %broadcast_select_fusion.3.refs_0_, f32[8,16,512]{2,1,0:T(8,128)S(1)} %collective-permute-done.24.refs_1_, f32[8,16,512]{2,1,0:T(8,128)S(1)} %collective-permute-done.25.refs_2_, ...), custom_call_target="tpu_custom_call" | custom-call | tf_op jit(solution)/shard_map/cond/branch_1_fun/pallas_call | solution.py:105
  34.4 10.4 %collective-permute-done.28.refs_2_.refs_8_ = f32[10,32,256]{2,1,0:T(8,128)S(1)} collective-permute-done((f32[10,32,256]{2,1,0:T(8,128)S(1)}, f32[10,32,256]{2,1,0:T(8,128)S(1)}, u32[]{:S(2)}, u32[]{:S(2)}) %collective-permute-start.28) | collective-permute-done | bytes 327712 | tf_op jit(solution)/shard_map/cond/branch_1_fun/ppermute | solution.py:448
  44.8 2.0 %branch_1_fun.9 = f32[2,6,32,256]{3,2,1,0:T(8,128)S(1)} custom-call(s32[2]{0:T(128)S(1)} %get-tuple-element.62.where_ref, s32[96]{0:T(128)S(1)} %get-tuple-element.63.fill_ref, f32[10,32,256]{2,1,0:T(8,128)S(1)} %branch_1_fun.6.refs_0_, f32[10,32,256]{2,1,0:T(8,128)S(1)} %collective-permute-done.22.refs_1_.refs_4_, ...), custom_call_target="tpu_custom_call" | custom-call | tf_op jit(solution)/shard_map/cond/branch_1_fun/pallas_call | solution.py:262
  46.8 1.3 %collective-permute-start.32 = (f32[2,6,32,256]{3,2,1,0:T(8,128)S(1)}, f32[2,6,32,256]{3,2,1,0:T(8,128)}, u32[]{:S(2)}, u32[]{:S(2)}) collective-permute-start(f32[2,6,32,256]{3,2,1,0:T(8,128)S(1)} %branch_1_fun.9), channel_id=1, source_target_pairs={{0,2},{1,3},{4,6},{5,7},{8,10},{9,11},{12,14},{13,15},{16,18},{17,... | collective-permute-start | bytes 1179656 | tf_op jit(solution)/shard_map/cond/branch_1_fun/ppermute | solution.py:459
  48.2 0.0 copy-start.5
  48.2 0.3 collective-permute-start.29
  48.5 0.3 collective-permute-start.30
  48.9 10.2 %collective-permute-done.32 = f32[2,6,32,256]{3,2,1,0:T(8,128)} collective-permute-done((f32[2,6,32,256]{3,2,1,0:T(8,128)S(1)}, f32[2,6,32,256]{3,2,1,0:T(8,128)}, u32[]{:S(2)}, u32[]{:S(2)}) %collective-permute-start.32) | collective-permute-done | bytes 393248 | tf_op jit(solution)/shard_map/cond/branch_1_fun/ppermute | solution.py:459
  59.1 1.0 %broadcast_select_fusion.2 = f32[2,6,32,256]{3,2,1,0:T(8,128)S(1)} fusion(f32[2,6,32,256]{3,2,1,0:T(8,128)} %collective-permute-done.32, f32[2,6,32,256]{3,2,1,0:T(8,128)S(1)} %branch_1_fun.9, pred[]{:T(512)S(6)} %ne.51), kind=kLoop, calls=%fused_computation.6 | loop fusion | flops 98304 | bytes 1179649 | tf_op jit(solution)/shard_map/cond/branch_1_fun/jit(_where)/select_n | solution.py:460
  60.2 0.3 collective-permute-start.34
  60.5 1.6 %collective-permute-start.33 = (f32[6,32,256]{2,1,0:T(8,128)S(1)}, f32[6,32,256]{2,1,0:T(8,128)S(1)}, u32[]{:S(2)}, u32[]{:S(2)}) collective-permute-start(f32[6,32,256]{2,1,0:T(8,128)S(1)} %get-tuple-element.120.refs_0_), channel_id=1, source_target_pairs={{0,1},{1,0},{2,3},{3,2},{4,5},{5,4},{6,7},{7,6},{8,9},{9,8},{10,11... | collective-permute-start | bytes 589832 | tf_op jit(solution)/shard_map/cond/branch_1_fun/ppermute | solution.py:434
  62.1 3.4 %branch_1_fun.8 = (f32[384,512]{1,0:T(8,128)}, s32[48]{0:T(128)S(1)}) custom-call(s32[2]{0:T(128)S(1)} %get-tuple-element.62.where_ref, s32[96]{0:T(128)S(1)} %get-tuple-element.63.fill_ref, f32[512,512]{1,0:T(8,128)S(1)} %branch_1_fun.7.w_ref, f32[384,512]{1,0:T(8,128)} %get-tuple-element.75.panel_ref), custom_call_target="tpu_custom_call" | custom-call | tf_op jit(solution)/shard_map/cond/branch_1_fun/pallas_call | solution.py:303
  65.5 0.0 collective-permute-done.29.refs_12_
  65.5 0.0 collective-permute-done.30.refs_10_
  65.5 1.3 %collective-permute-start.31 = (f32[10,32,256]{2,1,0:T(8,128)S(1)}, f32[10,32,256]{2,1,0:T(8,128)S(1)}, u32[]{:S(2)}, u32[]{:S(2)}) collective-permute-start(f32[10,32,256]{2,1,0:T(8,128)S(1)} %collective-permute-done.29.refs_12_), channel_id=1, source_target_pairs={{0,4},{4,0},{8,12},{12,8},{16,20},{20,16},{24,28},{28,24},{1,5},{5... | collective-permute-start | bytes 983048 | tf_op jit(solution)/shard_map/cond/branch_1_fun/ppermute | solution.py:434
  66.8 0.3 collective-permute-start.37
  67.1 0.2 collective-permute-start.39
  67.3 0.0 collective-permute-done.34.refs_2_
  67.3 0.3 collective-permute-start.38
  67.6 0.0 collective-permute-done.33.refs_1_
  67.6 0.2 collective-permute-start.35
  67.9 1.8 %collective-permute-done.35.refs_3_ = f32[6,32,256]{2,1,0:T(8,128)S(1)} collective-permute-done((f32[6,32,256]{2,1,0:T(8,128)S(1)}, f32[6,32,256]{2,1,0:T(8,128)S(1)}, u32[]{:S(2)}, u32[]{:S(2)}) %collective-permute-start.35) | collective-permute-done | bytes 196640 | tf_op jit(solution)/shard_map/cond/branch_1_fun/ppermute | solution.py:434
  69.7 0.3 collective-permute-start.36
  69.9 3.2 %branch_1_fun.10.column_ref = f32[512,512]{1,0:T(8,128)S(1)} custom-call(s32[2]{0:T(128)S(1)} %get-tuple-element.62.where_ref, s32[96]{0:T(128)S(1)} %get-tuple-element.63.fill_ref, f32[512,512]{1,0:T(8,128)S(1)} %branch_1_fun.7.w_ref, f32[6,32,256]{2,1,0:T(8,128)S(1)} %get-tuple-element.120.refs_0_, f32[6,32,256]{2,1,0:T(8,128)S(1)} %collective-permute-done.33.refs_1_, ...), custom_call_target="tpu_custom_call" | custom-call | tf_op jit(solution)/shard_map/cond/branch_1_fun/pallas_call | solution.py:344
  73.1 1.8 %collective-permute-done.31.refs_14_ = f32[10,32,256]{2,1,0:T(8,128)S(1)} collective-permute-done((f32[10,32,256]{2,1,0:T(8,128)S(1)}, f32[10,32,256]{2,1,0:T(8,128)S(1)}, u32[]{:S(2)}, u32[]{:S(2)}) %collective-permute-start.31) | collective-permute-done | bytes 327712 | tf_op jit(solution)/shard_map/cond/branch_1_fun/ppermute | solution.py:434
  75.0 0.8 collective-permute-start.40
  75.7 0.0 collective-permute-start.42
  75.7 0.5 collective-permute-start.41
  76.3 0.1 collective-permute-start.43
  76.3 0.0 collective-permute-done.36.refs_1_
  76.3 0.7 collective-permute-done.40.refs_9_
  77.0 0.9 %collective-permute-done.41.refs_11_ = f32[10,32,256]{2,1,0:T(8,128)S(1)} collective-permute-done((f32[10,32,256]{2,1,0:T(8,128)S(1)}, f32[10,32,256]{2,1,0:T(8,128)S(1)}, u32[]{:S(2)}, u32[]{:S(2)}) %collective-permute-start.41) | collective-permute-done | bytes 327712 | tf_op jit(solution)/shard_map/cond/branch_1_fun/ppermute | solution.py:434
  77.9 0.0 collective-permute-done.42.refs_13_
  77.9 0.5 collective-permute-done.43.refs_15_
  78.4 3.3 %branch_1_fun.11 = f32[3072,512]{1,0:T(8,128)} custom-call(s32[2]{0:T(128)S(1)} %get-tuple-element.62.where_ref, s32[48]{0:T(128)S(1)} %get-tuple-element.76.slot_ref, f32[512,512]{1,0:T(8,128)S(1)} %branch_1_fun.10.column_ref, f32[3072,512]{1,0:T(8,128)S(1)} %copy-done.5, f32[10,32,256]{2,1,0:T(8,128)S(1)} %branch_1_fun.6.refs_0_, ...), custom_call_target="tpu_custom_call" | custom-call | tf_op jit(solution)/shard_map/cond/branch_1_fun/pallas_call | solution.py:417
  (14 shorter events, 0.1 us)
Async XLA Ops:
  0.6 2.0 %copy-start = (f32[64,512]{1,0:T(8,128)S(1)}, f32[64,512]{1,0:T(8,128)}, u32[]{:S(2)}) copy-start(f32[64,512]{1,0:T(8,128)} %param.8) | copy-start | bytes 393220
  1.9 3.5 %collective-permute-start.44 = (f32[3,2,32,512]{3,2,1,0:T(8,128)S(1)}, f32[3,2,32,512]{3,2,1,0:T(8,128)S(1)}, u32[]{:S(2)}, u32[]{:S(2)}) collective-permute-start(f32[3,2,32,512]{3,2,1,0:T(8,128)S(1)} %get-tuple-element.122), channel_id=1, source_target_pairs={{0,1},{1,0},{2,3},{3,2},{4,5},{5,4},{6,7},{7,6},{8,9},{9,8},{10,11... | collective-permute-start | bytes 1179656 | tf_op jit(solution)/shard_map/ppermute | solution.py:434
  2.7 2.8 %collective-permute-start.45 = (f32[1,16,512]{2,1,0:T(8,128)S(1)}, f32[1,16,512]{2,1,0:T(8,128)S(1)}, u32[]{:S(2)}, u32[]{:S(2)}) collective-permute-start(f32[1,16,512]{2,1,0:T(8,128)S(1)} %dynamic-slice_bitcast_fusion.6), channel_id=1, source_target_pairs={{0,4},{4,0},{8,12},{12,8},{16,20},{20,16},{24,28},{28,24},{1,5},{5... | collective-permute-start | bytes 98312 | tf_op jit(solution)/shard_map/ppermute | solution.py:434
  5.4 3.2 %collective-permute-start.47 = (f32[2,16,512]{2,1,0:T(8,128)S(1)}, f32[2,16,512]{2,1,0:T(8,128)S(1)}, u32[]{:S(2)}, u32[]{:S(2)}) collective-permute-start(f32[2,16,512]{2,1,0:T(8,128)S(1)} %maximum_select_fusion.1), channel_id=1, source_target_pairs={{0,8},{4,12},{8,0},{12,4},{16,24},{20,28},{24,16},{28,20},{1,9},{5... | collective-permute-start | bytes 196616 | tf_op jit(solution)/shard_map/ppermute | solution.py:434
  5.7 9.1 %collective-permute-start.46 = (f32[2,3,32,512]{3,2,1,0:T(8,128)S(1)}, f32[2,3,32,512]{3,2,1,0:T(8,128)S(1)}, u32[]{:S(2)}, u32[]{:S(2)}) collective-permute-start(f32[2,3,32,512]{3,2,1,0:T(8,128)S(1)} %fusion.1), channel_id=1, source_target_pairs={{0,4},{4,0},{8,12},{12,8},{16,20},{20,16},{24,28},{28,24},{1,5},{5... | collective-permute-start | bytes 1179656 | tf_op jit(solution)/shard_map/ppermute | solution.py:434
  8.6 6.1 %collective-permute-start.48 = (f32[4,16,512]{2,1,0:T(8,128)S(1)}, f32[4,16,512]{2,1,0:T(8,128)S(1)}, u32[]{:S(2)}, u32[]{:S(2)}) collective-permute-start(f32[4,16,512]{2,1,0:T(8,128)S(1)} %maximum_select_fusion), channel_id=1, source_target_pairs={{0,16},{4,20},{8,24},{12,28},{16,0},{20,4},{24,8},{28,12},{1,17},{... | collective-permute-start | bytes 393224 | tf_op jit(solution)/shard_map/ppermute | solution.py:434
  15.1 7.5 %collective-permute-start.25 = (f32[8,16,512]{2,1,0:T(8,128)S(1)}, f32[8,16,512]{2,1,0:T(8,128)S(1)}, u32[]{:S(2)}, u32[]{:S(2)}) collective-permute-start(f32[8,16,512]{2,1,0:T(8,128)S(1)} %broadcast_select_fusion.3.refs_0_), channel_id=1, source_target_pairs={{0,2},{1,3},{2,0},{3,1},{4,6},{5,7},{6,4},{7,5},{8,10},{9,11},{10,... | collective-permute-start | bytes 786440 | tf_op jit(solution)/shard_map/cond/branch_1_fun/ppermute | solution.py:434
  16.9 8.2 %collective-permute-start.23 = (f32[10,32,256]{2,1,0:T(8,128)S(1)}, f32[10,32,256]{2,1,0:T(8,128)S(1)}, u32[]{:S(2)}, u32[]{:S(2)}) collective-permute-start(f32[10,32,256]{2,1,0:T(8,128)S(1)} %branch_1_fun.6.refs_0_), channel_id=1, source_target_pairs={{0,4},{4,0},{8,12},{12,8},{16,20},{20,16},{24,28},{28,24},{1,5},{5... | collective-permute-start | bytes 983048 | tf_op jit(solution)/shard_map/cond/branch_1_fun/ppermute | solution.py:434
  18.2 7.7 %collective-permute-start.22 = (f32[10,32,256]{2,1,0:T(8,128)S(1)}, f32[10,32,256]{2,1,0:T(8,128)S(1)}, u32[]{:S(2)}, u32[]{:S(2)}) collective-permute-start(f32[10,32,256]{2,1,0:T(8,128)S(1)} %branch_1_fun.6.refs_0_), channel_id=1, source_target_pairs={{0,24},{4,28},{8,0},{12,4},{16,8},{20,12},{24,16},{28,20},{1,25},{... | collective-permute-start | bytes 983048 | tf_op jit(solution)/shard_map/cond/branch_1_fun/ppermute | solution.py:448
  19.2 5.9 %collective-permute-start.24 = (f32[8,16,512]{2,1,0:T(8,128)S(1)}, f32[8,16,512]{2,1,0:T(8,128)S(1)}, u32[]{:S(2)}, u32[]{:S(2)}) collective-permute-start(f32[8,16,512]{2,1,0:T(8,128)S(1)} %broadcast_select_fusion.3.refs_0_), channel_id=1, source_target_pairs={{0,1},{1,0},{2,3},{3,2},{4,5},{5,4},{6,7},{7,6},{8,9},{9,8},{10,11... | collective-permute-start | bytes 786440 | tf_op jit(solution)/shard_map/cond/branch_1_fun/ppermute | solution.py:434
  22.6 3.7 %collective-permute-start.26 = (f32[8,16,512]{2,1,0:T(8,128)S(1)}, f32[8,16,512]{2,1,0:T(8,128)S(1)}, u32[]{:S(2)}, u32[]{:S(2)}) collective-permute-start(f32[8,16,512]{2,1,0:T(8,128)S(1)} %collective-permute-done.25.refs_2_), channel_id=1, source_target_pairs={{0,1},{1,0},{2,3},{3,2},{4,5},{5,4},{6,7},{7,6},{8,9},{9,8},{10,11... | collective-permute-start | bytes 786440 | tf_op jit(solution)/shard_map/cond/branch_1_fun/ppermute | solution.py:434
  25.1 19.7 %collective-permute-start.28 = (f32[10,32,256]{2,1,0:T(8,128)S(1)}, f32[10,32,256]{2,1,0:T(8,128)S(1)}, u32[]{:S(2)}, u32[]{:S(2)}) collective-permute-start(f32[10,32,256]{2,1,0:T(8,128)S(1)} %branch_1_fun.6.refs_0_), channel_id=1, source_target_pairs={{0,16},{4,20},{8,24},{12,28},{16,0},{20,4},{24,8},{28,12},{1,17},{... | collective-permute-start | bytes 983048 | tf_op jit(solution)/shard_map/cond/branch_1_fun/ppermute | solution.py:448
  26.3 18.5 %collective-permute-start.27 = (f32[10,32,256]{2,1,0:T(8,128)S(1)}, f32[10,32,256]{2,1,0:T(8,128)S(1)}, u32[]{:S(2)}, u32[]{:S(2)}) collective-permute-start(f32[10,32,256]{2,1,0:T(8,128)S(1)} %collective-permute-done.22.refs_1_.refs_4_), channel_id=1, source_target_pairs={{0,4},{4,0},{8,12},{12,8},{16,20},{20,16},{24,28},{28,24},{1,5},{5... | collective-permute-start | bytes 983048 | tf_op jit(solution)/shard_map/cond/branch_1_fun/ppermute | solution.py:434
  46.8 12.3 %collective-permute-start.32 = (f32[2,6,32,256]{3,2,1,0:T(8,128)S(1)}, f32[2,6,32,256]{3,2,1,0:T(8,128)}, u32[]{:S(2)}, u32[]{:S(2)}) collective-permute-start(f32[2,6,32,256]{3,2,1,0:T(8,128)S(1)} %branch_1_fun.9), channel_id=1, source_target_pairs={{0,2},{1,3},{4,6},{5,7},{8,10},{9,11},{12,14},{13,15},{16,18},{17,... | collective-permute-start | bytes 1179656 | tf_op jit(solution)/shard_map/cond/branch_1_fun/ppermute | solution.py:459
  48.2 30.2 %copy-start.5 = (f32[3072,512]{1,0:T(8,128)S(1)}, f32[3072,512]{1,0:T(8,128)}, u32[]{:S(2)}) copy-start(f32[3072,512]{1,0:T(8,128)} %get-tuple-element.108.window_ref) | copy-start | bytes 18874372 | tf_op jit(solution)/shard_map/cond
  48.2 17.3 %collective-permute-start.29 = (f32[10,32,256]{2,1,0:T(8,128)S(1)}, f32[10,32,256]{2,1,0:T(8,128)S(1)}, u32[]{:S(2)}, u32[]{:S(2)}) collective-permute-start(f32[10,32,256]{2,1,0:T(8,128)S(1)} %branch_1_fun.6.refs_0_), channel_id=1, source_target_pairs={{0,8},{4,12},{8,16},{12,20},{16,24},{20,28},{24,0},{28,4},{1,9},{5... | collective-permute-start | bytes 983048 | tf_op jit(solution)/shard_map/cond/branch_1_fun/ppermute | solution.py:448
  48.5 17.0 %collective-permute-start.30 = (f32[10,32,256]{2,1,0:T(8,128)S(1)}, f32[10,32,256]{2,1,0:T(8,128)S(1)}, u32[]{:S(2)}, u32[]{:S(2)}) collective-permute-start(f32[10,32,256]{2,1,0:T(8,128)S(1)} %collective-permute-done.28.refs_2_.refs_8_), channel_id=1, source_target_pairs={{0,4},{4,0},{8,12},{12,8},{16,20},{20,16},{24,28},{28,24},{1,5},{5... | collective-permute-start | bytes 983048 | tf_op jit(solution)/shard_map/cond/branch_1_fun/ppermute | solution.py:434
  60.2 7.1 %collective-permute-start.34 = (f32[6,32,256]{2,1,0:T(8,128)S(1)}, f32[6,32,256]{2,1,0:T(8,128)S(1)}, u32[]{:S(2)}, u32[]{:S(2)}) collective-permute-start(f32[6,32,256]{2,1,0:T(8,128)S(1)} %get-tuple-element.119), channel_id=1, source_target_pairs={{0,4},{4,0},{8,12},{12,8},{16,20},{20,16},{24,28},{28,24},{1,5},{5... | collective-permute-start | bytes 589832 | tf_op jit(solution)/shard_map/cond/branch_1_fun/ppermute | solution.py:434
  60.5 7.1 %collective-permute-start.33 = (f32[6,32,256]{2,1,0:T(8,128)S(1)}, f32[6,32,256]{2,1,0:T(8,128)S(1)}, u32[]{:S(2)}, u32[]{:S(2)}) collective-permute-start(f32[6,32,256]{2,1,0:T(8,128)S(1)} %get-tuple-element.120.refs_0_), channel_id=1, source_target_pairs={{0,1},{1,0},{2,3},{3,2},{4,5},{5,4},{6,7},{7,6},{8,9},{9,8},{10,11... | collective-permute-start | bytes 589832 | tf_op jit(solution)/shard_map/cond/branch_1_fun/ppermute | solution.py:434
  65.5 9.4 %collective-permute-start.31 = (f32[10,32,256]{2,1,0:T(8,128)S(1)}, f32[10,32,256]{2,1,0:T(8,128)S(1)}, u32[]{:S(2)}, u32[]{:S(2)}) collective-permute-start(f32[10,32,256]{2,1,0:T(8,128)S(1)} %collective-permute-done.29.refs_12_), channel_id=1, source_target_pairs={{0,4},{4,0},{8,12},{12,8},{16,20},{20,16},{24,28},{28,24},{1,5},{5... | collective-permute-start | bytes 983048 | tf_op jit(solution)/shard_map/cond/branch_1_fun/ppermute | solution.py:434
  66.8 8.9 %collective-permute-start.37 = (f32[10,32,256]{2,1,0:T(8,128)S(1)}, f32[10,32,256]{2,1,0:T(8,128)S(1)}, u32[]{:S(2)}, u32[]{:S(2)}) collective-permute-start(f32[10,32,256]{2,1,0:T(8,128)S(1)} %collective-permute-done.23.refs_2_), channel_id=1, source_target_pairs={{0,1},{1,0},{2,3},{3,2},{4,5},{5,4},{6,7},{7,6},{8,9},{9,8},{10,11... | collective-permute-start | bytes 983048 | tf_op jit(solution)/shard_map/cond/branch_1_fun/ppermute | solution.py:434
  67.1 8.6 %collective-permute-start.39 = (f32[10,32,256]{2,1,0:T(8,128)S(1)}, f32[10,32,256]{2,1,0:T(8,128)S(1)}, u32[]{:S(2)}, u32[]{:S(2)}) collective-permute-start(f32[10,32,256]{2,1,0:T(8,128)S(1)} %collective-permute-done.27.refs_6_), channel_id=1, source_target_pairs={{0,1},{1,0},{2,3},{3,2},{4,5},{5,4},{6,7},{7,6},{8,9},{9,8},{10,11... | collective-permute-start | bytes 983048 | tf_op jit(solution)/shard_map/cond/branch_1_fun/ppermute | solution.py:434
  67.3 8.9 %collective-permute-start.38 = (f32[10,32,256]{2,1,0:T(8,128)S(1)}, f32[10,32,256]{2,1,0:T(8,128)S(1)}, u32[]{:S(2)}, u32[]{:S(2)}) collective-permute-start(f32[10,32,256]{2,1,0:T(8,128)S(1)} %collective-permute-done.22.refs_1_.refs_4_), channel_id=1, source_target_pairs={{0,1},{1,0},{2,3},{3,2},{4,5},{5,4},{6,7},{7,6},{8,9},{9,8},{10,11... | collective-permute-start | bytes 983048 | tf_op jit(solution)/shard_map/cond/branch_1_fun/ppermute | solution.py:434
  67.6 2.1 %collective-permute-start.35 = (f32[6,32,256]{2,1,0:T(8,128)S(1)}, f32[6,32,256]{2,1,0:T(8,128)S(1)}, u32[]{:S(2)}, u32[]{:S(2)}) collective-permute-start(f32[6,32,256]{2,1,0:T(8,128)S(1)} %collective-permute-done.34.refs_2_), channel_id=1, source_target_pairs={{0,1},{1,0},{2,3},{3,2},{4,5},{5,4},{6,7},{7,6},{8,9},{9,8},{10,11... | collective-permute-start | bytes 589832 | tf_op jit(solution)/shard_map/cond/branch_1_fun/ppermute | solution.py:434
  69.7 6.7 %collective-permute-start.36 = (f32[10,32,256]{2,1,0:T(8,128)S(1)}, f32[10,32,256]{2,1,0:T(8,128)S(1)}, u32[]{:S(2)}, u32[]{:S(2)}) collective-permute-start(f32[10,32,256]{2,1,0:T(8,128)S(1)} %branch_1_fun.6.refs_0_), channel_id=1, source_target_pairs={{0,1},{1,0},{2,3},{3,2},{4,5},{5,4},{6,7},{7,6},{8,9},{9,8},{10,11... | collective-permute-start | bytes 983048 | tf_op jit(solution)/shard_map/cond/branch_1_fun/ppermute | solution.py:434
  75.0 2.0 %collective-permute-start.40 = (f32[10,32,256]{2,1,0:T(8,128)S(1)}, f32[10,32,256]{2,1,0:T(8,128)S(1)}, u32[]{:S(2)}, u32[]{:S(2)}) collective-permute-start(f32[10,32,256]{2,1,0:T(8,128)S(1)} %collective-permute-done.28.refs_2_.refs_8_), channel_id=1, source_target_pairs={{0,1},{1,0},{2,3},{3,2},{4,5},{5,4},{6,7},{7,6},{8,9},{9,8},{10,11... | collective-permute-start | bytes 983048 | tf_op jit(solution)/shard_map/cond/branch_1_fun/ppermute | solution.py:434
  75.7 2.2 %collective-permute-start.42 = (f32[10,32,256]{2,1,0:T(8,128)S(1)}, f32[10,32,256]{2,1,0:T(8,128)S(1)}, u32[]{:S(2)}, u32[]{:S(2)}) collective-permute-start(f32[10,32,256]{2,1,0:T(8,128)S(1)} %collective-permute-done.29.refs_12_), channel_id=1, source_target_pairs={{0,1},{1,0},{2,3},{3,2},{4,5},{5,4},{6,7},{7,6},{8,9},{9,8},{10,11... | collective-permute-start | bytes 983048 | tf_op jit(solution)/shard_map/cond/branch_1_fun/ppermute | solution.py:434
  75.7 2.2 %collective-permute-start.41 = (f32[10,32,256]{2,1,0:T(8,128)S(1)}, f32[10,32,256]{2,1,0:T(8,128)S(1)}, u32[]{:S(2)}, u32[]{:S(2)}) collective-permute-start(f32[10,32,256]{2,1,0:T(8,128)S(1)} %collective-permute-done.30.refs_10_), channel_id=1, source_target_pairs={{0,1},{1,0},{2,3},{3,2},{4,5},{5,4},{6,7},{7,6},{8,9},{9,8},{10,11... | collective-permute-start | bytes 983048 | tf_op jit(solution)/shard_map/cond/branch_1_fun/ppermute | solution.py:434
  76.3 2.1 %collective-permute-start.43 = (f32[10,32,256]{2,1,0:T(8,128)S(1)}, f32[10,32,256]{2,1,0:T(8,128)S(1)}, u32[]{:S(2)}, u32[]{:S(2)}) collective-permute-start(f32[10,32,256]{2,1,0:T(8,128)S(1)} %collective-permute-done.31.refs_14_), channel_id=1, source_target_pairs={{0,1},{1,0},{2,3},{3,2},{4,5},{5,4},{6,7},{7,6},{8,9},{9,8},{10,11... | collective-permute-start | bytes 983048 | tf_op jit(solution)/shard_map/cond/branch_1_fun/ppermute | solution.py:434
